TPU v7x, 32 devices: a whole 2x2x4 slice. The times are simulated.
32 devices in a mesh: dp: 2 (over y), blk: 16 (over z, x, core).
Axes of the slice: x: 2, y: 2, z: 4, core: 2. Of those that a mesh axis runs over, the one named last changes fastest.
Arguments:
- residues: bfloat16 [4, 2048, 768], P('dp', 'blk'), may hold values from -6 to 6
- coordinates: bfloat16 [4, 3, 2048], P('dp', None, 'blk'), may hold values from -48 to 48
- segment_ids: int32 [4, 2048], P('dp', 'blk'), may hold values from 0 to 2, as said below
- time_steps: int32 [4, 3], P('dp'), may hold values from 0 to 999
- time_weight: bfloat16 [768, 768], P('dp'), may hold values from -0.21875 to 0.21875
- norm1_gain: bfloat16 [768], P('dp'), may hold values from 0.099609375 to 1.8984375
- norm1_bias: bfloat16 [768], P('dp'), may hold values from -1.5 to 1.5
- qkv_weight: bfloat16 [768, 2304], P('dp'), may hold values from -0.21875 to 0.21875
- bias_weight: bfloat16 [128, 32], P('dp'), may hold values from -3 to 3
- out_weight: bfloat16 [768, 768], P('dp'), may hold values from -1.25 to 1.25
- norm2_gain: bfloat16 [768], P('dp'), may hold values from 0.099609375 to 1.8984375
- norm2_bias: bfloat16 [768], P('dp'), may hold values from -1.5 to 1.5
- up_weight: bfloat16 [768, 3072], P('dp'), may hold values from -0.21875 to 0.21875
- down_weight: bfloat16 [3072, 768], P('dp'), may hold values from -0.109375 to 0.109375
- force_weight: bfloat16 [3, 768], P(None, 'dp'), may hold values from -0.21875 to 0.21875
- out_cotangent: bfloat16 [4, 2048, 768], P('dp', 'blk'), may hold values from -6 to 6
- force_cotangent: float32 [4, 3, 2048], P('dp', None, 'blk'), may hold values from -6 to 6
Outputs:
- block_out: bfloat16 [4, 2048, 768], P('dp', 'blk')
- forces: float32 [4, 3, 2048], P('dp', None, 'blk')
- residues_grad: float32 [4, 2048, 768], P('dp', 'blk')
- time_weight_grad: float32 [768, 768], P('dp')
- norm1_gain_grad: float32 [768], P('dp')
- norm1_bias_grad: float32 [768], P('dp')
- qkv_weight_grad: float32 [768, 2304], P('dp')
- bias_weight_grad: float32 [128, 32], P('dp')
- out_weight_grad: float32 [768, 768], P('dp')
- norm2_gain_grad: float32 [768], P('dp')
- norm2_bias_grad: float32 [768], P('dp')
- up_weight_grad: float32 [768, 3072], P('dp')
- down_weight_grad: float32 [3072, 768], P('dp')
- force_weight_grad: float32 [3, 768], P(None, 'dp')
Inputs may be any that keep to these rules, and one draw needn't show every extreme that they name: `segment_ids`: each packed row holds proteins 0, 1 and 2 in that order, each one nonempty run of residues; protein 1 begins within the row's first 128 residues and ends within its last 128.
All inputs are finite; a program needn't handle non-finite values.
Results may differ from a plain program's by a relative error of at most 0.02.
Values may be sent and summed in bfloat16 or wider, within the bound.
No kernel may reach another device: no remote copies, remote signals or barrier semaphores. Data moves between devices by JAX's collectives and lax.ppermute only.
A program may use at most 256 MiB of HBM per device.

v0:
```python
import jax
import jax.numpy as jnp
from jax import lax
from jax.sharding import PartitionSpec as P

D = 768
HEADS = 32
HEAD_DIM = 24
KERNELS = 128


eps = 1e-05
cutoff = 24.0
masked_value = -1e30
key_block = 512
highest = lax.Precision.HIGHEST


def layer_norm(values, norm_gain, norm_shift):
    centred = values - jnp.mean(values, axis=-1, keepdims=True)
    spread = jnp.mean(centred * centred, axis=-1, keepdims=True)
    return centred * lax.rsqrt(spread + eps) * norm_gain + norm_shift


def exact_gelu(values):
    return jax.nn.gelu(values, approximate=False)


def time_features(stamps, feature_width):
    half_width = feature_width // 2
    frequency = jnp.exp(-jnp.log(10000.0) * jnp.arange(half_width, dtype=jnp.float32) / half_width)
    angles = stamps[:, None] * frequency[None, :]
    return jnp.concatenate([jnp.sin(angles), jnp.cos(angles)], axis=1)


def kernel_table(distance, kernel_count):
    centres = jnp.arange(kernel_count, dtype=jnp.float32) * (cutoff / kernel_count)
    scaled = (distance[..., None] - centres) * (kernel_count / (2.0 * cutoff))
    return jnp.exp(-0.5 * scaled * scaled)


def distances(query_points, key_points):
    squared = jnp.zeros((query_points.shape[0], key_points.shape[0]), jnp.float32)
    for component in range(3):
        offset = query_points[:, component][:, None] - key_points[:, component][None, :]
        squared = squared + offset * offset
    return jnp.sqrt(squared)


def fold_blocks(update, state, piece):
    key_count = piece[0].shape[0]
    parts_count = key_count // key_block
    stacked = tuple(
        (member.reshape((parts_count, key_block) + member.shape[1:]) for member in piece)
    )
    offsets = key_block * jnp.arange(parts_count, dtype=jnp.int32)

    def advance(inner, items):
        return (update(inner, items[0], items[1]), None)

    state, unused = lax.scan(advance, state, (stacked, offsets))
    return state


def run_micro(weights, residue_rows, coord_rows, segment_rows, step_rows, out_cot, force_cot):
    (
        time_full,
        gain_one,
        shift_one,
        qkv_full,
        bias_full,
        out_full,
        gain_two,
        shift_two,
        up_full,
        down_full,
        force_full,
    ) = weights
    row_count = residue_rows.shape[0]
    score_scale = 1.0 / HEAD_DIM**0.5
    choose = (
        segment_rows[:, None] == jnp.arange(step_rows.shape[0], dtype=jnp.int32)[None, :]
    ).astype(jnp.float32)
    stamps = jnp.dot(choose, step_rows.astype(jnp.float32), precision=highest)
    features = time_features(stamps, D).astype(jnp.bfloat16)
    first = residue_rows.astype(jnp.float32) + jnp.dot(
        features, time_full, preferred_element_type=jnp.float32
    )
    normed, norm_one_back = jax.vjp(
        layer_norm, first, gain_one.astype(jnp.float32), shift_one.astype(jnp.float32)
    )
    normed_low = normed.astype(jnp.bfloat16)
    projected = jnp.dot(normed_low, qkv_full, preferred_element_type=jnp.float32).astype(
        jnp.bfloat16
    )
    query_heads = projected[:, :D].reshape(row_count, HEADS, HEAD_DIM)
    pair_low = projected[:, D:]
    query_points = jnp.transpose(coord_rows).astype(jnp.float32)
    query_segments = (segment_rows + 1).astype(jnp.float32)
    where_rows = jnp.concatenate(
        [jnp.transpose(coord_rows), (segment_rows + 1).astype(jnp.bfloat16)[:, None]], axis=1
    )

    def score_parts(pair_rows, where_block):
        key_heads = pair_rows[:, :D].reshape(-1, HEADS, HEAD_DIM)
        value_heads = pair_rows[:, D:].reshape(-1, HEADS, HEAD_DIM)
        kernels = kernel_table(
            distances(query_points, where_block[:, :3].astype(jnp.float32)), KERNELS
        ).astype(jnp.bfloat16)
        pair_bias = jnp.einsum(
            "qkc,ch->hqk", kernels, bias_full, preferred_element_type=jnp.float32
        )
        logits = (
            jnp.einsum("qhd,khd->hqk", query_heads, key_heads, preferred_element_type=jnp.float32)
            * score_scale
            + pair_bias
        )
        matches = (query_segments[:, None] == where_block[:, 3].astype(jnp.float32)[None, :])[None]
        return (key_heads, value_heads, kernels, logits, matches)

    def forward_update(state, block, offset):
        run_max, run_sum, run_acc = state
        key_heads, value_heads, kernels, logits, matches = score_parts(block[0], block[1])
        new_max = jnp.maximum(run_max, jnp.max(jnp.where(matches, logits, masked_value), axis=2))
        weights_now = jnp.where(matches, jnp.exp(logits - new_max[:, :, None]), 0.0)
        factor = jnp.exp(run_max - new_max)
        run_sum = run_sum * factor + jnp.sum(weights_now, axis=2)
        mixed = jnp.einsum(
            "hqk,khd->qhd",
            weights_now.astype(jnp.bfloat16),
            value_heads,
            preferred_element_type=jnp.float32,
        )
        run_acc = run_acc * jnp.transpose(factor)[:, :, None] + mixed
        return (new_max, run_sum, run_acc)

    start_state = (
        jnp.full((HEADS, row_count), masked_value, jnp.float32),
        jnp.zeros((HEADS, row_count), jnp.float32),
        jnp.zeros((row_count, HEADS, HEAD_DIM), jnp.float32),
    )
    forward_state = fold_blocks(
        forward_update,
        start_state,
        (
            lax.all_gather(pair_low, "blk", axis=0, tiled=True),
            lax.all_gather(where_rows, "blk", axis=0, tiled=True),
        ),
    )
    run_max, run_sum, run_acc = forward_state
    attended = run_acc / jnp.transpose(run_sum)[:, :, None]
    log_total = run_max + jnp.log(run_sum)
    attended_low = attended.reshape(row_count, D).astype(jnp.bfloat16)
    second = first + jnp.dot(attended_low, out_full, preferred_element_type=jnp.float32)
    normed_two, norm_two_back = jax.vjp(
        layer_norm, second, gain_two.astype(jnp.float32), shift_two.astype(jnp.float32)
    )
    normed_two_low = normed_two.astype(jnp.bfloat16)
    hidden = jnp.dot(normed_two_low, up_full, preferred_element_type=jnp.float32)
    activated, gelu_back = jax.vjp(exact_gelu, hidden)
    activated_low = activated.astype(jnp.bfloat16)
    third = second + jnp.dot(activated_low, down_full, preferred_element_type=jnp.float32)
    block_low = third.astype(jnp.bfloat16)
    forces = jnp.einsum("cd,qd->cq", force_full, block_low, preferred_element_type=jnp.float32)
    third_grad = out_cot.astype(jnp.float32) + jnp.einsum(
        "cq,cd->qd", force_cot, force_full.astype(jnp.float32), precision=highest
    )
    force_grad = jnp.einsum(
        "cq,qd->cd", force_cot, block_low.astype(jnp.float32), precision=highest
    )
    third_low = third_grad.astype(jnp.bfloat16)
    down_grad = jnp.einsum(
        "qf,qd->fd", activated_low, third_low, preferred_element_type=jnp.float32
    )
    activated_grad = jnp.einsum(
        "qd,fd->qf", third_low, down_full, preferred_element_type=jnp.float32
    )
    hidden_grad = gelu_back(activated_grad)[0].astype(jnp.bfloat16)
    up_grad = jnp.einsum(
        "qd,qf->df", normed_two_low, hidden_grad, preferred_element_type=jnp.float32
    )
    normed_two_grad = jnp.einsum(
        "qf,df->qd", hidden_grad, up_full, preferred_element_type=jnp.float32
    )
    second_part, gain_two_grad, shift_two_grad = norm_two_back(normed_two_grad)
    second_grad = third_grad + second_part
    second_low = second_grad.astype(jnp.bfloat16)
    out_weight_grad = jnp.einsum(
        "qa,qd->ad", attended_low, second_low, preferred_element_type=jnp.float32
    )
    attended_grad = jnp.einsum(
        "qd,ad->qa", second_low, out_full, preferred_element_type=jnp.float32
    ).astype(jnp.bfloat16)
    grad_heads = attended_grad.reshape(row_count, HEADS, HEAD_DIM)
    delta = jnp.transpose(jnp.sum(grad_heads.astype(jnp.float32) * attended, axis=2))

    def block_grads(block):
        key_heads, value_heads, kernels, logits, matches = score_parts(block[0], block[1])
        probs = jnp.where(matches, jnp.exp(logits - log_total[:, :, None]), 0.0)
        prob_grad = jnp.einsum(
            "qhd,khd->hqk", grad_heads, value_heads, preferred_element_type=jnp.float32
        )
        logit_grad = (probs * (prob_grad - delta[:, :, None])).astype(jnp.bfloat16)
        query_add = (
            jnp.einsum("hqk,khd->qhd", logit_grad, key_heads, preferred_element_type=jnp.float32)
            * score_scale
        )
        bias_add = jnp.einsum(
            "qkc,hqk->ch", kernels, logit_grad, preferred_element_type=jnp.float32
        )
        key_part = (
            jnp.einsum("hqk,qhd->khd", logit_grad, query_heads, preferred_element_type=jnp.float32)
            * score_scale
        )
        value_part = jnp.einsum(
            "hqk,qhd->khd",
            probs.astype(jnp.bfloat16),
            grad_heads,
            preferred_element_type=jnp.float32,
        )
        key_total = key_part.shape[0]
        joined = jnp.concatenate(
            [key_part.reshape(key_total, D), value_part.reshape(key_total, D)], axis=1
        )
        return (query_add, bias_add, joined)

    def backward_update(state, block, offset):
        query_grad, bias_grad, pair_grad = state
        query_add, bias_add, joined = block_grads(block)
        current = lax.dynamic_slice_in_dim(pair_grad, offset, joined.shape[0], 0)
        pair_grad = lax.dynamic_update_slice_in_dim(pair_grad, current + joined, offset, 0)
        return (query_grad + query_add, bias_grad + bias_add, pair_grad)

    back_state = (
        jnp.zeros((row_count, HEADS, HEAD_DIM), jnp.float32),
        jnp.zeros((KERNELS, HEADS), jnp.float32),
        jnp.zeros((row_count * lax.axis_size("blk"), 2 * D), jnp.float32),
    )
    query_grad, bias_grad, pair_grad = fold_blocks(
        backward_update,
        back_state,
        (
            lax.all_gather(pair_low, "blk", axis=0, tiled=True),
            lax.all_gather(where_rows, "blk", axis=0, tiled=True),
        ),
    )
    pair_local = lax.psum_scatter(
        pair_grad.astype(jnp.bfloat16), "blk", scatter_dimension=0, tiled=True
    ).astype(jnp.float32)
    projected_grad = jnp.concatenate([query_grad.reshape(row_count, D), pair_local], axis=1).astype(
        jnp.bfloat16
    )
    qkv_grad = jnp.einsum(
        "qd,qe->de", normed_low, projected_grad, preferred_element_type=jnp.float32
    )
    normed_grad = jnp.einsum(
        "qe,de->qd", projected_grad, qkv_full, preferred_element_type=jnp.float32
    )
    first_part, gain_one_grad, shift_one_grad = norm_one_back(normed_grad)
    first_grad = second_grad + first_part
    time_grad = jnp.einsum(
        "qd,qe->de", features, first_grad.astype(jnp.bfloat16), preferred_element_type=jnp.float32
    )
    grads_local = (
        time_grad,
        gain_one_grad,
        shift_one_grad,
        qkv_grad,
        bias_grad,
        out_weight_grad,
        gain_two_grad,
        shift_two_grad,
        up_grad,
        down_grad,
        force_grad,
    )
    return (block_low, forces, first_grad, grads_local)


def body(
    residues,
    coordinates,
    segment_ids,
    time_steps,
    time_weight,
    norm1_gain,
    norm1_bias,
    qkv_weight,
    bias_weight,
    out_weight,
    norm2_gain,
    norm2_bias,
    up_weight,
    down_weight,
    force_weight,
    out_cotangent,
    force_cotangent,
):
    micro_count = residues.shape[0]
    block_list = []
    force_list = []
    residue_list = []
    totals = None
    for micro_index in range(micro_count):
        gathered = (
            lax.all_gather(time_weight, "dp", axis=0, tiled=True),
            lax.all_gather(norm1_gain, "dp", axis=0, tiled=True),
            lax.all_gather(norm1_bias, "dp", axis=0, tiled=True),
            lax.all_gather(qkv_weight, "dp", axis=0, tiled=True),
            lax.all_gather(bias_weight, "dp", axis=0, tiled=True),
            lax.all_gather(out_weight, "dp", axis=0, tiled=True),
            lax.all_gather(norm2_gain, "dp", axis=0, tiled=True),
            lax.all_gather(norm2_bias, "dp", axis=0, tiled=True),
            lax.all_gather(up_weight, "dp", axis=0, tiled=True),
            lax.all_gather(down_weight, "dp", axis=0, tiled=True),
            lax.all_gather(force_weight, "dp", axis=1, tiled=True),
        )
        block_low, forces, residue_grad, local = run_micro(
            gathered,
            residues[micro_index],
            coordinates[micro_index],
            segment_ids[micro_index],
            time_steps[micro_index],
            out_cotangent[micro_index],
            force_cotangent[micro_index],
        )
        block_list.append(block_low)
        force_list.append(forces)
        residue_list.append(residue_grad)
        shard_sums = (
            lax.psum_scatter(
                local[0].astype(jnp.bfloat16), "dp", scatter_dimension=0, tiled=True
            ).astype(jnp.float32),
            lax.psum_scatter(
                local[1].astype(jnp.bfloat16), "dp", scatter_dimension=0, tiled=True
            ).astype(jnp.float32),
            lax.psum_scatter(
                local[2].astype(jnp.bfloat16), "dp", scatter_dimension=0, tiled=True
            ).astype(jnp.float32),
            lax.psum_scatter(
                local[3].astype(jnp.bfloat16), "dp", scatter_dimension=0, tiled=True
            ).astype(jnp.float32),
            lax.psum_scatter(
                local[4].astype(jnp.bfloat16), "dp", scatter_dimension=0, tiled=True
            ).astype(jnp.float32),
            lax.psum_scatter(
                local[5].astype(jnp.bfloat16), "dp", scatter_dimension=0, tiled=True
            ).astype(jnp.float32),
            lax.psum_scatter(
                local[6].astype(jnp.bfloat16), "dp", scatter_dimension=0, tiled=True
            ).astype(jnp.float32),
            lax.psum_scatter(
                local[7].astype(jnp.bfloat16), "dp", scatter_dimension=0, tiled=True
            ).astype(jnp.float32),
            lax.psum_scatter(
                local[8].astype(jnp.bfloat16), "dp", scatter_dimension=0, tiled=True
            ).astype(jnp.float32),
            lax.psum_scatter(
                local[9].astype(jnp.bfloat16), "dp", scatter_dimension=0, tiled=True
            ).astype(jnp.float32),
            lax.psum_scatter(
                local[10].astype(jnp.bfloat16), "dp", scatter_dimension=1, tiled=True
            ).astype(jnp.float32),
        )
        totals = (
            shard_sums
            if micro_index == 0
            else tuple((earlier + later for earlier, later in zip(totals, shard_sums)))
        )
    summed = (
        lax.psum(totals[0].astype(jnp.bfloat16), "blk").astype(jnp.float32),
        lax.psum(totals[1].astype(jnp.bfloat16), "blk").astype(jnp.float32),
        lax.psum(totals[2].astype(jnp.bfloat16), "blk").astype(jnp.float32),
        lax.psum(totals[3].astype(jnp.bfloat16), "blk").astype(jnp.float32),
        lax.psum(totals[4].astype(jnp.bfloat16), "blk").astype(jnp.float32),
        lax.psum(totals[5].astype(jnp.bfloat16), "blk").astype(jnp.float32),
        lax.psum(totals[6].astype(jnp.bfloat16), "blk").astype(jnp.float32),
        lax.psum(totals[7].astype(jnp.bfloat16), "blk").astype(jnp.float32),
        lax.psum(totals[8].astype(jnp.bfloat16), "blk").astype(jnp.float32),
        lax.psum(totals[9].astype(jnp.bfloat16), "blk").astype(jnp.float32),
        lax.psum(totals[10].astype(jnp.bfloat16), "blk").astype(jnp.float32),
    )
    return (
        jnp.stack(block_list),
        jnp.stack(force_list),
        jnp.stack(residue_list),
        summed[0],
        summed[1],
        summed[2],
        summed[3],
        summed[4],
        summed[5],
        summed[6],
        summed[7],
        summed[8],
        summed[9],
        summed[10],
    )


def solution(mesh):
    return jax.shard_map(
        body,
        mesh=mesh,
        in_specs=(
            P("dp", "blk", None),
            P("dp", None, "blk"),
            P("dp", "blk"),
            P("dp", None),
            P("dp", None),
            P("dp"),
            P("dp"),
            P("dp", None),
            P("dp", None),
            P("dp", None),
            P("dp"),
            P("dp"),
            P("dp", None),
            P("dp", None),
            P(None, "dp"),
            P("dp", "blk", None),
            P("dp", None, "blk"),
        ),
        out_specs=(
            P("dp", "blk", None),
            P("dp", None, "blk"),
            P("dp", "blk", None),
            P("dp", None),
            P("dp"),
            P("dp"),
            P("dp", None),
            P("dp", None),
            P("dp", None),
            P("dp"),
            P("dp"),
            P("dp", None),
            P("dp", None),
            P(None, "dp"),
        ),
        check_vma=False,
    )
```

profile of v0, /device:TPU:1, one launch (start us, length us, event | category | flops | bytes accessed | tf_op | source)
XLA Modules:
  0.0 1902.4 jit_solution(13853155049392501133)
XLA Ops:
  19.1 15.3 all-gather.13.cloned.1.call-done
  36.4 49.0 %all-gather.15.cloned.1.call-done = bf16[768,2304]{1,0:T(8,128)(2,1)} async-done(((bf16[384,2304]{1,0:T(8,128)(2,1)}), bf16[768,2304]{1,0:T(8,128)(2,1)}) %all-gather.15.cloned.1.call-update) | async-done | bytes 3538960 | tf_op jit(solution)/shard_map/all_gather | solution.py:309
  111.4 25.6 %all_gather.72 = bf16[2048,4]{0,1:T(4,128)(2,1)} all-gather(bf16[128,4]{0,1:T(4,128)(2,1)S(1)} %pad_maximum_fusion.16), channel_id=1, replica_groups=mesh['dp'=2,'blk'=16] {'blk'}, dimensions={0}, use_global_device_ids=true | all-gather | bytes 17408 | tf_op jit(solution)/shard_map/all_gather | solution.py:147
  137.0 18.4 all_gather.61
  162.9 8.7 copy.133
  171.5 163.6 %while.68 = (s32[]{:T(128)}, f32[32,128]{1,0:T(8,128)S(1)}, f32[32,128]{1,0:T(8,128)S(1)}, f32[128,32,24]{0,2,1:T(8,128)S(1)}, f32[128]{0:T(128)}, /*index=5*/bf...) while((s32[]{:T(128)}, f32[32,128]{1,0:T(8,128)S(1)}, ...), condition=%wide.region_5.6_spmd.clone, body=%wide.region_2.5_spmd.clone.sunk | while | flops 802023552 | bytes 68671632 | solution.py:61
  175.7 17.9 fusion.340
  193.6 10.1 copy.206
  216.4 17.9 fusion.340
  234.3 10.0 copy.206
  258.0 17.9 fusion.340
  275.9 10.0 copy.206
  298.6 17.9 fusion.340
  316.5 10.1 copy.206
  344.5 163.2 %while.69 = (s32[]{:T(128)}, f32[32,128]{1,0:T(8,128)S(1)}, f32[32,128]{1,0:T(8,128)S(1)}, f32[128,32,24]{0,2,1:T(8,128)S(1)}, f32[128]{0:T(128)}, /*index=5*/bf...) while((s32[]{:T(128)}, f32[32,128]{1,0:T(8,128)S(1)}, ...), condition=%wide.region_13.14_spmd.clone, body=%wide.region_10.13_spmd.clone.sunk | while | flops 802023552 | bytes 68671632 | solution.py:61
  349.2 17.9 fusion.353
  367.2 10.0 copy.207
  389.9 17.9 fusion.353
  407.8 10.0 copy.207
  430.6 17.9 fusion.353
  448.5 10.0 copy.207
  471.2 17.9 fusion.353
  489.2 10.0 copy.207
  550.0 265.0 %while.71 = (s32[]{:T(128)}, f32[128,32,24]{0,2,1:T(8,128)}, f32[128,32]{0,1:T(8,128)}, f32[2048,1536]{0,1:T(8,128)}, bf16[4,512,1536]{1,2,0:T(8,128)(2,1)}, /*i...) while((s32[]{:T(128)}, f32[128,32,24]{0,2,1:T(8,128)}, ...), condition=%wide.region_28.29_spmd.clone, body=%wide.region_27.28_spmd.clone.sunk | while | flops 1680582784 | bytes 88857312 | solution.py:61
  557.5 10.3 fusion.397
  581.0 13.9 fusion.401
  600.4 15.2 dynamic_update_slice.17
  622.8 10.3 fusion.397
  647.3 14.6 fusion.401
  667.4 15.1 dynamic_update_slice.17
  689.7 10.3 fusion.397
  714.2 14.6 fusion.401
  734.3 15.1 dynamic_update_slice.17
  756.6 10.3 fusion.397
  781.1 14.6 fusion.401
  801.0 14.0 dynamic_update_slice.17
  838.1 279.5 %while.70 = (s32[]{:T(128)}, f32[128,32,24]{0,2,1:T(8,128)}, f32[128,32]{0,1:T(8,128)}, f32[2048,1536]{0,1:T(8,128)}, bf16[4,512,1536]{1,2,0:T(8,128)(2,1)}, /*i...) while((s32[]{:T(128)}, f32[128,32,24]{0,2,1:T(8,128)}, ...), condition=%wide.region_20.21_spmd.clone, body=%wide.region_19.20_spmd.clone.sunk | while | flops 1680582784 | bytes 88857312 | solution.py:61
  858.8 10.3 fusion.375
  882.3 13.9 fusion.379
  901.9 15.2 dynamic_update_slice.16
  924.6 10.3 fusion.375
  949.1 14.6 fusion.379
  969.1 15.1 dynamic_update_slice.16
  991.7 10.3 fusion.375
  1016.2 14.6 fusion.379
  1036.3 15.1 dynamic_update_slice.16
  1058.9 10.3 fusion.375
  1083.4 14.6 fusion.379
  1103.2 14.0 dynamic_update_slice.16
  1162.7 55.1 %reduce-scatter.49.cloned.1.call-done = bf16[128,1536]{1,0:T(8,128)(2,1)} async-done(((bf16[2048,1536]{1,0:T(8,128)(2,1)}), bf16[128,1536]{1,0:T(8,128)(2,1)}) %reduce-scatter.49.cloned.1.call-update) | async-done | bytes 393232
  1249.7 16.1 reduce-scatter.37.cloned.1.call-done
  1268.0 60.6 %reduce-scatter.43.cloned.1.call-done = bf16[384,3072]{1,0:T(8,128)(2,1)} async-done(((bf16[768,3072]{1,0:T(8,128)(2,1)}), bf16[384,3072]{1,0:T(8,128)(2,1)}) %reduce-scatter.43.cloned.1.call-update) | async-done | bytes 2359312 | tf_op jit(solution)/shard_map/reduce_scatter | solution.py:355
  1328.6 63.0 %reduce-scatter.41.cloned.1.call-done = bf16[384,3072]{1,0:T(8,128)(2,1)} async-done(((bf16[768,3072]{1,0:T(8,128)(2,1)}), bf16[384,3072]{1,0:T(8,128)(2,1)}) %reduce-scatter.41.cloned.1.call-update) | async-done | bytes 2359312 | tf_op jit(solution)/shard_map/reduce_scatter | solution.py:355
  1396.3 57.5 %reduce-scatter.45.cloned.1.call-done = bf16[1536,768]{1,0:T(8,128)(2,1)} async-done(((bf16[3072,768]{1,0:T(8,128)(2,1)}), bf16[1536,768]{1,0:T(8,128)(2,1)}) %reduce-scatter.45.cloned.1.call-update) | async-done | bytes 2359312 | tf_op jit(solution)/shard_map/reduce_scatter | solution.py:358
  1453.8 62.3 %reduce-scatter.47.cloned.1.call-done = bf16[1536,768]{1,0:T(8,128)(2,1)} async-done(((bf16[3072,768]{1,0:T(8,128)(2,1)}), bf16[1536,768]{1,0:T(8,128)(2,1)}) %reduce-scatter.47.cloned.1.call-update) | async-done | bytes 2359312 | tf_op jit(solution)/shard_map/reduce_scatter | solution.py:358
  1520.4 20.1 %reduce-scatter.31.cloned.1.call-done = bf16[384,768]{1,0:T(8,128)(2,1)} async-done(((bf16[768,768]{1,0:T(8,128)(2,1)}), bf16[384,768]{1,0:T(8,128)(2,1)}) %reduce-scatter.31.cloned.1.call-update) | async-done | bytes 589840 | tf_op jit(solution)/shard_map/reduce_scatter | solution.py:331
  1540.5 24.5 %reduce-scatter.29.cloned.1.call-done = bf16[384,768]{1,0:T(8,128)(2,1)} async-done(((bf16[768,768]{1,0:T(8,128)(2,1)}), bf16[384,768]{1,0:T(8,128)(2,1)}) %reduce-scatter.29.cloned.1.call-update) | async-done | bytes 589840 | tf_op jit(solution)/shard_map/reduce_scatter | solution.py:331
  1567.3 48.2 %reduce-scatter.35.cloned.1.call-done = bf16[384,2304]{1,0:T(8,128)(2,1)} async-done(((bf16[768,2304]{1,0:T(8,128)(2,1)}), bf16[384,2304]{1,0:T(8,128)(2,1)}) %reduce-scatter.35.cloned.1.call-update) | async-done | bytes 1769488 | tf_op jit(solution)/shard_map/reduce_scatter | solution.py:340
  1615.4 50.1 %reduce-scatter.33.cloned.1.call-done = bf16[384,2304]{1,0:T(8,128)(2,1)} async-done(((bf16[768,2304]{1,0:T(8,128)(2,1)}), bf16[384,2304]{1,0:T(8,128)(2,1)}) %reduce-scatter.33.cloned.1.call-update) | async-done | bytes 1769488 | tf_op jit(solution)/shard_map/reduce_scatter | solution.py:340
  1679.5 12.8 reduce-scatter.59.cloned.1.call-done
  1693.3 10.6 reduce-scatter.55.cloned.1.call-done
  1704.7 11.3 reduce-scatter.53.cloned.1.call-done
  1722.1 60.3 %all-reduce.8 = (bf16[384]{0:T(512)(128)(2,1)S(1)}, bf16[384]{0:T(512)(128)(2,1)S(1)}, bf16[64,32]{0,1:T(8,128)(2,1)S(1)}, bf16[384]{0:T(512)(128)(2,1)S(1)}, bf...) all-reduce(bf16[384]{0:T(512)(128)(2,1)S(1)} %add_convert_fusion.16, ...), channel_id=1, replica_groups=mesh['dp'=2,'blk'=16] {'blk'}, use_global_device_ids=true, to_apply=%region_39.40 | all-reduce | flops 4736 | bytes 18944 | tf_op jit(solution)/shard_map/psum | solution.py:372
  1787.1 95.7 %all-reduce.13.cloned.1.call-done = (bf16[384,768]{1,0:T(8,128)(2,1)}, bf16[384,2304]{1,0:T(8,128)(2,1)}, bf16[384,768]{1,0:T(8,128)(2,1)}, bf16[384,3072]{1,0:T(8,128)(2,1)}, bf16[1536,768]{1,0:T(8,128)(2,1)}) async-done(((bf16[384,768]{1,0:T(8,128)(2,1)}, bf16[384,2304]{1,0:T(8,128)(2,1)}, bf16[384,768]{1,0:T(8,128)(2,1)}, bf16[384,3072]{1,0:T(8,128)(2,1)}, bf16[1536,768]{1,0:T(8,128)(2,1)}), ...) | async-done | bytes 7667728 | tf_op jit(solution)/shard_map/psum | solution.py:371
  (767 shorter events, 549.5 us)
Async XLA Ops:
  7.2 27.3 %copy-start.79 = (bf16[2,128,768]{2,1,0:T(8,128)(2,1)S(1)}, bf16[2,128,768]{2,1,0:T(8,128)(2,1)}, u32[]{:S(2)}) copy-start(bf16[2,128,768]{2,1,0:T(8,128)(2,1)} %param.25) | copy-start | bytes 1179652
  7.2 27.3 %all-gather.13.cloned.1.call-start = ((), (), s32[]{:S(2)}) async-start(), calls=%async_computation.16 | async-start | bytes 1769472 | tf_op jit(solution)/shard_map/all_gather | solution.py:306
  8.0 77.5 %all-gather.15.cloned.1.call-start = ((), (), s32[]{:S(2)}) async-start(), calls=%async_computation.17 | async-start | bytes 5308416 | tf_op jit(solution)/shard_map/all_gather | solution.py:309
  8.7 154.2 %all-gather.17.cloned.1.call-start = ((), (), s32[]{:S(2)}) async-start(), calls=%async_computation.18 | async-start | bytes 6684672 | tf_op jit(solution)/shard_map/all_gather | solution.py:146
  12.6 80.2 %copy-start.85 = (f32[768]{0:T(1024)}, f32[768]{0:T(1024)S(1)}, u32[]{:S(2)}) copy-start(f32[768]{0:T(1024)S(1)} %reshape.973) | copy-start | bytes 9220
  15.8 76.9 %copy-start.87 = (f32[768]{0:T(1024)}, f32[768]{0:T(1024)S(1)}, u32[]{:S(2)}) copy-start(f32[768]{0:T(1024)S(1)} %reshape.974) | copy-start | bytes 9220
  19.1 66.3 %copy-start.68 = (bf16[128,384]{1,0:T(8,128)(2,1)}, bf16[128,384]{1,0:T(8,128)(2,1)S(1)}, u32[]{:S(2)}) copy-start(bf16[128,384]{1,0:T(8,128)(2,1)S(1)} %get-tuple-element.1229) | copy-start | bytes 294916
  19.1 66.3 %copy-start.70 = (bf16[128,384]{1,0:T(8,128)(2,1)}, bf16[128,384]{1,0:T(8,128)(2,1)S(1)}, u32[]{:S(2)}) copy-start(bf16[128,384]{1,0:T(8,128)(2,1)S(1)} %get-tuple-element.1230) | copy-start | bytes 294916
  36.2 49.3 %copy-start.20 = (f32[128,768]{1,0:T(8,128)}, f32[128,768]{1,0:T(8,128)S(1)}, u32[]{:S(2)}) copy-start(f32[128,768]{1,0:T(8,128)S(1)} %get-tuple-element.1249) | copy-start | bytes 1179652
  36.2 49.3 %copy-start.97 = (f32[128]{0:T(128)}, f32[128]{0:T(128)S(1)}, u32[]{:S(2)}) copy-start(f32[128]{0:T(128)S(1)} %broadcast_multiply_fusion.3) | copy-start | bytes 1540
  36.4 49.1 %copy-start.132 = (f32[128]{0:T(128)}, f32[128]{0:T(128)S(1)}, u32[]{:S(2)}) copy-start(f32[128]{0:T(128)S(1)} %multiply_reduce_fusion.13) | copy-start | bytes 1540
  36.4 49.1 %copy-start.111 = (f32[128]{0:T(128)}, f32[128]{0:T(128)S(1)}, u32[]{:S(2)}) copy-start(f32[128]{0:T(128)S(1)} %fusion.164) | copy-start | bytes 1540
  89.8 245.4 %all-gather.25.cloned.1.call-start = ((), (), s32[]{:S(2)}) async-start(), calls=%async_computation.22 | async-start | bytes 6684672 | tf_op jit(solution)/shard_map/all_gather | solution.py:146
  95.1 412.8 %all-gather.19.cloned.1.call-start = ((), (), s32[]{:S(2)}) async-start(), calls=%async_computation.19 | async-start | bytes 1769472 | tf_op jit(solution)/shard_map/all_gather | solution.py:311
  95.7 10.9 copy-start.110
  95.7 12.1 copy-start.117
  95.8 12.1 copy-start.118
  95.8 15.6 copy-start.123
  95.8 59.6 %copy-start.109 = (bf16[64,32]{0,1:T(8,128)(2,1)S(1)}, bf16[64,32]{0,1:T(8,128)(2,1)}, u32[]{:S(2)}) copy-start(bf16[64,32]{0,1:T(8,128)(2,1)} %param.33) | copy-start | bytes 12292
  95.8 63.8 %copy-start.80 = (bf16[2,128,768]{2,1,0:T(8,128)(2,1)S(1)}, bf16[2,128,768]{2,1,0:T(8,128)(2,1)}, u32[]{:S(2)}) copy-start(bf16[2,128,768]{2,1,0:T(8,128)(2,1)} %param.40) | copy-start | bytes 1179652
  95.8 415.7 %all-gather.21.cloned.1.call-start = ((), (), s32[]{:S(2)}) async-start(), calls=%async_computation.20 | async-start | bytes 7077888 | tf_op jit(solution)/shard_map/all_gather | solution.py:314
  96.4 65.5 %slice-start = ((bf16[128,2304]{1,0:T(8,128)(2,1)}), bf16[128,768]{1,0:T(8,128)(2,1)S(1)}, s32[]{:S(2)}) async-start(bf16[128,2304]{1,0:T(8,128)(2,1)} %copy-done.50), calls=%async_computation.40 | async-start | bytes 393216 | tf_op jit(solution)/shard_map/slice | solution.py:96
  96.4 65.7 %slice-start.1 = ((bf16[128,2304]{1,0:T(8,128)(2,1)}), bf16[128,768]{1,0:T(8,128)(2,1)S(1)}, s32[]{:S(2)}) async-start(bf16[128,2304]{1,0:T(8,128)(2,1)} %copy-done.51), calls=%async_computation.41 | async-start | bytes 393216 | tf_op jit(solution)/shard_map/slice | solution.py:96
  96.4 429.9 %all-gather.23.cloned.1.call-start = ((), (), s32[]{:S(2)}) async-start(), calls=%async_computation.21 | async-start | bytes 7077888 | tf_op jit(solution)/shard_map/all_gather | solution.py:315
  97.2 1063.6 %reduce-scatter.51.cloned.1.call-start = ((), (), s32[]{:S(2)}) async-start(), calls=%async_computation.34 | async-start | bytes 6684672
  107.9 63.7 %copy-start.89 = (f32[1,3,128]{2,0,1:T(1,128)}, f32[1,3,128]{2,0,1:T(1,128)S(1)}, u32[]{:S(2)}) copy-start(f32[1,3,128]{2,0,1:T(1,128)S(1)} %get-tuple-element.1228) | copy-start | bytes 4612
  107.9 63.7 %copy-start.91 = (f32[1,3,128]{2,0,1:T(1,128)}, f32[1,3,128]{2,0,1:T(1,128)S(1)}, u32[]{:S(2)}) copy-start(f32[1,3,128]{2,0,1:T(1,128)S(1)} %get-tuple-element.1227) | copy-start | bytes 4612
  111.4 60.1 %copy-start.83 = (bf16[3,768]{1,0:T(4,128)(2,1)}, bf16[3,768]{1,0:T(4,128)(2,1)S(1)}, u32[]{:S(2)}) copy-start(bf16[3,768]{1,0:T(4,128)(2,1)S(1)} %all_gather.74) | copy-start | bytes 13828
  344.5 163.2 %copy-start.9 = (f32[128,32,24]{0,2,1:T(8,128)S(1)}, f32[128,32,24]{0,2,1:T(8,128)}, u32[]{:S(2)}) copy-start(f32[128,32,24]{0,2,1:T(8,128)} %copy-done.8) | copy-start | bytes 1179652
  344.5 163.2 %copy-start.67 = (f32[32,128]{1,0:T(8,128)S(1)}, f32[32,128]{1,0:T(8,128)}, u32[]{:S(2)}) copy-start(f32[32,128]{1,0:T(8,128)} %copy-done.66) | copy-start | bytes 49156
  509.9 28.8 %copy-start.17 = (f32[128,768]{1,0:T(8,128)}, f32[128,768]{1,0:T(8,128)S(1)}, u32[]{:S(2)}) copy-start(f32[128,768]{1,0:T(8,128)S(1)} %get-tuple-element.1251) | copy-start | bytes 1179652
  510.4 28.3 %copy-start.14 = (f32[128,768]{1,0:T(8,128)}, f32[128,768]{1,0:T(8,128)S(1)}, u32[]{:S(2)}) copy-start(f32[128,768]{1,0:T(8,128)S(1)} %get-tuple-element.1246) | copy-start | bytes 1179652
  510.4 28.3 %copy-start.93 = (f32[128]{0:T(128)}, f32[128]{0:T(128)S(1)}, u32[]{:S(2)}) copy-start(f32[128]{0:T(128)S(1)} %get-tuple-element.1256) | copy-start | bytes 1540
  510.4 28.3 %copy-start.95 = (f32[128]{0:T(128)}, f32[128]{0:T(128)S(1)}, u32[]{:S(2)}) copy-start(f32[128]{0:T(128)S(1)} %get-tuple-element.1255) | copy-start | bytes 1540
  510.8 27.9 %copy-start.103 = (f32[128]{0:T(128)}, f32[128]{0:T(128)S(1)}, u32[]{:S(2)}) copy-start(f32[128]{0:T(128)S(1)} %fusion.167) | copy-start | bytes 1540
  510.8 27.9 %copy-start.101 = (f32[128]{0:T(128)}, f32[128]{0:T(128)S(1)}, u32[]{:S(2)}) copy-start(f32[128]{0:T(128)S(1)} %fusion.165) | copy-start | bytes 1540
  831.7 386.0 %reduce-scatter.49.cloned.1.call-start = ((), (), s32[]{:S(2)}) async-start(), calls=%async_computation.33 | async-start | bytes 6684672
  1134.4 115.3 %reduce-scatter.39.cloned.1.call-start = ((), (), s32[]{:S(2)}) async-start(), calls=%async_computation.28 | async-start | bytes 1769472 | tf_op jit(solution)/shard_map/reduce_scatter | solution.py:346
  1136.9 128.9 %reduce-scatter.37.cloned.1.call-start = ((), (), s32[]{:S(2)}) async-start(), calls=%async_computation.27 | async-start | bytes 1769472 | tf_op jit(solution)/shard_map/reduce_scatter | solution.py:346
  1138.5 190.1 %reduce-scatter.43.cloned.1.call-start = ((), (), s32[]{:S(2)}) async-start(), calls=%async_computation.30 | async-start | bytes 7077888 | tf_op jit(solution)/shard_map/reduce_scatter | solution.py:355
  1142.3 249.2 %reduce-scatter.41.cloned.1.call-start = ((), (), s32[]{:S(2)}) async-start(), calls=%async_computation.29 | async-start | bytes 7077888 | tf_op jit(solution)/shard_map/reduce_scatter | solution.py:355
  1147.4 306.4 %reduce-scatter.45.cloned.1.call-start = ((), (), s32[]{:S(2)}) async-start(), calls=%async_computation.31 | async-start | bytes 7077888 | tf_op jit(solution)/shard_map/reduce_scatter | solution.py:358
  1152.3 363.8 %reduce-scatter.47.cloned.1.call-start = ((), (), s32[]{:S(2)}) async-start(), calls=%async_computation.32 | async-start | bytes 7077888 | tf_op jit(solution)/shard_map/reduce_scatter | solution.py:358
  1157.1 62.6 %copy-start.4 = (bf16[768,2304]{1,0:T(8,128)(2,1)S(1)}, bf16[768,2304]{1,0:T(8,128)(2,1)}, u32[]{:S(2)}) copy-start(bf16[768,2304]{1,0:T(8,128)(2,1)} %all-gather.15.cloned.1.call-done) | copy-start | bytes 10616836
  1157.1 383.4 %reduce-scatter.31.cloned.1.call-start = ((), (), s32[]{:S(2)}) async-start(), calls=%async_computation.24 | async-start | bytes 1769472 | tf_op jit(solution)/shard_map/reduce_scatter | solution.py:331
  1227.0 338.1 %reduce-scatter.29.cloned.1.call-start = ((), (), s32[]{:S(2)}) async-start(), calls=%async_computation.23 | async-start | bytes 1769472 | tf_op jit(solution)/shard_map/reduce_scatter | solution.py:331
  1228.6 386.8 %reduce-scatter.35.cloned.1.call-start = ((), (), s32[]{:S(2)}) async-start(), calls=%async_computation.26 | async-start | bytes 5308416 | tf_op jit(solution)/shard_map/reduce_scatter | solution.py:340
  1232.0 433.5 %reduce-scatter.33.cloned.1.call-start = ((), (), s32[]{:S(2)}) async-start(), calls=%async_computation.25 | async-start | bytes 5308416 | tf_op jit(solution)/shard_map/reduce_scatter | solution.py:340
  1236.2 442.4 %reduce-scatter.57.cloned.1.call-start = ((), (), s32[]{:S(2)}) async-start(), calls=%async_computation.37 | async-start | bytes 294912
  1242.3 450.0 %reduce-scatter.59.cloned.1.call-start = ((), (), s32[]{:S(2)}) async-start(), calls=%async_computation.38 | async-start | bytes 294912
  1246.6 457.3 %reduce-scatter.55.cloned.1.call-start = ((), (), s32[]{:S(2)}) async-start(), calls=%async_computation.36 | async-start | bytes 49152
  1248.1 467.8 %reduce-scatter.53.cloned.1.call-start = ((), (), s32[]{:S(2)}) async-start(), calls=%async_computation.35 | async-start | bytes 49152
  1249.6 633.2 %all-reduce.13.cloned.1.call-start = ((), (), s32[]{:S(2)}) async-start(), calls=%async_computation.39 | async-start | bytes 15335424 | tf_op jit(solution)/shard_map/psum | solution.py:371
  1669.1 47.6 %copy-start.105 = (bf16[768]{0:T(1024)(128)(2,1)S(1)}, bf16[768]{0:T(1024)(128)(2,1)}, u32[]{:S(2)}) copy-start(bf16[768]{0:T(1024)(128)(2,1)} %get-tuple-element.1034) | copy-start | bytes 4612
  1669.1 47.6 %copy-start.106 = (bf16[768]{0:T(1024)(128)(2,1)S(1)}, bf16[768]{0:T(1024)(128)(2,1)}, u32[]{:S(2)}) copy-start(bf16[768]{0:T(1024)(128)(2,1)} %get-tuple-element.1042) | copy-start | bytes 4612
  1669.1 47.6 %copy-start.107 = (bf16[768]{0:T(1024)(128)(2,1)S(1)}, bf16[768]{0:T(1024)(128)(2,1)}, u32[]{:S(2)}) copy-start(bf16[768]{0:T(1024)(128)(2,1)} %get-tuple-element.1224) | copy-start | bytes 4612
  1669.1 47.6 %copy-start.108 = (bf16[768]{0:T(1024)(128)(2,1)S(1)}, bf16[768]{0:T(1024)(128)(2,1)}, u32[]{:S(2)}) copy-start(bf16[768]{0:T(1024)(128)(2,1)} %get-tuple-element.1226) | copy-start | bytes 4612
  1669.1 47.6 %copy-start.124 = (bf16[768]{0:T(1024)(128)(2,1)S(1)}, bf16[768]{0:T(1024)(128)(2,1)}, u32[]{:S(2)}) copy-start(bf16[768]{0:T(1024)(128)(2,1)} %get-tuple-element.1038) | copy-start | bytes 4612
  1669.2 47.6 %copy-start.125 = (bf16[768]{0:T(1024)(128)(2,1)S(1)}, bf16[768]{0:T(1024)(128)(2,1)}, u32[]{:S(2)}) copy-start(bf16[768]{0:T(1024)(128)(2,1)} %get-tuple-element.1044) | copy-start | bytes 4612
  1669.2 47.6 %copy-start.126 = (bf16[768]{0:T(1024)(128)(2,1)S(1)}, bf16[768]{0:T(1024)(128)(2,1)}, u32[]{:S(2)}) copy-start(bf16[768]{0:T(1024)(128)(2,1)} %get-tuple-element.1219) | copy-start | bytes 4612
  1669.2 47.6 %copy-start.127 = (bf16[768]{0:T(1024)(128)(2,1)S(1)}, bf16[768]{0:T(1024)(128)(2,1)}, u32[]{:S(2)}) copy-start(bf16[768]{0:T(1024)(128)(2,1)} %get-tuple-element.1221) | copy-start | bytes 4612
  1669.2 116.7 %copy-start.43 = (f32[128,768]{1,0:T(8,128)S(1)}, f32[128,768]{1,0:T(8,128)}, u32[]{:S(2)}) copy-start(f32[128,768]{1,0:T(8,128)} %copy-done.42) | copy-start | bytes 1179652
  1669.2 116.7 %copy-start.120 = (f32[128]{0:T(128)S(1)}, f32[128]{0:T(128)}, u32[]{:S(2)}) copy-start(f32[128]{0:T(128)} %copy-done.119) | copy-start | bytes 1540
  1669.2 116.8 %copy-start.122 = (f32[128]{0:T(128)S(1)}, f32[128]{0:T(128)}, u32[]{:S(2)}) copy-start(f32[128]{0:T(128)} %copy-done.121) | copy-start | bytes 1540
  (102 other events, 324.4 us)
Sparse Core Ops, SparseCore 0:
  9.6 24.8 all-gather.12
  36.0 49.3 all-gather.14
  89.9 62.4 all-gather.16
  155.1 60.5 all-gather.24
  217.0 20.9 all-gather.18
  239.4 62.6 all-gather.20
  303.7 62.7 all-gather.22
  831.9 83.2 reduce-scatter.50
  1134.5 83.1 reduce-scatter.48
  1219.8 21.7 reduce-scatter.38
  1244.0 21.7 reduce-scatter.36
  1268.5 59.9 reduce-scatter.42
  1331.6 59.9 reduce-scatter.40
  1393.7 59.9 reduce-scatter.44
  1456.0 59.9 reduce-scatter.46
  1518.7 21.7 reduce-scatter.30
  1543.3 21.7 reduce-scatter.28
  1567.7 47.6 reduce-scatter.34
  1617.8 47.6 reduce-scatter.32
  1667.6 10.9 reduce-scatter.56
  1681.3 10.9 reduce-scatter.58
  1694.5 9.3 reduce-scatter.54
  1706.1 9.8 reduce-scatter.52
  1721.3 161.4 all-reduce.12
where the time goes:
time: 1920 us; the launch traced here: 1900 us
  waiting for transfers between devices  662 us (34%)
  matrix products  605 us (32%)
  local copies, waits for them, and re-layouts  336 us (18%)
  blocking collectives  130 us (7%)
  other arithmetic  121 us (6%)
  loops' own time  30.3 us (2%)
    dot_general x16, matrix products, score_parts(): jnp.einsum('qkc,ch->hqk', kernels, bias_full, preferred_element_type=jnp....  226 us
    reduce_scatter x2, waiting for transfers between devices, body(): lax.psum_scatter(local[8].astype(jnp.bfloat16), 'dp', scatter_dimension=0...  124 us
    reduce_scatter x2, waiting for transfers between devices, body(): lax.psum_scatter(local[9].astype(jnp.bfloat16), 'dp', scatter_dimension=0...  120 us
    dynamic_update_slice x8, local copies, waits for them, and re-layouts, backward_update(): lax.dynamic_update_slice_in_dim(pair_grad, current + joined, offset, 0)  119 us
    dot_general x8, matrix products, block_grads(): jnp.einsum('qkc,hqk->ch', kernels, logit_grad, preferred_element_type=jnp...  116 us
    dot_general x16, matrix products, score_parts(): jnp.einsum('qhd,khd->hqk', query_heads, key_heads, preferred_element_type...  99.5 us
    unnamed x30, waiting for transfers between devices  99 us
    reduce_scatter x2, waiting for transfers between devices, body(): lax.psum_scatter(local[3].astype(jnp.bfloat16), 'dp', scatter_dimension=0...  98.2 us
  transfers between devices with their start and end apart: 24, of which 17 were waited for; matrix products, arithmetic and copies ran while one was open for 39% of the time, Pallas kernels for 0%

commit v1 on v0

v1 whole, which is shorter than its diff:
```python
import functools
import jax
import jax.numpy as jnp
import numpy as np
from jax import lax
from jax.sharding import PartitionSpec as P
from jax.experimental import pallas as pl
from jax.experimental.pallas import tpu as pltpu

D = 768
HEADS = 32
HEAD_DIM = 24
KERNELS = 128
GROUPS = 4
GROUP_HEADS = 8
GROUP_DIM = 192
GROUP_PAD = 256
LOG2E = 1.4426950408889634
SCALE = HEAD_DIM ** -0.5
SPAN = 8
NA = KERNELS // SPAN
masked_value = -1e30
VMEM_LIMIT = 60 * 2**20
FORWARD_TILE = 32
BACKWARD_TILE = 64
FINE = 8


def cost(micros, bytes_moved):
    return pl.CostEstimate(flops=int(micros * 1.1e9), bytes_accessed=int(bytes_moved), transcendentals=0)


def distance_tile(q_ref, k_ref):
    total = None
    for axis in range(3):
        offset = q_ref[:, axis:axis + 1] - k_ref[axis:axis + 1, :]
        total = offset * offset if total is None else total + offset * offset
    return jnp.sqrt(total) * (KERNELS / 48.0)


def kernel_rows(x):
    centre = lax.broadcasted_iota(jnp.int32, (NA, 1), 0).astype(jnp.float32) * (SPAN / 2.0) + SPAN / 4.0
    y = jnp.clip(x - centre, -24.0, 24.0)
    up_step = jnp.exp2(y * (0.5 * LOG2E))
    down_step = jnp.exp2(y * (-0.5 * LOG2E))
    middle = jnp.exp2((y * y) * (-0.5 * LOG2E))
    above = [middle]
    for _ in range(SPAN // 2 - 1):
        above.append(above[-1] * up_step)
    below = []
    current = middle
    for _ in range(SPAN // 2):
        current = current * down_step
        below.append(current)
    rows = below[::-1] + above
    return jnp.concatenate([r.astype(jnp.bfloat16) for r in rows], axis=0)


def kernel_order():
    step = np.arange(SPAN) - SPAN // 2
    order = np.array([[a * SPAN + SPAN // 2 + b for a in range(NA)] for b in step]).reshape(-1)
    factor = np.repeat(np.exp(-(step ** 2) / 8.0), NA).astype(np.float32)
    return order, factor


def bias_kernel(chunk, q_ref, k_ref, w_ref, *refs):
    out_ref, x_ref, m_ref = refs[-3:]
    rows = q_ref.shape[0]
    keys = k_ref.shape[1]
    x_ref[...] = distance_tile(q_ref, k_ref)
    m_ref[...] = jnp.where(q_ref[:, 3:4] == k_ref[3:4, :], 0.0, masked_value)
    w = w_ref[...]

    def step(t, carry):
        for start in range(0, keys, chunk):
            cols = slice(start, start + chunk)
            values = []
            for q in (2 * t, 2 * t + 1):
                value = jnp.dot(w, kernel_rows(x_ref[pl.ds(q, 1), cols]), preferred_element_type=jnp.float32)
                values.append(value + m_ref[pl.ds(q, 1), cols])
            for g in range(GROUPS):
                both = jnp.concatenate([value[g * GROUP_HEADS:(g + 1) * GROUP_HEADS] for value in values], axis=0)
                out_ref[g, pl.ds(t * 2 * GROUP_HEADS, 2 * GROUP_HEADS), cols] = both.astype(out_ref.dtype)
        return carry

    lax.fori_loop(0, rows // 2, step, 0, unroll=True)


def pair_bias(q_where, k_where, w, first, steps, previous):
    rows, keys = q_where.shape[0], k_where.shape[1]
    in_specs = [
        pl.BlockSpec((FINE, 8), lambda i: (i + first, 0)),
        pl.BlockSpec((8, keys), lambda i: (0, 0)),
        pl.BlockSpec((HEADS, KERNELS), lambda i: (0, 0)),
    ]
    operands = [q_where, k_where, w]
    aliases = {}
    if previous is not None:
        in_specs.append(pl.BlockSpec(memory_space=pl.ANY))
        operands.append(previous)
        aliases = {3: 0}
    return pl.pallas_call(
        functools.partial(bias_kernel, 256),
        grid=(steps,),
        in_specs=in_specs,
        out_specs=pl.BlockSpec((GROUPS, FINE * GROUP_HEADS, keys), lambda i: (0, i + first, 0)),
        out_shape=jax.ShapeDtypeStruct((GROUPS, rows * GROUP_HEADS, keys), jnp.bfloat16),
        scratch_shapes=[pltpu.VMEM((FINE, keys), jnp.float32), pltpu.VMEM((FINE, keys), jnp.float32)],
        input_output_aliases=aliases,
        cost_estimate=cost(1.5 * steps, FINE * steps * HEADS * keys * 2),
        compiler_params=pltpu.CompilerParams(vmem_limit_bytes=VMEM_LIMIT),
        name="pair_bias",
    )(*operands)


def project_kernel(x_ref, w_ref, turn_ref, key_ref, value_ref, w_turn_ref):
    @pl.when(pl.program_id(0) == 0)
    def turn_weight():
        w_turn_ref[...] = w_ref[...].T

    x = x_ref[...]
    rows = x.shape[0]
    turn_ref[...] = lax.dot_general(
        w_turn_ref[...], x, (((1,), (1,)), ((), ())), preferred_element_type=jnp.float32
    ).astype(turn_ref.dtype)
    flat = jnp.dot(x, w_ref[...], preferred_element_type=jnp.float32)
    for out_ref, first, filler in ((key_ref, 0, 0.0), (value_ref, D, 1.0)):
        for g in range(GROUPS):
            part = flat[:, first + g * GROUP_DIM:first + (g + 1) * GROUP_DIM]
            wide = jnp.concatenate([part, jnp.full((rows, GROUP_PAD - GROUP_DIM), filler, jnp.float32)], axis=1)
            out_ref[:, g * GROUP_PAD:(g + 1) * GROUP_PAD] = wide.astype(out_ref.dtype)


def project(values, weight):
    keys, depth = values.shape
    width = weight.shape[1]
    wide = GROUPS * GROUP_PAD
    block = 256
    return pl.pallas_call(
        project_kernel,
        grid=(keys // block,),
        in_specs=[
            pl.BlockSpec((block, depth), lambda i: (i, 0)),
            pl.BlockSpec((depth, width), lambda i: (0, 0)),
        ],
        out_specs=[
            pl.BlockSpec((width, block), lambda i: (0, i)),
            pl.BlockSpec((block, wide), lambda i: (i, 0)),
            pl.BlockSpec((block, wide), lambda i: (i, 0)),
        ],
        out_shape=[
            jax.ShapeDtypeStruct((width, keys), jnp.bfloat16),
            jax.ShapeDtypeStruct((keys, wide), jnp.bfloat16),
            jax.ShapeDtypeStruct((keys, wide), jnp.bfloat16),
        ],
        scratch_shapes=[pltpu.VMEM((width, depth), jnp.bfloat16)],
        cost_estimate=cost(12, keys * (depth + 3 * width) * 2),
        compiler_params=pltpu.CompilerParams(vmem_limit_bytes=VMEM_LIMIT),
        name="project",
    )(values, weight)


def head_mask(width):
    head = lax.broadcasted_iota(jnp.int32, (GROUP_HEADS, width), 0)
    lane = lax.broadcasted_iota(jnp.int32, (GROUP_HEADS, width), 1)
    return ((lane >= head * HEAD_DIM) & (lane < (head + 1) * HEAD_DIM)).astype(jnp.float32)


def spread_heads(values, mask):
    rows, width = values.shape
    return (values[:, None, :] * mask[None]).reshape(rows * GROUP_HEADS, width)


def gather_heads(values, mask):
    rows, width = values.shape
    return jnp.sum(values.reshape(rows // GROUP_HEADS, GROUP_HEADS, width) * mask[None], axis=1)


def forward_kernel(chunk, q_ref, kt_ref, v_ref, bias_ref, p_ref, o_ref, inv_ref, s_ref):
    keys = kt_ref.shape[1]
    mask = head_mask(GROUP_PAD)

    for g in range(GROUPS):
        rows = slice(g * GROUP_DIM, (g + 1) * GROUP_DIM)
        spread = spread_heads(q_ref[g].astype(jnp.float32), mask).astype(jnp.bfloat16)[:, :GROUP_DIM]
        peak = None
        for start in range(0, keys, chunk):
            s = jnp.dot(spread, kt_ref[rows, start:start + chunk], preferred_element_type=jnp.float32)
            s = s * (SCALE * LOG2E) + bias_ref[g, :, start:start + chunk].astype(jnp.float32)
            s_ref[:, start:start + chunk] = s
            for lane in range(0, chunk, 128):
                part = s[:, lane:lane + 128]
                peak = part if peak is None else jnp.maximum(peak, part)
        top = jnp.max(peak, axis=1, keepdims=True)
        for start in range(0, keys, chunk):
            p_ref[g, :, start:start + chunk] = jnp.exp2(s_ref[:, start:start + chunk] - top).astype(jnp.bfloat16)
        mixed = jnp.dot(p_ref[g], v_ref[:, g * GROUP_PAD:(g + 1) * GROUP_PAD], preferred_element_type=jnp.float32)
        inverse = 1.0 / mixed[:, GROUP_DIM:GROUP_DIM + 1]
        o_ref[g] = gather_heads(mixed * inverse, mask)
        inv_ref[g] = gather_heads(jnp.broadcast_to(inverse, mixed.shape), mask)


def attend(q, turned, value_flat, bias):
    rows, keys = q.shape[1], turned.shape[1]
    tile = min(FORWARD_TILE, FORWARD_TILE * 2048 // keys)
    whole = pl.Buffered(1)
    return pl.pallas_call(
        functools.partial(forward_kernel, 512),
        grid=(rows // tile,),
        in_specs=[
            pl.BlockSpec((GROUPS, tile, GROUP_PAD), lambda i: (0, i, 0)),
            pl.BlockSpec((D, keys), lambda i: (0, 0), pipeline_mode=whole),
            pl.BlockSpec((keys, GROUPS * GROUP_PAD), lambda i: (0, 0), pipeline_mode=whole),
            pl.BlockSpec((GROUPS, tile * GROUP_HEADS, keys), lambda i: (0, i, 0)),
        ],
        out_specs=[
            pl.BlockSpec((GROUPS, tile * GROUP_HEADS, keys), lambda i: (0, i, 0)),
            pl.BlockSpec((GROUPS, tile, GROUP_PAD), lambda i: (0, i, 0)),
            pl.BlockSpec((GROUPS, tile, GROUP_PAD), lambda i: (0, i, 0)),
        ],
        out_shape=[
            jax.ShapeDtypeStruct((GROUPS, rows * GROUP_HEADS, keys), jnp.bfloat16),
            jax.ShapeDtypeStruct((GROUPS, rows, GROUP_PAD), jnp.float32),
            jax.ShapeDtypeStruct((GROUPS, rows, GROUP_PAD), jnp.float32),
        ],
        scratch_shapes=[
            pltpu.VMEM((tile * GROUP_HEADS, keys), jnp.float32),
        ],
        input_output_aliases={3: 0},
        cost_estimate=cost(45, rows * HEADS * keys * 4),
        compiler_params=pltpu.CompilerParams(vmem_limit_bytes=VMEM_LIMIT),
        name="attend",
    )(q, turned, value_flat, bias)


def backward_kernel(chunk, q_ref, do_ref, o_ref, k_ref, vt_ref, p_ref, ds_ref, dq_ref, dkt_ref, dvt_ref, dk_acc, dv_acc):
    keys = vt_ref.shape[1]
    mask = head_mask(GROUP_PAD)
    tile = pl.program_id(0)
    groups = q_ref.shape[0]

    @pl.when(tile == 0)
    def start_group():
        dk_acc[...] = jnp.zeros_like(dk_acc)
        dv_acc[...] = jnp.zeros_like(dv_acc)

    for g in range(groups):
        rows = slice(g * GROUP_DIM, (g + 1) * GROUP_DIM)
        q_wide = spread_heads(q_ref[g].astype(jnp.float32), mask)
        do_wide = spread_heads(do_ref[g].astype(jnp.float32), mask)
        o_wide = spread_heads(o_ref[g], mask)
        delta = jnp.sum(do_wide * o_wide, axis=1, keepdims=True)
        do_low = do_wide.astype(jnp.bfloat16)[:, :GROUP_DIM]
        do_turn = do_wide[:, :GROUP_DIM].T.astype(jnp.bfloat16)
        q_turn = q_wide[:, :GROUP_DIM].T.astype(jnp.bfloat16)
        for start in range(0, keys, chunk):
            cols = slice(start, start + chunk)
            dp = jnp.dot(do_low, vt_ref[rows, cols], preferred_element_type=jnp.float32)
            p = p_ref[g, :, cols]
            ds = (p.astype(jnp.float32) * (dp - delta)).astype(jnp.bfloat16)
            ds_ref[g, :, cols] = ds
            dv_acc[rows, cols] += jnp.dot(do_turn, p, preferred_element_type=jnp.float32)
            dk_acc[rows, cols] += jnp.dot(q_turn, ds, preferred_element_type=jnp.float32)
        dq = jnp.dot(ds_ref[g], k_ref[:, g * GROUP_PAD:(g + 1) * GROUP_PAD], preferred_element_type=jnp.float32)
        dq_ref[g] = gather_heads(dq, mask) * SCALE

    @pl.when(tile == pl.num_programs(0) - 1)
    def finish():
        dkt_ref[...] = (dk_acc[...] * SCALE).astype(dkt_ref.dtype)
        dvt_ref[...] = dv_acc[...].astype(dvt_ref.dtype)


def attend_back(q, do, o, key_flat, turned, p, part, parts):
    rows, keys = q.shape[1], turned.shape[1]
    tile = min(BACKWARD_TILE, BACKWARD_TILE * 2048 // keys)
    groups = GROUPS // parts
    width = groups * GROUP_DIM
    whole = pl.Buffered(1)
    narrow = pl.BlockSpec((groups, tile, GROUP_PAD), lambda i: (part, i, 0))
    return pl.pallas_call(
        functools.partial(backward_kernel, 512),
        grid=(rows // tile,),
        in_specs=[
            narrow,
            narrow,
            narrow,
            pl.BlockSpec((keys, groups * GROUP_PAD), lambda i: (0, part), pipeline_mode=whole),
            pl.BlockSpec((width, keys), lambda i: (part + parts, 0), pipeline_mode=whole),
            pl.BlockSpec((groups, tile * GROUP_HEADS, keys), lambda i: (part, i, 0)),
        ],
        out_specs=[
            pl.BlockSpec((groups, tile * GROUP_HEADS, keys), lambda i: (part, i, 0)),
            pl.BlockSpec((groups, tile, GROUP_PAD), lambda i: (0, i, 0)),
            pl.BlockSpec((width, keys), lambda i: (0, 0), pipeline_mode=whole),
            pl.BlockSpec((width, keys), lambda i: (0, 0), pipeline_mode=whole),
        ],
        out_shape=[
            jax.ShapeDtypeStruct(p.shape, p.dtype),
            jax.ShapeDtypeStruct((groups, rows, GROUP_PAD), jnp.float32),
            jax.ShapeDtypeStruct((width, keys), jnp.bfloat16),
            jax.ShapeDtypeStruct((width, keys), jnp.bfloat16),
        ],
        scratch_shapes=[
            pltpu.VMEM((width, keys), jnp.float32),
            pltpu.VMEM((width, keys), jnp.float32),
        ],
        input_output_aliases={5: 0},
        cost_estimate=cost(56 / parts, rows * HEADS * keys * 4 // parts),
        compiler_params=pltpu.CompilerParams(vmem_limit_bytes=VMEM_LIMIT),
        name="attend_back",
    )(q, do, o, key_flat, turned, p)


def table_grad_kernel(chunk, q_ref, k_ref, ds_ref, out_ref, x_ref):
    rows = q_ref.shape[0]
    keys = k_ref.shape[1]
    pair = 2 * GROUP_HEADS

    @pl.when(pl.program_id(0) == 0)
    def start_zero():
        out_ref[...] = jnp.zeros_like(out_ref)

    x_ref[...] = distance_tile(q_ref, k_ref)

    def step(t, total):
        for start in range(0, keys, chunk):
            x = x_ref[pl.ds(2 * t, 2), start:start + chunk]
            table = jnp.concatenate([kernel_rows(x[0:1]), kernel_rows(x[1:2])], axis=0)
            grads = jnp.concatenate(
                [ds_ref[g, pl.ds(t * pair, pair), start:start + chunk] for g in range(GROUPS)], axis=0
            )
            total = total + lax.dot_general(table, grads, (((1,), (1,)), ((), ())), preferred_element_type=jnp.float32)
        return total

    out_ref[...] += lax.fori_loop(0, rows // 2, step, jnp.zeros(out_ref.shape, jnp.float32), unroll=True)


def table_grad(q_where, k_where, ds, first, steps):
    rows, keys = q_where.shape[0], k_where.shape[1]
    wide = 2 * HEADS
    return pl.pallas_call(
        functools.partial(table_grad_kernel, 256),
        grid=(steps,),
        in_specs=[
            pl.BlockSpec((FINE, 8), lambda i: (i + first, 0)),
            pl.BlockSpec((8, keys), lambda i: (0, 0)),
            pl.BlockSpec((GROUPS, FINE * GROUP_HEADS, keys), lambda i: (0, i + first, 0)),
        ],
        out_specs=pl.BlockSpec((2 * KERNELS, wide), lambda i: (0, 0)),
        out_shape=jax.ShapeDtypeStruct((2 * KERNELS, wide), jnp.float32),
        scratch_shapes=[pltpu.VMEM((FINE, keys), jnp.float32)],
        cost_estimate=cost(1.6 * steps, FINE * steps * HEADS * keys * 2),
        compiler_params=pltpu.CompilerParams(vmem_limit_bytes=VMEM_LIMIT),
        name="table_grad",
    )(q_where, k_where, ds)


def table_sums(sums):
    sums = sums.reshape(2, KERNELS, GROUPS, 2, GROUP_HEADS)
    both = (sums[0, :, :, 0] + sums[1, :, :, 1]).reshape(KERNELS, HEADS)
    order, factor = kernel_order()
    return (both * factor[:, None])[np.argsort(order)]


def place_kernel(steps, s_ref, *refs):
    own_ref = refs[0]
    mine, other = refs[1:1 + steps], refs[1 + steps:1 + 2 * steps]
    out_ref = refs[-1]
    j = pl.program_id(0)
    place, core = s_ref[0], s_ref[1]
    away = lax.rem(place - j // 2 + steps + 1, steps + 1)

    @pl.when(away == 0)
    def own_part():
        out_ref[...] = own_ref[...]

    for step in range(1, steps + 1):
        @pl.when((away == step) & (core == j % 2))
        def fetched_part():
            out_ref[...] = mine[step - 1][...]

        @pl.when((away == step) & (core != j % 2))
        def passed_part():
            out_ref[...] = other[step - 1][...]


def place_shards(where, own, mine, other):
    steps = len(mine)
    rows, columns = own.shape
    half = rows // 2
    fixed = pl.BlockSpec((half, columns), lambda j, s: (0, 0))
    return pl.pallas_call(
        functools.partial(place_kernel, steps),
        grid_spec=pltpu.PrefetchScalarGridSpec(
            num_scalar_prefetch=1,
            grid=(2 * (steps + 1),),
            in_specs=[pl.BlockSpec((half, columns), lambda j, s: (j % 2, 0))] + [fixed] * (2 * steps),
            out_specs=pl.BlockSpec((half, columns), lambda j, s: (j, 0)),
        ),
        out_shape=jax.ShapeDtypeStruct(((steps + 1) * rows, columns), own.dtype),
        cost_estimate=cost(3, 2 * (steps + 1) * own.size * 2),
        compiler_params=pltpu.CompilerParams(vmem_limit_bytes=VMEM_LIMIT),
        name="place_shards",
    )(where, own, *mine, *other)


def assemble_kernel(xs, s_ref, *refs):
    out_ref = refs[-1]
    own_refs, other_refs = refs[:xs], refs[xs:2 * xs]
    zs, rows, half = own_refs[0].shape
    x, z, core = s_ref[0], s_ref[1], s_ref[2]
    jx = pl.program_id(0)
    from_x = lax.rem(x - jx + xs, xs)
    for step in range(xs):
        @pl.when(from_x == step)
        def copy_piece():
            for jz in range(zs):
                from_z = lax.rem(z - jz + zs, zs)
                own = own_refs[step][from_z].astype(jnp.float32)
                other = other_refs[step][from_z].astype(jnp.float32)
                first = core == 0
                out_ref[0, jz, :, :half] = jnp.where(first, own, other)
                out_ref[0, jz, :, half:] = jnp.where(first, other, own)


def assemble(where, own, other):
    xs = len(own)
    zs, rows, half = own[0].shape
    spec = pl.BlockSpec((zs, rows, half), lambda i, s: (0, 0, 0))
    whole = pl.pallas_call(
        functools.partial(assemble_kernel, xs),
        grid_spec=pltpu.PrefetchScalarGridSpec(
            num_scalar_prefetch=1,
            grid=(xs,),
            in_specs=[spec] * (2 * xs),
            out_specs=pl.BlockSpec((1, zs, rows, 2 * half), lambda i, s: (i, 0, 0, 0)),
        ),
        out_shape=jax.ShapeDtypeStruct((xs, zs, rows, 2 * half), jnp.float32),
        cost_estimate=cost(4, xs * zs * rows * half * 12),
        compiler_params=pltpu.CompilerParams(vmem_limit_bytes=VMEM_LIMIT),
        name="assemble",
    )(where, *own, *other)
    return whole.reshape(xs * zs * rows, 2 * half)


eps = 1e-05
highest = lax.Precision.HIGHEST
CHIP_ROW = 4


def layer_norm(values, norm_gain, norm_shift):
    centred = values - jnp.mean(values, axis=-1, keepdims=True)
    spread = jnp.mean(centred * centred, axis=-1, keepdims=True)
    return centred * lax.rsqrt(spread + eps) * norm_gain + norm_shift


def exact_gelu(values):
    return jax.nn.gelu(values, approximate=False)


def time_features(stamps, feature_width):
    half_width = feature_width // 2
    frequency = jnp.exp(-jnp.log(10000.0) * jnp.arange(half_width, dtype=jnp.float32) / half_width)
    angles = stamps[:, None] * frequency[None, :]
    return jnp.concatenate([jnp.sin(angles), jnp.cos(angles)], axis=1)


def shifted(values, axis, step):
    size = lax.axis_size(axis)
    return lax.ppermute(values, axis, [(i, (i + step) % size) for i in range(size)])


def part_of(values, index, count, axis):
    length = values.shape[axis] // count
    return lax.dynamic_slice_in_dim(values, index * length, length, axis)


def dot32(left, right, contract):
    return lax.dot_general(left, right, ((contract[:1], contract[1:]), ((), ())), preferred_element_type=jnp.float32)


def in_order(pieces):
    count = len(pieces)
    place = lax.axis_index("dp")
    chosen = []
    for index in range(count):
        step = lax.rem(place - index + count, count)
        picked = pieces[0]
        for other in range(1, count):
            picked = jnp.where(step == other, pieces[other], picked)
        chosen.append(picked)
    return jnp.stack(chosen)


def spread_dp(values):
    return [values] + [shifted(values, "dp", step) for step in range(1, lax.axis_size("dp"))]


def fetch_shards(weight):
    half = part_of(weight, lax.axis_index("core"), 2, 0)
    return [shifted(half, "dp", step) for step in range(1, lax.axis_size("dp"))]


def pass_on(mine):
    return [shifted(piece, "core", 1) for piece in mine]


def gather_weight(weight, mine, other):
    where = jnp.stack([lax.axis_index("dp"), lax.axis_index("core")]).astype(jnp.int32)
    return place_shards(where, weight, mine, other)


def tie(*groups):
    return lax.optimization_barrier(groups)


def send_parts(values, axis):
    count = lax.axis_size(axis)
    place = lax.axis_index(axis)
    own = part_of(values, place, count, 0)
    incoming = [
        shifted(part_of(values, lax.rem(place + step, count), count, 0).astype(jnp.bfloat16), axis, step)
        for step in range(1, count)
    ]
    return own, incoming


def add_parts(own, incoming):
    total = own.astype(jnp.float32)
    for share in incoming:
        total = total + share.astype(jnp.float32)
    return total


def reduce_chain(owned):
    for axis in ("x", "z"):
        own, incoming = yield send_parts(owned, axis)
        owned = add_parts(own, incoming)
    owned = owned.astype(jnp.bfloat16)
    owned, incoming = yield owned, [shifted(owned, "z", step) for step in range(1, lax.axis_size("z"))]
    pieces = jnp.stack([owned] + incoming)
    own = yield [pieces] + [shifted(pieces, "x", step) for step in range(1, lax.axis_size("x"))]
    own, other = yield own, [shifted(piece, "core", 1) for piece in own]
    where = jnp.stack([lax.axis_index(axis) for axis in ("x", "z", "core")]).astype(jnp.int32)
    return assemble(where, own, other)


def weight_chain(inputs, grads):
    core = lax.axis_index("core")
    count = lax.axis_size("dp")
    place = lax.axis_index("dp")
    own_right = part_of(grads, core, 2, 1)
    inputs, other_left, own_right, other_right = yield (
        inputs, shifted(inputs, "core", 1), own_right, shifted(part_of(grads, 1 - core, 2, 1), "core", 1)
    )
    left = jnp.concatenate([inputs, other_left], axis=0)
    right = jnp.concatenate([own_right, other_right], axis=0)
    incoming = []
    for step in range(1, count):
        share = dot32(part_of(left, lax.rem(place + step, count), count, 1), right, (0, 0)).astype(jnp.bfloat16)
        incoming.append(shifted(share, "dp", step))
    left, right, incoming = yield left, right, incoming
    owned = add_parts(dot32(part_of(left, place, count, 1), right, (0, 0)), incoming)
    return (yield from reduce_chain(owned))


def table_chain(local):
    core = lax.axis_index("core")
    own = part_of(local, core, 2, 1)
    own, other = yield own, shifted(part_of(local, 1 - core, 2, 1), "core", 1)
    own, incoming = yield send_parts(own.astype(jnp.float32) + other.astype(jnp.float32), "dp")
    return (yield from reduce_chain(add_parts(own, incoming)))


def share_chain(shares):
    x_count, z_count = shares.shape[:2]
    own, incoming = yield shares[0], [shifted(shares[step], "x", -step) for step in range(1, x_count)]
    total = add_parts(own, incoming)
    low = total.astype(jnp.bfloat16)
    own, incoming = yield total[0], [shifted(low[step], "z", -step) for step in range(1, z_count)]
    return add_parts(own, incoming)


class Flight:
    def __init__(self, chain):
        self.chain = chain
        self.values = next(chain)
        self.result = None

    def land(self, values):
        try:
            self.values = self.chain.send(values)
        except StopIteration as stop:
            self.values, self.result = None, stop.value


def advance(inputs, *flights):
    flights = [flight for flight in flights if flight.values is not None]
    inputs, landed = lax.optimization_barrier((inputs, [flight.values for flight in flights]))
    for flight, values in zip(flights, landed):
        flight.land(values)
    return inputs


def finish(flight):
    while flight.values is not None:
        flight.land(flight.values)
    return flight.result


def sum_all(values):
    for axis in ("core", "dp", "x", "z"):
        values = functools.reduce(
            jnp.add, [shifted(values, axis, step) for step in range(1, lax.axis_size(axis))], values
        )
    return values


def by_group(values):
    wide = values.reshape(values.shape[0], GROUPS, GROUP_DIM)
    wide = jnp.pad(wide, ((0, 0), (0, 0), (0, GROUP_PAD - GROUP_DIM)))
    return jnp.transpose(wide, (1, 0, 2))


def flat_groups(values):
    return jnp.transpose(values[:, :, :GROUP_DIM], (1, 0, 2)).reshape(values.shape[1], D)


def body(
    residues,
    coordinates,
    segment_ids,
    time_steps,
    time_weight,
    norm1_gain,
    norm1_bias,
    qkv_weight,
    bias_weight,
    out_weight,
    norm2_gain,
    norm2_bias,
    up_weight,
    down_weight,
    force_weight,
    out_cotangent,
    force_cotangent,
):
    core = lax.axis_index("core")
    place = lax.axis_index("dp")
    dp_count = lax.axis_size("dp")
    x_count, z_count = lax.axis_size("x"), lax.axis_size("z")
    held = residues.shape[1]

    def take_row(values):
        mine = lax.dynamic_index_in_dim(values, core, 0, keepdims=False)
        other = lax.dynamic_index_in_dim(values, 1 - core, 0, keepdims=False)
        return mine, shifted(other, "core", 1)

    def give_row(values, axis):
        mine = lax.slice_in_dim(values, 0, held, axis=axis)
        other = shifted(lax.slice_in_dim(values, held, 2 * held, axis=axis), "core", 1)
        first_row = jnp.where(core == 0, mine, other)
        second_row = jnp.where(core == 0, other, mine)
        return jnp.stack([first_row, second_row])

    where_own = jnp.concatenate(
        [coordinates, segment_ids[:, None, :].astype(jnp.bfloat16)], axis=1
    )
    where_rows = jnp.concatenate(take_row(where_own), axis=1)
    bias_parts = [bias_weight] + [shifted(bias_weight, "dp", step) for step in range(1, dp_count)]
    residue_parts = take_row(residues)
    my_steps = lax.dynamic_index_in_dim(time_steps, core, 0, keepdims=False)
    step_list = [my_steps] + [shifted(my_steps, "dp", step) for step in range(1, dp_count)]

    where_keys = where_rows[None]
    reach = 1
    while reach < z_count:
        where_keys = jnp.concatenate([where_keys, shifted(where_keys, "z", reach)], axis=0)
        reach *= 2
    where_columns = [where_keys[:z_count]]
    for x_step in range(1, x_count):
        where_columns.append(shifted(where_columns[0], "x", x_step))
    (
        where_columns,
        where_rows,
        bias_parts,
        residue_parts,
        step_list,
        (norm1_gain, norm1_bias, norm2_gain, norm2_bias, force_weight),
        (time_weight, qkv_weight, out_weight, up_weight, down_weight),
        (out_cotangent, force_cotangent),
    ) = tie(
        where_columns,
        where_rows,
        bias_parts,
        residue_parts,
        step_list,
        (norm1_gain, norm1_bias, norm2_gain, norm2_bias, force_weight),
        (time_weight, qkv_weight, out_weight, up_weight, down_weight),
        (out_cotangent, force_cotangent),
    )
    key_where = jnp.transpose(jnp.concatenate(where_columns, axis=0).astype(jnp.float32), (1, 0, 2))
    key_where = jnp.pad(key_where.reshape(4, -1), ((0, 4), (0, 0)))
    query_where = jnp.pad(jnp.transpose(where_rows).astype(jnp.float32), ((0, 0), (0, 4)))
    segment_rows = where_rows[3]
    residue_rows = jnp.concatenate(residue_parts, axis=0).astype(jnp.float32)

    bias_full = in_order(bias_parts).reshape(KERNELS, HEADS)
    order, factor = kernel_order()
    table_weight = (
        jnp.transpose(bias_full).astype(jnp.float32)[:, order] * (factor * LOG2E)
    ).astype(jnp.bfloat16)
    tiles = 2 * held // FINE
    lead = tiles // 8
    bias = pair_bias(query_where, key_where, table_weight, 0, lead, None)

    vectors = in_order(
        spread_dp(jnp.concatenate([jnp.stack([norm1_gain, norm1_bias, norm2_gain, norm2_bias]), force_weight], axis=0))
    )
    vectors = jnp.transpose(vectors, (1, 0, 2)).reshape(7, D)
    gain_one, shift_one, gain_two, shift_two = [vectors[i:i + 1].astype(jnp.float32) for i in range(4)]
    force_full = vectors[4:]
    proteins = my_steps.shape[0]
    features = time_features(jnp.concatenate(step_list).astype(jnp.float32), D).astype(jnp.bfloat16)
    features = part_of(features, place, dp_count, 1)
    stamp_part = jnp.dot(features, time_weight, preferred_element_type=jnp.float32)
    stamp_rows = stamp_part[:proteins]
    for step in range(1, dp_count):
        stamp_rows = stamp_rows + shifted(
            stamp_part[step * proteins:(step + 1) * proteins], "dp", -step
        )
    query_own, pair_own = qkv_weight[:, :D], qkv_weight[:, D:]
    pair_half = fetch_shards(pair_own)
    query_half = fetch_shards(query_own)
    bias, stamp_rows, vectors_ready = tie(bias, stamp_rows, (gain_one, shift_one))
    gain_one, shift_one = vectors_ready

    def by_protein(table):
        picked = jnp.zeros((2 * held, table.shape[1]), jnp.float32)
        for index in range(proteins):
            picked = picked + jnp.where((segment_rows == index)[:, None], table[index][None, :], 0.0)
        return picked

    first = residue_rows + by_protein(stamp_rows)
    normed, norm_one_back = jax.vjp(layer_norm, first, gain_one, shift_one)
    normed_low = normed.astype(jnp.bfloat16)

    columns = [[None] * z_count for _ in range(x_count)]
    current = normed_low
    done = lead
    out_half = up_half = down_half = None
    for z_step in range(z_count):
        steps = (tiles - done) // (z_count - z_step)
        across = [current]
        for x_step in range(1, x_count):
            across.append(shifted(across[-1], "x", 1))
        following = shifted(current, "z", 1) if z_step < z_count - 1 else current
        bias = pair_bias(query_where, key_where, table_weight, done, steps, bias)
        done += steps
        bias, current, across = tie(bias, following, across)
        for x_step in range(x_count):
            columns[x_step][z_step] = across[x_step]
        if z_step == 1:
            bias, pair_half, query_half, later = tie(bias, pair_half, query_half, (out_weight, up_weight, down_weight))
            out_weight, up_weight, down_weight = later
            out_half, up_half, down_half = fetch_shards(out_weight), fetch_shards(up_weight), fetch_shards(down_weight)
            pair_passed = pass_on(pair_half)
            query_passed = pass_on(query_half)
    normed_all = jnp.concatenate([piece for column in columns for piece in column], axis=0)

    query_weight = gather_weight(query_own, query_half, query_passed)
    pair_weight = gather_weight(pair_own, pair_half, pair_passed)
    query = by_group(jnp.dot(normed_low, query_weight, preferred_element_type=jnp.float32).astype(jnp.bfloat16))
    turned, key_flat, value_flat = project(normed_all, pair_weight)
    probs, attended, inverse = attend(query, turned, value_flat, bias)
    attended_low = flat_groups(attended).astype(jnp.bfloat16)
    attended_low, out_half, up_half, down_half, cotangents = tie(
        attended_low, out_half, up_half, down_half, (out_cotangent, force_cotangent)
    )
    out_cotangent, force_cotangent = cotangents
    out_full = gather_weight(out_weight, out_half, pass_on(out_half))
    up_full = gather_weight(up_weight, up_half, pass_on(up_half))
    down_full = gather_weight(down_weight, down_half, pass_on(down_half))
    cot_rows = jnp.concatenate(take_row(out_cotangent), axis=0).astype(jnp.float32)
    force_cot = jnp.concatenate(take_row(force_cotangent), axis=1)

    second = first + jnp.dot(attended_low, out_full, preferred_element_type=jnp.float32)
    normed_two, norm_two_back = jax.vjp(layer_norm, second, gain_two, shift_two)
    normed_two_low = normed_two.astype(jnp.bfloat16)
    hidden = jnp.dot(normed_two_low, up_full, preferred_element_type=jnp.float32)
    activated, gelu_back = jax.vjp(exact_gelu, hidden)
    activated_low = activated.astype(jnp.bfloat16)
    third = second + jnp.dot(activated_low, down_full, preferred_element_type=jnp.float32)
    block_low = third.astype(jnp.bfloat16)
    forces = jnp.einsum("cd,qd->cq", force_full, block_low, preferred_element_type=jnp.float32)
    third_grad = cot_rows + jnp.einsum(
        "cq,cd->qd", force_cot, force_full.astype(jnp.float32), precision=highest
    )
    force_grad = jnp.einsum(
        "cq,qd->cd", force_cot, block_low.astype(jnp.float32), precision=highest
    )
    third_low = third_grad.astype(jnp.bfloat16)
    activated_grad = dot32(third_low, down_full, (1, 1))
    hidden_grad = gelu_back(activated_grad)[0].astype(jnp.bfloat16)
    normed_two_grad = dot32(hidden_grad, up_full, (1, 1))
    second_part, gain_two_grad, shift_two_grad = norm_two_back(normed_two_grad)
    second_grad = third_grad + second_part
    second_low = second_grad.astype(jnp.bfloat16)
    attended_grad = by_group(dot32(second_low, out_full, (1, 1)).astype(jnp.bfloat16))
    scaled_grad = (attended_grad.astype(jnp.float32) * inverse).astype(jnp.bfloat16)

    down = Flight(weight_chain(activated_low, third_low))
    up = Flight(weight_chain(normed_two_low, hidden_grad))
    out = Flight(weight_chain(attended_low, second_low))

    scaled_grad = advance(scaled_grad, down)
    first_back = attend_back(query, scaled_grad, attended, key_flat, turned, probs, 0, 2)
    first_back, scaled_grad = advance((first_back, scaled_grad), down, up, out)
    second_back = attend_back(query, scaled_grad, attended, key_flat, turned, first_back[0], 1, 2)
    backs = advance([first_back[1:], second_back[1:], second_back[0]], down, up, out)
    logit_grad = backs.pop()
    query_grad = flat_groups(jnp.concatenate([back[0] for back in backs], axis=0)).astype(jnp.bfloat16)
    pair_grad_turn = jnp.concatenate([back[1] for back in backs] + [back[2] for back in backs], axis=0)

    pair_share = dot32(pair_grad_turn, pair_weight, (0, 1)).astype(jnp.bfloat16)
    own = pair_share.reshape(x_count, z_count, 2 * held, D)
    shares = [Flight(share_chain(own[..., part * (D // 2):(part + 1) * (D // 2)])) for part in range(2)]
    query_part = dot32(normed_low, query_grad, (0, 0)).astype(jnp.bfloat16)
    pair_part = dot32(normed_all, pair_grad_turn, (0, 1)).astype(jnp.bfloat16)
    table = Flight(table_chain(jnp.concatenate([query_part, pair_part], axis=1)))

    sums = None
    flights = [down, up, out, table] + shares
    steps = tiles // 4
    for part in range(4):
        logit_grad = advance(logit_grad, *flights)
        piece = table_grad(query_where, key_where, logit_grad, part * steps, steps)
        piece, logit_grad = tie(piece, logit_grad)
        sums = piece if sums is None else sums + piece
    bias_grad = table_sums(sums)
    pair_normed_grad = jnp.concatenate([finish(share) for share in shares], axis=1)
    down_grad, up_grad, out_grad, qkv_grad = [finish(flight) for flight in (down, up, out, table)]

    normed_grad = dot32(query_grad, query_weight, (1, 1)) + pair_normed_grad
    first_part, gain_one_grad, shift_one_grad = norm_one_back(normed_grad)
    first_grad = second_grad + first_part
    first_low = first_grad.astype(jnp.bfloat16).astype(jnp.float32)
    protein_sum = jnp.stack(
        [
            jnp.sum(jnp.where((segment_rows == index)[:, None], first_low, 0.0), axis=0)
            for index in range(proteins)
        ]
    )
    slots = 2 * dp_count
    slot = jnp.arange(slots) == 2 * place + core
    protein_slots = jnp.where(slot[:, None, None], protein_sum[None], 0.0)
    packed = jnp.concatenate(
        [
            gain_one_grad.reshape(-1),
            shift_one_grad.reshape(-1),
            gain_two_grad.reshape(-1),
            shift_two_grad.reshape(-1),
            force_grad.reshape(-1),
            bias_grad.reshape(-1),
            protein_slots.reshape(-1),
        ]
    )
    packed = sum_all(packed)
    vectors = packed[:4 * D].reshape(4, D)
    vectors = part_of(vectors, place, dp_count, 1)
    force_sum = part_of(packed[4 * D:7 * D].reshape(3, D), place, dp_count, 1)
    table_end = 7 * D + KERNELS * HEADS
    bias_sum = part_of(packed[7 * D:table_end].reshape(KERNELS, HEADS), place, dp_count, 0)
    protein_all = packed[table_end:].reshape(slots, proteins, D)
    other_steps = lax.dynamic_index_in_dim(time_steps, 1 - core, 0, keepdims=False)
    both_steps = jnp.where(core == 0, jnp.stack([my_steps, other_steps]), jnp.stack([other_steps, my_steps]))
    all_features = time_features(both_steps.reshape(-1).astype(jnp.float32), D).astype(jnp.bfloat16)
    all_features = in_order(spread_dp(all_features)).reshape(slots * proteins, D)
    time_grad = jnp.einsum(
        "sd,se->de",
        part_of(all_features, place, dp_count, 1).astype(jnp.float32),
        protein_all.reshape(slots * proteins, D),
        precision=highest,
    )

    return (
        give_row(block_low, 0),
        give_row(forces, 1),
        give_row(first_grad, 0),
        time_grad,
        vectors[0],
        vectors[1],
        qkv_grad,
        bias_sum,
        out_grad,
        vectors[2],
        vectors[3],
        up_grad,
        down_grad,
        force_sum,
    )


def solution(mesh):
    chips = mesh.shape["blk"] // 2
    rows = CHIP_ROW if chips % CHIP_ROW == 0 else 1
    fine = jax.sharding.Mesh(
        mesh.devices.reshape(mesh.shape["dp"], rows, chips // rows, 2), ("dp", "z", "x", "core")
    )
    blk = ("z", "x", "core")
    return jax.shard_map(
        body,
        mesh=fine,
        in_specs=(
            P("dp", blk, None),
            P("dp", None, blk),
            P("dp", blk),
            P("dp", None),
            P("dp", None),
            P("dp"),
            P("dp"),
            P("dp", None),
            P("dp", None),
            P("dp", None),
            P("dp"),
            P("dp"),
            P("dp", None),
            P("dp", None),
            P(None, "dp"),
            P("dp", blk, None),
            P("dp", None, blk),
        ),
        out_specs=(
            P("dp", blk, None),
            P("dp", None, blk),
            P("dp", blk, None),
            P("dp", None),
            P("dp"),
            P("dp"),
            P("dp", None),
            P("dp", None),
            P("dp", None),
            P("dp"),
            P("dp"),
            P("dp", None),
            P("dp", None),
            P(None, "dp"),
        ),
        check_vma=False,
    )
```

time: 1920 us -> 641 us (0.33)
  waiting for transfers between devices: 662 us -> 101 us
  matrix products: 605 us -> 51.4 us
  local copies, waits for them, and re-layouts: 336 us -> 70.3 us
  Pallas kernels: 0 us -> 262 us
  blocking collectives: 130 us -> 0 us
  starting transfers between devices: 1.15 us -> 115 us
  other arithmetic: 121 us -> 30.1 us
  loops' own time: 30.3 us -> 0 us
    dot_general x116 -> x22, matrix products: 605 us -> 51.4 us  [the longest x13 37.1 us: dot32(): lax.dot_general(left, right, ((contract[:1], contract[1:]), ((), ())), pr...]
    reduce_scatter x10 -> x0, waiting for transfers between devices: 402 us -> none  [the longest x2 124 us: body(): lax.psum_scatter(local[8].astype(jnp.bfloat16), 'dp', scatter_dimension=0...]
    pallas_call x0 -> x22, Pallas kernels: none -> 262 us  [the longest x2 57.7 us: attend_back(): pl.pallas_call(functools.partial(backward_kernel, 512), grid=(rows // til...]
    dynamic_update_slice x8 -> x0, local copies, waits for them, and re-layouts: 119 us -> none  [backward_update(): lax.dynamic_update_slice_in_dim(pair_grad, current + joined, offset, 0)]
    ppermute x0 -> x97, starting transfers between devices: none -> 115 us  [shifted(): lax.ppermute(values, axis, [(i, (i + step) % size) for i in range(size)])]
    ppermute x0 -> x97, waiting for transfers between devices: none -> 101 us  [shifted(): lax.ppermute(values, axis, [(i, (i + step) % size) for i in range(size)])]
    unnamed x30 -> x0, waiting for transfers between devices: 99 us -> none
    psum x1 -> x0, waiting for transfers between devices: 95.7 us -> none  [body(): lax.psum(totals[0].astype(jnp.bfloat16), 'blk').astype(jnp.float32)]
  transfers between devices with their start and end apart: 24 -> 97, of which waited for: 17 -> 20; matrix products, arithmetic and copies ran while one was open for 39% -> 17% of each run, Pallas kernels for 0% -> 34%
where the time goes in v1:
time: 641 us; the launch traced here: 633 us
  Pallas kernels  262 us (41%)
  starting transfers between devices  115 us (18%)
  waiting for transfers between devices  101 us (16%)
  local copies, waits for them, and re-layouts  70.3 us (11%)
  matrix products  51.4 us (8%)
  other arithmetic  30.1 us (5%)
    ppermute x97, starting transfers between devices, shifted(): lax.ppermute(values, axis, [(i, (i + step) % size) for i in range(size)])  115 us
    ppermute x97, waiting for transfers between devices, shifted(): lax.ppermute(values, axis, [(i, (i + step) % size) for i in range(size)])  101 us
    pallas_call x2, Pallas kernels, attend_back(): pl.pallas_call(functools.partial(backward_kernel, 512), grid=(rows // til...  57.7 us
    pallas_call x5, Pallas kernels, pair_bias(): pl.pallas_call(functools.partial(bias_kernel, 256), grid=(steps,), in_spe...  53.4 us
    pallas_call x4, Pallas kernels, table_grad(): pl.pallas_call(functools.partial(table_grad_kernel, 256), grid=(steps,),...  52.3 us
    pallas_call x1, Pallas kernels, attend(): pl.pallas_call(functools.partial(forward_kernel, 512), grid=(rows // tile...  39.6 us
    dot_general x13, matrix products, dot32(): lax.dot_general(left, right, ((contract[:1], contract[1:]), ((), ())), pr...  37.1 us
    unnamed x331, local copies, waits for them, and re-layouts  34.5 us
  transfers between devices with their start and end apart: 97, of which 20 were waited for; matrix products, arithmetic and copies ran while one was open for 17% of the time, Pallas kernels for 34%

profile of v1, /device:TPU:1, one launch (start us, length us, event | category | flops | bytes accessed | tf_op | source)
XLA Modules:
  0.0 633.5 jit_solution(5521120625206240280)
XLA Ops:
  1.6 2.1 collective-permute-start.6
  8.7 1.8 collective-permute-start.1
  11.0 2.5 collective-permute-done.1
  14.6 2.3 collective-permute-done.2
  30.3 7.3 %pair_bias.5.refs_0_ = bf16[4,2048,2048]{2,1,0:T(8,128)(2,1)} custom-call(f32[256,8]{1,0:T(8,128)} %pad_convert_fusion.q_ref, f32[8,2048]{1,0:T(8,128)} %pad_convert_fusion.1.k_ref, bf16[32,128]{1,0:T(8,128)(2,1)} %fusion.35.w_ref), custom_call_target="tpu_custom_call" | custom-call | flops 6600000000 | bytes 4194304 | tf_op jit(solution)/shard_map/pair_bias/pallas_call | solution.py:102
  42.9 11.5 %pair_bias.6.refs_0_ = bf16[4,2048,2048]{2,1,0:T(8,128)(2,1)} custom-call(f32[256,8]{1,0:T(8,128)} %pad_convert_fusion.q_ref, f32[8,2048]{1,0:T(8,128)} %pad_convert_fusion.1.k_ref, bf16[32,128]{1,0:T(8,128)(2,1)} %fusion.35.w_ref, bf16[4,2048,2048]{2,1,0:T(8,128)(2,1)} %pair_bias.5.refs_0_), custom_call_target="tpu_custom_call", output_to_operand_aliasing={{}: (3, {})} | custom-call | flops 11550000128 | bytes 7340032 | tf_op jit(solution)/shard_map/pair_bias/pallas_call | solution.py:102
  55.5 11.5 %pair_bias.7.refs_0_ = bf16[4,2048,2048]{2,1,0:T(8,128)(2,1)} custom-call(f32[256,8]{1,0:T(8,128)} %pad_convert_fusion.q_ref, f32[8,2048]{1,0:T(8,128)} %pad_convert_fusion.1.k_ref, bf16[32,128]{1,0:T(8,128)(2,1)} %fusion.35.w_ref, bf16[4,2048,2048]{2,1,0:T(8,128)(2,1)} %pair_bias.6.refs_0_), custom_call_target="tpu_custom_call", output_to_operand_aliasing={{}: (3, {})} | custom-call | flops 11550000128 | bytes 7340032 | tf_op jit(solution)/shard_map/pair_bias/pallas_call | solution.py:102
  70.6 11.5 %pair_bias.8.refs_0_ = bf16[4,2048,2048]{2,1,0:T(8,128)(2,1)} custom-call(f32[256,8]{1,0:T(8,128)} %pad_convert_fusion.q_ref, f32[8,2048]{1,0:T(8,128)} %pad_convert_fusion.1.k_ref, bf16[32,128]{1,0:T(8,128)(2,1)} %fusion.35.w_ref, bf16[4,2048,2048]{2,1,0:T(8,128)(2,1)} %pair_bias.7.refs_0_), custom_call_target="tpu_custom_call", output_to_operand_aliasing={{}: (3, {})} | custom-call | flops 11550000128 | bytes 7340032 | tf_op jit(solution)/shard_map/pair_bias/pallas_call | solution.py:102
  83.1 6.9 %collective-permute-start.15 = (bf16[192,768]{1,0:T(8,128)(2,1)}, bf16[192,768]{1,0:T(8,128)(2,1)S(1)}, u32[]{:S(2)}, u32[]{:S(2)}) collective-permute-start(bf16[192,768]{1,0:T(8,128)(2,1)} %collective-permute-done.14.refs_1_), channel_id=1, source_target_pairs={{0,1},{1,0},{2,3},{3,2},{4,5},{5,4},{6,7},{7,6},{8,9},{9,8},{10,11... | collective-permute-start | bytes 884744 | tf_op jit(solution)/shard_map/ppermute | solution.py:470
  93.6 4.3 place_shards.5
  101.8 11.5 %pair_bias.9.bias_ref = bf16[4,2048,2048]{2,1,0:T(8,128)(2,1)} custom-call(f32[256,8]{1,0:T(8,128)} %pad_convert_fusion.q_ref, f32[8,2048]{1,0:T(8,128)} %pad_convert_fusion.1.k_ref, bf16[32,128]{1,0:T(8,128)(2,1)} %fusion.35.w_ref, bf16[4,2048,2048]{2,1,0:T(8,128)(2,1)} %pair_bias.8.refs_0_), custom_call_target="tpu_custom_call", output_to_operand_aliasing={{}: (3, {})} | custom-call | flops 11550000128 | bytes 7340032 | tf_op jit(solution)/shard_map/pair_bias/pallas_call | solution.py:102
  115.1 5.1 place_shards.6.w_ref
  126.0 15.3 %project.1 = (bf16[1536,2048]{1,0:T(8,128)(2,1)}, bf16[2048,1024]{1,0:T(8,128)(2,1)}, bf16[2048,1024]{1,0:T(8,128)(2,1)}) custom-call(bf16[2048,768]{1,0:T(8,128)(2,1)} %constant_dynamic-update-slice_fusion.x_ref, bf16[768,1536]{1,0:T(8,128)(2,1)} %place_shards.6.w_ref), custom_call_target="tpu_custom_call" | custom-call | flops 13200000000 | bytes 22020096 | tf_op jit(solution)/shard_map/project/pallas_call | solution.py:139
  141.3 39.6 %attend.1 = (bf16[4,2048,2048]{2,1,0:T(8,128)(2,1)}, f32[4,256,256]{2,1,0:T(8,128)}, f32[4,256,256]{2,1,0:T(8,128)}) custom-call(bf16[4,256,256]{2,1,0:T(8,128)(2,1)} %pad_bitcast_fusion.q_ref, bf16[1536,2048]{1,0:T(8,128)(2,1)} %get-tuple-element.227.kt_ref.vt_ref, bf16[2048,1024]{1,0:T(8,128)(2,1)} %get-tuple-element.228.v_ref, ...), custom_call_target="tpu_custom_call", output_to_operand_aliasing={{0}: (3, {})} | custom-call | flops 49500000256 | bytes 67108864 | tf_op jit(solution)/shard_map/attend/pallas_call | solution.py:207
  188.9 4.5 place_shards.7
  193.5 2.1 fusion.62
  197.8 6.4 %place_shards.8 = bf16[768,3072]{1,0:T(8,128)(2,1)} custom-call(s32[2]{0:T(128)} %pad_add_fusion.s_ref, bf16[384,3072]{1,0:T(8,128)(2,1)} %refs_0_.1, bf16[192,3072]{1,0:T(8,128)(2,1)} %collective-permute-done.21.refs_1_, bf16[192,3072]{1,0:T(8,128)(2,1)} %copy-done.138), custom_call_target="tpu_custom_call" | custom-call | flops 3300000000 | bytes 9437184 | tf_op jit(solution)/shard_map/place_shards/pallas_call | solution.py:392
  204.3 5.5 fusion.63
  209.8 6.4 %place_shards.9 = bf16[3072,768]{1,0:T(8,128)(2,1)} custom-call(s32[2]{0:T(128)} %pad_add_fusion.s_ref, bf16[1536,768]{1,0:T(8,128)(2,1)} %refs_0_.2, bf16[768,768]{1,0:T(8,128)(2,1)} %collective-permute-done.22.refs_1_, bf16[768,768]{1,0:T(8,128)(2,1)} %collective-permute-done.25.refs_2_), custom_call_target="tpu_custom_call" | custom-call | flops 3300000000 | bytes 9437184 | tf_op jit(solution)/shard_map/place_shards/pallas_call | solution.py:392
  216.2 10.6 %add_convert_fusion = (bf16[256,3072]{1,0:T(8,128)(2,1)S(1)}, f32[256,3072]{1,0:T(8,128)S(1)}) fusion(f32[256,3072]{1,0:T(8,128)} %fusion.63, bf16[256,768]{1,0:T(8,128)(2,1)S(1)} %get-tuple-element.525, bf16[3072,768]{1,0:T(8,128)(2,1)} %place_shards.9), kind=kOutput, calls=%fused_computation.11 | convolution fusion | flops 1264582656 | bytes 12976128 | tf_op jit(solution)/shard_map/dot_general | solution.py:479
  229.7 2.1 multiply_reduce_fusion
  235.8 2.2 fusion.11.do_ref
  247.4 2.0 convolution_convert_fusion.3
  250.5 29.0 %attend_back.2 = (bf16[4,2048,2048]{2,1,0:T(8,128)(2,1)}, f32[2,256,256]{2,1,0:T(8,128)}, bf16[384,2048]{1,0:T(8,128)(2,1)}, bf16[384,2048]{1,0:T(8,128)(2,1)}) custom-call(bf16[4,256,256]{2,1,0:T(8,128)(2,1)} %pad_bitcast_fusion.q_ref, bf16[4,256,256]{2,1,0:T(8,128)(2,1)} %fusion.11.do_ref, ...), custom_call_target="tpu_custom_call", output_to_operand_aliasing={{0}: (5, {})} | custom-call | flops 30799998976 | bytes 33554432 | tf_op jit(solution)/shard_map/attend_back/pallas_call | solution.py:280
  287.0 1.8 convolution_convert_fusion.2
  292.3 28.7 %attend_back.3 = (bf16[4,2048,2048]{2,1,0:T(8,128)(2,1)}, f32[2,256,256]{2,1,0:T(8,128)}, bf16[384,2048]{1,0:T(8,128)(2,1)}, bf16[384,2048]{1,0:T(8,128)(2,1)}) custom-call(bf16[4,256,256]{2,1,0:T(8,128)(2,1)} %pad_bitcast_fusion.q_ref, bf16[4,256,256]{2,1,0:T(8,128)(2,1)} %fusion.11.do_ref, ...), custom_call_target="tpu_custom_call", output_to_operand_aliasing={{0}: (5, {})} | custom-call | flops 30799998976 | bytes 33554432 | tf_op jit(solution)/shard_map/attend_back/pallas_call | solution.py:280
  326.0 6.3 convolution_convert_fusion
  332.3 6.7 %convolution_convert_fusion.1 = bf16[2048,768]{1,0:T(8,128)(2,1)} fusion(bf16[1536,2048]{1,0:T(8,128)(2,1)S(1)} %constant_dynamic-update-slice_fusion.20, bf16[768,1536]{1,0:T(8,128)(2,1)S(1)} %copy-done.148), kind=kOutput, calls=%fused_computation.9 | convolution fusion | flops 4833411072 | bytes 11796480 | tf_op jit(solution)/shard_map/dot_general | solution.py:479
  343.6 1.8 collective-permute-start.45
  346.6 2.0 collective-permute-start.42
  351.6 2.1 convolution_add_fusion
  356.8 8.0 %collective-permute-done.41 = bf16[192,384]{1,0:T(8,128)(2,1)S(1)} collective-permute-done((bf16[192,384]{1,0:T(8,128)(2,1)S(1)}, bf16[192,384]{1,0:T(8,128)(2,1)S(1)}, u32[]{:S(2)}, u32[]{:S(2)}) %collective-permute-start.41) | collective-permute-done | bytes 147488 | tf_op jit(solution)/shard_map/ppermute | solution.py:470
  364.9 6.3 collective-permute-done.40
  371.1 27.1 %collective-permute-done.43 = bf16[192,1536]{1,0:T(8,128)(2,1)S(1)} collective-permute-done((bf16[192,1536]{1,0:T(8,128)(2,1)S(1)}, bf16[192,1536]{1,0:T(8,128)(2,1)S(1)}, u32[]{:S(2)}, u32[]{:S(2)}) %collective-permute-start.43) | collective-permute-done | bytes 589856 | tf_op jit(solution)/shard_map/ppermute | solution.py:470
  400.8 13.0 %table_grad.4 = f32[256,64]{1,0:T(8,128)} custom-call(f32[256,8]{1,0:T(8,128)} %pad_convert_fusion.q_ref, f32[8,2048]{1,0:T(8,128)} %pad_convert_fusion.1.k_ref, bf16[4,2048,2048]{2,1,0:T(8,128)(2,1)} %get-tuple-element.346.ds_ref), custom_call_target="tpu_custom_call" | custom-call | flops 14080000000 | bytes 8388608 | tf_op jit(solution)/shard_map/table_grad/pallas_call | solution.py:341
  416.4 1.8 collective-permute-start.56
  422.1 1.9 collective-permute-start.49
  427.5 1.8 collective-permute-start.51
  431.4 7.6 %collective-permute-start.60 = (bf16[256,384]{1,0:T(8,128)(2,1)S(1)}, bf16[256,384]{1,0:T(8,128)(2,1)S(1)}, u32[]{:S(2)}, u32[]{:S(2)}) collective-permute-start(bf16[256,384]{1,0:T(8,128)(2,1)S(1)} %get-tuple-element.485), channel_id=1, source_target_pairs={{0,4},{4,8},{8,12},{12,0},{1,5},{5,9},{9,13},{13,1},{2,6},{6,10},{... | collective-permute-start | bytes 589832 | tf_op jit(solution)/shard_map/ppermute | solution.py:470
  439.7 2.4 collective-permute-start.59
  442.9 4.1 collective-permute-done.52
  448.5 10.3 %collective-permute-start.62 = (bf16[256,384]{1,0:T(8,128)(2,1)S(1)}, bf16[256,384]{1,0:T(8,128)(2,1)S(1)}, u32[]{:S(2)}, u32[]{:S(2)}) collective-permute-start(bf16[256,384]{1,0:T(8,128)(2,1)S(1)} %get-tuple-element.483), channel_id=1, source_target_pairs={{0,8},{4,12},{8,0},{12,4},{1,9},{5,13},{9,1},{13,5},{2,10},{6,14},... | collective-permute-start | bytes 589832 | tf_op jit(solution)/shard_map/ppermute | solution.py:470
  458.8 4.1 collective-permute-done.59
  462.9 5.2 collective-permute-start.61
  468.2 8.1 %collective-permute-done.62 = bf16[256,384]{1,0:T(8,128)(2,1)S(1)} collective-permute-done((bf16[256,384]{1,0:T(8,128)(2,1)S(1)}, bf16[256,384]{1,0:T(8,128)(2,1)S(1)}, u32[]{:S(2)}, u32[]{:S(2)}) %collective-permute-start.62) | collective-permute-done | bytes 196640 | tf_op jit(solution)/shard_map/ppermute | solution.py:470
  476.3 4.5 collective-permute-start.72
  483.3 13.3 %table_grad.5 = f32[256,64]{1,0:T(8,128)} custom-call(f32[256,8]{1,0:T(8,128)} %pad_convert_fusion.q_ref, f32[8,2048]{1,0:T(8,128)} %pad_convert_fusion.1.k_ref, bf16[4,2048,2048]{2,1,0:T(8,128)(2,1)} %get-tuple-element.346.ds_ref), custom_call_target="tpu_custom_call" | custom-call | flops 14080000000 | bytes 8388608 | tf_op jit(solution)/shard_map/table_grad/pallas_call | solution.py:341
  501.0 3.8 collective-permute-start.64
  513.2 3.0 collective-permute-start.69
  519.6 10.2 %collective-permute-done.68 = bf16[48,1536]{1,0:T(8,128)(2,1)S(1)} collective-permute-done((bf16[48,1536]{1,0:T(8,128)(2,1)S(1)}, bf16[48,1536]{1,0:T(8,128)(2,1)S(1)}, u32[]{:S(2)}, u32[]{:S(2)}) %collective-permute-start.68) | collective-permute-done | bytes 147488 | tf_op jit(solution)/shard_map/ppermute | solution.py:470
  529.9 13.0 %table_grad.6 = f32[256,64]{1,0:T(8,128)} custom-call(f32[256,8]{1,0:T(8,128)} %pad_convert_fusion.q_ref, f32[8,2048]{1,0:T(8,128)} %pad_convert_fusion.1.k_ref, bf16[4,2048,2048]{2,1,0:T(8,128)(2,1)} %get-tuple-element.346.ds_ref), custom_call_target="tpu_custom_call" | custom-call | flops 14080000000 | bytes 8388608 | tf_op jit(solution)/shard_map/table_grad/pallas_call | solution.py:341
  547.0 2.0 collective-permute-start.80
  551.8 5.5 collective-permute-done.79
  557.3 5.3 collective-permute-done.78
  563.5 13.0 %table_grad.7 = f32[256,64]{1,0:T(8,128)} custom-call(f32[256,8]{1,0:T(8,128)} %pad_convert_fusion.q_ref, f32[8,2048]{1,0:T(8,128)} %pad_convert_fusion.1.k_ref, bf16[4,2048,2048]{2,1,0:T(8,128)(2,1)} %get-tuple-element.346.ds_ref), custom_call_target="tpu_custom_call" | custom-call | flops 14080000000 | bytes 8388608 | tf_op jit(solution)/shard_map/table_grad/pallas_call | solution.py:341
  581.3 2.5 collective-permute-start.81
  587.9 4.7 assemble.7
  596.5 2.7 collective-permute-done.83
  601.8 2.9 assemble.5
  604.7 2.4 collective-permute-start.91
  610.5 8.9 %collective-permute-done.90.refs_1_ = bf16[4,48,1152]{2,1,0:T(8,128)(2,1)} collective-permute-done((bf16[4,48,1152]{2,1,0:T(8,128)(2,1)S(1)}, bf16[4,48,1152]{2,1,0:T(8,128)(2,1)}, u32[]{:S(2)}, u32[]{:S(2)}) %collective-permute-start.90) | collective-permute-done | bytes 442400 | tf_op jit(solution)/shard_map/ppermute | solution.py:470
  619.4 1.9 collective-permute-start.92
  624.1 4.7 assemble.6
  628.9 4.2 assemble.4
  (691 shorter events, 166.1 us)
Async XLA Ops:
  1.6 17.4 %collective-permute-start.6 = (s32[3]{0:T(128)S(1)}, s32[3]{0:T(128)S(1)}, u32[]{:S(2)}, u32[]{:S(2)}) collective-permute-start(s32[3]{0:T(128)S(1)} %bitcast.196), channel_id=1, source_target_pairs={{0,16},{16,0},{1,17},{17,1},{2,18},{18,2},{3,19},{19,3},{4,20},{20... | collective-permute-start | bytes 44 | tf_op jit(solution)/shard_map/ppermute | solution.py:470
  6.1 12.9 %collective-permute-start.4 = (bf16[64,32]{0,1:T(8,128)(2,1)}, bf16[64,32]{0,1:T(8,128)(2,1)S(1)}, u32[]{:S(2)}, u32[]{:S(2)}) collective-permute-start(bf16[64,32]{0,1:T(8,128)(2,1)} %param.31), channel_id=1, source_target_pairs={{0,16},{16,0},{1,17},{17,1},{2,18},{18,2},{3,19},{19,3},{4,20},{20... | collective-permute-start | bytes 12296 | tf_op jit(solution)/shard_map/ppermute | solution.py:470
  7.2 12.3 %collective-permute-start.5 = (bf16[128,768]{1,0:T(8,128)(2,1)S(1)}, bf16[128,768]{1,0:T(8,128)(2,1)S(1)}, u32[]{:S(2)}, u32[]{:S(2)}) collective-permute-start(bf16[128,768]{1,0:T(8,128)(2,1)S(1)} %get-tuple-element.496), channel_id=1, source_target_pairs={{0,1},{1,0},{2,3},{3,2},{4,5},{5,4},{6,7},{7,6},{8,9},{9,8},{10,11... | collective-permute-start | bytes 589832 | tf_op jit(solution)/shard_map/ppermute | solution.py:470
  22.6 15.0 %collective-permute-start.8 = (bf16[7,384]{1,0:T(8,128)(2,1)S(1)}, bf16[7,384]{1,0:T(8,128)(2,1)S(1)}, u32[]{:S(2)}, u32[]{:S(2)}) collective-permute-start(bf16[7,384]{1,0:T(8,128)(2,1)S(1)} %concatenate.88), channel_id=1, source_target_pairs={{0,16},{16,0},{1,17},{17,1},{2,18},{18,2},{3,19},{19,3},{4,20},{20... | collective-permute-start | bytes 16136 | tf_op jit(solution)/shard_map/ppermute | solution.py:470
  24.4 30.0 %collective-permute-start.65 = (bf16[6,768]{1,0:T(8,128)(2,1)S(1)}, bf16[6,768]{1,0:T(8,128)(2,1)S(1)}, u32[]{:S(2)}, u32[]{:S(2)}) collective-permute-start(bf16[6,768]{1,0:T(8,128)(2,1)S(1)} %pad_maximum_fusion.10), channel_id=1, source_target_pairs={{0,16},{16,0},{1,17},{17,1},{2,18},{18,2},{3,19},{19,3},{4,20},{20... | collective-permute-start | bytes 27656 | tf_op jit(solution)/shard_map/ppermute | solution.py:470
  24.7 14.9 %collective-permute-start.7 = (f32[3,768]{1,0:T(4,128)S(1)}, f32[3,768]{1,0:T(4,128)S(1)}, u32[]{:S(2)}, u32[]{:S(2)}) collective-permute-start(f32[3,768]{1,0:T(4,128)S(1)} %slice.204), channel_id=1, source_target_pairs={{0,16},{16,0},{1,17},{17,1},{2,18},{18,2},{3,19},{19,3},{4,20},{20... | collective-permute-start | bytes 27656 | tf_op jit(solution)/shard_map/ppermute | solution.py:470
  28.1 42.5 %collective-permute-start.14 = (bf16[192,768]{1,0:T(8,128)(2,1)S(1)}, bf16[192,768]{1,0:T(8,128)(2,1)}, u32[]{:S(2)}, u32[]{:S(2)}) collective-permute-start(bf16[192,768]{1,0:T(8,128)(2,1)S(1)} %constant_dynamic-slice_fusion.28), channel_id=1, source_target_pairs={{0,16},{16,0},{1,17},{17,1},{2,18},{18,2},{3,19},{19,3},{4,20},{20... | collective-permute-start | bytes 884744 | tf_op jit(solution)/shard_map/ppermute | solution.py:470
  28.4 42.2 %collective-permute-start.13 = (bf16[192,1536]{1,0:T(8,128)(2,1)S(1)}, bf16[192,1536]{1,0:T(8,128)(2,1)}, u32[]{:S(2)}, u32[]{:S(2)}) collective-permute-start(bf16[192,1536]{1,0:T(8,128)(2,1)S(1)} %constant_dynamic-slice_fusion.29), channel_id=1, source_target_pairs={{0,16},{16,0},{1,17},{17,1},{2,18},{18,2},{3,19},{19,3},{4,20},{20... | collective-permute-start | bytes 1769480 | tf_op jit(solution)/shard_map/ppermute | solution.py:470
  41.6 12.9 %collective-permute-start.10 = (bf16[256,768]{1,0:T(8,128)(2,1)S(1)}, bf16[256,768]{1,0:T(8,128)(2,1)S(1)}, u32[]{:S(2)}, u32[]{:S(2)}) collective-permute-start(bf16[256,768]{1,0:T(8,128)(2,1)S(1)} %add_convert_fusion.2), channel_id=1, source_target_pairs={{0,2},{2,0},{1,3},{3,1},{4,6},{6,4},{5,7},{7,5},{8,10},{10,8},{9,1... | collective-permute-start | bytes 1179656 | tf_op jit(solution)/shard_map/ppermute | solution.py:470
  42.9 11.6 %collective-permute-start.9 = (bf16[256,768]{1,0:T(8,128)(2,1)S(1)}, bf16[256,768]{1,0:T(8,128)(2,1)S(1)}, u32[]{:S(2)}, u32[]{:S(2)}) collective-permute-start(bf16[256,768]{1,0:T(8,128)(2,1)S(1)} %add_convert_fusion.2), channel_id=1, source_target_pairs={{0,4},{4,8},{8,12},{12,0},{1,5},{5,9},{9,13},{13,1},{2,6},{6,10},{... | collective-permute-start | bytes 1179656 | tf_op jit(solution)/shard_map/ppermute | solution.py:470
  54.5 13.3 %collective-permute-start.12 = (bf16[256,768]{1,0:T(8,128)(2,1)S(1)}, bf16[256,768]{1,0:T(8,128)(2,1)S(1)}, u32[]{:S(2)}, u32[]{:S(2)}) collective-permute-start(bf16[256,768]{1,0:T(8,128)(2,1)S(1)} %collective-permute-done.9), channel_id=1, source_target_pairs={{0,2},{2,0},{1,3},{3,1},{4,6},{6,4},{5,7},{7,5},{8,10},{10,8},{9,1... | collective-permute-start | bytes 1179656 | tf_op jit(solution)/shard_map/ppermute | solution.py:470
  54.8 13.0 %collective-permute-start.11 = (bf16[256,768]{1,0:T(8,128)(2,1)S(1)}, bf16[256,768]{1,0:T(8,128)(2,1)}, u32[]{:S(2)}, u32[]{:S(2)}) collective-permute-start(bf16[256,768]{1,0:T(8,128)(2,1)S(1)} %collective-permute-done.9), channel_id=1, source_target_pairs={{0,4},{4,8},{8,12},{12,0},{1,5},{5,9},{9,13},{13,1},{2,6},{6,10},{... | collective-permute-start | bytes 1179656 | tf_op jit(solution)/shard_map/ppermute | solution.py:470
  67.9 33.0 %collective-permute-start.17 = (bf16[256,768]{1,0:T(8,128)(2,1)}, bf16[256,768]{1,0:T(8,128)(2,1)}, u32[]{:S(2)}, u32[]{:S(2)}) collective-permute-start(bf16[256,768]{1,0:T(8,128)(2,1)} %collective-permute-done.11), channel_id=1, source_target_pairs={{0,2},{2,0},{1,3},{3,1},{4,6},{6,4},{5,7},{7,5},{8,10},{10,8},{9,1... | collective-permute-start | bytes 1179656 | tf_op jit(solution)/shard_map/ppermute | solution.py:470
  69.1 32.4 %collective-permute-start.16 = (bf16[256,768]{1,0:T(8,128)(2,1)}, bf16[256,768]{1,0:T(8,128)(2,1)}, u32[]{:S(2)}, u32[]{:S(2)}) collective-permute-start(bf16[256,768]{1,0:T(8,128)(2,1)} %collective-permute-done.11), channel_id=1, source_target_pairs={{0,4},{4,8},{8,12},{12,0},{1,5},{5,9},{9,13},{13,1},{2,6},{6,10},{... | collective-permute-start | bytes 1179656 | tf_op jit(solution)/shard_map/ppermute | solution.py:470
  82.9 100.3 %collective-permute-start.20 = (bf16[192,768]{1,0:T(8,128)(2,1)}, bf16[192,768]{1,0:T(8,128)(2,1)}, u32[]{:S(2)}, u32[]{:S(2)}) collective-permute-start(bf16[192,768]{1,0:T(8,128)(2,1)} %constant_dynamic-slice_fusion.27), channel_id=1, source_target_pairs={{0,16},{16,0},{1,17},{17,1},{2,18},{18,2},{3,19},{19,3},{4,20},{20... | collective-permute-start | bytes 884744 | tf_op jit(solution)/shard_map/ppermute | solution.py:470
  90.0 25.0 %collective-permute-start.19 = (bf16[192,1536]{1,0:T(8,128)(2,1)}, bf16[192,1536]{1,0:T(8,128)(2,1)}, u32[]{:S(2)}, u32[]{:S(2)}) collective-permute-start(bf16[192,1536]{1,0:T(8,128)(2,1)} %collective-permute-done.13.refs_1_), channel_id=1, source_target_pairs={{0,1},{1,0},{2,3},{3,2},{4,5},{5,4},{6,7},{7,6},{8,9},{9,8},{10,11... | collective-permute-start | bytes 1769480 | tf_op jit(solution)/shard_map/ppermute | solution.py:470
  92.3 90.9 %collective-permute-start.22 = (bf16[768,768]{1,0:T(8,128)(2,1)S(1)}, bf16[768,768]{1,0:T(8,128)(2,1)}, u32[]{:S(2)}, u32[]{:S(2)}) collective-permute-start(bf16[768,768]{1,0:T(8,128)(2,1)S(1)} %constant_dynamic-slice_fusion.25), channel_id=1, source_target_pairs={{0,16},{16,0},{1,17},{17,1},{2,18},{18,2},{3,19},{19,3},{4,20},{20... | collective-permute-start | bytes 3538952 | tf_op jit(solution)/shard_map/ppermute | solution.py:470
  100.9 82.3 %collective-permute-start.21 = (bf16[192,3072]{1,0:T(8,128)(2,1)S(1)}, bf16[192,3072]{1,0:T(8,128)(2,1)}, u32[]{:S(2)}, u32[]{:S(2)}) collective-permute-start(bf16[192,3072]{1,0:T(8,128)(2,1)S(1)} %constant_dynamic-slice_fusion.26), channel_id=1, source_target_pairs={{0,16},{16,0},{1,17},{17,1},{2,18},{18,2},{3,19},{19,3},{4,20},{20... | collective-permute-start | bytes 3538952 | tf_op jit(solution)/shard_map/ppermute | solution.py:470
  101.5 18.7 %collective-permute-start.18 = (bf16[256,768]{1,0:T(8,128)(2,1)}, bf16[256,768]{1,0:T(8,128)(2,1)S(1)}, u32[]{:S(2)}, u32[]{:S(2)}) collective-permute-start(bf16[256,768]{1,0:T(8,128)(2,1)} %collective-permute-done.16), channel_id=1, source_target_pairs={{0,2},{2,0},{1,3},{3,1},{4,6},{6,4},{5,7},{7,5},{8,10},{10,8},{9,1... | collective-permute-start | bytes 1179656 | tf_op jit(solution)/shard_map/ppermute | solution.py:470
  185.6 94.0 %collective-permute-start.35 = (bf16[256,768]{0,1:T(8,128)(2,1)}, bf16[256,768]{0,1:T(8,128)(2,1)}, u32[]{:S(2)}, u32[]{:S(2)}) collective-permute-start(bf16[256,768]{0,1:T(8,128)(2,1)} %bitcast.22), channel_id=1, source_target_pairs={{0,1},{1,0},{2,3},{3,2},{4,5},{5,4},{6,7},{7,6},{8,9},{9,8},{10,11... | collective-permute-start | bytes 1179656 | tf_op jit(solution)/shard_map/ppermute | solution.py:470
  185.6 11.2 %collective-permute-start.24 = (bf16[192,3072]{1,0:T(8,128)(2,1)}, bf16[192,3072]{1,0:T(8,128)(2,1)S(1)}, u32[]{:S(2)}, u32[]{:S(2)}) collective-permute-start(bf16[192,3072]{1,0:T(8,128)(2,1)} %collective-permute-done.21.refs_1_), channel_id=1, source_target_pairs={{0,1},{1,0},{2,3},{3,2},{4,5},{5,4},{6,7},{7,6},{8,9},{9,8},{10,11... | collective-permute-start | bytes 3538952 | tf_op jit(solution)/shard_map/ppermute | solution.py:470
  186.1 23.7 %collective-permute-start.25 = (bf16[768,768]{1,0:T(8,128)(2,1)}, bf16[768,768]{1,0:T(8,128)(2,1)}, u32[]{:S(2)}, u32[]{:S(2)}) collective-permute-start(bf16[768,768]{1,0:T(8,128)(2,1)} %collective-permute-done.22.refs_1_), channel_id=1, source_target_pairs={{0,1},{1,0},{2,3},{3,2},{4,5},{5,4},{6,7},{7,6},{8,9},{9,8},{10,11... | collective-permute-start | bytes 3538952 | tf_op jit(solution)/shard_map/ppermute | solution.py:470
  187.7 55.3 %collective-permute-start.31 = (bf16[256,384]{1,0:T(8,128)(2,1)}, bf16[256,384]{1,0:T(8,128)(2,1)}, u32[]{:S(2)}, u32[]{:S(2)}) collective-permute-start(bf16[256,384]{1,0:T(8,128)(2,1)} %get-tuple-element.492), channel_id=1, source_target_pairs={{0,1},{1,0},{2,3},{3,2},{4,5},{5,4},{6,7},{7,6},{8,9},{9,8},{10,11... | collective-permute-start | bytes 589832 | tf_op jit(solution)/shard_map/ppermute | solution.py:470
  196.8 82.8 %collective-permute-start.33 = (bf16[256,768]{1,0:T(8,128)(2,1)}, bf16[256,768]{1,0:T(8,128)(2,1)}, u32[]{:S(2)}, u32[]{:S(2)}) collective-permute-start(bf16[256,768]{1,0:T(8,128)(2,1)} %add_convert_fusion.1), channel_id=1, source_target_pairs={{0,1},{1,0},{2,3},{3,2},{4,5},{5,4},{6,7},{7,6},{8,9},{9,8},{10,11... | collective-permute-start | bytes 1179656 | tf_op jit(solution)/shard_map/ppermute | solution.py:470
  228.8 14.3 %collective-permute-start.30 = (bf16[256,3072]{1,0:T(8,128)(2,1)S(1)}, bf16[256,3072]{1,0:T(8,128)(2,1)}, u32[]{:S(2)}, u32[]{:S(2)}) collective-permute-start(bf16[256,3072]{1,0:T(8,128)(2,1)S(1)} %multiply_convert_fusion), channel_id=1, source_target_pairs={{0,1},{1,0},{2,3},{3,2},{4,5},{5,4},{6,7},{7,6},{8,9},{9,8},{10,11... | collective-permute-start | bytes 4718600 | tf_op jit(solution)/shard_map/ppermute | solution.py:470
  241.8 37.8 %collective-permute-start.36 = (bf16[256,384]{1,0:T(8,128)(2,1)}, bf16[256,384]{1,0:T(8,128)(2,1)S(1)}, u32[]{:S(2)}, u32[]{:S(2)}) collective-permute-start(bf16[256,384]{1,0:T(8,128)(2,1)} %get-tuple-element.490), channel_id=1, source_target_pairs={{0,1},{1,0},{2,3},{3,2},{4,5},{5,4},{6,7},{7,6},{8,9},{9,8},{10,11... | collective-permute-start | bytes 589832 | tf_op jit(solution)/shard_map/ppermute | solution.py:470
  242.9 36.7 %collective-permute-start.34 = (bf16[256,1536]{1,0:T(8,128)(2,1)}, bf16[256,1536]{1,0:T(8,128)(2,1)}, u32[]{:S(2)}, u32[]{:S(2)}) collective-permute-start(bf16[256,1536]{1,0:T(8,128)(2,1)} %get-tuple-element.469), channel_id=1, source_target_pairs={{0,1},{1,0},{2,3},{3,2},{4,5},{5,4},{6,7},{7,6},{8,9},{9,8},{10,11... | collective-permute-start | bytes 2359304 | tf_op jit(solution)/shard_map/ppermute | solution.py:470
  249.4 30.2 %collective-permute-start.32 = (bf16[1536,384]{1,0:T(8,128)(2,1)}, bf16[1536,384]{1,0:T(8,128)(2,1)S(1)}, u32[]{:S(2)}, u32[]{:S(2)}) collective-permute-start(bf16[1536,384]{1,0:T(8,128)(2,1)} %convolution_convert_fusion.3), channel_id=1, source_target_pairs={{0,16},{16,0},{1,17},{17,1},{2,18},{18,2},{3,19},{19,3},{4,20},{20... | collective-permute-start | bytes 3538952 | tf_op jit(solution)/shard_map/ppermute | solution.py:470
  284.1 37.1 %collective-permute-start.39 = (bf16[384,384]{1,0:T(8,128)(2,1)}, bf16[384,384]{1,0:T(8,128)(2,1)}, u32[]{:S(2)}, u32[]{:S(2)}) collective-permute-start(bf16[384,384]{1,0:T(8,128)(2,1)} %convolution_convert_fusion.7), channel_id=1, source_target_pairs={{0,16},{16,0},{1,17},{17,1},{2,18},{18,2},{3,19},{19,3},{4,20},{20... | collective-permute-start | bytes 884744 | tf_op jit(solution)/shard_map/ppermute | solution.py:470
  288.9 32.3 %collective-permute-start.38 = (bf16[384,1536]{1,0:T(8,128)(2,1)}, bf16[384,1536]{1,0:T(8,128)(2,1)}, u32[]{:S(2)}, u32[]{:S(2)}) collective-permute-start(bf16[384,1536]{1,0:T(8,128)(2,1)} %convolution_convert_fusion.2), channel_id=1, source_target_pairs={{0,16},{16,0},{1,17},{17,1},{2,18},{18,2},{3,19},{19,3},{4,20},{20... | collective-permute-start | bytes 3538952 | tf_op jit(solution)/shard_map/ppermute | solution.py:470
  291.1 30.1 %collective-permute-start.37 = (bf16[768,384]{1,0:T(8,128)(2,1)S(1)}, bf16[768,384]{1,0:T(8,128)(2,1)}, u32[]{:S(2)}, u32[]{:S(2)}) collective-permute-start(bf16[768,384]{1,0:T(8,128)(2,1)S(1)} %dynamic-slice_convert_fusion.2), channel_id=1, source_target_pairs={{0,2},{2,0},{1,3},{3,1},{4,6},{6,4},{5,7},{7,5},{8,10},{10,8},{9,1... | collective-permute-start | bytes 1769480 | tf_op jit(solution)/shard_map/ppermute | solution.py:470
  341.7 12.1 %collective-permute-start.44 = (bf16[192,384]{1,0:T(8,128)(2,1)S(1)}, bf16[192,384]{1,0:T(8,128)(2,1)S(1)}, u32[]{:S(2)}, u32[]{:S(2)}) collective-permute-start(bf16[192,384]{1,0:T(8,128)(2,1)S(1)} %dynamic-slice_convert_fusion.7), channel_id=1, source_target_pairs={{0,2},{2,0},{1,3},{3,1},{4,6},{6,4},{5,7},{7,5},{8,10},{10,8},{9,1... | collective-permute-start | bytes 442376 | tf_op jit(solution)/shard_map/ppermute | solution.py:470
  343.6 54.7 %collective-permute-start.45 = (bf16[768,1152]{1,0:T(8,128)(2,1)S(1)}, bf16[768,1152]{1,0:T(8,128)(2,1)S(1)}, u32[]{:S(2)}, u32[]{:S(2)}) collective-permute-start(bf16[768,1152]{1,0:T(8,128)(2,1)S(1)} %get-tuple-element.459), channel_id=1, source_target_pairs={{0,1},{1,0},{2,3},{3,2},{4,5},{5,4},{6,7},{7,6},{8,9},{9,8},{10,11... | collective-permute-start | bytes 5308424 | tf_op jit(solution)/shard_map/ppermute | solution.py:470
  350.1 48.2 %collective-permute-start.47 = (bf16[4,256,384]{2,1,0:T(8,128)(2,1)S(1)}, bf16[4,256,384]{2,1,0:T(8,128)(2,1)S(1)}, u32[]{:S(2)}, u32[]{:S(2)}) collective-permute-start(bf16[4,256,384]{2,1,0:T(8,128)(2,1)S(1)} %get-tuple-element.461), channel_id=1, source_target_pairs={{0,2},{2,0},{1,3},{3,1},{4,6},{6,4},{5,7},{7,5},{8,10},{10,8},{9,1... | collective-permute-start | bytes 2359304 | tf_op jit(solution)/shard_map/ppermute | solution.py:470
  351.3 47.0 %collective-permute-start.46 = (bf16[4,256,384]{2,1,0:T(8,128)(2,1)S(1)}, bf16[4,256,384]{2,1,0:T(8,128)(2,1)S(1)}, u32[]{:S(2)}, u32[]{:S(2)}) collective-permute-start(bf16[4,256,384]{2,1,0:T(8,128)(2,1)S(1)} %get-tuple-element.463), channel_id=1, source_target_pairs={{0,2},{2,0},{1,3},{3,1},{4,6},{6,4},{5,7},{7,5},{8,10},{10,8},{9,1... | collective-permute-start | bytes 2359304 | tf_op jit(solution)/shard_map/ppermute | solution.py:470
  353.8 44.5 %collective-permute-start.43 = (bf16[192,1536]{1,0:T(8,128)(2,1)S(1)}, bf16[192,1536]{1,0:T(8,128)(2,1)S(1)}, u32[]{:S(2)}, u32[]{:S(2)}) collective-permute-start(bf16[192,1536]{1,0:T(8,128)(2,1)S(1)} %dynamic-slice_convert_fusion.1), channel_id=1, source_target_pairs={{0,2},{2,0},{1,3},{3,1},{4,6},{6,4},{5,7},{7,5},{8,10},{10,8},{9,1... | collective-permute-start | bytes 1769480 | tf_op jit(solution)/shard_map/ppermute | solution.py:470
  414.9 12.5 %collective-permute-start.50 = (bf16[192,384]{1,0:T(8,128)(2,1)S(1)}, bf16[192,384]{1,0:T(8,128)(2,1)S(1)}, u32[]{:S(2)}, u32[]{:S(2)}) collective-permute-start(bf16[192,384]{1,0:T(8,128)(2,1)S(1)} %add_convert_fusion.4), channel_id=1, source_target_pairs={{0,12},{4,0},{8,4},{12,8},{1,13},{5,1},{9,5},{13,9},{2,14},{6,2},{... | collective-permute-start | bytes 442376 | tf_op jit(solution)/shard_map/ppermute | solution.py:470
  421.1 55.2 %collective-permute-start.57 = (bf16[384,1152]{1,0:T(8,128)(2,1)S(1)}, bf16[384,1152]{1,0:T(8,128)(2,1)S(1)}, u32[]{:S(2)}, u32[]{:S(2)}) collective-permute-start(bf16[384,1152]{1,0:T(8,128)(2,1)S(1)} %copy-done.40), channel_id=1, source_target_pairs={{0,16},{16,0},{1,17},{17,1},{2,18},{18,2},{3,19},{19,3},{4,20},{20... | collective-permute-start | bytes 2654216 | tf_op jit(solution)/shard_map/ppermute | solution.py:470
  425.7 13.3 %collective-permute-start.53 = (bf16[48,1536]{1,0:T(8,128)(2,1)S(1)}, bf16[48,1536]{1,0:T(8,128)(2,1)S(1)}, u32[]{:S(2)}, u32[]{:S(2)}) collective-permute-start(bf16[48,1536]{1,0:T(8,128)(2,1)S(1)} %get-tuple-element.473), channel_id=1, source_target_pairs={{0,12},{4,0},{8,4},{12,8},{1,13},{5,1},{9,5},{13,9},{2,14},{6,2},{... | collective-permute-start | bytes 442376 | tf_op jit(solution)/shard_map/ppermute | solution.py:470
  427.4 19.6 %collective-permute-start.52 = (bf16[48,1536]{1,0:T(8,128)(2,1)S(1)}, bf16[48,1536]{1,0:T(8,128)(2,1)S(1)}, u32[]{:S(2)}, u32[]{:S(2)}) collective-permute-start(bf16[48,1536]{1,0:T(8,128)(2,1)S(1)} %get-tuple-element.474), channel_id=1, source_target_pairs={{0,8},{4,12},{8,0},{12,4},{1,9},{5,13},{9,1},{13,5},{2,10},{6,14},... | collective-permute-start | bytes 442376 | tf_op jit(solution)/shard_map/ppermute | solution.py:470
  427.5 20.5 %collective-permute-start.51 = (bf16[48,1536]{1,0:T(8,128)(2,1)S(1)}, bf16[48,1536]{1,0:T(8,128)(2,1)S(1)}, u32[]{:S(2)}, u32[]{:S(2)}) collective-permute-start(bf16[48,1536]{1,0:T(8,128)(2,1)S(1)} %get-tuple-element.475), channel_id=1, source_target_pairs={{0,4},{4,8},{8,12},{12,0},{1,5},{5,9},{9,13},{13,1},{2,6},{6,10},{... | collective-permute-start | bytes 442376 | tf_op jit(solution)/shard_map/ppermute | solution.py:470
  431.4 17.0 %collective-permute-start.60 = (bf16[256,384]{1,0:T(8,128)(2,1)S(1)}, bf16[256,384]{1,0:T(8,128)(2,1)S(1)}, u32[]{:S(2)}, u32[]{:S(2)}) collective-permute-start(bf16[256,384]{1,0:T(8,128)(2,1)S(1)} %get-tuple-element.485), channel_id=1, source_target_pairs={{0,4},{4,8},{8,12},{12,0},{1,5},{5,9},{9,13},{13,1},{2,6},{6,10},{... | collective-permute-start | bytes 589832 | tf_op jit(solution)/shard_map/ppermute | solution.py:470
  439.7 23.2 %collective-permute-start.59 = (bf16[256,384]{1,0:T(8,128)(2,1)S(1)}, bf16[256,384]{1,0:T(8,128)(2,1)S(1)}, u32[]{:S(2)}, u32[]{:S(2)}) collective-permute-start(bf16[256,384]{1,0:T(8,128)(2,1)S(1)} %get-tuple-element.486), channel_id=1, source_target_pairs={{0,8},{4,12},{8,0},{12,4},{1,9},{5,13},{9,1},{13,5},{2,10},{6,14},... | collective-permute-start | bytes 589832 | tf_op jit(solution)/shard_map/ppermute | solution.py:470
  447.0 21.2 %collective-permute-start.58 = (bf16[256,384]{1,0:T(8,128)(2,1)S(1)}, bf16[256,384]{1,0:T(8,128)(2,1)S(1)}, u32[]{:S(2)}, u32[]{:S(2)}) collective-permute-start(bf16[256,384]{1,0:T(8,128)(2,1)S(1)} %get-tuple-element.487), channel_id=1, source_target_pairs={{0,12},{4,0},{8,4},{12,8},{1,13},{5,1},{9,5},{13,9},{2,14},{6,2},{... | collective-permute-start | bytes 589832 | tf_op jit(solution)/shard_map/ppermute | solution.py:470
  448.0 20.2 %collective-permute-start.63 = (bf16[256,384]{1,0:T(8,128)(2,1)S(1)}, bf16[256,384]{1,0:T(8,128)(2,1)S(1)}, u32[]{:S(2)}, u32[]{:S(2)}) collective-permute-start(bf16[256,384]{1,0:T(8,128)(2,1)S(1)} %get-tuple-element.482), channel_id=1, source_target_pairs={{0,4},{4,8},{8,12},{12,0},{1,5},{5,9},{9,13},{13,1},{2,6},{6,10},{... | collective-permute-start | bytes 589832 | tf_op jit(solution)/shard_map/ppermute | solution.py:470
  448.5 27.9 %collective-permute-start.62 = (bf16[256,384]{1,0:T(8,128)(2,1)S(1)}, bf16[256,384]{1,0:T(8,128)(2,1)S(1)}, u32[]{:S(2)}, u32[]{:S(2)}) collective-permute-start(bf16[256,384]{1,0:T(8,128)(2,1)S(1)} %get-tuple-element.483), channel_id=1, source_target_pairs={{0,8},{4,12},{8,0},{12,4},{1,9},{5,13},{9,1},{13,5},{2,10},{6,14},... | collective-permute-start | bytes 589832 | tf_op jit(solution)/shard_map/ppermute | solution.py:470
  462.9 13.4 %collective-permute-start.61 = (bf16[256,384]{1,0:T(8,128)(2,1)S(1)}, bf16[256,384]{1,0:T(8,128)(2,1)S(1)}, u32[]{:S(2)}, u32[]{:S(2)}) collective-permute-start(bf16[256,384]{1,0:T(8,128)(2,1)S(1)} %get-tuple-element.484), channel_id=1, source_target_pairs={{0,12},{4,0},{8,4},{12,8},{1,13},{5,1},{9,5},{13,9},{2,14},{6,2},{... | collective-permute-start | bytes 589832 | tf_op jit(solution)/shard_map/ppermute | solution.py:470
  476.3 35.2 %collective-permute-start.72 = (bf16[48,384]{1,0:T(8,128)(2,1)S(1)}, bf16[48,384]{1,0:T(8,128)(2,1)}, u32[]{:S(2)}, u32[]{:S(2)}) collective-permute-start(bf16[48,384]{1,0:T(8,128)(2,1)S(1)} %add_convert_fusion.6), channel_id=1, source_target_pairs={{0,12},{4,0},{8,4},{12,8},{1,13},{5,1},{9,5},{13,9},{2,14},{6,2},{... | collective-permute-start | bytes 110600 | tf_op jit(solution)/shard_map/ppermute | solution.py:470
  480.8 32.4 %collective-permute-start.71 = (bf16[48,384]{1,0:T(8,128)(2,1)S(1)}, bf16[48,384]{1,0:T(8,128)(2,1)}, u32[]{:S(2)}, u32[]{:S(2)}) collective-permute-start(bf16[48,384]{1,0:T(8,128)(2,1)S(1)} %add_convert_fusion.6), channel_id=1, source_target_pairs={{0,8},{4,12},{8,0},{12,4},{1,9},{5,13},{9,1},{13,5},{2,10},{6,14},... | collective-permute-start | bytes 110600 | tf_op jit(solution)/shard_map/ppermute | solution.py:470
  482.1 34.1 %collective-permute-start.70 = (bf16[48,384]{1,0:T(8,128)(2,1)S(1)}, bf16[48,384]{1,0:T(8,128)(2,1)}, u32[]{:S(2)}, u32[]{:S(2)}) collective-permute-start(bf16[48,384]{1,0:T(8,128)(2,1)S(1)} %add_convert_fusion.6), channel_id=1, source_target_pairs={{0,4},{4,8},{8,12},{12,0},{1,5},{5,9},{9,13},{13,1},{2,6},{6,10},{... | collective-permute-start | bytes 110600 | tf_op jit(solution)/shard_map/ppermute | solution.py:470
  501.0 16.0 %collective-permute-start.64 = (f32[128,768]{1,0:T(8,128)}, f32[128,768]{1,0:T(8,128)}, u32[]{:S(2)}, u32[]{:S(2)}) collective-permute-start(f32[128,768]{1,0:T(8,128)} %slice.228), channel_id=1, source_target_pairs={{0,1},{1,0},{2,3},{3,2},{4,5},{5,4},{6,7},{7,6},{8,9},{9,8},{10,11... | collective-permute-start | bytes 1179656 | tf_op jit(solution)/shard_map/ppermute | solution.py:470
  504.9 24.9 %collective-permute-start.66 = (bf16[4,192,384]{2,1,0:T(8,128)(2,1)S(1)}, bf16[4,192,384]{2,1,0:T(8,128)(2,1)}, u32[]{:S(2)}, u32[]{:S(2)}) collective-permute-start(bf16[4,192,384]{2,1,0:T(8,128)(2,1)S(1)} %pad_maximum_fusion.1.refs_0_), channel_id=1, source_target_pairs={{0,2},{2,0},{1,3},{3,1},{4,6},{6,4},{5,7},{7,5},{8,10},{10,8},{9,1... | collective-permute-start | bytes 1769480 | tf_op jit(solution)/shard_map/ppermute | solution.py:470
  511.5 18.3 %collective-permute-start.73 = (bf16[192,1152]{1,0:T(8,128)(2,1)S(1)}, bf16[192,1152]{1,0:T(8,128)(2,1)}, u32[]{:S(2)}, u32[]{:S(2)}) collective-permute-start(bf16[192,1152]{1,0:T(8,128)(2,1)S(1)} %copy-done.58), channel_id=1, source_target_pairs={{0,2},{2,0},{1,3},{3,1},{4,6},{6,4},{5,7},{7,5},{8,10},{10,8},{9,1... | collective-permute-start | bytes 1327112 | tf_op jit(solution)/shard_map/ppermute | solution.py:470
  516.2 13.7 %collective-permute-start.68 = (bf16[48,1536]{1,0:T(8,128)(2,1)S(1)}, bf16[48,1536]{1,0:T(8,128)(2,1)S(1)}, u32[]{:S(2)}, u32[]{:S(2)}) collective-permute-start(bf16[48,1536]{1,0:T(8,128)(2,1)S(1)} %add_convert_fusion.3), channel_id=1, source_target_pairs={{0,8},{4,12},{8,0},{12,4},{1,9},{5,13},{9,1},{13,5},{2,10},{6,14},... | collective-permute-start | bytes 442376 | tf_op jit(solution)/shard_map/ppermute | solution.py:470
  517.0 12.8 %collective-permute-start.67 = (bf16[48,1536]{1,0:T(8,128)(2,1)S(1)}, bf16[48,1536]{1,0:T(8,128)(2,1)S(1)}, u32[]{:S(2)}, u32[]{:S(2)}) collective-permute-start(bf16[48,1536]{1,0:T(8,128)(2,1)S(1)} %add_convert_fusion.3), channel_id=1, source_target_pairs={{0,4},{4,8},{8,12},{12,0},{1,5},{5,9},{9,13},{13,1},{2,6},{6,10},{... | collective-permute-start | bytes 442376 | tf_op jit(solution)/shard_map/ppermute | solution.py:470
  543.0 19.7 %collective-permute-start.76 = (bf16[4,48,1536]{2,1,0:T(8,128)(2,1)S(1)}, bf16[4,48,1536]{2,1,0:T(8,128)(2,1)S(1)}, u32[]{:S(2)}, u32[]{:S(2)}) collective-permute-start(bf16[4,48,1536]{2,1,0:T(8,128)(2,1)S(1)} %pad_maximum_fusion.2.refs_0_), channel_id=1, source_target_pairs={{0,2},{2,0},{1,3},{3,1},{4,6},{6,4},{5,7},{7,5},{8,10},{10,8},{9,1... | collective-permute-start | bytes 1769480 | tf_op jit(solution)/shard_map/ppermute | solution.py:470
  544.2 18.5 %collective-permute-start.74 = (bf16[4,192,384]{2,1,0:T(8,128)(2,1)S(1)}, bf16[4,192,384]{2,1,0:T(8,128)(2,1)S(1)}, u32[]{:S(2)}, u32[]{:S(2)}) collective-permute-start(bf16[4,192,384]{2,1,0:T(8,128)(2,1)S(1)} %pad_maximum_fusion.1.refs_0_), channel_id=1, source_target_pairs={{0,1},{1,0},{2,3},{3,2},{4,5},{5,4},{6,7},{7,6},{8,9},{9,8},{10,11... | collective-permute-start | bytes 1769480 | tf_op jit(solution)/shard_map/ppermute | solution.py:470
  545.9 17.6 %collective-permute-start.75 = (bf16[4,192,384]{2,1,0:T(8,128)(2,1)}, bf16[4,192,384]{2,1,0:T(8,128)(2,1)}, u32[]{:S(2)}, u32[]{:S(2)}) collective-permute-start(bf16[4,192,384]{2,1,0:T(8,128)(2,1)} %collective-permute-done.66.refs_1_), channel_id=1, source_target_pairs={{0,1},{1,0},{2,3},{3,2},{4,5},{5,4},{6,7},{7,6},{8,9},{9,8},{10,11... | collective-permute-start | bytes 1769480 | tf_op jit(solution)/shard_map/ppermute | solution.py:470
  551.4 11.2 %collective-permute-start.77 = (bf16[4,48,384]{2,1,0:T(8,128)(2,1)S(1)}, bf16[4,48,384]{2,1,0:T(8,128)(2,1)S(1)}, u32[]{:S(2)}, u32[]{:S(2)}) collective-permute-start(bf16[4,48,384]{2,1,0:T(8,128)(2,1)S(1)} %pad_maximum_fusion.8.refs_0_), channel_id=1, source_target_pairs={{0,2},{2,0},{1,3},{3,1},{4,6},{6,4},{5,7},{7,5},{8,10},{10,8},{9,1... | collective-permute-start | bytes 442376 | tf_op jit(solution)/shard_map/ppermute | solution.py:470
  584.1 11.2 %collective-permute-start.87 = (bf16[48,1152]{1,0:T(8,128)(2,1)S(1)}, bf16[48,1152]{1,0:T(8,128)(2,1)S(1)}, u32[]{:S(2)}, u32[]{:S(2)}) collective-permute-start(bf16[48,1152]{1,0:T(8,128)(2,1)S(1)} %add_convert_fusion.5), channel_id=1, source_target_pairs={{0,4},{4,8},{8,12},{12,0},{1,5},{5,9},{9,13},{13,1},{2,6},{6,10},{... | collective-permute-start | bytes 331784 | tf_op jit(solution)/shard_map/ppermute | solution.py:470
  585.4 14.6 %collective-permute-start.93 = (bf16[4,48,384]{2,1,0:T(8,128)(2,1)S(1)}, bf16[4,48,384]{2,1,0:T(8,128)(2,1)S(1)}, u32[]{:S(2)}, u32[]{:S(2)}) collective-permute-start(bf16[4,48,384]{2,1,0:T(8,128)(2,1)S(1)} %pad_maximum_fusion.8.refs_0_), channel_id=1, source_target_pairs={{0,1},{1,0},{2,3},{3,2},{4,5},{5,4},{6,7},{7,6},{8,9},{9,8},{10,11... | collective-permute-start | bytes 442376 | tf_op jit(solution)/shard_map/ppermute | solution.py:470
  593.0 30.2 %collective-permute-start.95 = (bf16[4,48,1536]{2,1,0:T(8,128)(2,1)S(1)}, bf16[4,48,1536]{2,1,0:T(8,128)(2,1)S(1)}, u32[]{:S(2)}, u32[]{:S(2)}) collective-permute-start(bf16[4,48,1536]{2,1,0:T(8,128)(2,1)S(1)} %pad_maximum_fusion.2.refs_0_), channel_id=1, source_target_pairs={{0,1},{1,0},{2,3},{3,2},{4,5},{5,4},{6,7},{7,6},{8,9},{9,8},{10,11... | collective-permute-start | bytes 1769480 | tf_op jit(solution)/shard_map/ppermute | solution.py:470
  594.3 29.0 %collective-permute-start.96 = (bf16[4,48,1536]{2,1,0:T(8,128)(2,1)S(1)}, bf16[4,48,1536]{2,1,0:T(8,128)(2,1)}, u32[]{:S(2)}, u32[]{:S(2)}) collective-permute-start(bf16[4,48,1536]{2,1,0:T(8,128)(2,1)S(1)} %collective-permute-done.76.refs_1_), channel_id=1, source_target_pairs={{0,1},{1,0},{2,3},{3,2},{4,5},{5,4},{6,7},{7,6},{8,9},{9,8},{10,11... | collective-permute-start | bytes 1769480 | tf_op jit(solution)/shard_map/ppermute | solution.py:470
  604.7 24.1 %collective-permute-start.91 = (bf16[4,48,1152]{2,1,0:T(8,128)(2,1)S(1)}, bf16[4,48,1152]{2,1,0:T(8,128)(2,1)}, u32[]{:S(2)}, u32[]{:S(2)}) collective-permute-start(bf16[4,48,1152]{2,1,0:T(8,128)(2,1)S(1)} %pad_maximum_fusion.4.refs_0_), channel_id=1, source_target_pairs={{0,1},{1,0},{2,3},{3,2},{4,5},{5,4},{6,7},{7,6},{8,9},{9,8},{10,11... | collective-permute-start | bytes 1327112 | tf_op jit(solution)/shard_map/ppermute | solution.py:470
  (184 other events, 1985.6 us)

commit v2 on v1

--- a/solution.py
+++ b/solution.py
@@ -24,10 +24,11 @@
 FORWARD_TILE = 32
 BACKWARD_TILE = 64
 FINE = 8
+KERNEL_COST = 2.5e8
 
 
 def cost(micros, bytes_moved):
-    return pl.CostEstimate(flops=int(micros * 1.1e9), bytes_accessed=int(bytes_moved), transcendentals=0)
+    return pl.CostEstimate(flops=int(micros * KERNEL_COST), bytes_accessed=int(bytes_moved), transcendentals=0)
 
 
 def distance_tile(q_ref, k_ref):
@@ -404,48 +405,50 @@
     )(where, own, *mine, *other)
 
 
-def assemble_kernel(xs, s_ref, *refs):
-    out_ref = refs[-1]
-    own_refs, other_refs = refs[:xs], refs[xs:2 * xs]
-    zs, rows, half = own_refs[0].shape
-    x, z, core = s_ref[0], s_ref[1], s_ref[2]
+def assemble_kernel(xs, widths, s_ref, *refs):
+    own_refs, other_refs, out_refs = refs[:xs], refs[xs:2 * xs], refs[2 * xs:]
+    zs = own_refs[0].shape[0]
+    x, core = s_ref[0], s_ref[1]
     jx = pl.program_id(0)
     from_x = lax.rem(x - jx + xs, xs)
+    first = core == 0
     for step in range(xs):
         @pl.when(from_x == step)
         def copy_piece():
             for jz in range(zs):
-                from_z = lax.rem(z - jz + zs, zs)
-                own = own_refs[step][from_z].astype(jnp.float32)
-                other = other_refs[step][from_z].astype(jnp.float32)
-                first = core == 0
-                out_ref[0, jz, :, :half] = jnp.where(first, own, other)
-                out_ref[0, jz, :, half:] = jnp.where(first, other, own)
-
-
-def assemble(where, own, other):
+                begin = 0
+                for half, out_ref in zip(widths, out_refs):
+                    own = own_refs[step][jz, :, begin:begin + half].astype(jnp.float32)
+                    other = other_refs[step][jz, :, begin:begin + half].astype(jnp.float32)
+                    out_ref[0, jz, :, :half] = jnp.where(first, own, other)
+                    out_ref[0, jz, :, half:] = jnp.where(first, other, own)
+                    begin += half
+
+
+def assemble(where, own, other, widths):
     xs = len(own)
-    zs, rows, half = own[0].shape
-    spec = pl.BlockSpec((zs, rows, half), lambda i, s: (0, 0, 0))
-    whole = pl.pallas_call(
-        functools.partial(assemble_kernel, xs),
+    zs, rows, columns = own[0].shape
+    spec = pl.BlockSpec((zs, rows, columns), lambda i, s: (0, 0, 0))
+    wholes = pl.pallas_call(
+        functools.partial(assemble_kernel, xs, widths),
         grid_spec=pltpu.PrefetchScalarGridSpec(
             num_scalar_prefetch=1,
             grid=(xs,),
             in_specs=[spec] * (2 * xs),
-            out_specs=pl.BlockSpec((1, zs, rows, 2 * half), lambda i, s: (i, 0, 0, 0)),
+            out_specs=[pl.BlockSpec((1, zs, rows, 2 * half), lambda i, s: (i, 0, 0, 0)) for half in widths],
         ),
-        out_shape=jax.ShapeDtypeStruct((xs, zs, rows, 2 * half), jnp.float32),
-        cost_estimate=cost(4, xs * zs * rows * half * 12),
+        out_shape=[jax.ShapeDtypeStruct((xs, zs, rows, 2 * half), jnp.float32) for half in widths],
+        cost_estimate=cost(4, xs * zs * rows * columns * 12),
         compiler_params=pltpu.CompilerParams(vmem_limit_bytes=VMEM_LIMIT),
         name="assemble",
     )(where, *own, *other)
-    return whole.reshape(xs * zs * rows, 2 * half)
+    return [whole.reshape(xs * zs * rows, -1) for whole in wholes]
 
 
 eps = 1e-05
 highest = lax.Precision.HIGHEST
 CHIP_ROW = 4
+Z_EXCHANGE = True
 
 
 def layer_norm(values, norm_gain, norm_shift):
@@ -514,17 +517,6 @@
     return lax.optimization_barrier(groups)
 
 
-def send_parts(values, axis):
-    count = lax.axis_size(axis)
-    place = lax.axis_index(axis)
-    own = part_of(values, place, count, 0)
-    incoming = [
-        shifted(part_of(values, lax.rem(place + step, count), count, 0).astype(jnp.bfloat16), axis, step)
-        for step in range(1, count)
-    ]
-    return own, incoming
-
-
 def add_parts(own, incoming):
     total = own.astype(jnp.float32)
     for share in incoming:
@@ -532,50 +524,83 @@
     return total
 
 
-def reduce_chain(owned):
-    for axis in ("x", "z"):
-        own, incoming = yield send_parts(owned, axis)
-        owned = add_parts(own, incoming)
-    owned = owned.astype(jnp.bfloat16)
-    owned, incoming = yield owned, [shifted(owned, "z", step) for step in range(1, lax.axis_size("z"))]
-    pieces = jnp.stack([owned] + incoming)
+def turn_back(values, axis):
+    count, place = lax.axis_size(axis), lax.axis_index(axis)
+    ring = jnp.concatenate([values, values], axis=0)[::-1]
+    return lax.dynamic_slice_in_dim(ring, count - 1 - place, count, 0)
+
+
+def reduce_chain(local, hops, widths):
+    left = ["dp", "x", "z"]
+    for axis in hops:
+        dim = left.index(axis)
+        left.pop(dim)
+        count, place = lax.axis_size(axis), lax.axis_index(axis)
+        if axis == "z" and Z_EXCHANGE:
+            local = yield lax.all_to_all(local.astype(jnp.bfloat16), "z", dim, 0)
+            local = jnp.sum(local.astype(jnp.float32), axis=0)
+            continue
+        own = lax.dynamic_index_in_dim(local, place, dim, keepdims=False)
+        incoming = [
+            shifted(
+                lax.dynamic_index_in_dim(local, lax.rem(place + step, count), dim, keepdims=False).astype(jnp.bfloat16),
+                axis,
+                step,
+            )
+            for step in range(1, count)
+        ]
+        own, incoming = yield own, incoming
+        local = add_parts(own, incoming)
+    owned = local.astype(jnp.bfloat16)
+    if Z_EXCHANGE:
+        copies = jnp.broadcast_to(owned[None], (lax.axis_size("z"),) + owned.shape)
+        pieces = yield lax.all_to_all(copies, "z", 0, 0)
+    else:
+        owned, incoming = yield owned, [shifted(owned, "z", step) for step in range(1, lax.axis_size("z"))]
+        pieces = turn_back(jnp.stack([owned] + incoming), "z")
     own = yield [pieces] + [shifted(pieces, "x", step) for step in range(1, lax.axis_size("x"))]
     own, other = yield own, [shifted(piece, "core", 1) for piece in own]
-    where = jnp.stack([lax.axis_index(axis) for axis in ("x", "z", "core")]).astype(jnp.int32)
-    return assemble(where, own, other)
-
-
-def weight_chain(inputs, grads):
+    where = jnp.stack([lax.axis_index(axis) for axis in ("x", "core")]).astype(jnp.int32)
+    return assemble(where, own, other, widths)
+
+
+def by_owner(values):
+    counts = [lax.axis_size(axis) for axis in ("dp", "x", "z")]
+    return values.reshape(counts + [-1, values.shape[1]])
+
+
+def weight_chain(factors, hops):
     core = lax.axis_index("core")
-    count = lax.axis_size("dp")
-    place = lax.axis_index("dp")
-    own_right = part_of(grads, core, 2, 1)
-    inputs, other_left, own_right, other_right = yield (
-        inputs, shifted(inputs, "core", 1), own_right, shifted(part_of(grads, 1 - core, 2, 1), "core", 1)
-    )
-    left = jnp.concatenate([inputs, other_left], axis=0)
-    right = jnp.concatenate([own_right, other_right], axis=0)
-    incoming = []
-    for step in range(1, count):
-        share = dot32(part_of(left, lax.rem(place + step, count), count, 1), right, (0, 0)).astype(jnp.bfloat16)
-        incoming.append(shifted(share, "dp", step))
-    left, right, incoming = yield left, right, incoming
-    owned = add_parts(dot32(part_of(left, place, count, 1), right, (0, 0)), incoming)
-    return (yield from reduce_chain(owned))
-
-
-def table_chain(local):
+    moving = []
+    for inputs, grads in factors:
+        moving.append((
+            inputs, shifted(inputs, "core", 1),
+            part_of(grads, core, 2, 1), shifted(part_of(grads, 1 - core, 2, 1), "core", 1),
+        ))
+    moving = yield moving
+    local = [
+        dot32(jnp.concatenate([left, other_left], axis=0), jnp.concatenate([right, other_right], axis=0), (0, 0))
+        .astype(jnp.bfloat16)
+        for left, other_left, right, other_right in moving
+    ]
+    return (yield from reduce_chain(by_owner(jnp.concatenate(local, axis=1)), hops, [part.shape[1] for part in local]))
+
+
+def table_chain(local, hops):
     core = lax.axis_index("core")
     own = part_of(local, core, 2, 1)
     own, other = yield own, shifted(part_of(local, 1 - core, 2, 1), "core", 1)
-    own, incoming = yield send_parts(own.astype(jnp.float32) + other.astype(jnp.float32), "dp")
-    return (yield from reduce_chain(add_parts(own, incoming)))
+    chip = (own.astype(jnp.float32) + other.astype(jnp.float32)).astype(jnp.bfloat16)
+    return (yield from reduce_chain(by_owner(chip), hops, [chip.shape[1]]))
 
 
 def share_chain(shares):
     x_count, z_count = shares.shape[:2]
     own, incoming = yield shares[0], [shifted(shares[step], "x", -step) for step in range(1, x_count)]
     total = add_parts(own, incoming)
+    if Z_EXCHANGE:
+        low = turn_back(total.astype(jnp.bfloat16), "z")
+        return jnp.sum((yield lax.all_to_all(low, "z", 0, 0)).astype(jnp.float32), axis=0)
     low = total.astype(jnp.bfloat16)
     own, incoming = yield total[0], [shifted(low[step], "z", -step) for step in range(1, z_count)]
     return add_parts(own, incoming)
@@ -809,37 +834,48 @@
     attended_grad = by_group(dot32(second_low, out_full, (1, 1)).astype(jnp.bfloat16))
     scaled_grad = (attended_grad.astype(jnp.float32) * inverse).astype(jnp.bfloat16)
 
-    down = Flight(weight_chain(activated_low, third_low))
-    up = Flight(weight_chain(normed_two_low, hidden_grad))
-    out = Flight(weight_chain(attended_low, second_low))
-
-    scaled_grad = advance(scaled_grad, down)
-    first_back = attend_back(query, scaled_grad, attended, key_flat, turned, probs, 0, 2)
-    first_back, scaled_grad = advance((first_back, scaled_grad), down, up, out)
-    second_back = attend_back(query, scaled_grad, attended, key_flat, turned, first_back[0], 1, 2)
-    backs = advance([first_back[1:], second_back[1:], second_back[0]], down, up, out)
-    logit_grad = backs.pop()
+    down = Flight(weight_chain([(activated_low, third_low)], ("dp", "x", "z")))
+    up = Flight(weight_chain([(normed_two_low, hidden_grad), (attended_low, second_low)], ("x", "dp", "z")))
+
+    scaled_grad = advance(scaled_grad, down, up)
+    back = attend_back(query, scaled_grad, attended, key_flat, turned, probs, 0, 4)
+    backs = [back[1:]]
+    pairs, scaled_grad = advance((back[0], scaled_grad))
+    back = attend_back(query, scaled_grad, attended, key_flat, turned, pairs, 1, 4)
+    backs.append(back[1:])
+    pairs, scaled_grad = advance((back[0], scaled_grad), down, up)
+    back = attend_back(query, scaled_grad, attended, key_flat, turned, pairs, 2, 4)
+    backs.append(back[1:])
+    pairs, scaled_grad = advance((back[0], scaled_grad), down, up)
+    back = attend_back(query, scaled_grad, attended, key_flat, turned, pairs, 3, 4)
+    backs.append(back[1:])
+    logit_grad, backs = advance((back[0], backs), down)
     query_grad = flat_groups(jnp.concatenate([back[0] for back in backs], axis=0)).astype(jnp.bfloat16)
     pair_grad_turn = jnp.concatenate([back[1] for back in backs] + [back[2] for back in backs], axis=0)
 
+    query_part = dot32(normed_low, query_grad, (0, 0)).astype(jnp.bfloat16)
+    pair_part = dot32(normed_all, pair_grad_turn, (0, 1)).astype(jnp.bfloat16)
+    table = Flight(table_chain(jnp.concatenate([query_part, pair_part], axis=1), ("dp", "x", "z")))
     pair_share = dot32(pair_grad_turn, pair_weight, (0, 1)).astype(jnp.bfloat16)
     own = pair_share.reshape(x_count, z_count, 2 * held, D)
-    shares = [Flight(share_chain(own[..., part * (D // 2):(part + 1) * (D // 2)])) for part in range(2)]
-    query_part = dot32(normed_low, query_grad, (0, 0)).astype(jnp.bfloat16)
-    pair_part = dot32(normed_all, pair_grad_turn, (0, 1)).astype(jnp.bfloat16)
-    table = Flight(table_chain(jnp.concatenate([query_part, pair_part], axis=1)))
-
-    sums = None
-    flights = [down, up, out, table] + shares
+    first_half, second_half = own[..., :D // 2], own[..., D // 2:]
+    share_one = Flight(share_chain(first_half))
     steps = tiles // 4
-    for part in range(4):
-        logit_grad = advance(logit_grad, *flights)
-        piece = table_grad(query_where, key_where, logit_grad, part * steps, steps)
-        piece, logit_grad = tie(piece, logit_grad)
-        sums = piece if sums is None else sums + piece
-    bias_grad = table_sums(sums)
-    pair_normed_grad = jnp.concatenate([finish(share) for share in shares], axis=1)
-    down_grad, up_grad, out_grad, qkv_grad = [finish(flight) for flight in (down, up, out, table)]
+    logit_grad, second_half = advance((logit_grad, second_half), up, table)
+    sums = table_grad(query_where, key_where, logit_grad, 0, steps)
+    sums, logit_grad, second_half = advance((sums, logit_grad, second_half), share_one, down)
+    share_two = Flight(share_chain(second_half))
+    piece = table_grad(query_where, key_where, logit_grad, steps, steps)
+    sums, piece, logit_grad = advance((sums, piece, logit_grad), share_one, share_two, table)
+    sums = sums + piece
+    piece = table_grad(query_where, key_where, logit_grad, 2 * steps, steps)
+    sums, piece, logit_grad = advance((sums, piece, logit_grad), share_two, table, up)
+    sums = sums + piece
+    piece = table_grad(query_where, key_where, logit_grad, 3 * steps, steps)
+    sums, piece = advance((sums, piece), table, down)
+    bias_grad = table_sums(sums + piece)
+    pair_normed_grad = jnp.concatenate([finish(share_one), finish(share_two)], axis=1)
+    (down_grad,), (up_grad, out_grad), (qkv_grad,) = [finish(flight) for flight in (down, up, table)]
 
     normed_grad = dot32(query_grad, query_weight, (1, 1)) + pair_normed_grad
     first_part, gain_one_grad, shift_one_grad = norm_one_back(normed_grad)
@@ -854,24 +890,23 @@
     slots = 2 * dp_count
     slot = jnp.arange(slots) == 2 * place + core
     protein_slots = jnp.where(slot[:, None, None], protein_sum[None], 0.0)
-    packed = jnp.concatenate(
+    padding = jnp.zeros((6 * D - KERNELS * HEADS,), jnp.float32)
+    last = sum_all(jnp.concatenate(
         [
-            gain_one_grad.reshape(-1),
-            shift_one_grad.reshape(-1),
-            gain_two_grad.reshape(-1),
-            shift_two_grad.reshape(-1),
-            force_grad.reshape(-1),
-            bias_grad.reshape(-1),
-            protein_slots.reshape(-1),
-        ]
-    )
-    packed = sum_all(packed)
-    vectors = packed[:4 * D].reshape(4, D)
-    vectors = part_of(vectors, place, dp_count, 1)
-    force_sum = part_of(packed[4 * D:7 * D].reshape(3, D), place, dp_count, 1)
-    table_end = 7 * D + KERNELS * HEADS
-    bias_sum = part_of(packed[7 * D:table_end].reshape(KERNELS, HEADS), place, dp_count, 0)
-    protein_all = packed[table_end:].reshape(slots, proteins, D)
+            gain_one_grad,
+            shift_one_grad,
+            gain_two_grad,
+            shift_two_grad,
+            force_grad,
+            jnp.concatenate([bias_grad.reshape(-1), padding]).reshape(6, D),
+            protein_slots.reshape(slots * proteins, D),
+        ],
+        axis=0,
+    ))
+    vectors = part_of(last[:4], place, dp_count, 1)
+    force_sum = part_of(last[4:7], place, dp_count, 1)
+    bias_sum = part_of(last[7:13].reshape(-1)[:KERNELS * HEADS].reshape(KERNELS, HEADS), place, dp_count, 0)
+    protein_all = last[13:]
     other_steps = lax.dynamic_index_in_dim(time_steps, 1 - core, 0, keepdims=False)
     both_steps = jnp.where(core == 0, jnp.stack([my_steps, other_steps]), jnp.stack([other_steps, my_steps]))
     all_features = time_features(both_steps.reshape(-1).astype(jnp.float32), D).astype(jnp.bfloat16)
@@ -879,7 +914,7 @@
     time_grad = jnp.einsum(
         "sd,se->de",
         part_of(all_features, place, dp_count, 1).astype(jnp.float32),
-        protein_all.reshape(slots * proteins, D),
+        protein_all,
         precision=highest,
     )
 

time: 641 us -> 618 us (0.964)
  waiting for transfers between devices: 101 us -> 64.7 us
  other arithmetic: 30.1 us -> 52.9 us
  starting transfers between devices: 115 us -> 93 us
  local copies, waits for them, and re-layouts: 70.3 us -> 78.1 us
    ppermute x97 -> x62, starting transfers between devices: 115 us -> 56.9 us  [shifted(): lax.ppermute(values, axis, [(i, (i + step) % size) for i in range(size)])]
    ppermute x97 -> x62, waiting for transfers between devices: 101 us -> 50 us  [shifted(): lax.ppermute(values, axis, [(i, (i + step) % size) for i in range(size)])]
    all_to_all x0 -> x8, starting transfers between devices: none -> 36.1 us  [the longest x3 14 us: reduce_chain(): pieces = (yield lax.all_to_all(copies, 'z', 0, 0))]
    all_to_all x0 -> x8, waiting for transfers between devices: none -> 14.8 us  [the longest x2 14.8 us: share_chain(): lax.all_to_all(low, 'z', 0, 0)]
    pallas_call x2 -> x4, Pallas kernels: 57.7 us -> 66.1 us  [attend_back(): pl.pallas_call(functools.partial(backward_kernel, 512), grid=(rows // til...]
    convert_element_type x6, other arithmetic: 3.11 us -> 10.9 us  [the longest x3 6.25 us: reduce_chain(): local = (yield lax.all_to_all(local.astype(jnp.bfloat16), 'z', dim, 0))]
    concatenate x7 -> x2, local copies, waits for them, and re-layouts: 7.59 us -> 0.29 us  [the longest x1 0.29 us: body(): jnp.concatenate([gain_one_grad, shift_one_grad, gain_two_grad, shift_two_...]
    unnamed x331 -> x185, local copies, waits for them, and re-layouts: 34.5 us -> 27.4 us
  transfers between devices with their start and end apart: 97 -> 70, of which waited for: 20 -> 13; matrix products, arithmetic and copies ran while one was open for 17% -> 25% of each run, Pallas kernels for 34% -> 43%
where the time goes in v2:
time: 618 us; the launch traced here: 610 us
  Pallas kernels  268 us (43%)
  starting transfers between devices  93 us (15%)
  local copies, waits for them, and re-layouts  78.1 us (13%)
  waiting for transfers between devices  64.7 us (10%)
  other arithmetic  52.9 us (9%)
  matrix products  51.3 us (8%)
    pallas_call x4, Pallas kernels, attend_back(): pl.pallas_call(functools.partial(backward_kernel, 512), grid=(rows // til...  66.1 us
    ppermute x62, starting transfers between devices, shifted(): lax.ppermute(values, axis, [(i, (i + step) % size) for i in range(size)])  56.9 us
    pallas_call x5, Pallas kernels, pair_bias(): pl.pallas_call(functools.partial(bias_kernel, 256), grid=(steps,), in_spe...  53.5 us
    pallas_call x4, Pallas kernels, table_grad(): pl.pallas_call(functools.partial(table_grad_kernel, 256), grid=(steps,),...  52.1 us
    ppermute x62, waiting for transfers between devices, shifted(): lax.ppermute(values, axis, [(i, (i + step) % size) for i in range(size)])  50 us
    pallas_call x1, Pallas kernels, attend(): pl.pallas_call(functools.partial(forward_kernel, 512), grid=(rows // tile...  39.6 us
    dot_general x10, matrix products, dot32(): lax.dot_general(left, right, ((contract[:1], contract[1:]), ((), ())), pr...  34.7 us
    unnamed x185, local copies, waits for them, and re-layouts  27.4 us
  transfers between devices with their start and end apart: 70, of which 13 were waited for; matrix products, arithmetic and copies ran while one was open for 25% of the time, Pallas kernels for 43%

profile of v2, /device:TPU:1, one launch (start us, length us, event | category | flops | bytes accessed | tf_op | source)
XLA Modules:
  0.0 610.3 jit_solution(321572870113464555)
XLA Ops:
  1.4 2.1 collective-permute-start.6
  8.5 1.8 collective-permute-start.1
  10.3 3.0 collective-permute-done.1
  13.8 2.9 collective-permute-done.2
  29.2 7.3 %pair_bias.5.refs_0_ = bf16[4,2048,2048]{2,1,0:T(8,128)(2,1)} custom-call(f32[256,8]{1,0:T(8,128)} %pad_convert_fusion.q_ref, f32[8,2048]{1,0:T(8,128)} %pad_convert_fusion.1.k_ref, bf16[32,128]{1,0:T(8,128)(2,1)} %fusion.47.w_ref), custom_call_target="tpu_custom_call" | custom-call | flops 1500000000 | bytes 4194304 | tf_op jit(solution)/shard_map/pair_bias/pallas_call | solution.py:103
  39.8 2.2 collective-permute-done.7
  46.4 11.6 %pair_bias.6.refs_0_ = bf16[4,2048,2048]{2,1,0:T(8,128)(2,1)} custom-call(f32[256,8]{1,0:T(8,128)} %pad_convert_fusion.q_ref, f32[8,2048]{1,0:T(8,128)} %pad_convert_fusion.1.k_ref, bf16[32,128]{1,0:T(8,128)(2,1)} %fusion.47.w_ref, bf16[4,2048,2048]{2,1,0:T(8,128)(2,1)} %pair_bias.5.refs_0_), custom_call_target="tpu_custom_call", output_to_operand_aliasing={{}: (3, {})} | custom-call | flops 2624999936 | bytes 7340032 | tf_op jit(solution)/shard_map/pair_bias/pallas_call | solution.py:103
  61.8 11.6 %pair_bias.7.refs_0_ = bf16[4,2048,2048]{2,1,0:T(8,128)(2,1)} custom-call(f32[256,8]{1,0:T(8,128)} %pad_convert_fusion.q_ref, f32[8,2048]{1,0:T(8,128)} %pad_convert_fusion.1.k_ref, bf16[32,128]{1,0:T(8,128)(2,1)} %fusion.47.w_ref, bf16[4,2048,2048]{2,1,0:T(8,128)(2,1)} %pair_bias.6.refs_0_), custom_call_target="tpu_custom_call", output_to_operand_aliasing={{}: (3, {})} | custom-call | flops 2624999936 | bytes 7340032 | tf_op jit(solution)/shard_map/pair_bias/pallas_call | solution.py:103
  77.2 7.6 %collective-permute-start.15 = (bf16[192,768]{1,0:T(8,128)(2,1)}, bf16[192,768]{1,0:T(8,128)(2,1)}, u32[]{:S(2)}, u32[]{:S(2)}) collective-permute-start(bf16[192,768]{1,0:T(8,128)(2,1)} %collective-permute-done.14.refs_1_), channel_id=1, source_target_pairs={{0,1},{1,0},{2,3},{3,2},{4,5},{5,4},{6,7},{7,6},{8,9},{9,8},{10,11... | collective-permute-start | bytes 884744 | tf_op jit(solution)/shard_map/ppermute | solution.py:473
  88.8 11.5 %pair_bias.8.refs_0_ = bf16[4,2048,2048]{2,1,0:T(8,128)(2,1)} custom-call(f32[256,8]{1,0:T(8,128)} %pad_convert_fusion.q_ref, f32[8,2048]{1,0:T(8,128)} %pad_convert_fusion.1.k_ref, bf16[32,128]{1,0:T(8,128)(2,1)} %fusion.47.w_ref, bf16[4,2048,2048]{2,1,0:T(8,128)(2,1)} %pair_bias.7.refs_0_), custom_call_target="tpu_custom_call", output_to_operand_aliasing={{}: (3, {})} | custom-call | flops 2624999936 | bytes 7340032 | tf_op jit(solution)/shard_map/pair_bias/pallas_call | solution.py:103
  101.5 4.3 place_shards.5
  111.1 11.5 %pair_bias.9.bias_ref = bf16[4,2048,2048]{2,1,0:T(8,128)(2,1)} custom-call(f32[256,8]{1,0:T(8,128)} %pad_convert_fusion.q_ref, f32[8,2048]{1,0:T(8,128)} %pad_convert_fusion.1.k_ref, bf16[32,128]{1,0:T(8,128)(2,1)} %fusion.47.w_ref, bf16[4,2048,2048]{2,1,0:T(8,128)(2,1)} %pair_bias.8.refs_0_), custom_call_target="tpu_custom_call", output_to_operand_aliasing={{}: (3, {})} | custom-call | flops 2624999936 | bytes 7340032 | tf_op jit(solution)/shard_map/pair_bias/pallas_call | solution.py:103
  123.4 4.9 place_shards.6.w_ref
  135.2 15.3 %project.1 = (bf16[1536,2048]{1,0:T(8,128)(2,1)}, bf16[2048,1024]{1,0:T(8,128)(2,1)}, bf16[2048,1024]{1,0:T(8,128)(2,1)}) custom-call(bf16[2048,768]{1,0:T(8,128)(2,1)} %constant_dynamic-update-slice_fusion.x_ref, bf16[768,1536]{1,0:T(8,128)(2,1)} %place_shards.6.w_ref), custom_call_target="tpu_custom_call" | custom-call | flops 3000000000 | bytes 22020096 | tf_op jit(solution)/shard_map/project/pallas_call | solution.py:140
  150.5 39.6 %attend.1 = (bf16[4,2048,2048]{2,1,0:T(8,128)(2,1)}, f32[4,256,256]{2,1,0:T(8,128)}, f32[4,256,256]{2,1,0:T(8,128)}) custom-call(bf16[4,256,256]{2,1,0:T(8,128)(2,1)} %pad_bitcast_fusion.q_ref, bf16[1536,2048]{1,0:T(8,128)(2,1)} %get-tuple-element.202.kt_ref.vt_ref, bf16[2048,1024]{1,0:T(8,128)(2,1)} %get-tuple-element.203.v_ref, ...), custom_call_target="tpu_custom_call", output_to_operand_aliasing={{0}: (3, {})} | custom-call | flops 11249999872 | bytes 67108864 | tf_op jit(solution)/shard_map/attend/pallas_call | solution.py:208
  198.8 4.8 place_shards.7
  203.7 2.1 fusion.75
  207.1 6.4 %place_shards.8 = bf16[768,3072]{1,0:T(8,128)(2,1)} custom-call(s32[2]{0:T(128)} %pad_add_fusion.s_ref, bf16[384,3072]{1,0:T(8,128)(2,1)} %refs_0_.1, bf16[192,3072]{1,0:T(8,128)(2,1)} %collective-permute-done.21.refs_1_, bf16[192,3072]{1,0:T(8,128)(2,1)} %collective-permute-done.24.refs_2_), custom_call_target="tpu_custom_call" | custom-call | flops 750000000 | bytes 9437184 | tf_op jit(solution)/shard_map/place_shards/pallas_call | solution.py:393
  213.5 5.5 fusion.76
  219.1 6.6 %place_shards.9 = bf16[3072,768]{1,0:T(8,128)(2,1)} custom-call(s32[2]{0:T(128)} %pad_add_fusion.s_ref, bf16[1536,768]{1,0:T(8,128)(2,1)} %refs_0_.2, bf16[768,768]{1,0:T(8,128)(2,1)} %copy-done.30, bf16[768,768]{1,0:T(8,128)(2,1)} %collective-permute-done.25.refs_2_), custom_call_target="tpu_custom_call" | custom-call | flops 750000000 | bytes 9437184 | tf_op jit(solution)/shard_map/place_shards/pallas_call | solution.py:393
  225.6 10.5 %add_convert_fusion.1 = (bf16[256,3072]{1,0:T(8,128)(2,1)S(1)}, f32[256,3072]{1,0:T(8,128)S(1)}) fusion(f32[256,3072]{1,0:T(8,128)} %fusion.76, bf16[256,768]{1,0:T(8,128)(2,1)S(1)} %get-tuple-element.459, bf16[3072,768]{1,0:T(8,128)(2,1)} %place_shards.9), kind=kOutput, calls=%fused_computation.16 | convolution fusion | flops 1264582656 | bytes 12976128 | tf_op jit(solution)/shard_map/dot_general | solution.py:482
  247.7 2.8 convolution_convert_fusion.2
  253.2 3.7 convolution_convert_fusion
  261.1 24.6 %collective-permute-done.46 = bf16[6,768]{1,0:T(8,128)(2,1)S(1)} collective-permute-done((bf16[6,768]{1,0:T(8,128)(2,1)S(1)}, bf16[6,768]{1,0:T(8,128)(2,1)S(1)}, u32[]{:S(2)}, u32[]{:S(2)}) %collective-permute-start.46) | collective-permute-done | bytes 9248 | tf_op jit(solution)/shard_map/ppermute | solution.py:473
  285.7 16.4 %attend_back.4 = (bf16[4,2048,2048]{2,1,0:T(8,128)(2,1)}, f32[1,256,256]{2,1,0:T(8,128)}, bf16[192,2048]{1,0:T(8,128)(2,1)}, bf16[192,2048]{1,0:T(8,128)(2,1)}) custom-call(bf16[4,256,256]{2,1,0:T(8,128)(2,1)} %pad_bitcast_fusion.q_ref, bf16[4,256,256]{2,1,0:T(8,128)(2,1)} %fusion.15.do_ref, ...), custom_call_target="tpu_custom_call", output_to_operand_aliasing={{0}: (5, {})} | custom-call | flops 3500000000 | bytes 16777216 | tf_op jit(solution)/shard_map/attend_back/pallas_call | solution.py:281
  302.2 16.7 %attend_back.5 = (bf16[4,2048,2048]{2,1,0:T(8,128)(2,1)}, f32[1,256,256]{2,1,0:T(8,128)}, bf16[192,2048]{1,0:T(8,128)(2,1)}, bf16[192,2048]{1,0:T(8,128)(2,1)}) custom-call(bf16[4,256,256]{2,1,0:T(8,128)(2,1)} %pad_bitcast_fusion.q_ref, bf16[4,256,256]{2,1,0:T(8,128)(2,1)} %fusion.15.do_ref, ...), custom_call_target="tpu_custom_call", output_to_operand_aliasing={{0}: (5, {})} | custom-call | flops 3500000000 | bytes 16777216 | tf_op jit(solution)/shard_map/attend_back/pallas_call | solution.py:281
  325.6 16.5 %attend_back.6 = (bf16[4,2048,2048]{2,1,0:T(8,128)(2,1)}, f32[1,256,256]{2,1,0:T(8,128)}, bf16[192,2048]{1,0:T(8,128)(2,1)}, bf16[192,2048]{1,0:T(8,128)(2,1)}) custom-call(bf16[4,256,256]{2,1,0:T(8,128)(2,1)} %pad_bitcast_fusion.q_ref, bf16[4,256,256]{2,1,0:T(8,128)(2,1)} %fusion.15.do_ref, ...), custom_call_target="tpu_custom_call", output_to_operand_aliasing={{0}: (5, {})} | custom-call | flops 3500000000 | bytes 16777216 | tf_op jit(solution)/shard_map/attend_back/pallas_call | solution.py:281
  342.1 2.0 add_convert_fusion.5
  344.1 3.5 all-to-all-start
  348.2 16.5 %attend_back.7 = (bf16[4,2048,2048]{2,1,0:T(8,128)(2,1)}, f32[1,256,256]{2,1,0:T(8,128)}, bf16[192,2048]{1,0:T(8,128)(2,1)}, bf16[192,2048]{1,0:T(8,128)(2,1)}) custom-call(bf16[4,256,256]{2,1,0:T(8,128)(2,1)} %pad_bitcast_fusion.q_ref, bf16[4,256,256]{2,1,0:T(8,128)(2,1)} %fusion.15.do_ref, ...), custom_call_target="tpu_custom_call", output_to_operand_aliasing={{0}: (5, {})} | custom-call | flops 3500000000 | bytes 16777216 | tf_op jit(solution)/shard_map/attend_back/pallas_call | solution.py:281
  364.7 2.1 add_convert_fusion.4
  367.6 4.9 all-to-all-start.1
  383.7 5.3 convolution_convert_fusion.1
  389.0 2.2 fusion.9
  391.3 2.6 collective-permute-start.40
  393.9 5.3 convolution_convert_fusion.3
  405.7 5.0 all-to-all-start.2
  410.7 4.3 fusion.14
  419.1 13.1 %table_grad.4 = f32[256,64]{1,0:T(8,128)} custom-call(f32[256,8]{1,0:T(8,128)} %pad_convert_fusion.q_ref, f32[8,2048]{1,0:T(8,128)} %pad_convert_fusion.1.k_ref, bf16[4,2048,2048]{2,1,0:T(8,128)(2,1)} %get-tuple-element.298.ds_ref), custom_call_target="tpu_custom_call" | custom-call | flops 3200000000 | bytes 8388608 | tf_op jit(solution)/shard_map/table_grad/pallas_call | solution.py:342
  434.8 2.7 rev.6
  437.5 2.1 constant_dynamic-slice_fusion.7
  439.6 4.8 all-to-all-start.3
  444.4 2.0 add_convert_fusion
  450.5 13.5 %all-to-all-done.3 = bf16[4,256,384]{2,1,0:T(8,128)(2,1)S(1)} async-done(((bf16[4,256,384]{2,1,0:T(8,128)(2,1)}), bf16[4,256,384]{2,1,0:T(8,128)(2,1)S(1)}, u32[]{:S(2)}, u32[]{:S(2)}) %all-to-all-start.3) | async-done | bytes 786464 | tf_op jit(solution)/shard_map/all_to_all | solution.py:603
  465.1 4.2 all-to-all-start.5
  470.1 13.0 %table_grad.5 = f32[256,64]{1,0:T(8,128)} custom-call(f32[256,8]{1,0:T(8,128)} %pad_convert_fusion.q_ref, f32[8,2048]{1,0:T(8,128)} %pad_convert_fusion.1.k_ref, bf16[4,2048,2048]{2,1,0:T(8,128)(2,1)} %get-tuple-element.298.ds_ref), custom_call_target="tpu_custom_call" | custom-call | flops 3200000000 | bytes 8388608 | tf_op jit(solution)/shard_map/table_grad/pallas_call | solution.py:342
  485.9 2.1 constant_dynamic-slice_fusion.6
  488.0 4.6 all-to-all-start.4
  497.9 13.1 %table_grad.6 = f32[256,64]{1,0:T(8,128)} custom-call(f32[256,8]{1,0:T(8,128)} %pad_convert_fusion.q_ref, f32[8,2048]{1,0:T(8,128)} %pad_convert_fusion.1.k_ref, bf16[4,2048,2048]{2,1,0:T(8,128)(2,1)} %get-tuple-element.298.ds_ref), custom_call_target="tpu_custom_call" | custom-call | flops 3200000000 | bytes 8388608 | tf_op jit(solution)/shard_map/table_grad/pallas_call | solution.py:342
  512.4 2.8 fusion.70
  518.6 2.1 add_convert_fusion.6
  520.7 4.3 all-to-all-start.6
  525.1 2.5 fusion.16
  528.8 2.4 collective-permute-start.45
  533.3 13.0 %table_grad.7 = f32[256,64]{1,0:T(8,128)} custom-call(f32[256,8]{1,0:T(8,128)} %pad_convert_fusion.q_ref, f32[8,2048]{1,0:T(8,128)} %pad_convert_fusion.1.k_ref, bf16[4,2048,2048]{2,1,0:T(8,128)(2,1)} %get-tuple-element.298.ds_ref), custom_call_target="tpu_custom_call" | custom-call | flops 3200000000 | bytes 8388608 | tf_op jit(solution)/shard_map/table_grad/pallas_call | solution.py:342
  551.1 4.8 all-to-all-start.7
  557.9 2.9 collective-permute-done.49
  564.4 3.2 collective-permute-start.53
  569.4 3.3 collective-permute-start.58
  572.8 3.8 collective-permute-done.52
  581.8 8.3 %collective-permute-done.54.refs_1_ = bf16[4,48,1152]{2,1,0:T(8,128)(2,1)S(1)} collective-permute-done((bf16[4,48,1152]{2,1,0:T(8,128)(2,1)S(1)}, bf16[4,48,1152]{2,1,0:T(8,128)(2,1)S(1)}, u32[]{:S(2)}, u32[]{:S(2)}) %collective-permute-start.54) | collective-permute-done | bytes 442400 | tf_op jit(solution)/shard_map/ppermute | solution.py:473
  593.4 4.7 assemble.5
  599.0 5.5 assemble.4
  606.0 4.1 assemble.3
  (487 shorter events, 157.5 us)
Async XLA Ops:
  1.4 17.3 %collective-permute-start.6 = (s32[3]{0:T(128)S(1)}, s32[3]{0:T(128)S(1)}, u32[]{:S(2)}, u32[]{:S(2)}) collective-permute-start(s32[3]{0:T(128)S(1)} %bitcast.178), channel_id=1, source_target_pairs={{0,16},{16,0},{1,17},{17,1},{2,18},{18,2},{3,19},{19,3},{4,20},{20... | collective-permute-start | bytes 44 | tf_op jit(solution)/shard_map/ppermute | solution.py:473
  5.0 3.5 collective-permute-start
  6.0 12.7 %collective-permute-start.4 = (bf16[64,32]{0,1:T(8,128)(2,1)}, bf16[64,32]{0,1:T(8,128)(2,1)S(1)}, u32[]{:S(2)}, u32[]{:S(2)}) collective-permute-start(bf16[64,32]{0,1:T(8,128)(2,1)} %param.31), channel_id=1, source_target_pairs={{0,16},{16,0},{1,17},{17,1},{2,18},{18,2},{3,19},{19,3},{4,20},{20... | collective-permute-start | bytes 12296 | tf_op jit(solution)/shard_map/ppermute | solution.py:473
  7.0 12.3 %collective-permute-start.5 = (bf16[128,768]{1,0:T(8,128)(2,1)S(1)}, bf16[128,768]{1,0:T(8,128)(2,1)S(1)}, u32[]{:S(2)}, u32[]{:S(2)}) collective-permute-start(bf16[128,768]{1,0:T(8,128)(2,1)S(1)} %get-tuple-element.433), channel_id=1, source_target_pairs={{0,1},{1,0},{2,3},{3,2},{4,5},{5,4},{6,7},{7,6},{8,9},{9,8},{10,11... | collective-permute-start | bytes 589832 | tf_op jit(solution)/shard_map/ppermute | solution.py:473
  8.5 4.8 collective-permute-start.1
  13.3 3.4 collective-permute-start.2
  22.8 16.9 %collective-permute-start.8 = (bf16[7,384]{1,0:T(8,128)(2,1)S(1)}, bf16[7,384]{1,0:T(8,128)(2,1)S(1)}, u32[]{:S(2)}, u32[]{:S(2)}) collective-permute-start(bf16[7,384]{1,0:T(8,128)(2,1)S(1)} %concatenate.100), channel_id=1, source_target_pairs={{0,16},{16,0},{1,17},{17,1},{2,18},{18,2},{3,19},{19,3},{4,20},{20... | collective-permute-start | bytes 16136 | tf_op jit(solution)/shard_map/ppermute | solution.py:473
  44.0 13.9 %collective-permute-start.10 = (bf16[256,768]{1,0:T(8,128)(2,1)S(1)}, bf16[256,768]{1,0:T(8,128)(2,1)S(1)}, u32[]{:S(2)}, u32[]{:S(2)}) collective-permute-start(bf16[256,768]{1,0:T(8,128)(2,1)S(1)} %add_convert_fusion.8), channel_id=1, source_target_pairs={{0,2},{2,0},{1,3},{3,1},{4,6},{6,4},{5,7},{7,5},{8,10},{10,8},{9,1... | collective-permute-start | bytes 1179656 | tf_op jit(solution)/shard_map/ppermute | solution.py:473
  45.3 12.7 %collective-permute-start.9 = (bf16[256,768]{1,0:T(8,128)(2,1)S(1)}, bf16[256,768]{1,0:T(8,128)(2,1)}, u32[]{:S(2)}, u32[]{:S(2)}) collective-permute-start(bf16[256,768]{1,0:T(8,128)(2,1)S(1)} %add_convert_fusion.8), channel_id=1, source_target_pairs={{0,4},{4,8},{8,12},{12,0},{1,5},{5,9},{9,13},{13,1},{2,6},{6,10},{... | collective-permute-start | bytes 1179656 | tf_op jit(solution)/shard_map/ppermute | solution.py:473
  46.2 30.1 %collective-permute-start.13 = (bf16[192,1536]{1,0:T(8,128)(2,1)}, bf16[192,1536]{1,0:T(8,128)(2,1)}, u32[]{:S(2)}, u32[]{:S(2)}) collective-permute-start(bf16[192,1536]{1,0:T(8,128)(2,1)} %constant_dynamic-slice_fusion.20), channel_id=1, source_target_pairs={{0,16},{16,0},{1,17},{17,1},{2,18},{18,2},{3,19},{19,3},{4,20},{20... | collective-permute-start | bytes 1769480 | tf_op jit(solution)/shard_map/ppermute | solution.py:473
  58.0 15.4 %collective-permute-start.12 = (bf16[256,768]{1,0:T(8,128)(2,1)}, bf16[256,768]{1,0:T(8,128)(2,1)}, u32[]{:S(2)}, u32[]{:S(2)}) collective-permute-start(bf16[256,768]{1,0:T(8,128)(2,1)} %collective-permute-done.9), channel_id=1, source_target_pairs={{0,2},{2,0},{1,3},{3,1},{4,6},{6,4},{5,7},{7,5},{8,10},{10,8},{9,1... | collective-permute-start | bytes 1179656 | tf_op jit(solution)/shard_map/ppermute | solution.py:473
  58.3 15.1 %collective-permute-start.11 = (bf16[256,768]{1,0:T(8,128)(2,1)}, bf16[256,768]{1,0:T(8,128)(2,1)}, u32[]{:S(2)}, u32[]{:S(2)}) collective-permute-start(bf16[256,768]{1,0:T(8,128)(2,1)} %collective-permute-done.9), channel_id=1, source_target_pairs={{0,4},{4,8},{8,12},{12,0},{1,5},{5,9},{9,13},{13,1},{2,6},{6,10},{... | collective-permute-start | bytes 1179656 | tf_op jit(solution)/shard_map/ppermute | solution.py:473
  59.8 16.5 %collective-permute-start.14 = (bf16[192,768]{1,0:T(8,128)(2,1)}, bf16[192,768]{1,0:T(8,128)(2,1)}, u32[]{:S(2)}, u32[]{:S(2)}) collective-permute-start(bf16[192,768]{1,0:T(8,128)(2,1)} %constant_dynamic-slice_fusion.19), channel_id=1, source_target_pairs={{0,16},{16,0},{1,17},{17,1},{2,18},{18,2},{3,19},{19,3},{4,20},{20... | collective-permute-start | bytes 884744 | tf_op jit(solution)/shard_map/ppermute | solution.py:473
  73.4 35.5 %collective-permute-start.17 = (bf16[256,768]{1,0:T(8,128)(2,1)}, bf16[256,768]{1,0:T(8,128)(2,1)}, u32[]{:S(2)}, u32[]{:S(2)}) collective-permute-start(bf16[256,768]{1,0:T(8,128)(2,1)} %collective-permute-done.11), channel_id=1, source_target_pairs={{0,2},{2,0},{1,3},{3,1},{4,6},{6,4},{5,7},{7,5},{8,10},{10,8},{9,1... | collective-permute-start | bytes 1179656 | tf_op jit(solution)/shard_map/ppermute | solution.py:473
  74.7 34.4 %collective-permute-start.16 = (bf16[256,768]{1,0:T(8,128)(2,1)}, bf16[256,768]{1,0:T(8,128)(2,1)}, u32[]{:S(2)}, u32[]{:S(2)}) collective-permute-start(bf16[256,768]{1,0:T(8,128)(2,1)} %collective-permute-done.11), channel_id=1, source_target_pairs={{0,4},{4,8},{8,12},{12,0},{1,5},{5,9},{9,13},{13,1},{2,6},{6,10},{... | collective-permute-start | bytes 1179656 | tf_op jit(solution)/shard_map/ppermute | solution.py:473
  77.0 115.3 %collective-permute-start.20 = (bf16[192,768]{1,0:T(8,128)(2,1)}, bf16[192,768]{1,0:T(8,128)(2,1)}, u32[]{:S(2)}, u32[]{:S(2)}) collective-permute-start(bf16[192,768]{1,0:T(8,128)(2,1)} %constant_dynamic-slice_fusion.18), channel_id=1, source_target_pairs={{0,16},{16,0},{1,17},{17,1},{2,18},{18,2},{3,19},{19,3},{4,20},{20... | collective-permute-start | bytes 884744 | tf_op jit(solution)/shard_map/ppermute | solution.py:473
  77.2 23.1 %collective-permute-start.15 = (bf16[192,768]{1,0:T(8,128)(2,1)}, bf16[192,768]{1,0:T(8,128)(2,1)}, u32[]{:S(2)}, u32[]{:S(2)}) collective-permute-start(bf16[192,768]{1,0:T(8,128)(2,1)} %collective-permute-done.14.refs_1_), channel_id=1, source_target_pairs={{0,1},{1,0},{2,3},{3,2},{4,5},{5,4},{6,7},{7,6},{8,9},{9,8},{10,11... | collective-permute-start | bytes 884744 | tf_op jit(solution)/shard_map/ppermute | solution.py:473
  84.8 37.8 %collective-permute-start.19 = (bf16[192,1536]{1,0:T(8,128)(2,1)}, bf16[192,1536]{1,0:T(8,128)(2,1)S(1)}, u32[]{:S(2)}, u32[]{:S(2)}) collective-permute-start(bf16[192,1536]{1,0:T(8,128)(2,1)} %collective-permute-done.13.refs_1_), channel_id=1, source_target_pairs={{0,1},{1,0},{2,3},{3,2},{4,5},{5,4},{6,7},{7,6},{8,9},{9,8},{10,11... | collective-permute-start | bytes 1769480 | tf_op jit(solution)/shard_map/ppermute | solution.py:473
  100.3 92.0 %collective-permute-start.22 = (bf16[768,768]{1,0:T(8,128)(2,1)}, bf16[768,768]{1,0:T(8,128)(2,1)S(1)}, u32[]{:S(2)}, u32[]{:S(2)}) collective-permute-start(bf16[768,768]{1,0:T(8,128)(2,1)} %constant_dynamic-slice_fusion.16), channel_id=1, source_target_pairs={{0,16},{16,0},{1,17},{17,1},{2,18},{18,2},{3,19},{19,3},{4,20},{20... | collective-permute-start | bytes 3538952 | tf_op jit(solution)/shard_map/ppermute | solution.py:473
  108.9 83.5 %collective-permute-start.21 = (bf16[192,3072]{1,0:T(8,128)(2,1)}, bf16[192,3072]{1,0:T(8,128)(2,1)}, u32[]{:S(2)}, u32[]{:S(2)}) collective-permute-start(bf16[192,3072]{1,0:T(8,128)(2,1)} %constant_dynamic-slice_fusion.17), channel_id=1, source_target_pairs={{0,16},{16,0},{1,17},{17,1},{2,18},{18,2},{3,19},{19,3},{4,20},{20... | collective-permute-start | bytes 3538952 | tf_op jit(solution)/shard_map/ppermute | solution.py:473
  109.1 19.2 %collective-permute-start.18 = (bf16[256,768]{1,0:T(8,128)(2,1)}, bf16[256,768]{1,0:T(8,128)(2,1)S(1)}, u32[]{:S(2)}, u32[]{:S(2)}) collective-permute-start(bf16[256,768]{1,0:T(8,128)(2,1)} %collective-permute-done.16), channel_id=1, source_target_pairs={{0,2},{2,0},{1,3},{3,1},{4,6},{6,4},{5,7},{7,5},{8,10},{10,8},{9,1... | collective-permute-start | bytes 1179656 | tf_op jit(solution)/shard_map/ppermute | solution.py:473
  195.6 48.2 %collective-permute-start.34 = (bf16[256,768]{0,1:T(8,128)(2,1)}, bf16[256,768]{0,1:T(8,128)(2,1)}, u32[]{:S(2)}, u32[]{:S(2)}) collective-permute-start(bf16[256,768]{0,1:T(8,128)(2,1)} %bitcast.22), channel_id=1, source_target_pairs={{0,1},{1,0},{2,3},{3,2},{4,5},{5,4},{6,7},{7,6},{8,9},{9,8},{10,11... | collective-permute-start | bytes 1179656 | tf_op jit(solution)/shard_map/ppermute | solution.py:473
  195.7 11.4 %collective-permute-start.24 = (bf16[192,3072]{1,0:T(8,128)(2,1)}, bf16[192,3072]{1,0:T(8,128)(2,1)}, u32[]{:S(2)}, u32[]{:S(2)}) collective-permute-start(bf16[192,3072]{1,0:T(8,128)(2,1)} %collective-permute-done.21.refs_1_), channel_id=1, source_target_pairs={{0,1},{1,0},{2,3},{3,2},{4,5},{5,4},{6,7},{7,6},{8,9},{9,8},{10,11... | collective-permute-start | bytes 3538952 | tf_op jit(solution)/shard_map/ppermute | solution.py:473
  196.1 22.9 %collective-permute-start.25 = (bf16[768,768]{1,0:T(8,128)(2,1)}, bf16[768,768]{1,0:T(8,128)(2,1)}, u32[]{:S(2)}, u32[]{:S(2)}) collective-permute-start(bf16[768,768]{1,0:T(8,128)(2,1)} %copy-done.30), channel_id=1, source_target_pairs={{0,1},{1,0},{2,3},{3,2},{4,5},{5,4},{6,7},{7,6},{8,9},{9,8},{10,11... | collective-permute-start | bytes 3538952 | tf_op jit(solution)/shard_map/ppermute | solution.py:473
  197.7 47.4 %collective-permute-start.31 = (bf16[256,384]{1,0:T(8,128)(2,1)}, bf16[256,384]{1,0:T(8,128)(2,1)}, u32[]{:S(2)}, u32[]{:S(2)}) collective-permute-start(bf16[256,384]{1,0:T(8,128)(2,1)} %get-tuple-element.429), channel_id=1, source_target_pairs={{0,1},{1,0},{2,3},{3,2},{4,5},{5,4},{6,7},{7,6},{8,9},{9,8},{10,11... | collective-permute-start | bytes 589832 | tf_op jit(solution)/shard_map/ppermute | solution.py:473
  206.9 38.2 %collective-permute-start.32 = (bf16[256,768]{1,0:T(8,128)(2,1)}, bf16[256,768]{1,0:T(8,128)(2,1)}, u32[]{:S(2)}, u32[]{:S(2)}) collective-permute-start(bf16[256,768]{1,0:T(8,128)(2,1)} %add_convert_fusion.7), channel_id=1, source_target_pairs={{0,1},{1,0},{2,3},{3,2},{4,5},{5,4},{6,7},{7,6},{8,9},{9,8},{10,11... | collective-permute-start | bytes 1179656 | tf_op jit(solution)/shard_map/ppermute | solution.py:473
  241.1 4.8 collective-permute-start.33
  241.4 4.5 collective-permute-start.30
  252.0 66.9 %collective-permute-start.37 = (bf16[2,4,48,1920]{3,2,1,0:T(8,128)(2,1)}, bf16[2,4,48,1920]{3,2,1,0:T(8,128)(2,1)}, u32[]{:S(2)}, u32[]{:S(2)}) collective-permute-start(bf16[2,4,48,1920]{3,2,1,0:T(8,128)(2,1)} %get-tuple-element.413), channel_id=1, source_target_pairs={{0,2},{2,0},{1,3},{3,1},{4,6},{6,4},{5,7},{7,5},{8,10},{10,8},{9,1... | collective-permute-start | bytes 4423688 | tf_op jit(solution)/shard_map/ppermute | solution.py:473
  258.3 60.6 %collective-permute-start.36 = (bf16[2,4,192,384]{3,2,1,0:T(8,128)(2,1)}, bf16[2,4,192,384]{3,2,1,0:T(8,128)(2,1)}, u32[]{:S(2)}, u32[]{:S(2)}) collective-permute-start(bf16[2,4,192,384]{3,2,1,0:T(8,128)(2,1)} %get-tuple-element.415), channel_id=1, source_target_pairs={{0,16},{16,0},{1,17},{17,1},{2,18},{18,2},{3,19},{19,3},{4,20},{20... | collective-permute-start | bytes 3538952 | tf_op jit(solution)/shard_map/ppermute | solution.py:473
  260.2 25.6 %collective-permute-start.46 = (bf16[6,768]{1,0:T(8,128)(2,1)S(1)}, bf16[6,768]{1,0:T(8,128)(2,1)S(1)}, u32[]{:S(2)}, u32[]{:S(2)}) collective-permute-start(bf16[6,768]{1,0:T(8,128)(2,1)S(1)} %pad_maximum_fusion.11), channel_id=1, source_target_pairs={{0,16},{16,0},{1,17},{17,1},{2,18},{18,2},{3,19},{19,3},{4,20},{20... | collective-permute-start | bytes 27656 | tf_op jit(solution)/shard_map/ppermute | solution.py:473
  321.5 20.6 %collective-permute-start.39 = (bf16[4,48,1920]{2,1,0:T(8,128)(2,1)}, bf16[4,48,1920]{2,1,0:T(8,128)(2,1)}, u32[]{:S(2)}, u32[]{:S(2)}) collective-permute-start(bf16[4,48,1920]{2,1,0:T(8,128)(2,1)} %fusion.25), channel_id=1, source_target_pairs={{0,16},{16,0},{1,17},{17,1},{2,18},{18,2},{3,19},{19,3},{4,20},{20... | collective-permute-start | bytes 2211848 | tf_op jit(solution)/shard_map/ppermute | solution.py:473
  325.2 16.9 %collective-permute-start.38 = (bf16[4,192,384]{2,1,0:T(8,128)(2,1)}, bf16[4,192,384]{2,1,0:T(8,128)(2,1)}, u32[]{:S(2)}, u32[]{:S(2)}) collective-permute-start(bf16[4,192,384]{2,1,0:T(8,128)(2,1)} %fusion.28), channel_id=1, source_target_pairs={{0,2},{2,0},{1,3},{3,1},{4,6},{6,4},{5,7},{7,5},{8,10},{10,8},{9,1... | collective-permute-start | bytes 1769480 | tf_op jit(solution)/shard_map/ppermute | solution.py:473
  344.1 22.7 %all-to-all-start = ((bf16[4,192,384]{2,1,0:T(8,128)(2,1)}), bf16[4,192,384]{2,1,0:T(8,128)(2,1)S(1)}, u32[]{:S(2)}, u32[]{:S(2)}) async-start(bf16[4,192,384]{2,1,0:T(8,128)(2,1)} %add_convert_fusion.5), calls=%async_computation | async-start | bytes 1179648 | tf_op jit(solution)/shard_map/all_to_all | solution.py:540
  367.6 37.0 %all-to-all-start.1 = ((bf16[4,48,1920]{2,1,0:T(8,128)(2,1)}), bf16[4,48,1920]{2,1,0:T(8,128)(2,1)S(1)}, u32[]{:S(2)}, u32[]{:S(2)}) async-start(bf16[4,48,1920]{2,1,0:T(8,128)(2,1)} %add_convert_fusion.4), calls=%async_computation.1 | async-start | bytes 1474560 | tf_op jit(solution)/shard_map/all_to_all | solution.py:540
  391.3 27.8 %collective-permute-start.40 = (bf16[768,1152]{1,0:T(8,128)(2,1)}, bf16[768,1152]{1,0:T(8,128)(2,1)}, u32[]{:S(2)}, u32[]{:S(2)}) collective-permute-start(bf16[768,1152]{1,0:T(8,128)(2,1)} %get-tuple-element.409), channel_id=1, source_target_pairs={{0,1},{1,0},{2,3},{3,2},{4,5},{5,4},{6,7},{7,6},{8,9},{9,8},{10,11... | collective-permute-start | bytes 5308424 | tf_op jit(solution)/shard_map/ppermute | solution.py:473
  402.2 30.0 %collective-permute-start.41 = (bf16[4,256,384]{2,1,0:T(8,128)(2,1)}, bf16[4,256,384]{2,1,0:T(8,128)(2,1)}, u32[]{:S(2)}, u32[]{:S(2)}) collective-permute-start(bf16[4,256,384]{2,1,0:T(8,128)(2,1)} %get-tuple-element.411), channel_id=1, source_target_pairs={{0,2},{2,0},{1,3},{3,1},{4,6},{6,4},{5,7},{7,5},{8,10},{10,8},{9,1... | collective-permute-start | bytes 2359304 | tf_op jit(solution)/shard_map/ppermute | solution.py:473
  405.7 26.5 %all-to-all-start.2 = ((bf16[4,192,384]{2,1,0:T(8,128)(2,1)}), bf16[4,192,384]{2,1,0:T(8,128)(2,1)}, u32[]{:S(2)}, u32[]{:S(2)}) async-start(bf16[4,192,384]{2,1,0:T(8,128)(2,1)} %broadcast_in_dim.162), calls=%async_computation.2 | async-start | bytes 1179648 | tf_op jit(solution)/shard_map/all_to_all | solution.py:557
  417.2 52.0 %collective-permute-start.27 = (f32[3,128]{1,0:T(4,128)S(1)}, f32[3,128]{1,0:T(4,128)S(1)}, u32[]{:S(2)}, u32[]{:S(2)}) collective-permute-start(f32[3,128]{1,0:T(4,128)S(1)} %slice.180), channel_id=1, source_target_pairs={{0,1},{1,0},{2,3},{3,2},{4,5},{5,4},{6,7},{7,6},{8,9},{9,8},{10,11... | collective-permute-start | bytes 4616 | tf_op jit(solution)/shard_map/ppermute | solution.py:473
  417.8 138.1 %collective-permute-start.26 = (bf16[128,768]{1,0:T(8,128)(2,1)}, bf16[128,768]{1,0:T(8,128)(2,1)}, u32[]{:S(2)}, u32[]{:S(2)}) collective-permute-start(bf16[128,768]{1,0:T(8,128)(2,1)} %slice.177), channel_id=1, source_target_pairs={{0,1},{1,0},{2,3},{3,2},{4,5},{5,4},{6,7},{7,6},{8,9},{9,8},{10,11... | collective-permute-start | bytes 589832 | tf_op jit(solution)/shard_map/ppermute | solution.py:473
  439.6 24.4 %all-to-all-start.3 = ((bf16[4,256,384]{2,1,0:T(8,128)(2,1)}), bf16[4,256,384]{2,1,0:T(8,128)(2,1)S(1)}, u32[]{:S(2)}, u32[]{:S(2)}) async-start(bf16[4,256,384]{2,1,0:T(8,128)(2,1)} %constant_dynamic-slice_fusion.7), calls=%async_computation.3 | async-start | bytes 1572864 | tf_op jit(solution)/shard_map/all_to_all | solution.py:603
  447.5 35.5 %collective-permute-start.43 = (bf16[2,4,48,1152]{3,2,1,0:T(8,128)(2,1)}, bf16[2,4,48,1152]{3,2,1,0:T(8,128)(2,1)}, u32[]{:S(2)}, u32[]{:S(2)}) collective-permute-start(bf16[2,4,48,1152]{3,2,1,0:T(8,128)(2,1)} %get-tuple-element.417), channel_id=1, source_target_pairs={{0,16},{16,0},{1,17},{17,1},{2,18},{18,2},{3,19},{19,3},{4,20},{20... | collective-permute-start | bytes 2654216 | tf_op jit(solution)/shard_map/ppermute | solution.py:473
  448.8 34.3 %collective-permute-start.42 = (bf16[4,256,384]{2,1,0:T(8,128)(2,1)}, bf16[4,256,384]{2,1,0:T(8,128)(2,1)}, u32[]{:S(2)}, u32[]{:S(2)}) collective-permute-start(bf16[4,256,384]{2,1,0:T(8,128)(2,1)} %get-tuple-element.419), channel_id=1, source_target_pairs={{0,2},{2,0},{1,3},{3,1},{4,6},{6,4},{5,7},{7,5},{8,10},{10,8},{9,1... | collective-permute-start | bytes 2359304 | tf_op jit(solution)/shard_map/ppermute | solution.py:473
  465.1 23.0 %all-to-all-start.5 = ((bf16[4,48,1920]{2,1,0:T(8,128)(2,1)}), bf16[4,48,1920]{2,1,0:T(8,128)(2,1)}, u32[]{:S(2)}, u32[]{:S(2)}) async-start(bf16[4,48,1920]{2,1,0:T(8,128)(2,1)} %broadcast_in_dim.163), calls=%async_computation.5 | async-start | bytes 1474560 | tf_op jit(solution)/shard_map/all_to_all | solution.py:557
  469.9 76.4 %collective-permute-start.47 = (bf16[4,192,384]{2,1,0:T(8,128)(2,1)}, bf16[4,192,384]{2,1,0:T(8,128)(2,1)}, u32[]{:S(2)}, u32[]{:S(2)}) collective-permute-start(bf16[4,192,384]{2,1,0:T(8,128)(2,1)} %all-to-all-done.2.refs_0_), channel_id=1, source_target_pairs={{0,2},{2,0},{1,3},{3,1},{4,6},{6,4},{5,7},{7,5},{8,10},{10,8},{9,1... | collective-permute-start | bytes 1769480 | tf_op jit(solution)/shard_map/ppermute | solution.py:473
  488.0 24.2 %all-to-all-start.4 = ((bf16[4,256,384]{2,1,0:T(8,128)(2,1)}), bf16[4,256,384]{2,1,0:T(8,128)(2,1)S(1)}, u32[]{:S(2)}, u32[]{:S(2)}) async-start(bf16[4,256,384]{2,1,0:T(8,128)(2,1)} %constant_dynamic-slice_fusion.6), calls=%async_computation.4 | async-start | bytes 1572864 | tf_op jit(solution)/shard_map/all_to_all | solution.py:603
  494.1 16.9 %collective-permute-start.44 = (bf16[4,48,1152]{2,1,0:T(8,128)(2,1)S(1)}, bf16[4,48,1152]{2,1,0:T(8,128)(2,1)}, u32[]{:S(2)}, u32[]{:S(2)}) collective-permute-start(bf16[4,48,1152]{2,1,0:T(8,128)(2,1)S(1)} %fusion.32), channel_id=1, source_target_pairs={{0,2},{2,0},{1,3},{3,1},{4,6},{6,4},{5,7},{7,5},{8,10},{10,8},{9,1... | collective-permute-start | bytes 1327112 | tf_op jit(solution)/shard_map/ppermute | solution.py:473
  520.7 25.5 %all-to-all-start.6 = ((bf16[4,48,1152]{2,1,0:T(8,128)(2,1)}), bf16[4,48,1152]{2,1,0:T(8,128)(2,1)}, u32[]{:S(2)}, u32[]{:S(2)}) async-start(bf16[4,48,1152]{2,1,0:T(8,128)(2,1)} %add_convert_fusion.6), calls=%async_computation.6 | async-start | bytes 884736 | tf_op jit(solution)/shard_map/all_to_all | solution.py:540
  528.8 33.2 %collective-permute-start.45 = (f32[128,768]{1,0:T(8,128)S(1)}, f32[128,768]{1,0:T(8,128)S(1)}, u32[]{:S(2)}, u32[]{:S(2)}) collective-permute-start(f32[128,768]{1,0:T(8,128)S(1)} %slice.185), channel_id=1, source_target_pairs={{0,1},{1,0},{2,3},{3,2},{4,5},{5,4},{6,7},{7,6},{8,9},{9,8},{10,11... | collective-permute-start | bytes 1179656 | tf_op jit(solution)/shard_map/ppermute | solution.py:473
  531.1 38.2 %collective-permute-start.57 = (bf16[4,48,1920]{2,1,0:T(8,128)(2,1)}, bf16[4,48,1920]{2,1,0:T(8,128)(2,1)}, u32[]{:S(2)}, u32[]{:S(2)}) collective-permute-start(bf16[4,48,1920]{2,1,0:T(8,128)(2,1)} %all-to-all-done.5.refs_0_), channel_id=1, source_target_pairs={{0,2},{2,0},{1,3},{3,1},{4,6},{6,4},{5,7},{7,5},{8,10},{10,8},{9,1... | collective-permute-start | bytes 2211848 | tf_op jit(solution)/shard_map/ppermute | solution.py:473
  548.8 8.1 %collective-permute-start.48 = (f32[25,768]{1,0:T(8,128)S(1)}, f32[25,768]{1,0:T(8,128)S(1)}, u32[]{:S(2)}, u32[]{:S(2)}) collective-permute-start(f32[25,768]{1,0:T(8,128)S(1)} %concatenate.119), channel_id=1, source_target_pairs={{0,1},{1,0},{2,3},{3,2},{4,5},{5,4},{6,7},{7,6},{8,9},{9,8},{10,11... | collective-permute-start | bytes 230408 | tf_op jit(solution)/shard_map/ppermute | solution.py:473
  551.1 27.1 %all-to-all-start.7 = ((bf16[4,48,1152]{2,1,0:T(8,128)(2,1)}), bf16[4,48,1152]{2,1,0:T(8,128)(2,1)S(1)}, u32[]{:S(2)}, u32[]{:S(2)}) async-start(bf16[4,48,1152]{2,1,0:T(8,128)(2,1)} %broadcast_in_dim.173), calls=%async_computation.7 | async-start | bytes 884736 | tf_op jit(solution)/shard_map/all_to_all | solution.py:557
  556.8 4.0 collective-permute-start.49
  560.8 3.5 collective-permute-start.50
  562.1 19.4 %collective-permute-start.60 = (bf16[4,192,384]{2,1,0:T(8,128)(2,1)}, bf16[4,192,384]{2,1,0:T(8,128)(2,1)S(1)}, u32[]{:S(2)}, u32[]{:S(2)}) collective-permute-start(bf16[4,192,384]{2,1,0:T(8,128)(2,1)} %all-to-all-done.2.refs_0_), channel_id=1, source_target_pairs={{0,1},{1,0},{2,3},{3,2},{4,5},{5,4},{6,7},{7,6},{8,9},{9,8},{10,11... | collective-permute-start | bytes 1769480 | tf_op jit(solution)/shard_map/ppermute | solution.py:473
  564.4 8.2 %collective-permute-start.53 = (f32[25,768]{1,0:T(8,128)S(1)}, f32[25,768]{1,0:T(8,128)S(1)}, u32[]{:S(2)}, u32[]{:S(2)}) collective-permute-start(f32[25,768]{1,0:T(8,128)S(1)} %add.309), channel_id=1, source_target_pairs={{0,12},{4,0},{8,4},{12,8},{1,13},{5,1},{9,5},{13,9},{2,14},{6,2},{... | collective-permute-start | bytes 230408 | tf_op jit(solution)/shard_map/ppermute | solution.py:473
  567.6 9.0 %collective-permute-start.52 = (f32[25,768]{1,0:T(8,128)S(1)}, f32[25,768]{1,0:T(8,128)S(1)}, u32[]{:S(2)}, u32[]{:S(2)}) collective-permute-start(f32[25,768]{1,0:T(8,128)S(1)} %add.309), channel_id=1, source_target_pairs={{0,8},{4,12},{8,0},{12,4},{1,9},{5,13},{9,1},{13,5},{2,10},{6,14},... | collective-permute-start | bytes 230408 | tf_op jit(solution)/shard_map/ppermute | solution.py:473
  567.6 10.6 %collective-permute-start.51 = (f32[25,768]{1,0:T(8,128)S(1)}, f32[25,768]{1,0:T(8,128)S(1)}, u32[]{:S(2)}, u32[]{:S(2)}) collective-permute-start(f32[25,768]{1,0:T(8,128)S(1)} %add.309), channel_id=1, source_target_pairs={{0,4},{4,8},{8,12},{12,0},{1,5},{5,9},{9,13},{13,1},{2,6},{6,10},{... | collective-permute-start | bytes 230408 | tf_op jit(solution)/shard_map/ppermute | solution.py:473
  569.4 28.8 %collective-permute-start.58 = (bf16[4,48,1920]{2,1,0:T(8,128)(2,1)}, bf16[4,48,1920]{2,1,0:T(8,128)(2,1)S(1)}, u32[]{:S(2)}, u32[]{:S(2)}) collective-permute-start(bf16[4,48,1920]{2,1,0:T(8,128)(2,1)} %all-to-all-done.5.refs_0_), channel_id=1, source_target_pairs={{0,1},{1,0},{2,3},{3,2},{4,5},{5,4},{6,7},{7,6},{8,9},{9,8},{10,11... | collective-permute-start | bytes 2211848 | tf_op jit(solution)/shard_map/ppermute | solution.py:473
  572.6 19.9 %collective-permute-start.61 = (bf16[4,192,384]{2,1,0:T(8,128)(2,1)}, bf16[4,192,384]{2,1,0:T(8,128)(2,1)S(1)}, u32[]{:S(2)}, u32[]{:S(2)}) collective-permute-start(bf16[4,192,384]{2,1,0:T(8,128)(2,1)} %collective-permute-done.47.refs_1_), channel_id=1, source_target_pairs={{0,1},{1,0},{2,3},{3,2},{4,5},{5,4},{6,7},{7,6},{8,9},{9,8},{10,11... | collective-permute-start | bytes 1769480 | tf_op jit(solution)/shard_map/ppermute | solution.py:473
  576.6 21.5 %collective-permute-start.59 = (bf16[4,48,1920]{2,1,0:T(8,128)(2,1)}, bf16[4,48,1920]{2,1,0:T(8,128)(2,1)}, u32[]{:S(2)}, u32[]{:S(2)}) collective-permute-start(bf16[4,48,1920]{2,1,0:T(8,128)(2,1)} %collective-permute-done.57.refs_1_), channel_id=1, source_target_pairs={{0,1},{1,0},{2,3},{3,2},{4,5},{5,4},{6,7},{7,6},{8,9},{9,8},{10,11... | collective-permute-start | bytes 2211848 | tf_op jit(solution)/shard_map/ppermute | solution.py:473
  578.2 11.9 %collective-permute-start.54 = (bf16[4,48,1152]{2,1,0:T(8,128)(2,1)S(1)}, bf16[4,48,1152]{2,1,0:T(8,128)(2,1)S(1)}, u32[]{:S(2)}, u32[]{:S(2)}) collective-permute-start(bf16[4,48,1152]{2,1,0:T(8,128)(2,1)S(1)} %all-to-all-done.7.refs_0_), channel_id=1, source_target_pairs={{0,2},{2,0},{1,3},{3,1},{4,6},{6,4},{5,7},{7,5},{8,10},{10,8},{9,1... | collective-permute-start | bytes 1327112 | tf_op jit(solution)/shard_map/ppermute | solution.py:473
  581.5 22.9 %collective-permute-start.55 = (bf16[4,48,1152]{2,1,0:T(8,128)(2,1)S(1)}, bf16[4,48,1152]{2,1,0:T(8,128)(2,1)S(1)}, u32[]{:S(2)}, u32[]{:S(2)}) collective-permute-start(bf16[4,48,1152]{2,1,0:T(8,128)(2,1)S(1)} %all-to-all-done.7.refs_0_), channel_id=1, source_target_pairs={{0,1},{1,0},{2,3},{3,2},{4,5},{5,4},{6,7},{7,6},{8,9},{9,8},{10,11... | collective-permute-start | bytes 1327112 | tf_op jit(solution)/shard_map/ppermute | solution.py:473
  590.1 14.4 %collective-permute-start.56 = (bf16[4,48,1152]{2,1,0:T(8,128)(2,1)S(1)}, bf16[4,48,1152]{2,1,0:T(8,128)(2,1)S(1)}, u32[]{:S(2)}, u32[]{:S(2)}) collective-permute-start(bf16[4,48,1152]{2,1,0:T(8,128)(2,1)S(1)} %collective-permute-done.54.refs_1_), channel_id=1, source_target_pairs={{0,1},{1,0},{2,3},{3,2},{4,5},{5,4},{6,7},{7,6},{8,9},{9,8},{10,11... | collective-permute-start | bytes 1327112 | tf_op jit(solution)/shard_map/ppermute | solution.py:473
  (88 other events, 1368.7 us)

commit v3 on v2

--- a/solution.py
+++ b/solution.py
@@ -598,9 +598,6 @@
     x_count, z_count = shares.shape[:2]
     own, incoming = yield shares[0], [shifted(shares[step], "x", -step) for step in range(1, x_count)]
     total = add_parts(own, incoming)
-    if Z_EXCHANGE:
-        low = turn_back(total.astype(jnp.bfloat16), "z")
-        return jnp.sum((yield lax.all_to_all(low, "z", 0, 0)).astype(jnp.float32), axis=0)
     low = total.astype(jnp.bfloat16)
     own, incoming = yield total[0], [shifted(low[step], "z", -step) for step in range(1, z_count)]
     return add_parts(own, incoming)
@@ -694,8 +691,7 @@
     where_rows = jnp.concatenate(take_row(where_own), axis=1)
     bias_parts = [bias_weight] + [shifted(bias_weight, "dp", step) for step in range(1, dp_count)]
     residue_parts = take_row(residues)
-    my_steps = lax.dynamic_index_in_dim(time_steps, core, 0, keepdims=False)
-    step_list = [my_steps] + [shifted(my_steps, "dp", step) for step in range(1, dp_count)]
+    step_list = spread_dp(time_steps)
 
     where_keys = where_rows[None]
     reach = 1
@@ -745,8 +741,9 @@
     vectors = jnp.transpose(vectors, (1, 0, 2)).reshape(7, D)
     gain_one, shift_one, gain_two, shift_two = [vectors[i:i + 1].astype(jnp.float32) for i in range(4)]
     force_full = vectors[4:]
-    proteins = my_steps.shape[0]
-    features = time_features(jnp.concatenate(step_list).astype(jnp.float32), D).astype(jnp.bfloat16)
+    proteins = time_steps.shape[1]
+    row_steps = [lax.dynamic_index_in_dim(steps, core, 0, keepdims=False) for steps in step_list]
+    features = time_features(jnp.concatenate(row_steps).astype(jnp.float32), D).astype(jnp.bfloat16)
     features = part_of(features, place, dp_count, 1)
     stamp_part = jnp.dot(features, time_weight, preferred_element_type=jnp.float32)
     stamp_rows = stamp_part[:proteins]
@@ -907,10 +904,8 @@
     force_sum = part_of(last[4:7], place, dp_count, 1)
     bias_sum = part_of(last[7:13].reshape(-1)[:KERNELS * HEADS].reshape(KERNELS, HEADS), place, dp_count, 0)
     protein_all = last[13:]
-    other_steps = lax.dynamic_index_in_dim(time_steps, 1 - core, 0, keepdims=False)
-    both_steps = jnp.where(core == 0, jnp.stack([my_steps, other_steps]), jnp.stack([other_steps, my_steps]))
-    all_features = time_features(both_steps.reshape(-1).astype(jnp.float32), D).astype(jnp.bfloat16)
-    all_features = in_order(spread_dp(all_features)).reshape(slots * proteins, D)
+    all_steps = in_order(step_list).reshape(slots * proteins).astype(jnp.float32)
+    all_features = time_features(all_steps, D).astype(jnp.bfloat16)
     time_grad = jnp.einsum(
         "sd,se->de",
         part_of(all_features, place, dp_count, 1).astype(jnp.float32),

time: 618 us -> 578 us (0.935)
  waiting for transfers between devices: 64.7 us -> 28 us
  local copies, waits for them, and re-layouts: 78.1 us -> 68.5 us
    ppermute x62 -> x67, waiting for transfers between devices: 50 us -> 28 us  [shifted(): lax.ppermute(values, axis, [(i, (i + step) % size) for i in range(size)])]
    all_to_all x2 -> x0, waiting for transfers between devices: 14.8 us -> none  [share_chain(): lax.all_to_all(low, 'z', 0, 0)]
    ppermute x62 -> x67, starting transfers between devices: 56.9 us -> 71.6 us  [shifted(): lax.ppermute(values, axis, [(i, (i + step) % size) for i in range(size)])]
    all_to_all x2 -> x0, starting transfers between devices: 9.42 us -> none  [share_chain(): lax.all_to_all(low, 'z', 0, 0)]
    unnamed x185 -> x221, local copies, waits for them, and re-layouts: 27.4 us -> 24.8 us
  transfers between devices with their start and end apart: 70 -> 73, of which waited for: 13 -> 12; matrix products, arithmetic and copies ran while one was open for 25% -> 25% of each run, Pallas kernels for 43% -> 46%
where the time goes in v3:
time: 578 us; the launch traced here: 570 us
  Pallas kernels  268 us (46%)
  starting transfers between devices  98.6 us (17%)
  local copies, waits for them, and re-layouts  68.5 us (12%)
  matrix products  54.2 us (9%)
  other arithmetic  50 us (9%)
  waiting for transfers between devices  28 us (5%)
    ppermute x67, starting transfers between devices, shifted(): lax.ppermute(values, axis, [(i, (i + step) % size) for i in range(size)])  71.6 us
    pallas_call x4, Pallas kernels, attend_back(): pl.pallas_call(functools.partial(backward_kernel, 512), grid=(rows // til...  66.3 us
    pallas_call x5, Pallas kernels, pair_bias(): pl.pallas_call(functools.partial(bias_kernel, 256), grid=(steps,), in_spe...  53.6 us
    pallas_call x4, Pallas kernels, table_grad(): pl.pallas_call(functools.partial(table_grad_kernel, 256), grid=(steps,),...  52 us
    pallas_call x1, Pallas kernels, attend(): pl.pallas_call(functools.partial(forward_kernel, 512), grid=(rows // tile...  39.7 us
    dot_general x10, matrix products, dot32(): lax.dot_general(left, right, ((contract[:1], contract[1:]), ((), ())), pr...  38.4 us
    ppermute x67, waiting for transfers between devices, shifted(): lax.ppermute(values, axis, [(i, (i + step) % size) for i in range(size)])  28 us
    pallas_call x5, Pallas kernels, place_shards(): pl.pallas_call(functools.partial(place_kernel, steps), grid_spec=pltpu.Pr...  26.7 us
  transfers between devices with their start and end apart: 73, of which 12 were waited for; matrix products, arithmetic and copies ran while one was open for 25% of the time, Pallas kernels for 46%

profile of v3, /device:TPU:1, one launch (start us, length us, event | category | flops | bytes accessed | tf_op | source)
XLA Modules:
  0.0 569.9 jit_solution(9559443140118328971)
XLA Ops:
  2.3 2.7 collective-permute-start.6
  10.3 2.4 collective-permute-done.1
  13.8 2.3 collective-permute-done.2
  29.7 7.4 %pair_bias.5.refs_0_ = bf16[4,2048,2048]{2,1,0:T(8,128)(2,1)} custom-call(f32[256,8]{1,0:T(8,128)} %pad_convert_fusion.q_ref, f32[8,2048]{1,0:T(8,128)} %pad_convert_fusion.1.k_ref, bf16[32,128]{1,0:T(8,128)(2,1)} %fusion.48.w_ref), custom_call_target="tpu_custom_call" | custom-call | flops 1500000000 | bytes 4194304 | tf_op jit(solution)/shard_map/pair_bias/pallas_call | solution.py:103
  37.7 2.2 collective-permute-done.7
  45.4 11.5 %pair_bias.6.refs_0_ = bf16[4,2048,2048]{2,1,0:T(8,128)(2,1)} custom-call(f32[256,8]{1,0:T(8,128)} %pad_convert_fusion.q_ref, f32[8,2048]{1,0:T(8,128)} %pad_convert_fusion.1.k_ref, bf16[32,128]{1,0:T(8,128)(2,1)} %fusion.48.w_ref, bf16[4,2048,2048]{2,1,0:T(8,128)(2,1)} %pair_bias.5.refs_0_), custom_call_target="tpu_custom_call", output_to_operand_aliasing={{}: (3, {})} | custom-call | flops 2624999936 | bytes 7340032 | tf_op jit(solution)/shard_map/pair_bias/pallas_call | solution.py:103
  61.3 11.6 %pair_bias.7.refs_0_ = bf16[4,2048,2048]{2,1,0:T(8,128)(2,1)} custom-call(f32[256,8]{1,0:T(8,128)} %pad_convert_fusion.q_ref, f32[8,2048]{1,0:T(8,128)} %pad_convert_fusion.1.k_ref, bf16[32,128]{1,0:T(8,128)(2,1)} %fusion.48.w_ref, bf16[4,2048,2048]{2,1,0:T(8,128)(2,1)} %pair_bias.6.refs_0_), custom_call_target="tpu_custom_call", output_to_operand_aliasing={{}: (3, {})} | custom-call | flops 2624999936 | bytes 7340032 | tf_op jit(solution)/shard_map/pair_bias/pallas_call | solution.py:103
  74.2 1.8 collective-permute-start.16
  76.0 1.8 constant_dynamic-slice_fusion.15
  78.0 7.5 %collective-permute-start.15 = (bf16[192,768]{1,0:T(8,128)(2,1)S(1)}, bf16[192,768]{1,0:T(8,128)(2,1)}, u32[]{:S(2)}, u32[]{:S(2)}) collective-permute-start(bf16[192,768]{1,0:T(8,128)(2,1)S(1)} %collective-permute-done.14.refs_1_), channel_id=1, source_target_pairs={{0,1},{1,0},{2,3},{3,2},{4,5},{5,4},{6,7},{7,6},{8,9},{9,8},{10,11... | collective-permute-start | bytes 884744 | tf_op jit(solution)/shard_map/ppermute | solution.py:473
  89.5 11.5 %pair_bias.8.refs_0_ = bf16[4,2048,2048]{2,1,0:T(8,128)(2,1)} custom-call(f32[256,8]{1,0:T(8,128)} %pad_convert_fusion.q_ref, f32[8,2048]{1,0:T(8,128)} %pad_convert_fusion.1.k_ref, bf16[32,128]{1,0:T(8,128)(2,1)} %fusion.48.w_ref, bf16[4,2048,2048]{2,1,0:T(8,128)(2,1)} %pair_bias.7.refs_0_), custom_call_target="tpu_custom_call", output_to_operand_aliasing={{}: (3, {})} | custom-call | flops 2624999936 | bytes 7340032 | tf_op jit(solution)/shard_map/pair_bias/pallas_call | solution.py:103
  102.2 4.3 place_shards.5
  111.8 11.6 %pair_bias.9.bias_ref = bf16[4,2048,2048]{2,1,0:T(8,128)(2,1)} custom-call(f32[256,8]{1,0:T(8,128)} %pad_convert_fusion.q_ref, f32[8,2048]{1,0:T(8,128)} %pad_convert_fusion.1.k_ref, bf16[32,128]{1,0:T(8,128)(2,1)} %fusion.48.w_ref, bf16[4,2048,2048]{2,1,0:T(8,128)(2,1)} %pair_bias.8.refs_0_), custom_call_target="tpu_custom_call", output_to_operand_aliasing={{}: (3, {})} | custom-call | flops 2624999936 | bytes 7340032 | tf_op jit(solution)/shard_map/pair_bias/pallas_call | solution.py:103
  124.2 5.0 place_shards.6.w_ref
  135.1 15.3 %project.1 = (bf16[1536,2048]{1,0:T(8,128)(2,1)}, bf16[2048,1024]{1,0:T(8,128)(2,1)}, bf16[2048,1024]{1,0:T(8,128)(2,1)}) custom-call(bf16[2048,768]{1,0:T(8,128)(2,1)} %constant_dynamic-update-slice_fusion.x_ref, bf16[768,1536]{1,0:T(8,128)(2,1)} %place_shards.6.w_ref), custom_call_target="tpu_custom_call" | custom-call | flops 3000000000 | bytes 22020096 | tf_op jit(solution)/shard_map/project/pallas_call | solution.py:140
  150.4 39.7 %attend.1 = (bf16[4,2048,2048]{2,1,0:T(8,128)(2,1)}, f32[4,256,256]{2,1,0:T(8,128)}, f32[4,256,256]{2,1,0:T(8,128)}) custom-call(bf16[4,256,256]{2,1,0:T(8,128)(2,1)} %pad_bitcast_fusion.q_ref, bf16[1536,2048]{1,0:T(8,128)(2,1)} %get-tuple-element.208.kt_ref.vt_ref, bf16[2048,1024]{1,0:T(8,128)(2,1)} %get-tuple-element.209.v_ref, ...), custom_call_target="tpu_custom_call", output_to_operand_aliasing={{0}: (3, {})} | custom-call | flops 11249999872 | bytes 67108864 | tf_op jit(solution)/shard_map/attend/pallas_call | solution.py:208
  198.9 4.4 place_shards.7
  203.4 2.1 fusion.80
  206.8 6.4 %place_shards.8 = bf16[768,3072]{1,0:T(8,128)(2,1)} custom-call(s32[2]{0:T(128)} %pad_add_fusion.s_ref, bf16[384,3072]{1,0:T(8,128)(2,1)} %refs_0_.1, bf16[192,3072]{1,0:T(8,128)(2,1)} %collective-permute-done.21.refs_1_, bf16[192,3072]{1,0:T(8,128)(2,1)} %collective-permute-done.24.refs_2_), custom_call_target="tpu_custom_call" | custom-call | flops 750000000 | bytes 9437184 | tf_op jit(solution)/shard_map/place_shards/pallas_call | solution.py:393
  213.2 5.5 fusion.81
  218.7 6.6 %place_shards.9 = bf16[3072,768]{1,0:T(8,128)(2,1)} custom-call(s32[2]{0:T(128)} %pad_add_fusion.s_ref, bf16[1536,768]{1,0:T(8,128)(2,1)} %refs_0_.2, bf16[768,768]{1,0:T(8,128)(2,1)} %copy-done.29, bf16[768,768]{1,0:T(8,128)(2,1)} %collective-permute-done.25.refs_2_), custom_call_target="tpu_custom_call" | custom-call | flops 750000000 | bytes 9437184 | tf_op jit(solution)/shard_map/place_shards/pallas_call | solution.py:393
  225.3 10.6 %add_convert_fusion.1 = (bf16[256,3072]{1,0:T(8,128)(2,1)S(1)}, f32[256,3072]{1,0:T(8,128)S(1)}) fusion(f32[256,3072]{1,0:T(8,128)} %fusion.81, bf16[256,768]{1,0:T(8,128)(2,1)S(1)} %get-tuple-element.477, bf16[3072,768]{1,0:T(8,128)(2,1)} %place_shards.9), kind=kOutput, calls=%fused_computation.16 | convolution fusion | flops 1264582656 | bytes 12976128 | tf_op jit(solution)/shard_map/dot_general | solution.py:482
  247.3 2.8 convolution_convert_fusion.2
  252.9 3.7 convolution_convert_fusion
  259.9 3.5 fusion.14
  263.5 16.8 %attend_back.4 = (bf16[4,2048,2048]{2,1,0:T(8,128)(2,1)}, f32[1,256,256]{2,1,0:T(8,128)}, bf16[192,2048]{1,0:T(8,128)(2,1)}, bf16[192,2048]{1,0:T(8,128)(2,1)}) custom-call(bf16[4,256,256]{2,1,0:T(8,128)(2,1)} %pad_bitcast_fusion.q_ref, bf16[4,256,256]{2,1,0:T(8,128)(2,1)} %fusion.15.do_ref, ...), custom_call_target="tpu_custom_call", output_to_operand_aliasing={{0}: (5, {})} | custom-call | flops 3500000000 | bytes 16777216 | tf_op jit(solution)/shard_map/attend_back/pallas_call | solution.py:281
  280.3 16.5 %attend_back.5 = (bf16[4,2048,2048]{2,1,0:T(8,128)(2,1)}, f32[1,256,256]{2,1,0:T(8,128)}, bf16[192,2048]{1,0:T(8,128)(2,1)}, bf16[192,2048]{1,0:T(8,128)(2,1)}) custom-call(bf16[4,256,256]{2,1,0:T(8,128)(2,1)} %pad_bitcast_fusion.q_ref, bf16[4,256,256]{2,1,0:T(8,128)(2,1)} %fusion.15.do_ref, ...), custom_call_target="tpu_custom_call", output_to_operand_aliasing={{0}: (5, {})} | custom-call | flops 3500000000 | bytes 16777216 | tf_op jit(solution)/shard_map/attend_back/pallas_call | solution.py:281
  303.1 16.5 %attend_back.6 = (bf16[4,2048,2048]{2,1,0:T(8,128)(2,1)}, f32[1,256,256]{2,1,0:T(8,128)}, bf16[192,2048]{1,0:T(8,128)(2,1)}, bf16[192,2048]{1,0:T(8,128)(2,1)}) custom-call(bf16[4,256,256]{2,1,0:T(8,128)(2,1)} %pad_bitcast_fusion.q_ref, bf16[4,256,256]{2,1,0:T(8,128)(2,1)} %fusion.15.do_ref, ...), custom_call_target="tpu_custom_call", output_to_operand_aliasing={{0}: (5, {})} | custom-call | flops 3500000000 | bytes 16777216 | tf_op jit(solution)/shard_map/attend_back/pallas_call | solution.py:281
  319.6 2.1 add_convert_fusion.3
  321.7 3.6 all-to-all-start
  326.8 16.5 %attend_back.7 = (bf16[4,2048,2048]{2,1,0:T(8,128)(2,1)}, f32[1,256,256]{2,1,0:T(8,128)}, bf16[192,2048]{1,0:T(8,128)(2,1)}, bf16[192,2048]{1,0:T(8,128)(2,1)}) custom-call(bf16[4,256,256]{2,1,0:T(8,128)(2,1)} %pad_bitcast_fusion.q_ref, bf16[4,256,256]{2,1,0:T(8,128)(2,1)} %fusion.15.do_ref, ...), custom_call_target="tpu_custom_call", output_to_operand_aliasing={{0}: (5, {})} | custom-call | flops 3500000000 | bytes 16777216 | tf_op jit(solution)/shard_map/attend_back/pallas_call | solution.py:281
  343.3 2.2 add_convert_fusion.2
  345.5 5.0 all-to-all-start.1
  359.7 5.3 convolution_convert_fusion.1
  365.0 2.2 fusion.9
  368.7 9.1 %convolution_convert_fusion.3 = bf16[2048,768]{1,0:T(8,128)(2,1)} fusion(bf16[1536,2048]{1,0:T(8,128)(2,1)} %copy-done.60, bf16[768,1536]{1,0:T(8,128)(2,1)} %place_shards.6.w_ref), kind=kOutput, calls=%fused_computation.11 | convolution fusion | flops 4833411072 | bytes 11796480 | tf_op jit(solution)/shard_map/dot_general | solution.py:482
  378.7 5.0 all-to-all-start.2
  383.7 2.8 slice_bitcast_fusion
  390.6 13.0 %table_grad.4 = f32[256,64]{1,0:T(8,128)} custom-call(f32[256,8]{1,0:T(8,128)} %pad_convert_fusion.q_ref, f32[8,2048]{1,0:T(8,128)} %pad_convert_fusion.1.k_ref, bf16[4,2048,2048]{2,1,0:T(8,128)(2,1)} %get-tuple-element.310.ds_ref), custom_call_target="tpu_custom_call" | custom-call | flops 3200000000 | bytes 8388608 | tf_op jit(solution)/shard_map/table_grad/pallas_call | solution.py:342
  403.6 2.1 collective-permute-done.41
  407.9 4.2 all-to-all-start.3
  414.5 1.9 add_convert_fusion
  422.3 2.1 collective-permute-start.43
  425.6 13.0 %table_grad.5 = f32[256,64]{1,0:T(8,128)} custom-call(f32[256,8]{1,0:T(8,128)} %pad_convert_fusion.q_ref, f32[8,2048]{1,0:T(8,128)} %pad_convert_fusion.1.k_ref, bf16[4,2048,2048]{2,1,0:T(8,128)(2,1)} %get-tuple-element.310.ds_ref), custom_call_target="tpu_custom_call" | custom-call | flops 3200000000 | bytes 8388608 | tf_op jit(solution)/shard_map/table_grad/pallas_call | solution.py:342
  438.6 3.4 collective-permute-start.26
  447.0 4.5 collective-permute-start.49
  451.8 1.9 collective-permute-start.47
  455.3 13.0 %table_grad.6 = f32[256,64]{1,0:T(8,128)} custom-call(f32[256,8]{1,0:T(8,128)} %pad_convert_fusion.q_ref, f32[8,2048]{1,0:T(8,128)} %pad_convert_fusion.1.k_ref, bf16[4,2048,2048]{2,1,0:T(8,128)(2,1)} %get-tuple-element.310.ds_ref), custom_call_target="tpu_custom_call" | custom-call | flops 3200000000 | bytes 8388608 | tf_op jit(solution)/shard_map/table_grad/pallas_call | solution.py:342
  468.3 2.0 convert_add_fusion.7
  472.3 2.7 fusion.75
  478.5 2.1 add_convert_fusion.4
  480.7 4.4 all-to-all-start.4
  485.1 2.1 fusion.16
  488.4 2.4 collective-permute-start.51
  493.6 13.0 %table_grad.7 = f32[256,64]{1,0:T(8,128)} custom-call(f32[256,8]{1,0:T(8,128)} %pad_convert_fusion.q_ref, f32[8,2048]{1,0:T(8,128)} %pad_convert_fusion.1.k_ref, bf16[4,2048,2048]{2,1,0:T(8,128)(2,1)} %get-tuple-element.310.ds_ref), custom_call_target="tpu_custom_call" | custom-call | flops 3200000000 | bytes 8388608 | tf_op jit(solution)/shard_map/table_grad/pallas_call | solution.py:342
  511.4 4.8 all-to-all-start.5
  519.3 1.9 collective-permute-done.54
  524.8 3.1 collective-permute-start.58
  529.7 3.3 collective-permute-start.63
  533.1 3.8 collective-permute-done.57
  541.5 9.0 %collective-permute-done.59.refs_1_ = bf16[4,48,1152]{2,1,0:T(8,128)(2,1)S(1)} collective-permute-done((bf16[4,48,1152]{2,1,0:T(8,128)(2,1)S(1)}, bf16[4,48,1152]{2,1,0:T(8,128)(2,1)S(1)}, u32[]{:S(2)}, u32[]{:S(2)}) %collective-permute-start.59) | collective-permute-done | bytes 442400 | tf_op jit(solution)/shard_map/ppermute | solution.py:473
  553.8 4.7 assemble.5
  558.5 5.5 assemble.4
  565.5 4.1 assemble.3
  (526 shorter events, 151.2 us)
Async XLA Ops:
  2.2 5.7 collective-permute-start
  2.3 15.8 %collective-permute-start.6 = (s32[2,3]{1,0:T(2,128)}, s32[2,3]{1,0:T(2,128)S(1)}, u32[]{:S(2)}, u32[]{:S(2)}) collective-permute-start(s32[2,3]{1,0:T(2,128)} %param.26), channel_id=1, source_target_pairs={{0,16},{16,0},{1,17},{17,1},{2,18},{18,2},{3,19},{19,3},{4,20},{20... | collective-permute-start | bytes 80 | tf_op jit(solution)/shard_map/ppermute | solution.py:473
  5.0 13.1 %collective-permute-start.4 = (bf16[64,32]{0,1:T(8,128)(2,1)}, bf16[64,32]{0,1:T(8,128)(2,1)S(1)}, u32[]{:S(2)}, u32[]{:S(2)}) collective-permute-start(bf16[64,32]{0,1:T(8,128)(2,1)} %param.31), channel_id=1, source_target_pairs={{0,16},{16,0},{1,17},{17,1},{2,18},{18,2},{3,19},{19,3},{4,20},{20... | collective-permute-start | bytes 12296 | tf_op jit(solution)/shard_map/ppermute | solution.py:473
  6.1 12.6 %collective-permute-start.5 = (bf16[128,768]{1,0:T(8,128)(2,1)S(1)}, bf16[128,768]{1,0:T(8,128)(2,1)S(1)}, u32[]{:S(2)}, u32[]{:S(2)}) collective-permute-start(bf16[128,768]{1,0:T(8,128)(2,1)S(1)} %get-tuple-element.455), channel_id=1, source_target_pairs={{0,1},{1,0},{2,3},{3,2},{4,5},{5,4},{6,7},{7,6},{8,9},{9,8},{10,11... | collective-permute-start | bytes 589832 | tf_op jit(solution)/shard_map/ppermute | solution.py:473
  7.9 4.8 collective-permute-start.1
  22.2 15.4 %collective-permute-start.8 = (bf16[7,384]{1,0:T(8,128)(2,1)S(1)}, bf16[7,384]{1,0:T(8,128)(2,1)S(1)}, u32[]{:S(2)}, u32[]{:S(2)}) collective-permute-start(bf16[7,384]{1,0:T(8,128)(2,1)S(1)} %concatenate.100), channel_id=1, source_target_pairs={{0,16},{16,0},{1,17},{17,1},{2,18},{18,2},{3,19},{19,3},{4,20},{20... | collective-permute-start | bytes 16136 | tf_op jit(solution)/shard_map/ppermute | solution.py:473
  41.9 15.0 %collective-permute-start.10 = (bf16[256,768]{1,0:T(8,128)(2,1)S(1)}, bf16[256,768]{1,0:T(8,128)(2,1)S(1)}, u32[]{:S(2)}, u32[]{:S(2)}) collective-permute-start(bf16[256,768]{1,0:T(8,128)(2,1)S(1)} %add_convert_fusion.6), channel_id=1, source_target_pairs={{0,2},{2,0},{1,3},{3,1},{4,6},{6,4},{5,7},{7,5},{8,10},{10,8},{9,1... | collective-permute-start | bytes 1179656 | tf_op jit(solution)/shard_map/ppermute | solution.py:473
  43.2 13.7 %collective-permute-start.9 = (bf16[256,768]{1,0:T(8,128)(2,1)S(1)}, bf16[256,768]{1,0:T(8,128)(2,1)}, u32[]{:S(2)}, u32[]{:S(2)}) collective-permute-start(bf16[256,768]{1,0:T(8,128)(2,1)S(1)} %add_convert_fusion.6), channel_id=1, source_target_pairs={{0,4},{4,8},{8,12},{12,0},{1,5},{5,9},{9,13},{13,1},{2,6},{6,10},{... | collective-permute-start | bytes 1179656 | tf_op jit(solution)/shard_map/ppermute | solution.py:473
  44.4 31.6 %collective-permute-start.13 = (bf16[192,1536]{1,0:T(8,128)(2,1)}, bf16[192,1536]{1,0:T(8,128)(2,1)}, u32[]{:S(2)}, u32[]{:S(2)}) collective-permute-start(bf16[192,1536]{1,0:T(8,128)(2,1)} %constant_dynamic-slice_fusion.17), channel_id=1, source_target_pairs={{0,16},{16,0},{1,17},{17,1},{2,18},{18,2},{3,19},{19,3},{4,20},{20... | collective-permute-start | bytes 1769480 | tf_op jit(solution)/shard_map/ppermute | solution.py:473
  57.7 15.3 %collective-permute-start.12 = (bf16[256,768]{1,0:T(8,128)(2,1)}, bf16[256,768]{1,0:T(8,128)(2,1)S(1)}, u32[]{:S(2)}, u32[]{:S(2)}) collective-permute-start(bf16[256,768]{1,0:T(8,128)(2,1)} %collective-permute-done.9), channel_id=1, source_target_pairs={{0,2},{2,0},{1,3},{3,1},{4,6},{6,4},{5,7},{7,5},{8,10},{10,8},{9,1... | collective-permute-start | bytes 1179656 | tf_op jit(solution)/shard_map/ppermute | solution.py:473
  57.9 15.0 %collective-permute-start.11 = (bf16[256,768]{1,0:T(8,128)(2,1)}, bf16[256,768]{1,0:T(8,128)(2,1)}, u32[]{:S(2)}, u32[]{:S(2)}) collective-permute-start(bf16[256,768]{1,0:T(8,128)(2,1)} %collective-permute-done.9), channel_id=1, source_target_pairs={{0,4},{4,8},{8,12},{12,0},{1,5},{5,9},{9,13},{13,1},{2,6},{6,10},{... | collective-permute-start | bytes 1179656 | tf_op jit(solution)/shard_map/ppermute | solution.py:473
  59.3 16.7 %collective-permute-start.14 = (bf16[192,768]{1,0:T(8,128)(2,1)}, bf16[192,768]{1,0:T(8,128)(2,1)S(1)}, u32[]{:S(2)}, u32[]{:S(2)}) collective-permute-start(bf16[192,768]{1,0:T(8,128)(2,1)} %constant_dynamic-slice_fusion.16), channel_id=1, source_target_pairs={{0,16},{16,0},{1,17},{17,1},{2,18},{18,2},{3,19},{19,3},{4,20},{20... | collective-permute-start | bytes 884744 | tf_op jit(solution)/shard_map/ppermute | solution.py:473
  73.0 36.6 %collective-permute-start.17 = (bf16[256,768]{1,0:T(8,128)(2,1)}, bf16[256,768]{1,0:T(8,128)(2,1)}, u32[]{:S(2)}, u32[]{:S(2)}) collective-permute-start(bf16[256,768]{1,0:T(8,128)(2,1)} %collective-permute-done.11), channel_id=1, source_target_pairs={{0,2},{2,0},{1,3},{3,1},{4,6},{6,4},{5,7},{7,5},{8,10},{10,8},{9,1... | collective-permute-start | bytes 1179656 | tf_op jit(solution)/shard_map/ppermute | solution.py:473
  74.2 35.6 %collective-permute-start.16 = (bf16[256,768]{1,0:T(8,128)(2,1)}, bf16[256,768]{1,0:T(8,128)(2,1)}, u32[]{:S(2)}, u32[]{:S(2)}) collective-permute-start(bf16[256,768]{1,0:T(8,128)(2,1)} %collective-permute-done.11), channel_id=1, source_target_pairs={{0,4},{4,8},{8,12},{12,0},{1,5},{5,9},{9,13},{13,1},{2,6},{6,10},{... | collective-permute-start | bytes 1179656 | tf_op jit(solution)/shard_map/ppermute | solution.py:473
  77.8 114.6 %collective-permute-start.20 = (bf16[192,768]{1,0:T(8,128)(2,1)}, bf16[192,768]{1,0:T(8,128)(2,1)}, u32[]{:S(2)}, u32[]{:S(2)}) collective-permute-start(bf16[192,768]{1,0:T(8,128)(2,1)} %constant_dynamic-slice_fusion.15), channel_id=1, source_target_pairs={{0,16},{16,0},{1,17},{17,1},{2,18},{18,2},{3,19},{19,3},{4,20},{20... | collective-permute-start | bytes 884744 | tf_op jit(solution)/shard_map/ppermute | solution.py:473
  78.0 22.9 %collective-permute-start.15 = (bf16[192,768]{1,0:T(8,128)(2,1)S(1)}, bf16[192,768]{1,0:T(8,128)(2,1)}, u32[]{:S(2)}, u32[]{:S(2)}) collective-permute-start(bf16[192,768]{1,0:T(8,128)(2,1)S(1)} %collective-permute-done.14.refs_1_), channel_id=1, source_target_pairs={{0,1},{1,0},{2,3},{3,2},{4,5},{5,4},{6,7},{7,6},{8,9},{9,8},{10,11... | collective-permute-start | bytes 884744 | tf_op jit(solution)/shard_map/ppermute | solution.py:473
  85.5 37.9 %collective-permute-start.19 = (bf16[192,1536]{1,0:T(8,128)(2,1)}, bf16[192,1536]{1,0:T(8,128)(2,1)S(1)}, u32[]{:S(2)}, u32[]{:S(2)}) collective-permute-start(bf16[192,1536]{1,0:T(8,128)(2,1)} %collective-permute-done.13.refs_1_), channel_id=1, source_target_pairs={{0,1},{1,0},{2,3},{3,2},{4,5},{5,4},{6,7},{7,6},{8,9},{9,8},{10,11... | collective-permute-start | bytes 1769480 | tf_op jit(solution)/shard_map/ppermute | solution.py:473
  101.0 91.4 %collective-permute-start.22 = (bf16[768,768]{1,0:T(8,128)(2,1)}, bf16[768,768]{1,0:T(8,128)(2,1)S(1)}, u32[]{:S(2)}, u32[]{:S(2)}) collective-permute-start(bf16[768,768]{1,0:T(8,128)(2,1)} %constant_dynamic-slice_fusion.13), channel_id=1, source_target_pairs={{0,16},{16,0},{1,17},{17,1},{2,18},{18,2},{3,19},{19,3},{4,20},{20... | collective-permute-start | bytes 3538952 | tf_op jit(solution)/shard_map/ppermute | solution.py:473
  109.6 82.8 %collective-permute-start.21 = (bf16[192,3072]{1,0:T(8,128)(2,1)}, bf16[192,3072]{1,0:T(8,128)(2,1)}, u32[]{:S(2)}, u32[]{:S(2)}) collective-permute-start(bf16[192,3072]{1,0:T(8,128)(2,1)} %constant_dynamic-slice_fusion.14), channel_id=1, source_target_pairs={{0,16},{16,0},{1,17},{17,1},{2,18},{18,2},{3,19},{19,3},{4,20},{20... | collective-permute-start | bytes 3538952 | tf_op jit(solution)/shard_map/ppermute | solution.py:473
  109.8 19.4 %collective-permute-start.18 = (bf16[256,768]{1,0:T(8,128)(2,1)}, bf16[256,768]{1,0:T(8,128)(2,1)S(1)}, u32[]{:S(2)}, u32[]{:S(2)}) collective-permute-start(bf16[256,768]{1,0:T(8,128)(2,1)} %collective-permute-done.16), channel_id=1, source_target_pairs={{0,2},{2,0},{1,3},{3,1},{4,6},{6,4},{5,7},{7,5},{8,10},{10,8},{9,1... | collective-permute-start | bytes 1179656 | tf_op jit(solution)/shard_map/ppermute | solution.py:473
  195.6 47.7 %collective-permute-start.34 = (bf16[256,768]{0,1:T(8,128)(2,1)}, bf16[256,768]{0,1:T(8,128)(2,1)}, u32[]{:S(2)}, u32[]{:S(2)}) collective-permute-start(bf16[256,768]{0,1:T(8,128)(2,1)} %bitcast.23), channel_id=1, source_target_pairs={{0,1},{1,0},{2,3},{3,2},{4,5},{5,4},{6,7},{7,6},{8,9},{9,8},{10,11... | collective-permute-start | bytes 1179656 | tf_op jit(solution)/shard_map/ppermute | solution.py:473
  195.7 11.0 %collective-permute-start.24 = (bf16[192,3072]{1,0:T(8,128)(2,1)}, bf16[192,3072]{1,0:T(8,128)(2,1)}, u32[]{:S(2)}, u32[]{:S(2)}) collective-permute-start(bf16[192,3072]{1,0:T(8,128)(2,1)} %collective-permute-done.21.refs_1_), channel_id=1, source_target_pairs={{0,1},{1,0},{2,3},{3,2},{4,5},{5,4},{6,7},{7,6},{8,9},{9,8},{10,11... | collective-permute-start | bytes 3538952 | tf_op jit(solution)/shard_map/ppermute | solution.py:473
  196.2 22.5 %collective-permute-start.25 = (bf16[768,768]{1,0:T(8,128)(2,1)}, bf16[768,768]{1,0:T(8,128)(2,1)}, u32[]{:S(2)}, u32[]{:S(2)}) collective-permute-start(bf16[768,768]{1,0:T(8,128)(2,1)} %copy-done.29), channel_id=1, source_target_pairs={{0,1},{1,0},{2,3},{3,2},{4,5},{5,4},{6,7},{7,6},{8,9},{9,8},{10,11... | collective-permute-start | bytes 3538952 | tf_op jit(solution)/shard_map/ppermute | solution.py:473
  197.8 47.0 %collective-permute-start.31 = (bf16[256,384]{1,0:T(8,128)(2,1)}, bf16[256,384]{1,0:T(8,128)(2,1)}, u32[]{:S(2)}, u32[]{:S(2)}) collective-permute-start(bf16[256,384]{1,0:T(8,128)(2,1)} %get-tuple-element.451), channel_id=1, source_target_pairs={{0,1},{1,0},{2,3},{3,2},{4,5},{5,4},{6,7},{7,6},{8,9},{9,8},{10,11... | collective-permute-start | bytes 589832 | tf_op jit(solution)/shard_map/ppermute | solution.py:473
  206.6 38.2 %collective-permute-start.32 = (bf16[256,768]{1,0:T(8,128)(2,1)}, bf16[256,768]{1,0:T(8,128)(2,1)}, u32[]{:S(2)}, u32[]{:S(2)}) collective-permute-start(bf16[256,768]{1,0:T(8,128)(2,1)} %add_convert_fusion.5), channel_id=1, source_target_pairs={{0,1},{1,0},{2,3},{3,2},{4,5},{5,4},{6,7},{7,6},{8,9},{9,8},{10,11... | collective-permute-start | bytes 1179656 | tf_op jit(solution)/shard_map/ppermute | solution.py:473
  240.7 4.8 collective-permute-start.33
  241.1 4.5 collective-permute-start.30
  251.7 45.2 %collective-permute-start.37 = (bf16[2,4,48,1920]{3,2,1,0:T(8,128)(2,1)}, bf16[2,4,48,1920]{3,2,1,0:T(8,128)(2,1)}, u32[]{:S(2)}, u32[]{:S(2)}) collective-permute-start(bf16[2,4,48,1920]{3,2,1,0:T(8,128)(2,1)} %get-tuple-element.425), channel_id=1, source_target_pairs={{0,2},{2,0},{1,3},{3,1},{4,6},{6,4},{5,7},{7,5},{8,10},{10,8},{9,1... | collective-permute-start | bytes 4423688 | tf_op jit(solution)/shard_map/ppermute | solution.py:473
  257.9 38.9 %collective-permute-start.36 = (bf16[2,4,192,384]{3,2,1,0:T(8,128)(2,1)}, bf16[2,4,192,384]{3,2,1,0:T(8,128)(2,1)}, u32[]{:S(2)}, u32[]{:S(2)}) collective-permute-start(bf16[2,4,192,384]{3,2,1,0:T(8,128)(2,1)} %get-tuple-element.427), channel_id=1, source_target_pairs={{0,16},{16,0},{1,17},{17,1},{2,18},{18,2},{3,19},{19,3},{4,20},{20... | collective-permute-start | bytes 3538952 | tf_op jit(solution)/shard_map/ppermute | solution.py:473
  299.5 20.1 %collective-permute-start.39 = (bf16[4,48,1920]{2,1,0:T(8,128)(2,1)}, bf16[4,48,1920]{2,1,0:T(8,128)(2,1)}, u32[]{:S(2)}, u32[]{:S(2)}) collective-permute-start(bf16[4,48,1920]{2,1,0:T(8,128)(2,1)} %fusion.25), channel_id=1, source_target_pairs={{0,16},{16,0},{1,17},{17,1},{2,18},{18,2},{3,19},{19,3},{4,20},{20... | collective-permute-start | bytes 2211848 | tf_op jit(solution)/shard_map/ppermute | solution.py:473
  302.2 17.4 %collective-permute-start.38 = (bf16[4,192,384]{2,1,0:T(8,128)(2,1)}, bf16[4,192,384]{2,1,0:T(8,128)(2,1)}, u32[]{:S(2)}, u32[]{:S(2)}) collective-permute-start(bf16[4,192,384]{2,1,0:T(8,128)(2,1)} %fusion.28), channel_id=1, source_target_pairs={{0,2},{2,0},{1,3},{3,1},{4,6},{6,4},{5,7},{7,5},{8,10},{10,8},{9,1... | collective-permute-start | bytes 1769480 | tf_op jit(solution)/shard_map/ppermute | solution.py:473
  321.7 23.8 %all-to-all-start = ((bf16[4,192,384]{2,1,0:T(8,128)(2,1)}), bf16[4,192,384]{2,1,0:T(8,128)(2,1)S(1)}, u32[]{:S(2)}, u32[]{:S(2)}) async-start(bf16[4,192,384]{2,1,0:T(8,128)(2,1)} %add_convert_fusion.3), calls=%async_computation | async-start | bytes 1179648 | tf_op jit(solution)/shard_map/all_to_all | solution.py:540
  325.5 64.2 %collective-permute-start.27 = (f32[3,128]{1,0:T(4,128)S(1)}, f32[3,128]{1,0:T(4,128)S(1)}, u32[]{:S(2)}, u32[]{:S(2)}) collective-permute-start(f32[3,128]{1,0:T(4,128)S(1)} %slice.212), channel_id=1, source_target_pairs={{0,1},{1,0},{2,3},{3,2},{4,5},{5,4},{6,7},{7,6},{8,9},{9,8},{10,11... | collective-permute-start | bytes 4616 | tf_op jit(solution)/shard_map/ppermute | solution.py:473
  345.5 32.2 %all-to-all-start.1 = ((bf16[4,48,1920]{2,1,0:T(8,128)(2,1)}), bf16[4,48,1920]{2,1,0:T(8,128)(2,1)}, u32[]{:S(2)}, u32[]{:S(2)}) async-start(bf16[4,48,1920]{2,1,0:T(8,128)(2,1)} %add_convert_fusion.2), calls=%async_computation.1 | async-start | bytes 1474560 | tf_op jit(solution)/shard_map/all_to_all | solution.py:540
  367.2 23.3 %collective-permute-start.40 = (bf16[768,1152]{1,0:T(8,128)(2,1)}, bf16[768,1152]{1,0:T(8,128)(2,1)}, u32[]{:S(2)}, u32[]{:S(2)}) collective-permute-start(bf16[768,1152]{1,0:T(8,128)(2,1)} %get-tuple-element.421), channel_id=1, source_target_pairs={{0,1},{1,0},{2,3},{3,2},{4,5},{5,4},{6,7},{7,6},{8,9},{9,8},{10,11... | collective-permute-start | bytes 5308424 | tf_op jit(solution)/shard_map/ppermute | solution.py:473
  378.7 27.0 %all-to-all-start.2 = ((bf16[4,192,384]{2,1,0:T(8,128)(2,1)}), bf16[4,192,384]{2,1,0:T(8,128)(2,1)}, u32[]{:S(2)}, u32[]{:S(2)}) async-start(bf16[4,192,384]{2,1,0:T(8,128)(2,1)} %broadcast_in_dim.162), calls=%async_computation.2 | async-start | bytes 1179648 | tf_op jit(solution)/shard_map/all_to_all | solution.py:557
  386.5 19.2 %collective-permute-start.41 = (bf16[4,256,384]{2,1,0:T(8,128)(2,1)}, bf16[4,256,384]{2,1,0:T(8,128)(2,1)}, u32[]{:S(2)}, u32[]{:S(2)}) collective-permute-start(bf16[4,256,384]{2,1,0:T(8,128)(2,1)} %get-tuple-element.423), channel_id=1, source_target_pairs={{0,2},{2,0},{1,3},{3,1},{4,6},{6,4},{5,7},{7,5},{8,10},{10,8},{9,1... | collective-permute-start | bytes 2359304 | tf_op jit(solution)/shard_map/ppermute | solution.py:473
  407.9 63.2 %all-to-all-start.3 = ((bf16[4,48,1920]{2,1,0:T(8,128)(2,1)}), bf16[4,48,1920]{2,1,0:T(8,128)(2,1)}, u32[]{:S(2)}, u32[]{:S(2)}) async-start(bf16[4,48,1920]{2,1,0:T(8,128)(2,1)} %broadcast_in_dim.163), calls=%async_computation.3 | async-start | bytes 1474560 | tf_op jit(solution)/shard_map/all_to_all | solution.py:557
  413.4 30.0 %collective-permute-start.45 = (bf16[4,256,384]{2,1,0:T(8,128)(2,1)}, bf16[4,256,384]{2,1,0:T(8,128)(2,1)S(1)}, u32[]{:S(2)}, u32[]{:S(2)}) collective-permute-start(bf16[4,256,384]{2,1,0:T(8,128)(2,1)} %get-tuple-element.433), channel_id=1, source_target_pairs={{0,2},{2,0},{1,3},{3,1},{4,6},{6,4},{5,7},{7,5},{8,10},{10,8},{9,1... | collective-permute-start | bytes 2359304 | tf_op jit(solution)/shard_map/ppermute | solution.py:473
  417.5 25.9 %collective-permute-start.46 = (bf16[2,4,48,1152]{3,2,1,0:T(8,128)(2,1)}, bf16[2,4,48,1152]{3,2,1,0:T(8,128)(2,1)}, u32[]{:S(2)}, u32[]{:S(2)}) collective-permute-start(bf16[2,4,48,1152]{3,2,1,0:T(8,128)(2,1)} %get-tuple-element.429), channel_id=1, source_target_pairs={{0,16},{16,0},{1,17},{17,1},{2,18},{18,2},{3,19},{19,3},{4,20},{20... | collective-permute-start | bytes 2654216 | tf_op jit(solution)/shard_map/ppermute | solution.py:473
  420.8 17.7 %collective-permute-start.44 = (bf16[256,384]{1,0:T(8,128)(2,1)}, bf16[256,384]{1,0:T(8,128)(2,1)}, u32[]{:S(2)}, u32[]{:S(2)}) collective-permute-start(bf16[256,384]{1,0:T(8,128)(2,1)} %get-tuple-element.444), channel_id=1, source_target_pairs={{0,4},{4,8},{8,12},{12,0},{1,5},{5,9},{9,13},{13,1},{2,6},{6,10},{... | collective-permute-start | bytes 589832 | tf_op jit(solution)/shard_map/ppermute | solution.py:473
  422.3 21.1 %collective-permute-start.43 = (bf16[256,384]{1,0:T(8,128)(2,1)S(1)}, bf16[256,384]{1,0:T(8,128)(2,1)}, u32[]{:S(2)}, u32[]{:S(2)}) collective-permute-start(bf16[256,384]{1,0:T(8,128)(2,1)S(1)} %get-tuple-element.445), channel_id=1, source_target_pairs={{0,8},{4,12},{8,0},{12,4},{1,9},{5,13},{9,1},{13,5},{2,10},{6,14},... | collective-permute-start | bytes 589832 | tf_op jit(solution)/shard_map/ppermute | solution.py:473
  424.4 19.0 %collective-permute-start.42 = (bf16[256,384]{1,0:T(8,128)(2,1)S(1)}, bf16[256,384]{1,0:T(8,128)(2,1)}, u32[]{:S(2)}, u32[]{:S(2)}) collective-permute-start(bf16[256,384]{1,0:T(8,128)(2,1)S(1)} %get-tuple-element.446), channel_id=1, source_target_pairs={{0,12},{4,0},{8,4},{12,8},{1,13},{5,1},{9,5},{13,9},{2,14},{6,2},{... | collective-permute-start | bytes 589832 | tf_op jit(solution)/shard_map/ppermute | solution.py:473
  438.6 77.6 %collective-permute-start.26 = (bf16[128,768]{1,0:T(8,128)(2,1)}, bf16[128,768]{1,0:T(8,128)(2,1)}, u32[]{:S(2)}, u32[]{:S(2)}) collective-permute-start(bf16[128,768]{1,0:T(8,128)(2,1)} %slice.209), channel_id=1, source_target_pairs={{0,1},{1,0},{2,3},{3,2},{4,5},{5,4},{6,7},{7,6},{8,9},{9,8},{10,11... | collective-permute-start | bytes 589832 | tf_op jit(solution)/shard_map/ppermute | solution.py:473
  445.6 25.5 %collective-permute-start.50 = (bf16[4,48,1152]{2,1,0:T(8,128)(2,1)}, bf16[4,48,1152]{2,1,0:T(8,128)(2,1)}, u32[]{:S(2)}, u32[]{:S(2)}) collective-permute-start(bf16[4,48,1152]{2,1,0:T(8,128)(2,1)} %fusion.32), channel_id=1, source_target_pairs={{0,2},{2,0},{1,3},{3,1},{4,6},{6,4},{5,7},{7,5},{8,10},{10,8},{9,1... | collective-permute-start | bytes 1327112 | tf_op jit(solution)/shard_map/ppermute | solution.py:473
  447.0 23.4 %collective-permute-start.49 = (bf16[256,384]{1,0:T(8,128)(2,1)S(1)}, bf16[256,384]{1,0:T(8,128)(2,1)S(1)}, u32[]{:S(2)}, u32[]{:S(2)}) collective-permute-start(bf16[256,384]{1,0:T(8,128)(2,1)S(1)} %get-tuple-element.441), channel_id=1, source_target_pairs={{0,4},{4,8},{8,12},{12,0},{1,5},{5,9},{9,13},{13,1},{2,6},{6,10},{... | collective-permute-start | bytes 589832 | tf_op jit(solution)/shard_map/ppermute | solution.py:473
  451.5 19.3 %collective-permute-start.48 = (bf16[256,384]{1,0:T(8,128)(2,1)S(1)}, bf16[256,384]{1,0:T(8,128)(2,1)}, u32[]{:S(2)}, u32[]{:S(2)}) collective-permute-start(bf16[256,384]{1,0:T(8,128)(2,1)S(1)} %get-tuple-element.442), channel_id=1, source_target_pairs={{0,8},{4,12},{8,0},{12,4},{1,9},{5,13},{9,1},{13,5},{2,10},{6,14},... | collective-permute-start | bytes 589832 | tf_op jit(solution)/shard_map/ppermute | solution.py:473
  451.8 19.3 %collective-permute-start.47 = (bf16[256,384]{1,0:T(8,128)(2,1)S(1)}, bf16[256,384]{1,0:T(8,128)(2,1)}, u32[]{:S(2)}, u32[]{:S(2)}) collective-permute-start(bf16[256,384]{1,0:T(8,128)(2,1)S(1)} %get-tuple-element.443), channel_id=1, source_target_pairs={{0,12},{4,0},{8,4},{12,8},{1,13},{5,1},{9,5},{13,9},{2,14},{6,2},{... | collective-permute-start | bytes 589832 | tf_op jit(solution)/shard_map/ppermute | solution.py:473
  470.4 36.2 %collective-permute-start.52 = (bf16[4,192,384]{2,1,0:T(8,128)(2,1)}, bf16[4,192,384]{2,1,0:T(8,128)(2,1)}, u32[]{:S(2)}, u32[]{:S(2)}) collective-permute-start(bf16[4,192,384]{2,1,0:T(8,128)(2,1)} %all-to-all-done.2.refs_0_), channel_id=1, source_target_pairs={{0,2},{2,0},{1,3},{3,1},{4,6},{6,4},{5,7},{7,5},{8,10},{10,8},{9,1... | collective-permute-start | bytes 1769480 | tf_op jit(solution)/shard_map/ppermute | solution.py:473
  480.7 26.0 %all-to-all-start.4 = ((bf16[4,48,1152]{2,1,0:T(8,128)(2,1)}), bf16[4,48,1152]{2,1,0:T(8,128)(2,1)}, u32[]{:S(2)}, u32[]{:S(2)}) async-start(bf16[4,48,1152]{2,1,0:T(8,128)(2,1)} %add_convert_fusion.4), calls=%async_computation.4 | async-start | bytes 884736 | tf_op jit(solution)/shard_map/all_to_all | solution.py:540
  488.4 33.3 %collective-permute-start.51 = (f32[128,768]{1,0:T(8,128)S(1)}, f32[128,768]{1,0:T(8,128)S(1)}, u32[]{:S(2)}, u32[]{:S(2)}) collective-permute-start(f32[128,768]{1,0:T(8,128)S(1)} %slice.225), channel_id=1, source_target_pairs={{0,1},{1,0},{2,3},{3,2},{4,5},{5,4},{6,7},{7,6},{8,9},{9,8},{10,11... | collective-permute-start | bytes 1179656 | tf_op jit(solution)/shard_map/ppermute | solution.py:473
  490.8 38.9 %collective-permute-start.62 = (bf16[4,48,1920]{2,1,0:T(8,128)(2,1)}, bf16[4,48,1920]{2,1,0:T(8,128)(2,1)S(1)}, u32[]{:S(2)}, u32[]{:S(2)}) collective-permute-start(bf16[4,48,1920]{2,1,0:T(8,128)(2,1)} %all-to-all-done.3.refs_0_), channel_id=1, source_target_pairs={{0,2},{2,0},{1,3},{3,1},{4,6},{6,4},{5,7},{7,5},{8,10},{10,8},{9,1... | collective-permute-start | bytes 2211848 | tf_op jit(solution)/shard_map/ppermute | solution.py:473
  509.1 8.1 %collective-permute-start.53 = (f32[25,768]{1,0:T(8,128)S(1)}, f32[25,768]{1,0:T(8,128)S(1)}, u32[]{:S(2)}, u32[]{:S(2)}) collective-permute-start(f32[25,768]{1,0:T(8,128)S(1)} %concatenate.117), channel_id=1, source_target_pairs={{0,1},{1,0},{2,3},{3,2},{4,5},{5,4},{6,7},{7,6},{8,9},{9,8},{10,11... | collective-permute-start | bytes 230408 | tf_op jit(solution)/shard_map/ppermute | solution.py:473
  511.4 27.2 %all-to-all-start.5 = ((bf16[4,48,1152]{2,1,0:T(8,128)(2,1)}), bf16[4,48,1152]{2,1,0:T(8,128)(2,1)S(1)}, u32[]{:S(2)}, u32[]{:S(2)}) async-start(bf16[4,48,1152]{2,1,0:T(8,128)(2,1)} %broadcast_in_dim.173), calls=%async_computation.5 | async-start | bytes 884736 | tf_op jit(solution)/shard_map/all_to_all | solution.py:557
  521.7 19.4 %collective-permute-start.65 = (bf16[4,192,384]{2,1,0:T(8,128)(2,1)}, bf16[4,192,384]{2,1,0:T(8,128)(2,1)S(1)}, u32[]{:S(2)}, u32[]{:S(2)}) collective-permute-start(bf16[4,192,384]{2,1,0:T(8,128)(2,1)} %all-to-all-done.2.refs_0_), channel_id=1, source_target_pairs={{0,1},{1,0},{2,3},{3,2},{4,5},{5,4},{6,7},{7,6},{8,9},{9,8},{10,11... | collective-permute-start | bytes 1769480 | tf_op jit(solution)/shard_map/ppermute | solution.py:473
  524.8 8.2 %collective-permute-start.58 = (f32[25,768]{1,0:T(8,128)S(1)}, f32[25,768]{1,0:T(8,128)S(1)}, u32[]{:S(2)}, u32[]{:S(2)}) collective-permute-start(f32[25,768]{1,0:T(8,128)S(1)} %add.327), channel_id=1, source_target_pairs={{0,12},{4,0},{8,4},{12,8},{1,13},{5,1},{9,5},{13,9},{2,14},{6,2},{... | collective-permute-start | bytes 230408 | tf_op jit(solution)/shard_map/ppermute | solution.py:473
  527.9 9.0 %collective-permute-start.57 = (f32[25,768]{1,0:T(8,128)S(1)}, f32[25,768]{1,0:T(8,128)S(1)}, u32[]{:S(2)}, u32[]{:S(2)}) collective-permute-start(f32[25,768]{1,0:T(8,128)S(1)} %add.327), channel_id=1, source_target_pairs={{0,8},{4,12},{8,0},{12,4},{1,9},{5,13},{9,1},{13,5},{2,10},{6,14},... | collective-permute-start | bytes 230408 | tf_op jit(solution)/shard_map/ppermute | solution.py:473
  527.9 10.6 %collective-permute-start.56 = (f32[25,768]{1,0:T(8,128)S(1)}, f32[25,768]{1,0:T(8,128)S(1)}, u32[]{:S(2)}, u32[]{:S(2)}) collective-permute-start(f32[25,768]{1,0:T(8,128)S(1)} %add.327), channel_id=1, source_target_pairs={{0,4},{4,8},{8,12},{12,0},{1,5},{5,9},{9,13},{13,1},{2,6},{6,10},{... | collective-permute-start | bytes 230408 | tf_op jit(solution)/shard_map/ppermute | solution.py:473
  529.7 28.8 %collective-permute-start.63 = (bf16[4,48,1920]{2,1,0:T(8,128)(2,1)}, bf16[4,48,1920]{2,1,0:T(8,128)(2,1)}, u32[]{:S(2)}, u32[]{:S(2)}) collective-permute-start(bf16[4,48,1920]{2,1,0:T(8,128)(2,1)} %all-to-all-done.3.refs_0_), channel_id=1, source_target_pairs={{0,1},{1,0},{2,3},{3,2},{4,5},{5,4},{6,7},{7,6},{8,9},{9,8},{10,11... | collective-permute-start | bytes 2211848 | tf_op jit(solution)/shard_map/ppermute | solution.py:473
  533.0 20.0 %collective-permute-start.66 = (bf16[4,192,384]{2,1,0:T(8,128)(2,1)}, bf16[4,192,384]{2,1,0:T(8,128)(2,1)S(1)}, u32[]{:S(2)}, u32[]{:S(2)}) collective-permute-start(bf16[4,192,384]{2,1,0:T(8,128)(2,1)} %collective-permute-done.52.refs_1_), channel_id=1, source_target_pairs={{0,1},{1,0},{2,3},{3,2},{4,5},{5,4},{6,7},{7,6},{8,9},{9,8},{10,11... | collective-permute-start | bytes 1769480 | tf_op jit(solution)/shard_map/ppermute | solution.py:473
  537.0 21.6 %collective-permute-start.64 = (bf16[4,48,1920]{2,1,0:T(8,128)(2,1)S(1)}, bf16[4,48,1920]{2,1,0:T(8,128)(2,1)}, u32[]{:S(2)}, u32[]{:S(2)}) collective-permute-start(bf16[4,48,1920]{2,1,0:T(8,128)(2,1)S(1)} %collective-permute-done.62.refs_1_), channel_id=1, source_target_pairs={{0,1},{1,0},{2,3},{3,2},{4,5},{5,4},{6,7},{7,6},{8,9},{9,8},{10,11... | collective-permute-start | bytes 2211848 | tf_op jit(solution)/shard_map/ppermute | solution.py:473
  538.6 11.9 %collective-permute-start.59 = (bf16[4,48,1152]{2,1,0:T(8,128)(2,1)S(1)}, bf16[4,48,1152]{2,1,0:T(8,128)(2,1)S(1)}, u32[]{:S(2)}, u32[]{:S(2)}) collective-permute-start(bf16[4,48,1152]{2,1,0:T(8,128)(2,1)S(1)} %all-to-all-done.5.refs_0_), channel_id=1, source_target_pairs={{0,2},{2,0},{1,3},{3,1},{4,6},{6,4},{5,7},{7,5},{8,10},{10,8},{9,1... | collective-permute-start | bytes 1327112 | tf_op jit(solution)/shard_map/ppermute | solution.py:473
  541.2 22.8 %collective-permute-start.60 = (bf16[4,48,1152]{2,1,0:T(8,128)(2,1)S(1)}, bf16[4,48,1152]{2,1,0:T(8,128)(2,1)S(1)}, u32[]{:S(2)}, u32[]{:S(2)}) collective-permute-start(bf16[4,48,1152]{2,1,0:T(8,128)(2,1)S(1)} %all-to-all-done.5.refs_0_), channel_id=1, source_target_pairs={{0,1},{1,0},{2,3},{3,2},{4,5},{5,4},{6,7},{7,6},{8,9},{9,8},{10,11... | collective-permute-start | bytes 1327112 | tf_op jit(solution)/shard_map/ppermute | solution.py:473
  550.4 13.6 %collective-permute-start.61 = (bf16[4,48,1152]{2,1,0:T(8,128)(2,1)S(1)}, bf16[4,48,1152]{2,1,0:T(8,128)(2,1)S(1)}, u32[]{:S(2)}, u32[]{:S(2)}) collective-permute-start(bf16[4,48,1152]{2,1,0:T(8,128)(2,1)S(1)} %collective-permute-done.59.refs_1_), channel_id=1, source_target_pairs={{0,1},{1,0},{2,3},{3,2},{4,5},{5,4},{6,7},{7,6},{8,9},{9,8},{10,11... | collective-permute-start | bytes 1327112 | tf_op jit(solution)/shard_map/ppermute | solution.py:473
  (109 other events, 1202.6 us)

commit v4 on v3

--- a/solution.py
+++ b/solution.py
@@ -872,7 +872,12 @@
     sums, piece = advance((sums, piece), table, down)
     bias_grad = table_sums(sums + piece)
     pair_normed_grad = jnp.concatenate([finish(share_one), finish(share_two)], axis=1)
-    (down_grad,), (up_grad, out_grad), (qkv_grad,) = [finish(flight) for flight in (down, up, table)]
+    (down_grad,), (up_grad, out_grad) = finish(down), finish(up)
+    table.land(table.values)
+    table.land(table.values)
+    (down_grad, up_grad, out_grad), last_pieces = tie((down_grad, up_grad, out_grad), table.values)
+    table.land(last_pieces)
+    (qkv_grad,) = finish(table)
 
     normed_grad = dot32(query_grad, query_weight, (1, 1)) + pair_normed_grad
     first_part, gain_one_grad, shift_one_grad = norm_one_back(normed_grad)

time: 578 us -> 577 us (level)
  no operation moved by 1% of the time
where the time goes in v4:
time: 577 us; the launch traced here: 569 us
  Pallas kernels  268 us (46%)
  starting transfers between devices  98.6 us (17%)
  local copies, waits for them, and re-layouts  67.9 us (12%)
  matrix products  54.2 us (9%)
  other arithmetic  50 us (9%)
  waiting for transfers between devices  28 us (5%)
    ppermute x67, starting transfers between devices, shifted(): lax.ppermute(values, axis, [(i, (i + step) % size) for i in range(size)])  71.6 us
    pallas_call x4, Pallas kernels, attend_back(): pl.pallas_call(functools.partial(backward_kernel, 512), grid=(rows // til...  66.3 us
    pallas_call x5, Pallas kernels, pair_bias(): pl.pallas_call(functools.partial(bias_kernel, 256), grid=(steps,), in_spe...  53.6 us
    pallas_call x4, Pallas kernels, table_grad(): pl.pallas_call(functools.partial(table_grad_kernel, 256), grid=(steps,),...  52 us
    pallas_call x1, Pallas kernels, attend(): pl.pallas_call(functools.partial(forward_kernel, 512), grid=(rows // tile...  39.7 us
    dot_general x10, matrix products, dot32(): lax.dot_general(left, right, ((contract[:1], contract[1:]), ((), ())), pr...  38.4 us
    ppermute x67, waiting for transfers between devices, shifted(): lax.ppermute(values, axis, [(i, (i + step) % size) for i in range(size)])  28 us
    pallas_call x5, Pallas kernels, place_shards(): pl.pallas_call(functools.partial(place_kernel, steps), grid_spec=pltpu.Pr...  26.7 us
  transfers between devices with their start and end apart: 73, of which 12 were waited for; matrix products, arithmetic and copies ran while one was open for 25% of the time, Pallas kernels for 46%

profile of v4, /device:TPU:1, one launch (start us, length us, event | category | flops | bytes accessed | tf_op | source)
XLA Modules:
  0.0 569.3 jit_solution(2814504346624319808)
XLA Ops:
  2.3 2.7 collective-permute-start.6
  10.3 2.4 collective-permute-done.1
  13.8 2.3 collective-permute-done.2
  29.7 7.4 %pair_bias.5.refs_0_ = bf16[4,2048,2048]{2,1,0:T(8,128)(2,1)} custom-call(f32[256,8]{1,0:T(8,128)} %pad_convert_fusion.q_ref, f32[8,2048]{1,0:T(8,128)} %pad_convert_fusion.1.k_ref, bf16[32,128]{1,0:T(8,128)(2,1)} %fusion.48.w_ref), custom_call_target="tpu_custom_call" | custom-call | flops 1500000000 | bytes 4194304 | tf_op jit(solution)/shard_map/pair_bias/pallas_call | solution.py:103
  37.7 2.2 collective-permute-done.7
  45.4 11.5 %pair_bias.6.refs_0_ = bf16[4,2048,2048]{2,1,0:T(8,128)(2,1)} custom-call(f32[256,8]{1,0:T(8,128)} %pad_convert_fusion.q_ref, f32[8,2048]{1,0:T(8,128)} %pad_convert_fusion.1.k_ref, bf16[32,128]{1,0:T(8,128)(2,1)} %fusion.48.w_ref, bf16[4,2048,2048]{2,1,0:T(8,128)(2,1)} %pair_bias.5.refs_0_), custom_call_target="tpu_custom_call", output_to_operand_aliasing={{}: (3, {})} | custom-call | flops 2624999936 | bytes 7340032 | tf_op jit(solution)/shard_map/pair_bias/pallas_call | solution.py:103
  61.3 11.6 %pair_bias.7.refs_0_ = bf16[4,2048,2048]{2,1,0:T(8,128)(2,1)} custom-call(f32[256,8]{1,0:T(8,128)} %pad_convert_fusion.q_ref, f32[8,2048]{1,0:T(8,128)} %pad_convert_fusion.1.k_ref, bf16[32,128]{1,0:T(8,128)(2,1)} %fusion.48.w_ref, bf16[4,2048,2048]{2,1,0:T(8,128)(2,1)} %pair_bias.6.refs_0_), custom_call_target="tpu_custom_call", output_to_operand_aliasing={{}: (3, {})} | custom-call | flops 2624999936 | bytes 7340032 | tf_op jit(solution)/shard_map/pair_bias/pallas_call | solution.py:103
  74.2 1.8 collective-permute-start.16
  76.0 1.8 constant_dynamic-slice_fusion.15
  78.0 7.5 %collective-permute-start.15 = (bf16[192,768]{1,0:T(8,128)(2,1)S(1)}, bf16[192,768]{1,0:T(8,128)(2,1)}, u32[]{:S(2)}, u32[]{:S(2)}) collective-permute-start(bf16[192,768]{1,0:T(8,128)(2,1)S(1)} %collective-permute-done.14.refs_1_), channel_id=1, source_target_pairs={{0,1},{1,0},{2,3},{3,2},{4,5},{5,4},{6,7},{7,6},{8,9},{9,8},{10,11... | collective-permute-start | bytes 884744 | tf_op jit(solution)/shard_map/ppermute | solution.py:473
  89.5 11.5 %pair_bias.8.refs_0_ = bf16[4,2048,2048]{2,1,0:T(8,128)(2,1)} custom-call(f32[256,8]{1,0:T(8,128)} %pad_convert_fusion.q_ref, f32[8,2048]{1,0:T(8,128)} %pad_convert_fusion.1.k_ref, bf16[32,128]{1,0:T(8,128)(2,1)} %fusion.48.w_ref, bf16[4,2048,2048]{2,1,0:T(8,128)(2,1)} %pair_bias.7.refs_0_), custom_call_target="tpu_custom_call", output_to_operand_aliasing={{}: (3, {})} | custom-call | flops 2624999936 | bytes 7340032 | tf_op jit(solution)/shard_map/pair_bias/pallas_call | solution.py:103
  102.2 4.3 place_shards.5
  111.8 11.6 %pair_bias.9.bias_ref = bf16[4,2048,2048]{2,1,0:T(8,128)(2,1)} custom-call(f32[256,8]{1,0:T(8,128)} %pad_convert_fusion.q_ref, f32[8,2048]{1,0:T(8,128)} %pad_convert_fusion.1.k_ref, bf16[32,128]{1,0:T(8,128)(2,1)} %fusion.48.w_ref, bf16[4,2048,2048]{2,1,0:T(8,128)(2,1)} %pair_bias.8.refs_0_), custom_call_target="tpu_custom_call", output_to_operand_aliasing={{}: (3, {})} | custom-call | flops 2624999936 | bytes 7340032 | tf_op jit(solution)/shard_map/pair_bias/pallas_call | solution.py:103
  124.2 5.0 place_shards.6.w_ref
  135.1 15.3 %project.1 = (bf16[1536,2048]{1,0:T(8,128)(2,1)}, bf16[2048,1024]{1,0:T(8,128)(2,1)}, bf16[2048,1024]{1,0:T(8,128)(2,1)}) custom-call(bf16[2048,768]{1,0:T(8,128)(2,1)} %constant_dynamic-update-slice_fusion.x_ref, bf16[768,1536]{1,0:T(8,128)(2,1)} %place_shards.6.w_ref), custom_call_target="tpu_custom_call" | custom-call | flops 3000000000 | bytes 22020096 | tf_op jit(solution)/shard_map/project/pallas_call | solution.py:140
  150.4 39.7 %attend.1 = (bf16[4,2048,2048]{2,1,0:T(8,128)(2,1)}, f32[4,256,256]{2,1,0:T(8,128)}, f32[4,256,256]{2,1,0:T(8,128)}) custom-call(bf16[4,256,256]{2,1,0:T(8,128)(2,1)} %pad_bitcast_fusion.q_ref, bf16[1536,2048]{1,0:T(8,128)(2,1)} %get-tuple-element.215.kt_ref.vt_ref, bf16[2048,1024]{1,0:T(8,128)(2,1)} %get-tuple-element.216.v_ref, ...), custom_call_target="tpu_custom_call", output_to_operand_aliasing={{0}: (3, {})} | custom-call | flops 11249999872 | bytes 67108864 | tf_op jit(solution)/shard_map/attend/pallas_call | solution.py:208
  198.9 4.4 place_shards.7
  203.4 2.1 fusion.80
  206.8 6.4 %place_shards.8 = bf16[768,3072]{1,0:T(8,128)(2,1)} custom-call(s32[2]{0:T(128)} %pad_add_fusion.s_ref, bf16[384,3072]{1,0:T(8,128)(2,1)} %refs_0_.1, bf16[192,3072]{1,0:T(8,128)(2,1)} %collective-permute-done.21.refs_1_, bf16[192,3072]{1,0:T(8,128)(2,1)} %collective-permute-done.24.refs_2_), custom_call_target="tpu_custom_call" | custom-call | flops 750000000 | bytes 9437184 | tf_op jit(solution)/shard_map/place_shards/pallas_call | solution.py:393
  213.2 5.5 fusion.81
  218.7 6.6 %place_shards.9 = bf16[3072,768]{1,0:T(8,128)(2,1)} custom-call(s32[2]{0:T(128)} %pad_add_fusion.s_ref, bf16[1536,768]{1,0:T(8,128)(2,1)} %refs_0_.2, bf16[768,768]{1,0:T(8,128)(2,1)} %copy-done.29, bf16[768,768]{1,0:T(8,128)(2,1)} %collective-permute-done.25.refs_2_), custom_call_target="tpu_custom_call" | custom-call | flops 750000000 | bytes 9437184 | tf_op jit(solution)/shard_map/place_shards/pallas_call | solution.py:393
  225.3 10.6 %add_convert_fusion.1 = (bf16[256,3072]{1,0:T(8,128)(2,1)S(1)}, f32[256,3072]{1,0:T(8,128)S(1)}) fusion(f32[256,3072]{1,0:T(8,128)} %fusion.81, bf16[256,768]{1,0:T(8,128)(2,1)S(1)} %get-tuple-element.491, bf16[3072,768]{1,0:T(8,128)(2,1)} %place_shards.9), kind=kOutput, calls=%fused_computation.16 | convolution fusion | flops 1264582656 | bytes 12976128 | tf_op jit(solution)/shard_map/dot_general | solution.py:482
  247.3 2.8 convolution_convert_fusion.2
  252.9 3.7 convolution_convert_fusion
  259.9 3.5 fusion.14
  263.5 16.8 %attend_back.4 = (bf16[4,2048,2048]{2,1,0:T(8,128)(2,1)}, f32[1,256,256]{2,1,0:T(8,128)}, bf16[192,2048]{1,0:T(8,128)(2,1)}, bf16[192,2048]{1,0:T(8,128)(2,1)}) custom-call(bf16[4,256,256]{2,1,0:T(8,128)(2,1)} %pad_bitcast_fusion.q_ref, bf16[4,256,256]{2,1,0:T(8,128)(2,1)} %fusion.15.do_ref, ...), custom_call_target="tpu_custom_call", output_to_operand_aliasing={{0}: (5, {})} | custom-call | flops 3500000000 | bytes 16777216 | tf_op jit(solution)/shard_map/attend_back/pallas_call | solution.py:281
  280.3 16.5 %attend_back.5 = (bf16[4,2048,2048]{2,1,0:T(8,128)(2,1)}, f32[1,256,256]{2,1,0:T(8,128)}, bf16[192,2048]{1,0:T(8,128)(2,1)}, bf16[192,2048]{1,0:T(8,128)(2,1)}) custom-call(bf16[4,256,256]{2,1,0:T(8,128)(2,1)} %pad_bitcast_fusion.q_ref, bf16[4,256,256]{2,1,0:T(8,128)(2,1)} %fusion.15.do_ref, ...), custom_call_target="tpu_custom_call", output_to_operand_aliasing={{0}: (5, {})} | custom-call | flops 3500000000 | bytes 16777216 | tf_op jit(solution)/shard_map/attend_back/pallas_call | solution.py:281
  303.1 16.5 %attend_back.6 = (bf16[4,2048,2048]{2,1,0:T(8,128)(2,1)}, f32[1,256,256]{2,1,0:T(8,128)}, bf16[192,2048]{1,0:T(8,128)(2,1)}, bf16[192,2048]{1,0:T(8,128)(2,1)}) custom-call(bf16[4,256,256]{2,1,0:T(8,128)(2,1)} %pad_bitcast_fusion.q_ref, bf16[4,256,256]{2,1,0:T(8,128)(2,1)} %fusion.15.do_ref, ...), custom_call_target="tpu_custom_call", output_to_operand_aliasing={{0}: (5, {})} | custom-call | flops 3500000000 | bytes 16777216 | tf_op jit(solution)/shard_map/attend_back/pallas_call | solution.py:281
  319.6 2.1 add_convert_fusion.3
  321.7 3.6 all-to-all-start
  326.8 16.5 %attend_back.7 = (bf16[4,2048,2048]{2,1,0:T(8,128)(2,1)}, f32[1,256,256]{2,1,0:T(8,128)}, bf16[192,2048]{1,0:T(8,128)(2,1)}, bf16[192,2048]{1,0:T(8,128)(2,1)}) custom-call(bf16[4,256,256]{2,1,0:T(8,128)(2,1)} %pad_bitcast_fusion.q_ref, bf16[4,256,256]{2,1,0:T(8,128)(2,1)} %fusion.15.do_ref, ...), custom_call_target="tpu_custom_call", output_to_operand_aliasing={{0}: (5, {})} | custom-call | flops 3500000000 | bytes 16777216 | tf_op jit(solution)/shard_map/attend_back/pallas_call | solution.py:281
  343.3 2.2 add_convert_fusion.2
  345.5 5.0 all-to-all-start.1
  359.7 5.3 convolution_convert_fusion.1
  365.0 2.2 fusion.9
  368.7 9.1 %convolution_convert_fusion.3 = bf16[2048,768]{1,0:T(8,128)(2,1)} fusion(bf16[1536,2048]{1,0:T(8,128)(2,1)} %copy-done.60, bf16[768,1536]{1,0:T(8,128)(2,1)} %place_shards.6.w_ref), kind=kOutput, calls=%fused_computation.11 | convolution fusion | flops 4833411072 | bytes 11796480 | tf_op jit(solution)/shard_map/dot_general | solution.py:482
  378.7 5.0 all-to-all-start.2
  383.7 2.8 slice_bitcast_fusion
  390.6 13.0 %table_grad.4 = f32[256,64]{1,0:T(8,128)} custom-call(f32[256,8]{1,0:T(8,128)} %pad_convert_fusion.q_ref, f32[8,2048]{1,0:T(8,128)} %pad_convert_fusion.1.k_ref, bf16[4,2048,2048]{2,1,0:T(8,128)(2,1)} %get-tuple-element.317.ds_ref), custom_call_target="tpu_custom_call" | custom-call | flops 3200000000 | bytes 8388608 | tf_op jit(solution)/shard_map/table_grad/pallas_call | solution.py:342
  403.6 2.1 collective-permute-done.41
  407.9 4.2 all-to-all-start.3
  414.5 1.9 add_convert_fusion
  422.3 2.1 collective-permute-start.43
  425.6 13.0 %table_grad.5 = f32[256,64]{1,0:T(8,128)} custom-call(f32[256,8]{1,0:T(8,128)} %pad_convert_fusion.q_ref, f32[8,2048]{1,0:T(8,128)} %pad_convert_fusion.1.k_ref, bf16[4,2048,2048]{2,1,0:T(8,128)(2,1)} %get-tuple-element.317.ds_ref), custom_call_target="tpu_custom_call" | custom-call | flops 3200000000 | bytes 8388608 | tf_op jit(solution)/shard_map/table_grad/pallas_call | solution.py:342
  438.6 3.4 collective-permute-start.26
  447.0 4.5 collective-permute-start.49
  451.8 1.9 collective-permute-start.47
  455.3 13.0 %table_grad.6 = f32[256,64]{1,0:T(8,128)} custom-call(f32[256,8]{1,0:T(8,128)} %pad_convert_fusion.q_ref, f32[8,2048]{1,0:T(8,128)} %pad_convert_fusion.1.k_ref, bf16[4,2048,2048]{2,1,0:T(8,128)(2,1)} %get-tuple-element.317.ds_ref), custom_call_target="tpu_custom_call" | custom-call | flops 3200000000 | bytes 8388608 | tf_op jit(solution)/shard_map/table_grad/pallas_call | solution.py:342
  468.3 2.0 convert_add_fusion.7
  472.3 2.7 fusion.75
  478.5 2.1 add_convert_fusion.4
  480.7 4.4 all-to-all-start.4
  485.1 2.1 fusion.16
  488.4 2.4 collective-permute-start.51
  493.6 13.0 %table_grad.7 = f32[256,64]{1,0:T(8,128)} custom-call(f32[256,8]{1,0:T(8,128)} %pad_convert_fusion.q_ref, f32[8,2048]{1,0:T(8,128)} %pad_convert_fusion.1.k_ref, bf16[4,2048,2048]{2,1,0:T(8,128)(2,1)} %get-tuple-element.317.ds_ref), custom_call_target="tpu_custom_call" | custom-call | flops 3200000000 | bytes 8388608 | tf_op jit(solution)/shard_map/table_grad/pallas_call | solution.py:342
  511.4 4.8 all-to-all-start.5
  519.3 1.9 collective-permute-done.54
  524.8 3.1 collective-permute-start.58
  529.7 3.3 collective-permute-start.62
  533.1 3.8 collective-permute-done.57
  541.5 9.0 %collective-permute-done.64.refs_1_ = bf16[4,48,1152]{2,1,0:T(8,128)(2,1)S(1)} collective-permute-done((bf16[4,48,1152]{2,1,0:T(8,128)(2,1)S(1)}, bf16[4,48,1152]{2,1,0:T(8,128)(2,1)S(1)}, u32[]{:S(2)}, u32[]{:S(2)}) %collective-permute-start.64) | collective-permute-done | bytes 442400 | tf_op jit(solution)/shard_map/ppermute | solution.py:473
  553.8 4.7 assemble.3
  558.5 5.5 assemble.4
  564.9 4.1 assemble.5
  (526 shorter events, 150.6 us)
Async XLA Ops:
  2.2 5.7 collective-permute-start
  2.3 15.8 %collective-permute-start.6 = (s32[2,3]{1,0:T(2,128)}, s32[2,3]{1,0:T(2,128)S(1)}, u32[]{:S(2)}, u32[]{:S(2)}) collective-permute-start(s32[2,3]{1,0:T(2,128)} %param.26), channel_id=1, source_target_pairs={{0,16},{16,0},{1,17},{17,1},{2,18},{18,2},{3,19},{19,3},{4,20},{20... | collective-permute-start | bytes 80 | tf_op jit(solution)/shard_map/ppermute | solution.py:473
  5.0 13.1 %collective-permute-start.4 = (bf16[64,32]{0,1:T(8,128)(2,1)}, bf16[64,32]{0,1:T(8,128)(2,1)S(1)}, u32[]{:S(2)}, u32[]{:S(2)}) collective-permute-start(bf16[64,32]{0,1:T(8,128)(2,1)} %param.31), channel_id=1, source_target_pairs={{0,16},{16,0},{1,17},{17,1},{2,18},{18,2},{3,19},{19,3},{4,20},{20... | collective-permute-start | bytes 12296 | tf_op jit(solution)/shard_map/ppermute | solution.py:473
  6.1 12.6 %collective-permute-start.5 = (bf16[128,768]{1,0:T(8,128)(2,1)S(1)}, bf16[128,768]{1,0:T(8,128)(2,1)S(1)}, u32[]{:S(2)}, u32[]{:S(2)}) collective-permute-start(bf16[128,768]{1,0:T(8,128)(2,1)S(1)} %get-tuple-element.469), channel_id=1, source_target_pairs={{0,1},{1,0},{2,3},{3,2},{4,5},{5,4},{6,7},{7,6},{8,9},{9,8},{10,11... | collective-permute-start | bytes 589832 | tf_op jit(solution)/shard_map/ppermute | solution.py:473
  7.9 4.8 collective-permute-start.1
  22.2 15.4 %collective-permute-start.8 = (bf16[7,384]{1,0:T(8,128)(2,1)S(1)}, bf16[7,384]{1,0:T(8,128)(2,1)S(1)}, u32[]{:S(2)}, u32[]{:S(2)}) collective-permute-start(bf16[7,384]{1,0:T(8,128)(2,1)S(1)} %concatenate.100), channel_id=1, source_target_pairs={{0,16},{16,0},{1,17},{17,1},{2,18},{18,2},{3,19},{19,3},{4,20},{20... | collective-permute-start | bytes 16136 | tf_op jit(solution)/shard_map/ppermute | solution.py:473
  41.9 15.0 %collective-permute-start.10 = (bf16[256,768]{1,0:T(8,128)(2,1)S(1)}, bf16[256,768]{1,0:T(8,128)(2,1)S(1)}, u32[]{:S(2)}, u32[]{:S(2)}) collective-permute-start(bf16[256,768]{1,0:T(8,128)(2,1)S(1)} %add_convert_fusion.6), channel_id=1, source_target_pairs={{0,2},{2,0},{1,3},{3,1},{4,6},{6,4},{5,7},{7,5},{8,10},{10,8},{9,1... | collective-permute-start | bytes 1179656 | tf_op jit(solution)/shard_map/ppermute | solution.py:473
  43.2 13.7 %collective-permute-start.9 = (bf16[256,768]{1,0:T(8,128)(2,1)S(1)}, bf16[256,768]{1,0:T(8,128)(2,1)}, u32[]{:S(2)}, u32[]{:S(2)}) collective-permute-start(bf16[256,768]{1,0:T(8,128)(2,1)S(1)} %add_convert_fusion.6), channel_id=1, source_target_pairs={{0,4},{4,8},{8,12},{12,0},{1,5},{5,9},{9,13},{13,1},{2,6},{6,10},{... | collective-permute-start | bytes 1179656 | tf_op jit(solution)/shard_map/ppermute | solution.py:473
  44.4 31.6 %collective-permute-start.13 = (bf16[192,1536]{1,0:T(8,128)(2,1)}, bf16[192,1536]{1,0:T(8,128)(2,1)}, u32[]{:S(2)}, u32[]{:S(2)}) collective-permute-start(bf16[192,1536]{1,0:T(8,128)(2,1)} %constant_dynamic-slice_fusion.17), channel_id=1, source_target_pairs={{0,16},{16,0},{1,17},{17,1},{2,18},{18,2},{3,19},{19,3},{4,20},{20... | collective-permute-start | bytes 1769480 | tf_op jit(solution)/shard_map/ppermute | solution.py:473
  57.7 15.3 %collective-permute-start.12 = (bf16[256,768]{1,0:T(8,128)(2,1)}, bf16[256,768]{1,0:T(8,128)(2,1)S(1)}, u32[]{:S(2)}, u32[]{:S(2)}) collective-permute-start(bf16[256,768]{1,0:T(8,128)(2,1)} %collective-permute-done.9), channel_id=1, source_target_pairs={{0,2},{2,0},{1,3},{3,1},{4,6},{6,4},{5,7},{7,5},{8,10},{10,8},{9,1... | collective-permute-start | bytes 1179656 | tf_op jit(solution)/shard_map/ppermute | solution.py:473
  57.9 15.0 %collective-permute-start.11 = (bf16[256,768]{1,0:T(8,128)(2,1)}, bf16[256,768]{1,0:T(8,128)(2,1)}, u32[]{:S(2)}, u32[]{:S(2)}) collective-permute-start(bf16[256,768]{1,0:T(8,128)(2,1)} %collective-permute-done.9), channel_id=1, source_target_pairs={{0,4},{4,8},{8,12},{12,0},{1,5},{5,9},{9,13},{13,1},{2,6},{6,10},{... | collective-permute-start | bytes 1179656 | tf_op jit(solution)/shard_map/ppermute | solution.py:473
  59.3 16.7 %collective-permute-start.14 = (bf16[192,768]{1,0:T(8,128)(2,1)}, bf16[192,768]{1,0:T(8,128)(2,1)S(1)}, u32[]{:S(2)}, u32[]{:S(2)}) collective-permute-start(bf16[192,768]{1,0:T(8,128)(2,1)} %constant_dynamic-slice_fusion.16), channel_id=1, source_target_pairs={{0,16},{16,0},{1,17},{17,1},{2,18},{18,2},{3,19},{19,3},{4,20},{20... | collective-permute-start | bytes 884744 | tf_op jit(solution)/shard_map/ppermute | solution.py:473
  73.0 36.6 %collective-permute-start.17 = (bf16[256,768]{1,0:T(8,128)(2,1)}, bf16[256,768]{1,0:T(8,128)(2,1)}, u32[]{:S(2)}, u32[]{:S(2)}) collective-permute-start(bf16[256,768]{1,0:T(8,128)(2,1)} %collective-permute-done.11), channel_id=1, source_target_pairs={{0,2},{2,0},{1,3},{3,1},{4,6},{6,4},{5,7},{7,5},{8,10},{10,8},{9,1... | collective-permute-start | bytes 1179656 | tf_op jit(solution)/shard_map/ppermute | solution.py:473
  74.2 35.6 %collective-permute-start.16 = (bf16[256,768]{1,0:T(8,128)(2,1)}, bf16[256,768]{1,0:T(8,128)(2,1)}, u32[]{:S(2)}, u32[]{:S(2)}) collective-permute-start(bf16[256,768]{1,0:T(8,128)(2,1)} %collective-permute-done.11), channel_id=1, source_target_pairs={{0,4},{4,8},{8,12},{12,0},{1,5},{5,9},{9,13},{13,1},{2,6},{6,10},{... | collective-permute-start | bytes 1179656 | tf_op jit(solution)/shard_map/ppermute | solution.py:473
  77.8 114.6 %collective-permute-start.20 = (bf16[192,768]{1,0:T(8,128)(2,1)}, bf16[192,768]{1,0:T(8,128)(2,1)}, u32[]{:S(2)}, u32[]{:S(2)}) collective-permute-start(bf16[192,768]{1,0:T(8,128)(2,1)} %constant_dynamic-slice_fusion.15), channel_id=1, source_target_pairs={{0,16},{16,0},{1,17},{17,1},{2,18},{18,2},{3,19},{19,3},{4,20},{20... | collective-permute-start | bytes 884744 | tf_op jit(solution)/shard_map/ppermute | solution.py:473
  78.0 22.9 %collective-permute-start.15 = (bf16[192,768]{1,0:T(8,128)(2,1)S(1)}, bf16[192,768]{1,0:T(8,128)(2,1)}, u32[]{:S(2)}, u32[]{:S(2)}) collective-permute-start(bf16[192,768]{1,0:T(8,128)(2,1)S(1)} %collective-permute-done.14.refs_1_), channel_id=1, source_target_pairs={{0,1},{1,0},{2,3},{3,2},{4,5},{5,4},{6,7},{7,6},{8,9},{9,8},{10,11... | collective-permute-start | bytes 884744 | tf_op jit(solution)/shard_map/ppermute | solution.py:473
  85.5 37.9 %collective-permute-start.19 = (bf16[192,1536]{1,0:T(8,128)(2,1)}, bf16[192,1536]{1,0:T(8,128)(2,1)S(1)}, u32[]{:S(2)}, u32[]{:S(2)}) collective-permute-start(bf16[192,1536]{1,0:T(8,128)(2,1)} %collective-permute-done.13.refs_1_), channel_id=1, source_target_pairs={{0,1},{1,0},{2,3},{3,2},{4,5},{5,4},{6,7},{7,6},{8,9},{9,8},{10,11... | collective-permute-start | bytes 1769480 | tf_op jit(solution)/shard_map/ppermute | solution.py:473
  101.0 91.4 %collective-permute-start.22 = (bf16[768,768]{1,0:T(8,128)(2,1)}, bf16[768,768]{1,0:T(8,128)(2,1)S(1)}, u32[]{:S(2)}, u32[]{:S(2)}) collective-permute-start(bf16[768,768]{1,0:T(8,128)(2,1)} %constant_dynamic-slice_fusion.13), channel_id=1, source_target_pairs={{0,16},{16,0},{1,17},{17,1},{2,18},{18,2},{3,19},{19,3},{4,20},{20... | collective-permute-start | bytes 3538952 | tf_op jit(solution)/shard_map/ppermute | solution.py:473
  109.6 82.8 %collective-permute-start.21 = (bf16[192,3072]{1,0:T(8,128)(2,1)}, bf16[192,3072]{1,0:T(8,128)(2,1)}, u32[]{:S(2)}, u32[]{:S(2)}) collective-permute-start(bf16[192,3072]{1,0:T(8,128)(2,1)} %constant_dynamic-slice_fusion.14), channel_id=1, source_target_pairs={{0,16},{16,0},{1,17},{17,1},{2,18},{18,2},{3,19},{19,3},{4,20},{20... | collective-permute-start | bytes 3538952 | tf_op jit(solution)/shard_map/ppermute | solution.py:473
  109.8 19.4 %collective-permute-start.18 = (bf16[256,768]{1,0:T(8,128)(2,1)}, bf16[256,768]{1,0:T(8,128)(2,1)S(1)}, u32[]{:S(2)}, u32[]{:S(2)}) collective-permute-start(bf16[256,768]{1,0:T(8,128)(2,1)} %collective-permute-done.16), channel_id=1, source_target_pairs={{0,2},{2,0},{1,3},{3,1},{4,6},{6,4},{5,7},{7,5},{8,10},{10,8},{9,1... | collective-permute-start | bytes 1179656 | tf_op jit(solution)/shard_map/ppermute | solution.py:473
  195.6 47.7 %collective-permute-start.34 = (bf16[256,768]{0,1:T(8,128)(2,1)}, bf16[256,768]{0,1:T(8,128)(2,1)}, u32[]{:S(2)}, u32[]{:S(2)}) collective-permute-start(bf16[256,768]{0,1:T(8,128)(2,1)} %bitcast.23), channel_id=1, source_target_pairs={{0,1},{1,0},{2,3},{3,2},{4,5},{5,4},{6,7},{7,6},{8,9},{9,8},{10,11... | collective-permute-start | bytes 1179656 | tf_op jit(solution)/shard_map/ppermute | solution.py:473
  195.7 11.0 %collective-permute-start.24 = (bf16[192,3072]{1,0:T(8,128)(2,1)}, bf16[192,3072]{1,0:T(8,128)(2,1)}, u32[]{:S(2)}, u32[]{:S(2)}) collective-permute-start(bf16[192,3072]{1,0:T(8,128)(2,1)} %collective-permute-done.21.refs_1_), channel_id=1, source_target_pairs={{0,1},{1,0},{2,3},{3,2},{4,5},{5,4},{6,7},{7,6},{8,9},{9,8},{10,11... | collective-permute-start | bytes 3538952 | tf_op jit(solution)/shard_map/ppermute | solution.py:473
  196.2 22.5 %collective-permute-start.25 = (bf16[768,768]{1,0:T(8,128)(2,1)}, bf16[768,768]{1,0:T(8,128)(2,1)}, u32[]{:S(2)}, u32[]{:S(2)}) collective-permute-start(bf16[768,768]{1,0:T(8,128)(2,1)} %copy-done.29), channel_id=1, source_target_pairs={{0,1},{1,0},{2,3},{3,2},{4,5},{5,4},{6,7},{7,6},{8,9},{9,8},{10,11... | collective-permute-start | bytes 3538952 | tf_op jit(solution)/shard_map/ppermute | solution.py:473
  197.8 47.0 %collective-permute-start.31 = (bf16[256,384]{1,0:T(8,128)(2,1)}, bf16[256,384]{1,0:T(8,128)(2,1)}, u32[]{:S(2)}, u32[]{:S(2)}) collective-permute-start(bf16[256,384]{1,0:T(8,128)(2,1)} %get-tuple-element.465), channel_id=1, source_target_pairs={{0,1},{1,0},{2,3},{3,2},{4,5},{5,4},{6,7},{7,6},{8,9},{9,8},{10,11... | collective-permute-start | bytes 589832 | tf_op jit(solution)/shard_map/ppermute | solution.py:473
  206.6 38.2 %collective-permute-start.32 = (bf16[256,768]{1,0:T(8,128)(2,1)}, bf16[256,768]{1,0:T(8,128)(2,1)}, u32[]{:S(2)}, u32[]{:S(2)}) collective-permute-start(bf16[256,768]{1,0:T(8,128)(2,1)} %add_convert_fusion.5), channel_id=1, source_target_pairs={{0,1},{1,0},{2,3},{3,2},{4,5},{5,4},{6,7},{7,6},{8,9},{9,8},{10,11... | collective-permute-start | bytes 1179656 | tf_op jit(solution)/shard_map/ppermute | solution.py:473
  240.7 4.8 collective-permute-start.33
  241.1 4.5 collective-permute-start.30
  251.7 45.2 %collective-permute-start.37 = (bf16[2,4,48,1920]{3,2,1,0:T(8,128)(2,1)}, bf16[2,4,48,1920]{3,2,1,0:T(8,128)(2,1)}, u32[]{:S(2)}, u32[]{:S(2)}) collective-permute-start(bf16[2,4,48,1920]{3,2,1,0:T(8,128)(2,1)} %get-tuple-element.439), channel_id=1, source_target_pairs={{0,2},{2,0},{1,3},{3,1},{4,6},{6,4},{5,7},{7,5},{8,10},{10,8},{9,1... | collective-permute-start | bytes 4423688 | tf_op jit(solution)/shard_map/ppermute | solution.py:473
  257.9 38.9 %collective-permute-start.36 = (bf16[2,4,192,384]{3,2,1,0:T(8,128)(2,1)}, bf16[2,4,192,384]{3,2,1,0:T(8,128)(2,1)}, u32[]{:S(2)}, u32[]{:S(2)}) collective-permute-start(bf16[2,4,192,384]{3,2,1,0:T(8,128)(2,1)} %get-tuple-element.441), channel_id=1, source_target_pairs={{0,16},{16,0},{1,17},{17,1},{2,18},{18,2},{3,19},{19,3},{4,20},{20... | collective-permute-start | bytes 3538952 | tf_op jit(solution)/shard_map/ppermute | solution.py:473
  299.5 20.1 %collective-permute-start.39 = (bf16[4,48,1920]{2,1,0:T(8,128)(2,1)}, bf16[4,48,1920]{2,1,0:T(8,128)(2,1)}, u32[]{:S(2)}, u32[]{:S(2)}) collective-permute-start(bf16[4,48,1920]{2,1,0:T(8,128)(2,1)} %fusion.25), channel_id=1, source_target_pairs={{0,16},{16,0},{1,17},{17,1},{2,18},{18,2},{3,19},{19,3},{4,20},{20... | collective-permute-start | bytes 2211848 | tf_op jit(solution)/shard_map/ppermute | solution.py:473
  302.2 17.4 %collective-permute-start.38 = (bf16[4,192,384]{2,1,0:T(8,128)(2,1)}, bf16[4,192,384]{2,1,0:T(8,128)(2,1)}, u32[]{:S(2)}, u32[]{:S(2)}) collective-permute-start(bf16[4,192,384]{2,1,0:T(8,128)(2,1)} %fusion.28), channel_id=1, source_target_pairs={{0,2},{2,0},{1,3},{3,1},{4,6},{6,4},{5,7},{7,5},{8,10},{10,8},{9,1... | collective-permute-start | bytes 1769480 | tf_op jit(solution)/shard_map/ppermute | solution.py:473
  321.7 23.8 %all-to-all-start = ((bf16[4,192,384]{2,1,0:T(8,128)(2,1)}), bf16[4,192,384]{2,1,0:T(8,128)(2,1)S(1)}, u32[]{:S(2)}, u32[]{:S(2)}) async-start(bf16[4,192,384]{2,1,0:T(8,128)(2,1)} %add_convert_fusion.3), calls=%async_computation | async-start | bytes 1179648 | tf_op jit(solution)/shard_map/all_to_all | solution.py:540
  325.5 64.2 %collective-permute-start.27 = (f32[3,128]{1,0:T(4,128)S(1)}, f32[3,128]{1,0:T(4,128)S(1)}, u32[]{:S(2)}, u32[]{:S(2)}) collective-permute-start(f32[3,128]{1,0:T(4,128)S(1)} %slice.212), channel_id=1, source_target_pairs={{0,1},{1,0},{2,3},{3,2},{4,5},{5,4},{6,7},{7,6},{8,9},{9,8},{10,11... | collective-permute-start | bytes 4616 | tf_op jit(solution)/shard_map/ppermute | solution.py:473
  345.5 32.2 %all-to-all-start.1 = ((bf16[4,48,1920]{2,1,0:T(8,128)(2,1)}), bf16[4,48,1920]{2,1,0:T(8,128)(2,1)}, u32[]{:S(2)}, u32[]{:S(2)}) async-start(bf16[4,48,1920]{2,1,0:T(8,128)(2,1)} %add_convert_fusion.2), calls=%async_computation.1 | async-start | bytes 1474560 | tf_op jit(solution)/shard_map/all_to_all | solution.py:540
  367.2 23.3 %collective-permute-start.40 = (bf16[768,1152]{1,0:T(8,128)(2,1)}, bf16[768,1152]{1,0:T(8,128)(2,1)}, u32[]{:S(2)}, u32[]{:S(2)}) collective-permute-start(bf16[768,1152]{1,0:T(8,128)(2,1)} %get-tuple-element.435), channel_id=1, source_target_pairs={{0,1},{1,0},{2,3},{3,2},{4,5},{5,4},{6,7},{7,6},{8,9},{9,8},{10,11... | collective-permute-start | bytes 5308424 | tf_op jit(solution)/shard_map/ppermute | solution.py:473
  378.7 27.0 %all-to-all-start.2 = ((bf16[4,192,384]{2,1,0:T(8,128)(2,1)}), bf16[4,192,384]{2,1,0:T(8,128)(2,1)}, u32[]{:S(2)}, u32[]{:S(2)}) async-start(bf16[4,192,384]{2,1,0:T(8,128)(2,1)} %broadcast_in_dim.162), calls=%async_computation.2 | async-start | bytes 1179648 | tf_op jit(solution)/shard_map/all_to_all | solution.py:557
  386.5 19.2 %collective-permute-start.41 = (bf16[4,256,384]{2,1,0:T(8,128)(2,1)}, bf16[4,256,384]{2,1,0:T(8,128)(2,1)}, u32[]{:S(2)}, u32[]{:S(2)}) collective-permute-start(bf16[4,256,384]{2,1,0:T(8,128)(2,1)} %get-tuple-element.437), channel_id=1, source_target_pairs={{0,2},{2,0},{1,3},{3,1},{4,6},{6,4},{5,7},{7,5},{8,10},{10,8},{9,1... | collective-permute-start | bytes 2359304 | tf_op jit(solution)/shard_map/ppermute | solution.py:473
  407.9 63.2 %all-to-all-start.3 = ((bf16[4,48,1920]{2,1,0:T(8,128)(2,1)}), bf16[4,48,1920]{2,1,0:T(8,128)(2,1)}, u32[]{:S(2)}, u32[]{:S(2)}) async-start(bf16[4,48,1920]{2,1,0:T(8,128)(2,1)} %broadcast_in_dim.163), calls=%async_computation.3 | async-start | bytes 1474560 | tf_op jit(solution)/shard_map/all_to_all | solution.py:557
  413.4 30.0 %collective-permute-start.45 = (bf16[4,256,384]{2,1,0:T(8,128)(2,1)}, bf16[4,256,384]{2,1,0:T(8,128)(2,1)S(1)}, u32[]{:S(2)}, u32[]{:S(2)}) collective-permute-start(bf16[4,256,384]{2,1,0:T(8,128)(2,1)} %get-tuple-element.447), channel_id=1, source_target_pairs={{0,2},{2,0},{1,3},{3,1},{4,6},{6,4},{5,7},{7,5},{8,10},{10,8},{9,1... | collective-permute-start | bytes 2359304 | tf_op jit(solution)/shard_map/ppermute | solution.py:473
  417.5 25.9 %collective-permute-start.46 = (bf16[2,4,48,1152]{3,2,1,0:T(8,128)(2,1)}, bf16[2,4,48,1152]{3,2,1,0:T(8,128)(2,1)}, u32[]{:S(2)}, u32[]{:S(2)}) collective-permute-start(bf16[2,4,48,1152]{3,2,1,0:T(8,128)(2,1)} %get-tuple-element.443), channel_id=1, source_target_pairs={{0,16},{16,0},{1,17},{17,1},{2,18},{18,2},{3,19},{19,3},{4,20},{20... | collective-permute-start | bytes 2654216 | tf_op jit(solution)/shard_map/ppermute | solution.py:473
  420.8 17.7 %collective-permute-start.44 = (bf16[256,384]{1,0:T(8,128)(2,1)}, bf16[256,384]{1,0:T(8,128)(2,1)}, u32[]{:S(2)}, u32[]{:S(2)}) collective-permute-start(bf16[256,384]{1,0:T(8,128)(2,1)} %get-tuple-element.458), channel_id=1, source_target_pairs={{0,4},{4,8},{8,12},{12,0},{1,5},{5,9},{9,13},{13,1},{2,6},{6,10},{... | collective-permute-start | bytes 589832 | tf_op jit(solution)/shard_map/ppermute | solution.py:473
  422.3 21.1 %collective-permute-start.43 = (bf16[256,384]{1,0:T(8,128)(2,1)S(1)}, bf16[256,384]{1,0:T(8,128)(2,1)}, u32[]{:S(2)}, u32[]{:S(2)}) collective-permute-start(bf16[256,384]{1,0:T(8,128)(2,1)S(1)} %get-tuple-element.459), channel_id=1, source_target_pairs={{0,8},{4,12},{8,0},{12,4},{1,9},{5,13},{9,1},{13,5},{2,10},{6,14},... | collective-permute-start | bytes 589832 | tf_op jit(solution)/shard_map/ppermute | solution.py:473
  424.4 19.0 %collective-permute-start.42 = (bf16[256,384]{1,0:T(8,128)(2,1)S(1)}, bf16[256,384]{1,0:T(8,128)(2,1)}, u32[]{:S(2)}, u32[]{:S(2)}) collective-permute-start(bf16[256,384]{1,0:T(8,128)(2,1)S(1)} %get-tuple-element.460), channel_id=1, source_target_pairs={{0,12},{4,0},{8,4},{12,8},{1,13},{5,1},{9,5},{13,9},{2,14},{6,2},{... | collective-permute-start | bytes 589832 | tf_op jit(solution)/shard_map/ppermute | solution.py:473
  438.6 77.6 %collective-permute-start.26 = (bf16[128,768]{1,0:T(8,128)(2,1)}, bf16[128,768]{1,0:T(8,128)(2,1)}, u32[]{:S(2)}, u32[]{:S(2)}) collective-permute-start(bf16[128,768]{1,0:T(8,128)(2,1)} %slice.209), channel_id=1, source_target_pairs={{0,1},{1,0},{2,3},{3,2},{4,5},{5,4},{6,7},{7,6},{8,9},{9,8},{10,11... | collective-permute-start | bytes 589832 | tf_op jit(solution)/shard_map/ppermute | solution.py:473
  445.6 25.5 %collective-permute-start.50 = (bf16[4,48,1152]{2,1,0:T(8,128)(2,1)}, bf16[4,48,1152]{2,1,0:T(8,128)(2,1)}, u32[]{:S(2)}, u32[]{:S(2)}) collective-permute-start(bf16[4,48,1152]{2,1,0:T(8,128)(2,1)} %fusion.32), channel_id=1, source_target_pairs={{0,2},{2,0},{1,3},{3,1},{4,6},{6,4},{5,7},{7,5},{8,10},{10,8},{9,1... | collective-permute-start | bytes 1327112 | tf_op jit(solution)/shard_map/ppermute | solution.py:473
  447.0 23.4 %collective-permute-start.49 = (bf16[256,384]{1,0:T(8,128)(2,1)S(1)}, bf16[256,384]{1,0:T(8,128)(2,1)S(1)}, u32[]{:S(2)}, u32[]{:S(2)}) collective-permute-start(bf16[256,384]{1,0:T(8,128)(2,1)S(1)} %get-tuple-element.455), channel_id=1, source_target_pairs={{0,4},{4,8},{8,12},{12,0},{1,5},{5,9},{9,13},{13,1},{2,6},{6,10},{... | collective-permute-start | bytes 589832 | tf_op jit(solution)/shard_map/ppermute | solution.py:473
  451.5 19.3 %collective-permute-start.48 = (bf16[256,384]{1,0:T(8,128)(2,1)S(1)}, bf16[256,384]{1,0:T(8,128)(2,1)}, u32[]{:S(2)}, u32[]{:S(2)}) collective-permute-start(bf16[256,384]{1,0:T(8,128)(2,1)S(1)} %get-tuple-element.456), channel_id=1, source_target_pairs={{0,8},{4,12},{8,0},{12,4},{1,9},{5,13},{9,1},{13,5},{2,10},{6,14},... | collective-permute-start | bytes 589832 | tf_op jit(solution)/shard_map/ppermute | solution.py:473
  451.8 19.3 %collective-permute-start.47 = (bf16[256,384]{1,0:T(8,128)(2,1)S(1)}, bf16[256,384]{1,0:T(8,128)(2,1)}, u32[]{:S(2)}, u32[]{:S(2)}) collective-permute-start(bf16[256,384]{1,0:T(8,128)(2,1)S(1)} %get-tuple-element.457), channel_id=1, source_target_pairs={{0,12},{4,0},{8,4},{12,8},{1,13},{5,1},{9,5},{13,9},{2,14},{6,2},{... | collective-permute-start | bytes 589832 | tf_op jit(solution)/shard_map/ppermute | solution.py:473
  470.4 36.2 %collective-permute-start.52 = (bf16[4,192,384]{2,1,0:T(8,128)(2,1)}, bf16[4,192,384]{2,1,0:T(8,128)(2,1)}, u32[]{:S(2)}, u32[]{:S(2)}) collective-permute-start(bf16[4,192,384]{2,1,0:T(8,128)(2,1)} %all-to-all-done.2.refs_0_), channel_id=1, source_target_pairs={{0,2},{2,0},{1,3},{3,1},{4,6},{6,4},{5,7},{7,5},{8,10},{10,8},{9,1... | collective-permute-start | bytes 1769480 | tf_op jit(solution)/shard_map/ppermute | solution.py:473
  480.7 26.0 %all-to-all-start.4 = ((bf16[4,48,1152]{2,1,0:T(8,128)(2,1)}), bf16[4,48,1152]{2,1,0:T(8,128)(2,1)}, u32[]{:S(2)}, u32[]{:S(2)}) async-start(bf16[4,48,1152]{2,1,0:T(8,128)(2,1)} %add_convert_fusion.4), calls=%async_computation.4 | async-start | bytes 884736 | tf_op jit(solution)/shard_map/all_to_all | solution.py:540
  488.4 33.3 %collective-permute-start.51 = (f32[128,768]{1,0:T(8,128)S(1)}, f32[128,768]{1,0:T(8,128)S(1)}, u32[]{:S(2)}, u32[]{:S(2)}) collective-permute-start(f32[128,768]{1,0:T(8,128)S(1)} %slice.225), channel_id=1, source_target_pairs={{0,1},{1,0},{2,3},{3,2},{4,5},{5,4},{6,7},{7,6},{8,9},{9,8},{10,11... | collective-permute-start | bytes 1179656 | tf_op jit(solution)/shard_map/ppermute | solution.py:473
  490.8 38.9 %collective-permute-start.61 = (bf16[4,48,1920]{2,1,0:T(8,128)(2,1)}, bf16[4,48,1920]{2,1,0:T(8,128)(2,1)S(1)}, u32[]{:S(2)}, u32[]{:S(2)}) collective-permute-start(bf16[4,48,1920]{2,1,0:T(8,128)(2,1)} %all-to-all-done.3.refs_0_), channel_id=1, source_target_pairs={{0,2},{2,0},{1,3},{3,1},{4,6},{6,4},{5,7},{7,5},{8,10},{10,8},{9,1... | collective-permute-start | bytes 2211848 | tf_op jit(solution)/shard_map/ppermute | solution.py:473
  509.1 8.1 %collective-permute-start.53 = (f32[25,768]{1,0:T(8,128)S(1)}, f32[25,768]{1,0:T(8,128)S(1)}, u32[]{:S(2)}, u32[]{:S(2)}) collective-permute-start(f32[25,768]{1,0:T(8,128)S(1)} %concatenate.117), channel_id=1, source_target_pairs={{0,1},{1,0},{2,3},{3,2},{4,5},{5,4},{6,7},{7,6},{8,9},{9,8},{10,11... | collective-permute-start | bytes 230408 | tf_op jit(solution)/shard_map/ppermute | solution.py:473
  511.4 27.2 %all-to-all-start.5 = ((bf16[4,48,1152]{2,1,0:T(8,128)(2,1)}), bf16[4,48,1152]{2,1,0:T(8,128)(2,1)S(1)}, u32[]{:S(2)}, u32[]{:S(2)}) async-start(bf16[4,48,1152]{2,1,0:T(8,128)(2,1)} %broadcast_in_dim.173), calls=%async_computation.5 | async-start | bytes 884736 | tf_op jit(solution)/shard_map/all_to_all | solution.py:557
  521.7 19.4 %collective-permute-start.59 = (bf16[4,192,384]{2,1,0:T(8,128)(2,1)}, bf16[4,192,384]{2,1,0:T(8,128)(2,1)S(1)}, u32[]{:S(2)}, u32[]{:S(2)}) collective-permute-start(bf16[4,192,384]{2,1,0:T(8,128)(2,1)} %all-to-all-done.2.refs_0_), channel_id=1, source_target_pairs={{0,1},{1,0},{2,3},{3,2},{4,5},{5,4},{6,7},{7,6},{8,9},{9,8},{10,11... | collective-permute-start | bytes 1769480 | tf_op jit(solution)/shard_map/ppermute | solution.py:473
  524.8 8.2 %collective-permute-start.58 = (f32[25,768]{1,0:T(8,128)S(1)}, f32[25,768]{1,0:T(8,128)S(1)}, u32[]{:S(2)}, u32[]{:S(2)}) collective-permute-start(f32[25,768]{1,0:T(8,128)S(1)} %add.327), channel_id=1, source_target_pairs={{0,12},{4,0},{8,4},{12,8},{1,13},{5,1},{9,5},{13,9},{2,14},{6,2},{... | collective-permute-start | bytes 230408 | tf_op jit(solution)/shard_map/ppermute | solution.py:473
  527.9 9.0 %collective-permute-start.57 = (f32[25,768]{1,0:T(8,128)S(1)}, f32[25,768]{1,0:T(8,128)S(1)}, u32[]{:S(2)}, u32[]{:S(2)}) collective-permute-start(f32[25,768]{1,0:T(8,128)S(1)} %add.327), channel_id=1, source_target_pairs={{0,8},{4,12},{8,0},{12,4},{1,9},{5,13},{9,1},{13,5},{2,10},{6,14},... | collective-permute-start | bytes 230408 | tf_op jit(solution)/shard_map/ppermute | solution.py:473
  527.9 10.6 %collective-permute-start.56 = (f32[25,768]{1,0:T(8,128)S(1)}, f32[25,768]{1,0:T(8,128)S(1)}, u32[]{:S(2)}, u32[]{:S(2)}) collective-permute-start(f32[25,768]{1,0:T(8,128)S(1)} %add.327), channel_id=1, source_target_pairs={{0,4},{4,8},{8,12},{12,0},{1,5},{5,9},{9,13},{13,1},{2,6},{6,10},{... | collective-permute-start | bytes 230408 | tf_op jit(solution)/shard_map/ppermute | solution.py:473
  529.7 28.8 %collective-permute-start.62 = (bf16[4,48,1920]{2,1,0:T(8,128)(2,1)}, bf16[4,48,1920]{2,1,0:T(8,128)(2,1)}, u32[]{:S(2)}, u32[]{:S(2)}) collective-permute-start(bf16[4,48,1920]{2,1,0:T(8,128)(2,1)} %all-to-all-done.3.refs_0_), channel_id=1, source_target_pairs={{0,1},{1,0},{2,3},{3,2},{4,5},{5,4},{6,7},{7,6},{8,9},{9,8},{10,11... | collective-permute-start | bytes 2211848 | tf_op jit(solution)/shard_map/ppermute | solution.py:473
  533.0 20.0 %collective-permute-start.60 = (bf16[4,192,384]{2,1,0:T(8,128)(2,1)}, bf16[4,192,384]{2,1,0:T(8,128)(2,1)S(1)}, u32[]{:S(2)}, u32[]{:S(2)}) collective-permute-start(bf16[4,192,384]{2,1,0:T(8,128)(2,1)} %collective-permute-done.52.refs_1_), channel_id=1, source_target_pairs={{0,1},{1,0},{2,3},{3,2},{4,5},{5,4},{6,7},{7,6},{8,9},{9,8},{10,11... | collective-permute-start | bytes 1769480 | tf_op jit(solution)/shard_map/ppermute | solution.py:473
  537.0 21.6 %collective-permute-start.63 = (bf16[4,48,1920]{2,1,0:T(8,128)(2,1)S(1)}, bf16[4,48,1920]{2,1,0:T(8,128)(2,1)}, u32[]{:S(2)}, u32[]{:S(2)}) collective-permute-start(bf16[4,48,1920]{2,1,0:T(8,128)(2,1)S(1)} %collective-permute-done.61.refs_1_), channel_id=1, source_target_pairs={{0,1},{1,0},{2,3},{3,2},{4,5},{5,4},{6,7},{7,6},{8,9},{9,8},{10,11... | collective-permute-start | bytes 2211848 | tf_op jit(solution)/shard_map/ppermute | solution.py:473
  538.6 11.9 %collective-permute-start.64 = (bf16[4,48,1152]{2,1,0:T(8,128)(2,1)S(1)}, bf16[4,48,1152]{2,1,0:T(8,128)(2,1)S(1)}, u32[]{:S(2)}, u32[]{:S(2)}) collective-permute-start(bf16[4,48,1152]{2,1,0:T(8,128)(2,1)S(1)} %all-to-all-done.5.refs_0_), channel_id=1, source_target_pairs={{0,2},{2,0},{1,3},{3,1},{4,6},{6,4},{5,7},{7,5},{8,10},{10,8},{9,1... | collective-permute-start | bytes 1327112 | tf_op jit(solution)/shard_map/ppermute | solution.py:473
  541.2 22.8 %collective-permute-start.65 = (bf16[4,48,1152]{2,1,0:T(8,128)(2,1)S(1)}, bf16[4,48,1152]{2,1,0:T(8,128)(2,1)S(1)}, u32[]{:S(2)}, u32[]{:S(2)}) collective-permute-start(bf16[4,48,1152]{2,1,0:T(8,128)(2,1)S(1)} %all-to-all-done.5.refs_0_), channel_id=1, source_target_pairs={{0,1},{1,0},{2,3},{3,2},{4,5},{5,4},{6,7},{7,6},{8,9},{9,8},{10,11... | collective-permute-start | bytes 1327112 | tf_op jit(solution)/shard_map/ppermute | solution.py:473
  550.4 13.6 %collective-permute-start.66 = (bf16[4,48,1152]{2,1,0:T(8,128)(2,1)S(1)}, bf16[4,48,1152]{2,1,0:T(8,128)(2,1)S(1)}, u32[]{:S(2)}, u32[]{:S(2)}) collective-permute-start(bf16[4,48,1152]{2,1,0:T(8,128)(2,1)S(1)} %collective-permute-done.64.refs_1_), channel_id=1, source_target_pairs={{0,1},{1,0},{2,3},{3,2},{4,5},{5,4},{6,7},{7,6},{8,9},{9,8},{10,11... | collective-permute-start | bytes 1327112 | tf_op jit(solution)/shard_map/ppermute | solution.py:473
  (109 other events, 1202.1 us)

commit v5 on v4

--- a/solution.py
+++ b/solution.py
@@ -408,7 +408,7 @@
 def assemble_kernel(xs, widths, s_ref, *refs):
     own_refs, other_refs, out_refs = refs[:xs], refs[xs:2 * xs], refs[2 * xs:]
     zs = own_refs[0].shape[0]
-    x, core = s_ref[0], s_ref[1]
+    x, core, z = s_ref[0], s_ref[1], s_ref[2]
     jx = pl.program_id(0)
     from_x = lax.rem(x - jx + xs, xs)
     first = core == 0
@@ -416,10 +416,11 @@
         @pl.when(from_x == step)
         def copy_piece():
             for jz in range(zs):
+                from_z = lax.rem(z - jz + zs, zs)
                 begin = 0
                 for half, out_ref in zip(widths, out_refs):
-                    own = own_refs[step][jz, :, begin:begin + half].astype(jnp.float32)
-                    other = other_refs[step][jz, :, begin:begin + half].astype(jnp.float32)
+                    own = own_refs[step][from_z, :, begin:begin + half].astype(jnp.float32)
+                    other = other_refs[step][from_z, :, begin:begin + half].astype(jnp.float32)
                     out_ref[0, jz, :, :half] = jnp.where(first, own, other)
                     out_ref[0, jz, :, half:] = jnp.where(first, other, own)
                     begin += half
@@ -522,12 +523,6 @@
     for share in incoming:
         total = total + share.astype(jnp.float32)
     return total
-
-
-def turn_back(values, axis):
-    count, place = lax.axis_size(axis), lax.axis_index(axis)
-    ring = jnp.concatenate([values, values], axis=0)[::-1]
-    return lax.dynamic_slice_in_dim(ring, count - 1 - place, count, 0)
 
 
 def reduce_chain(local, hops, widths):
@@ -552,15 +547,11 @@
         own, incoming = yield own, incoming
         local = add_parts(own, incoming)
     owned = local.astype(jnp.bfloat16)
-    if Z_EXCHANGE:
-        copies = jnp.broadcast_to(owned[None], (lax.axis_size("z"),) + owned.shape)
-        pieces = yield lax.all_to_all(copies, "z", 0, 0)
-    else:
-        owned, incoming = yield owned, [shifted(owned, "z", step) for step in range(1, lax.axis_size("z"))]
-        pieces = turn_back(jnp.stack([owned] + incoming), "z")
+    owned, incoming = yield owned, [shifted(owned, "z", step) for step in range(1, lax.axis_size("z"))]
+    pieces = jnp.stack([owned] + incoming)
     own = yield [pieces] + [shifted(pieces, "x", step) for step in range(1, lax.axis_size("x"))]
     own, other = yield own, [shifted(piece, "core", 1) for piece in own]
-    where = jnp.stack([lax.axis_index(axis) for axis in ("x", "core")]).astype(jnp.int32)
+    where = jnp.stack([lax.axis_index(axis) for axis in ("x", "core", "z")]).astype(jnp.int32)
     return assemble(where, own, other, widths)
 
 

time: 577 us -> 568 us (0.984)
  starting transfers between devices: 98.6 us -> 88.8 us
    all_to_all x3 -> x0, starting transfers between devices: 14 us -> none  [reduce_chain(): pieces = (yield lax.all_to_all(copies, 'z', 0, 0))]
    ppermute x67 -> x76, waiting for transfers between devices: 28 us -> 32.6 us  [shifted(): lax.ppermute(values, axis, [(i, (i + step) % size) for i in range(size)])]
    ppermute x67 -> x76, starting transfers between devices: 71.6 us -> 74.2 us  [shifted(): lax.ppermute(values, axis, [(i, (i + step) % size) for i in range(size)])]
  transfers between devices with their start and end apart: 73 -> 79, of which waited for: 12 -> 9; matrix products, arithmetic and copies ran while one was open for 25% -> 26% of each run, Pallas kernels for 46% -> 47%
where the time goes in v5:
time: 568 us; the launch traced here: 560 us
  Pallas kernels  268 us (47%)
  starting transfers between devices  88.8 us (16%)
  local copies, waits for them, and re-layouts  66.9 us (12%)
  other arithmetic  51.2 us (9%)
  matrix products  49.6 us (9%)
  waiting for transfers between devices  32.6 us (6%)
    ppermute x76, starting transfers between devices, shifted(): lax.ppermute(values, axis, [(i, (i + step) % size) for i in range(size)])  74.2 us
    pallas_call x4, Pallas kernels, attend_back(): pl.pallas_call(functools.partial(backward_kernel, 512), grid=(rows // til...  66.3 us
    pallas_call x5, Pallas kernels, pair_bias(): pl.pallas_call(functools.partial(bias_kernel, 256), grid=(steps,), in_spe...  53.4 us
    pallas_call x4, Pallas kernels, table_grad(): pl.pallas_call(functools.partial(table_grad_kernel, 256), grid=(steps,),...  52.1 us
    pallas_call x1, Pallas kernels, attend(): pl.pallas_call(functools.partial(forward_kernel, 512), grid=(rows // tile...  39.6 us
    dot_general x10, matrix products, dot32(): lax.dot_general(left, right, ((contract[:1], contract[1:]), ((), ())), pr...  33.6 us
    ppermute x76, waiting for transfers between devices, shifted(): lax.ppermute(values, axis, [(i, (i + step) % size) for i in range(size)])  32.6 us
    pallas_call x5, Pallas kernels, place_shards(): pl.pallas_call(functools.partial(place_kernel, steps), grid_spec=pltpu.Pr...  26.7 us
  transfers between devices with their start and end apart: 79, of which 9 were waited for; matrix products, arithmetic and copies ran while one was open for 26% of the time, Pallas kernels for 47%

profile of v5, /device:TPU:1, one launch (start us, length us, event | category | flops | bytes accessed | tf_op | source)
XLA Modules:
  0.0 559.7 jit_solution(16908780399943563770)
XLA Ops:
  2.5 2.7 collective-permute-start.6
  9.8 3.0 collective-permute-done.1
  13.9 2.3 collective-permute-done.2
  28.9 7.3 %pair_bias.5.refs_0_ = bf16[4,2048,2048]{2,1,0:T(8,128)(2,1)} custom-call(f32[256,8]{1,0:T(8,128)} %pad_convert_fusion.q_ref, f32[8,2048]{1,0:T(8,128)} %pad_convert_fusion.1.k_ref, bf16[32,128]{1,0:T(8,128)(2,1)} %fusion.48.w_ref), custom_call_target="tpu_custom_call" | custom-call | flops 1500000000 | bytes 4194304 | tf_op jit(solution)/shard_map/pair_bias/pallas_call | solution.py:103
  40.3 11.5 %pair_bias.6.refs_0_ = bf16[4,2048,2048]{2,1,0:T(8,128)(2,1)} custom-call(f32[256,8]{1,0:T(8,128)} %pad_convert_fusion.q_ref, f32[8,2048]{1,0:T(8,128)} %pad_convert_fusion.1.k_ref, bf16[32,128]{1,0:T(8,128)(2,1)} %fusion.48.w_ref, bf16[4,2048,2048]{2,1,0:T(8,128)(2,1)} %pair_bias.5.refs_0_), custom_call_target="tpu_custom_call", output_to_operand_aliasing={{}: (3, {})} | custom-call | flops 2624999936 | bytes 7340032 | tf_op jit(solution)/shard_map/pair_bias/pallas_call | solution.py:103
  54.0 11.6 %pair_bias.7.refs_0_ = bf16[4,2048,2048]{2,1,0:T(8,128)(2,1)} custom-call(f32[256,8]{1,0:T(8,128)} %pad_convert_fusion.q_ref, f32[8,2048]{1,0:T(8,128)} %pad_convert_fusion.1.k_ref, bf16[32,128]{1,0:T(8,128)(2,1)} %fusion.48.w_ref, bf16[4,2048,2048]{2,1,0:T(8,128)(2,1)} %pair_bias.6.refs_0_), custom_call_target="tpu_custom_call", output_to_operand_aliasing={{}: (3, {})} | custom-call | flops 2624999936 | bytes 7340032 | tf_op jit(solution)/shard_map/pair_bias/pallas_call | solution.py:103
  66.9 1.8 collective-permute-start.16
  70.7 6.5 %collective-permute-start.15 = (bf16[192,768]{1,0:T(8,128)(2,1)}, bf16[192,768]{1,0:T(8,128)(2,1)S(1)}, u32[]{:S(2)}, u32[]{:S(2)}) collective-permute-start(bf16[192,768]{1,0:T(8,128)(2,1)} %collective-permute-done.14.refs_1_), channel_id=1, source_target_pairs={{0,1},{1,0},{2,3},{3,2},{4,5},{5,4},{6,7},{7,6},{8,9},{9,8},{10,11... | collective-permute-start | bytes 884744 | tf_op jit(solution)/shard_map/ppermute | solution.py:474
  81.2 11.5 %pair_bias.8.refs_0_ = bf16[4,2048,2048]{2,1,0:T(8,128)(2,1)} custom-call(f32[256,8]{1,0:T(8,128)} %pad_convert_fusion.q_ref, f32[8,2048]{1,0:T(8,128)} %pad_convert_fusion.1.k_ref, bf16[32,128]{1,0:T(8,128)(2,1)} %fusion.48.w_ref, bf16[4,2048,2048]{2,1,0:T(8,128)(2,1)} %pair_bias.7.refs_0_), custom_call_target="tpu_custom_call", output_to_operand_aliasing={{}: (3, {})} | custom-call | flops 2624999936 | bytes 7340032 | tf_op jit(solution)/shard_map/pair_bias/pallas_call | solution.py:103
  93.4 4.3 place_shards.5
  103.6 11.5 %pair_bias.9.bias_ref = bf16[4,2048,2048]{2,1,0:T(8,128)(2,1)} custom-call(f32[256,8]{1,0:T(8,128)} %pad_convert_fusion.q_ref, f32[8,2048]{1,0:T(8,128)} %pad_convert_fusion.1.k_ref, bf16[32,128]{1,0:T(8,128)(2,1)} %fusion.48.w_ref, bf16[4,2048,2048]{2,1,0:T(8,128)(2,1)} %pair_bias.8.refs_0_), custom_call_target="tpu_custom_call", output_to_operand_aliasing={{}: (3, {})} | custom-call | flops 2624999936 | bytes 7340032 | tf_op jit(solution)/shard_map/pair_bias/pallas_call | solution.py:103
  115.8 5.0 place_shards.6.w_ref
  120.8 1.8 constant_dynamic-update-slice_fusion.4
  127.7 15.3 %project.1 = (bf16[1536,2048]{1,0:T(8,128)(2,1)}, bf16[2048,1024]{1,0:T(8,128)(2,1)}, bf16[2048,1024]{1,0:T(8,128)(2,1)}) custom-call(bf16[2048,768]{1,0:T(8,128)(2,1)} %constant_dynamic-update-slice_fusion.x_ref, bf16[768,1536]{1,0:T(8,128)(2,1)} %place_shards.6.w_ref), custom_call_target="tpu_custom_call" | custom-call | flops 3000000000 | bytes 22020096 | tf_op jit(solution)/shard_map/project/pallas_call | solution.py:140
  143.0 39.6 %attend.1 = (bf16[4,2048,2048]{2,1,0:T(8,128)(2,1)}, f32[4,256,256]{2,1,0:T(8,128)}, f32[4,256,256]{2,1,0:T(8,128)}) custom-call(bf16[4,256,256]{2,1,0:T(8,128)(2,1)} %pad_bitcast_fusion.q_ref, bf16[1536,2048]{1,0:T(8,128)(2,1)} %get-tuple-element.221.kt_ref.vt_ref, bf16[2048,1024]{1,0:T(8,128)(2,1)} %get-tuple-element.222.v_ref, ...), custom_call_target="tpu_custom_call", output_to_operand_aliasing={{0}: (3, {})} | custom-call | flops 11249999872 | bytes 67108864 | tf_op jit(solution)/shard_map/attend/pallas_call | solution.py:208
  190.2 4.4 place_shards.7
  194.7 2.1 fusion.80
  198.1 6.4 %place_shards.8 = bf16[768,3072]{1,0:T(8,128)(2,1)} custom-call(s32[2]{0:T(128)} %pad_add_fusion.s_ref, bf16[384,3072]{1,0:T(8,128)(2,1)} %refs_0_.1, bf16[192,3072]{1,0:T(8,128)(2,1)} %collective-permute-done.21.refs_1_, bf16[192,3072]{1,0:T(8,128)(2,1)} %collective-permute-done.24.refs_2_), custom_call_target="tpu_custom_call" | custom-call | flops 750000000 | bytes 9437184 | tf_op jit(solution)/shard_map/place_shards/pallas_call | solution.py:393
  204.5 5.5 fusion.81
  210.1 6.6 %place_shards.9 = bf16[3072,768]{1,0:T(8,128)(2,1)} custom-call(s32[2]{0:T(128)} %pad_add_fusion.s_ref, bf16[1536,768]{1,0:T(8,128)(2,1)} %refs_0_.2, bf16[768,768]{1,0:T(8,128)(2,1)} %collective-permute-done.22.refs_1_, bf16[768,768]{1,0:T(8,128)(2,1)} %collective-permute-done.25.refs_2_), custom_call_target="tpu_custom_call" | custom-call | flops 750000000 | bytes 9437184 | tf_op jit(solution)/shard_map/place_shards/pallas_call | solution.py:393
  216.7 10.6 %add_convert_fusion.1 = (bf16[256,3072]{1,0:T(8,128)(2,1)S(1)}, f32[256,3072]{1,0:T(8,128)S(1)}) fusion(f32[256,3072]{1,0:T(8,128)} %fusion.81, bf16[256,768]{1,0:T(8,128)(2,1)S(1)} %get-tuple-element.503, bf16[3072,768]{1,0:T(8,128)(2,1)} %place_shards.9), kind=kOutput, calls=%fused_computation.16 | convolution fusion | flops 1264582656 | bytes 12976128 | tf_op jit(solution)/shard_map/dot_general | solution.py:483
  236.5 2.2 fusion.15.do_ref
  240.4 2.8 convolution_convert_fusion.2
  243.5 1.8 dynamic-slice_bitcast_fusion.1
  246.5 3.7 convolution_convert_fusion
  252.2 2.8 fusion.14
  257.3 16.8 %attend_back.4 = (bf16[4,2048,2048]{2,1,0:T(8,128)(2,1)}, f32[1,256,256]{2,1,0:T(8,128)}, bf16[192,2048]{1,0:T(8,128)(2,1)}, bf16[192,2048]{1,0:T(8,128)(2,1)}) custom-call(bf16[4,256,256]{2,1,0:T(8,128)(2,1)} %pad_bitcast_fusion.q_ref, bf16[4,256,256]{2,1,0:T(8,128)(2,1)} %fusion.15.do_ref, ...), custom_call_target="tpu_custom_call", output_to_operand_aliasing={{0}: (5, {})} | custom-call | flops 3500000000 | bytes 16777216 | tf_op jit(solution)/shard_map/attend_back/pallas_call | solution.py:281
  274.2 16.6 %attend_back.5 = (bf16[4,2048,2048]{2,1,0:T(8,128)(2,1)}, f32[1,256,256]{2,1,0:T(8,128)}, bf16[192,2048]{1,0:T(8,128)(2,1)}, bf16[192,2048]{1,0:T(8,128)(2,1)}) custom-call(bf16[4,256,256]{2,1,0:T(8,128)(2,1)} %pad_bitcast_fusion.q_ref, bf16[4,256,256]{2,1,0:T(8,128)(2,1)} %fusion.15.do_ref, ...), custom_call_target="tpu_custom_call", output_to_operand_aliasing={{0}: (5, {})} | custom-call | flops 3500000000 | bytes 16777216 | tf_op jit(solution)/shard_map/attend_back/pallas_call | solution.py:281
  298.8 16.5 %attend_back.6 = (bf16[4,2048,2048]{2,1,0:T(8,128)(2,1)}, f32[1,256,256]{2,1,0:T(8,128)}, bf16[192,2048]{1,0:T(8,128)(2,1)}, bf16[192,2048]{1,0:T(8,128)(2,1)}) custom-call(bf16[4,256,256]{2,1,0:T(8,128)(2,1)} %pad_bitcast_fusion.q_ref, bf16[4,256,256]{2,1,0:T(8,128)(2,1)} %fusion.15.do_ref, ...), custom_call_target="tpu_custom_call", output_to_operand_aliasing={{0}: (5, {})} | custom-call | flops 3500000000 | bytes 16777216 | tf_op jit(solution)/shard_map/attend_back/pallas_call | solution.py:281
  315.3 2.4 add_convert_fusion.3
  317.7 4.3 all-to-all-start
  324.5 16.4 %attend_back.7 = (bf16[4,2048,2048]{2,1,0:T(8,128)(2,1)}, f32[1,256,256]{2,1,0:T(8,128)}, bf16[192,2048]{1,0:T(8,128)(2,1)}, bf16[192,2048]{1,0:T(8,128)(2,1)}) custom-call(bf16[4,256,256]{2,1,0:T(8,128)(2,1)} %pad_bitcast_fusion.q_ref, bf16[4,256,256]{2,1,0:T(8,128)(2,1)} %fusion.15.do_ref, ...), custom_call_target="tpu_custom_call", output_to_operand_aliasing={{0}: (5, {})} | custom-call | flops 3500000000 | bytes 16777216 | tf_op jit(solution)/shard_map/attend_back/pallas_call | solution.py:281
  340.9 2.2 add_convert_fusion.2
  343.1 4.6 all-to-all-start.1
  359.6 5.3 convolution_convert_fusion.1
  365.0 2.2 fusion.9
  368.8 5.3 convolution_convert_fusion.3
  381.1 1.8 reduce_sum.193
  382.9 3.5 collective-permute-start.44
  387.2 2.7 slice.213
  389.9 13.0 %table_grad.4 = f32[256,64]{1,0:T(8,128)} custom-call(f32[256,8]{1,0:T(8,128)} %pad_convert_fusion.q_ref, f32[8,2048]{1,0:T(8,128)} %pad_convert_fusion.1.k_ref, bf16[4,2048,2048]{2,1,0:T(8,128)(2,1)} %get-tuple-element.323.ds_ref), custom_call_target="tpu_custom_call" | custom-call | flops 3200000000 | bytes 8388608 | tf_op jit(solution)/shard_map/table_grad/pallas_call | solution.py:342
  402.9 2.7 slice_bitcast_fusion.2
  406.1 1.9 add_convert_fusion
  409.4 2.5 fusion.71
  412.8 1.9 reduce_sum.194
  414.7 2.1 collective-permute-start.47
  418.9 2.0 pad_maximum_fusion.3.refs_0_
  421.0 13.0 %table_grad.5 = f32[256,64]{1,0:T(8,128)} custom-call(f32[256,8]{1,0:T(8,128)} %pad_convert_fusion.q_ref, f32[8,2048]{1,0:T(8,128)} %pad_convert_fusion.1.k_ref, bf16[4,2048,2048]{2,1,0:T(8,128)(2,1)} %get-tuple-element.323.ds_ref), custom_call_target="tpu_custom_call" | custom-call | flops 3200000000 | bytes 8388608 | tf_op jit(solution)/shard_map/table_grad/pallas_call | solution.py:342
  439.3 13.1 %table_grad.6 = f32[256,64]{1,0:T(8,128)} custom-call(f32[256,8]{1,0:T(8,128)} %pad_convert_fusion.q_ref, f32[8,2048]{1,0:T(8,128)} %pad_convert_fusion.1.k_ref, bf16[4,2048,2048]{2,1,0:T(8,128)(2,1)} %get-tuple-element.323.ds_ref), custom_call_target="tpu_custom_call" | custom-call | flops 3200000000 | bytes 8388608 | tf_op jit(solution)/shard_map/table_grad/pallas_call | solution.py:342
  454.9 2.2 collective-permute-start.52
  461.3 9.7 %collective-permute-done.51 = bf16[256,384]{1,0:T(8,128)(2,1)S(1)} collective-permute-done((bf16[256,384]{1,0:T(8,128)(2,1)S(1)}, bf16[256,384]{1,0:T(8,128)(2,1)S(1)}, u32[]{:S(2)}, u32[]{:S(2)}) %collective-permute-start.51) | collective-permute-done | bytes 196640 | tf_op jit(solution)/shard_map/ppermute | solution.py:474
  473.6 2.8 collective-permute-start.57
  476.4 1.8 add_convert_fusion.4
  478.2 5.7 %all-to-all-start.2 = ((bf16[4,48,1152]{2,1,0:T(8,128)(2,1)}), bf16[4,48,1152]{2,1,0:T(8,128)(2,1)S(1)}, u32[]{:S(2)}, u32[]{:S(2)}) async-start(bf16[4,48,1152]{2,1,0:T(8,128)(2,1)} %add_convert_fusion.4), calls=%async_computation.2 | async-start | bytes 884736 | tf_op jit(solution)/shard_map/all_to_all | solution.py:535
  485.9 13.1 %table_grad.7 = f32[256,64]{1,0:T(8,128)} custom-call(f32[256,8]{1,0:T(8,128)} %pad_convert_fusion.q_ref, f32[8,2048]{1,0:T(8,128)} %pad_convert_fusion.1.k_ref, bf16[4,2048,2048]{2,1,0:T(8,128)(2,1)} %get-tuple-element.323.ds_ref), custom_call_target="tpu_custom_call" | custom-call | flops 3200000000 | bytes 8388608 | tf_op jit(solution)/shard_map/table_grad/pallas_call | solution.py:342
  505.4 3.6 collective-permute-start.72
  513.1 2.6 collective-permute-start.65
  515.8 2.5 collective-permute-start.64
  519.5 2.7 collective-permute-start.68
  522.3 6.1 %collective-permute-done.63 = f32[25,768]{1,0:T(8,128)S(1)} collective-permute-done((f32[25,768]{1,0:T(8,128)S(1)}, f32[25,768]{1,0:T(8,128)S(1)}, u32[]{:S(2)}, u32[]{:S(2)}) %collective-permute-start.63) | collective-permute-done | bytes 76832 | tf_op jit(solution)/shard_map/ppermute | solution.py:474
  532.3 8.7 %collective-permute-done.73.refs_1_ = bf16[4,48,1152]{2,1,0:T(8,128)(2,1)S(1)} collective-permute-done((bf16[4,48,1152]{2,1,0:T(8,128)(2,1)S(1)}, bf16[4,48,1152]{2,1,0:T(8,128)(2,1)S(1)}, u32[]{:S(2)}, u32[]{:S(2)}) %collective-permute-start.73) | collective-permute-done | bytes 442400 | tf_op jit(solution)/shard_map/ppermute | solution.py:474
  544.4 4.7 assemble.3
  549.1 5.5 assemble.4
  555.4 4.1 assemble.5
  (538 shorter events, 143.6 us)
Async XLA Ops:
  2.5 16.4 %collective-permute-start.6 = (s32[2,3]{1,0:T(2,128)}, s32[2,3]{1,0:T(2,128)S(1)}, u32[]{:S(2)}, u32[]{:S(2)}) collective-permute-start(s32[2,3]{1,0:T(2,128)} %param.26), channel_id=1, source_target_pairs={{0,16},{16,0},{1,17},{17,1},{2,18},{18,2},{3,19},{19,3},{4,20},{20... | collective-permute-start | bytes 80 | tf_op jit(solution)/shard_map/ppermute | solution.py:474
  5.2 13.7 %collective-permute-start.4 = (bf16[64,32]{0,1:T(8,128)(2,1)}, bf16[64,32]{0,1:T(8,128)(2,1)S(1)}, u32[]{:S(2)}, u32[]{:S(2)}) collective-permute-start(bf16[64,32]{0,1:T(8,128)(2,1)} %param.31), channel_id=1, source_target_pairs={{0,16},{16,0},{1,17},{17,1},{2,18},{18,2},{3,19},{19,3},{4,20},{20... | collective-permute-start | bytes 12296 | tf_op jit(solution)/shard_map/ppermute | solution.py:474
  6.2 12.6 %collective-permute-start.5 = (bf16[128,768]{1,0:T(8,128)(2,1)S(1)}, bf16[128,768]{1,0:T(8,128)(2,1)S(1)}, u32[]{:S(2)}, u32[]{:S(2)}) collective-permute-start(bf16[128,768]{1,0:T(8,128)(2,1)S(1)} %get-tuple-element.481), channel_id=1, source_target_pairs={{0,1},{1,0},{2,3},{3,2},{4,5},{5,4},{6,7},{7,6},{8,9},{9,8},{10,11... | collective-permute-start | bytes 589832 | tf_op jit(solution)/shard_map/ppermute | solution.py:474
  22.6 13.7 %collective-permute-start.8 = (bf16[7,384]{1,0:T(8,128)(2,1)S(1)}, bf16[7,384]{1,0:T(8,128)(2,1)S(1)}, u32[]{:S(2)}, u32[]{:S(2)}) collective-permute-start(bf16[7,384]{1,0:T(8,128)(2,1)S(1)} %concatenate.100), channel_id=1, source_target_pairs={{0,16},{16,0},{1,17},{17,1},{2,18},{18,2},{3,19},{19,3},{4,20},{20... | collective-permute-start | bytes 16136 | tf_op jit(solution)/shard_map/ppermute | solution.py:474
  23.8 12.5 %collective-permute-start.7 = (f32[3,768]{1,0:T(4,128)S(1)}, f32[3,768]{1,0:T(4,128)S(1)}, u32[]{:S(2)}, u32[]{:S(2)}) collective-permute-start(f32[3,768]{1,0:T(4,128)S(1)} %slice.202), channel_id=1, source_target_pairs={{0,16},{16,0},{1,17},{17,1},{2,18},{18,2},{3,19},{19,3},{4,20},{20... | collective-permute-start | bytes 27656 | tf_op jit(solution)/shard_map/ppermute | solution.py:474
  27.0 41.6 %collective-permute-start.13 = (bf16[192,1536]{1,0:T(8,128)(2,1)}, bf16[192,1536]{1,0:T(8,128)(2,1)}, u32[]{:S(2)}, u32[]{:S(2)}) collective-permute-start(bf16[192,1536]{1,0:T(8,128)(2,1)} %constant_dynamic-slice_fusion.17), channel_id=1, source_target_pairs={{0,16},{16,0},{1,17},{17,1},{2,18},{18,2},{3,19},{19,3},{4,20},{20... | collective-permute-start | bytes 1769480 | tf_op jit(solution)/shard_map/ppermute | solution.py:474
  38.3 13.5 %collective-permute-start.10 = (bf16[256,768]{1,0:T(8,128)(2,1)S(1)}, bf16[256,768]{1,0:T(8,128)(2,1)S(1)}, u32[]{:S(2)}, u32[]{:S(2)}) collective-permute-start(bf16[256,768]{1,0:T(8,128)(2,1)S(1)} %add_convert_fusion.6), channel_id=1, source_target_pairs={{0,2},{2,0},{1,3},{3,1},{4,6},{6,4},{5,7},{7,5},{8,10},{10,8},{9,1... | collective-permute-start | bytes 1179656 | tf_op jit(solution)/shard_map/ppermute | solution.py:474
  39.5 12.3 %collective-permute-start.9 = (bf16[256,768]{1,0:T(8,128)(2,1)S(1)}, bf16[256,768]{1,0:T(8,128)(2,1)}, u32[]{:S(2)}, u32[]{:S(2)}) collective-permute-start(bf16[256,768]{1,0:T(8,128)(2,1)S(1)} %add_convert_fusion.6), channel_id=1, source_target_pairs={{0,4},{4,8},{8,12},{12,0},{1,5},{5,9},{9,13},{13,1},{2,6},{6,10},{... | collective-permute-start | bytes 1179656 | tf_op jit(solution)/shard_map/ppermute | solution.py:474
  51.8 13.9 %collective-permute-start.12 = (bf16[256,768]{1,0:T(8,128)(2,1)}, bf16[256,768]{1,0:T(8,128)(2,1)}, u32[]{:S(2)}, u32[]{:S(2)}) collective-permute-start(bf16[256,768]{1,0:T(8,128)(2,1)} %collective-permute-done.9), channel_id=1, source_target_pairs={{0,2},{2,0},{1,3},{3,1},{4,6},{6,4},{5,7},{7,5},{8,10},{10,8},{9,1... | collective-permute-start | bytes 1179656 | tf_op jit(solution)/shard_map/ppermute | solution.py:474
  52.2 13.5 %collective-permute-start.11 = (bf16[256,768]{1,0:T(8,128)(2,1)}, bf16[256,768]{1,0:T(8,128)(2,1)}, u32[]{:S(2)}, u32[]{:S(2)}) collective-permute-start(bf16[256,768]{1,0:T(8,128)(2,1)} %collective-permute-done.9), channel_id=1, source_target_pairs={{0,4},{4,8},{8,12},{12,0},{1,5},{5,9},{9,13},{13,1},{2,6},{6,10},{... | collective-permute-start | bytes 1179656 | tf_op jit(solution)/shard_map/ppermute | solution.py:474
  53.0 15.7 %collective-permute-start.14 = (bf16[192,768]{1,0:T(8,128)(2,1)S(1)}, bf16[192,768]{1,0:T(8,128)(2,1)}, u32[]{:S(2)}, u32[]{:S(2)}) collective-permute-start(bf16[192,768]{1,0:T(8,128)(2,1)S(1)} %constant_dynamic-slice_fusion.16), channel_id=1, source_target_pairs={{0,16},{16,0},{1,17},{17,1},{2,18},{18,2},{3,19},{19,3},{4,20},{20... | collective-permute-start | bytes 884744 | tf_op jit(solution)/shard_map/ppermute | solution.py:474
  65.7 35.0 %collective-permute-start.17 = (bf16[256,768]{1,0:T(8,128)(2,1)}, bf16[256,768]{1,0:T(8,128)(2,1)}, u32[]{:S(2)}, u32[]{:S(2)}) collective-permute-start(bf16[256,768]{1,0:T(8,128)(2,1)} %collective-permute-done.11), channel_id=1, source_target_pairs={{0,2},{2,0},{1,3},{3,1},{4,6},{6,4},{5,7},{7,5},{8,10},{10,8},{9,1... | collective-permute-start | bytes 1179656 | tf_op jit(solution)/shard_map/ppermute | solution.py:474
  66.9 34.6 %collective-permute-start.16 = (bf16[256,768]{1,0:T(8,128)(2,1)}, bf16[256,768]{1,0:T(8,128)(2,1)}, u32[]{:S(2)}, u32[]{:S(2)}) collective-permute-start(bf16[256,768]{1,0:T(8,128)(2,1)} %collective-permute-done.11), channel_id=1, source_target_pairs={{0,4},{4,8},{8,12},{12,0},{1,5},{5,9},{9,13},{13,1},{2,6},{6,10},{... | collective-permute-start | bytes 1179656 | tf_op jit(solution)/shard_map/ppermute | solution.py:474
  69.5 115.4 %collective-permute-start.20 = (bf16[192,768]{1,0:T(8,128)(2,1)}, bf16[192,768]{1,0:T(8,128)(2,1)}, u32[]{:S(2)}, u32[]{:S(2)}) collective-permute-start(bf16[192,768]{1,0:T(8,128)(2,1)} %constant_dynamic-slice_fusion.15), channel_id=1, source_target_pairs={{0,16},{16,0},{1,17},{17,1},{2,18},{18,2},{3,19},{19,3},{4,20},{20... | collective-permute-start | bytes 884744 | tf_op jit(solution)/shard_map/ppermute | solution.py:474
  70.7 22.0 %collective-permute-start.15 = (bf16[192,768]{1,0:T(8,128)(2,1)}, bf16[192,768]{1,0:T(8,128)(2,1)S(1)}, u32[]{:S(2)}, u32[]{:S(2)}) collective-permute-start(bf16[192,768]{1,0:T(8,128)(2,1)} %collective-permute-done.14.refs_1_), channel_id=1, source_target_pairs={{0,1},{1,0},{2,3},{3,2},{4,5},{5,4},{6,7},{7,6},{8,9},{9,8},{10,11... | collective-permute-start | bytes 884744 | tf_op jit(solution)/shard_map/ppermute | solution.py:474
  77.2 37.8 %collective-permute-start.19 = (bf16[192,1536]{1,0:T(8,128)(2,1)}, bf16[192,1536]{1,0:T(8,128)(2,1)S(1)}, u32[]{:S(2)}, u32[]{:S(2)}) collective-permute-start(bf16[192,1536]{1,0:T(8,128)(2,1)} %collective-permute-done.13.refs_1_), channel_id=1, source_target_pairs={{0,1},{1,0},{2,3},{3,2},{4,5},{5,4},{6,7},{7,6},{8,9},{9,8},{10,11... | collective-permute-start | bytes 1769480 | tf_op jit(solution)/shard_map/ppermute | solution.py:474
  92.7 92.1 %collective-permute-start.22 = (bf16[768,768]{1,0:T(8,128)(2,1)}, bf16[768,768]{1,0:T(8,128)(2,1)}, u32[]{:S(2)}, u32[]{:S(2)}) collective-permute-start(bf16[768,768]{1,0:T(8,128)(2,1)} %constant_dynamic-slice_fusion.13), channel_id=1, source_target_pairs={{0,16},{16,0},{1,17},{17,1},{2,18},{18,2},{3,19},{19,3},{4,20},{20... | collective-permute-start | bytes 3538952 | tf_op jit(solution)/shard_map/ppermute | solution.py:474
  100.7 84.2 %collective-permute-start.21 = (bf16[192,3072]{1,0:T(8,128)(2,1)S(1)}, bf16[192,3072]{1,0:T(8,128)(2,1)}, u32[]{:S(2)}, u32[]{:S(2)}) collective-permute-start(bf16[192,3072]{1,0:T(8,128)(2,1)S(1)} %copy-done.25), channel_id=1, source_target_pairs={{0,16},{16,0},{1,17},{17,1},{2,18},{18,2},{3,19},{19,3},{4,20},{20... | collective-permute-start | bytes 3538952 | tf_op jit(solution)/shard_map/ppermute | solution.py:474
  101.5 19.3 %collective-permute-start.18 = (bf16[256,768]{1,0:T(8,128)(2,1)}, bf16[256,768]{1,0:T(8,128)(2,1)S(1)}, u32[]{:S(2)}, u32[]{:S(2)}) collective-permute-start(bf16[256,768]{1,0:T(8,128)(2,1)} %collective-permute-done.16), channel_id=1, source_target_pairs={{0,2},{2,0},{1,3},{3,1},{4,6},{6,4},{5,7},{7,5},{8,10},{10,8},{9,1... | collective-permute-start | bytes 1179656 | tf_op jit(solution)/shard_map/ppermute | solution.py:474
  187.1 49.0 %collective-permute-start.34 = (bf16[256,768]{0,1:T(8,128)(2,1)}, bf16[256,768]{0,1:T(8,128)(2,1)}, u32[]{:S(2)}, u32[]{:S(2)}) collective-permute-start(bf16[256,768]{0,1:T(8,128)(2,1)} %bitcast.23), channel_id=1, source_target_pairs={{0,1},{1,0},{2,3},{3,2},{4,5},{5,4},{6,7},{7,6},{8,9},{9,8},{10,11... | collective-permute-start | bytes 1179656 | tf_op jit(solution)/shard_map/ppermute | solution.py:474
  187.2 10.9 %collective-permute-start.24 = (bf16[192,3072]{1,0:T(8,128)(2,1)}, bf16[192,3072]{1,0:T(8,128)(2,1)}, u32[]{:S(2)}, u32[]{:S(2)}) collective-permute-start(bf16[192,3072]{1,0:T(8,128)(2,1)} %collective-permute-done.21.refs_1_), channel_id=1, source_target_pairs={{0,1},{1,0},{2,3},{3,2},{4,5},{5,4},{6,7},{7,6},{8,9},{9,8},{10,11... | collective-permute-start | bytes 3538952 | tf_op jit(solution)/shard_map/ppermute | solution.py:474
  187.6 22.5 %collective-permute-start.25 = (bf16[768,768]{1,0:T(8,128)(2,1)}, bf16[768,768]{1,0:T(8,128)(2,1)}, u32[]{:S(2)}, u32[]{:S(2)}) collective-permute-start(bf16[768,768]{1,0:T(8,128)(2,1)} %collective-permute-done.22.refs_1_), channel_id=1, source_target_pairs={{0,1},{1,0},{2,3},{3,2},{4,5},{5,4},{6,7},{7,6},{8,9},{9,8},{10,11... | collective-permute-start | bytes 3538952 | tf_op jit(solution)/shard_map/ppermute | solution.py:474
  189.1 49.6 %collective-permute-start.31 = (bf16[256,384]{1,0:T(8,128)(2,1)}, bf16[256,384]{1,0:T(8,128)(2,1)}, u32[]{:S(2)}, u32[]{:S(2)}) collective-permute-start(bf16[256,384]{1,0:T(8,128)(2,1)} %get-tuple-element.477), channel_id=1, source_target_pairs={{0,1},{1,0},{2,3},{3,2},{4,5},{5,4},{6,7},{7,6},{8,9},{9,8},{10,11... | collective-permute-start | bytes 589832 | tf_op jit(solution)/shard_map/ppermute | solution.py:474
  197.9 40.8 %collective-permute-start.32 = (bf16[256,768]{1,0:T(8,128)(2,1)}, bf16[256,768]{1,0:T(8,128)(2,1)}, u32[]{:S(2)}, u32[]{:S(2)}) collective-permute-start(bf16[256,768]{1,0:T(8,128)(2,1)} %add_convert_fusion.5), channel_id=1, source_target_pairs={{0,1},{1,0},{2,3},{3,2},{4,5},{5,4},{6,7},{7,6},{8,9},{9,8},{10,11... | collective-permute-start | bytes 1179656 | tf_op jit(solution)/shard_map/ppermute | solution.py:474
  245.2 45.5 %collective-permute-start.37 = (bf16[2,4,48,1920]{3,2,1,0:T(8,128)(2,1)}, bf16[2,4,48,1920]{3,2,1,0:T(8,128)(2,1)}, u32[]{:S(2)}, u32[]{:S(2)}) collective-permute-start(bf16[2,4,48,1920]{3,2,1,0:T(8,128)(2,1)} %get-tuple-element.451), channel_id=1, source_target_pairs={{0,2},{2,0},{1,3},{3,1},{4,6},{6,4},{5,7},{7,5},{8,10},{10,8},{9,1... | collective-permute-start | bytes 4423688 | tf_op jit(solution)/shard_map/ppermute | solution.py:474
  251.9 38.9 %collective-permute-start.36 = (bf16[2,4,192,384]{3,2,1,0:T(8,128)(2,1)}, bf16[2,4,192,384]{3,2,1,0:T(8,128)(2,1)}, u32[]{:S(2)}, u32[]{:S(2)}) collective-permute-start(bf16[2,4,192,384]{3,2,1,0:T(8,128)(2,1)} %get-tuple-element.453), channel_id=1, source_target_pairs={{0,16},{16,0},{1,17},{17,1},{2,18},{18,2},{3,19},{19,3},{4,20},{20... | collective-permute-start | bytes 3538952 | tf_op jit(solution)/shard_map/ppermute | solution.py:474
  256.6 121.5 %collective-permute-start.27 = (f32[3,128]{1,0:T(4,128)}, f32[3,128]{1,0:T(4,128)}, u32[]{:S(2)}, u32[]{:S(2)}) collective-permute-start(f32[3,128]{1,0:T(4,128)} %slice.212), channel_id=1, source_target_pairs={{0,1},{1,0},{2,3},{3,2},{4,5},{5,4},{6,7},{7,6},{8,9},{9,8},{10,11... | collective-permute-start | bytes 4616 | tf_op jit(solution)/shard_map/ppermute | solution.py:474
  257.3 122.0 %collective-permute-start.26 = (bf16[128,768]{1,0:T(8,128)(2,1)}, bf16[128,768]{1,0:T(8,128)(2,1)}, u32[]{:S(2)}, u32[]{:S(2)}) collective-permute-start(bf16[128,768]{1,0:T(8,128)(2,1)} %slice.209), channel_id=1, source_target_pairs={{0,1},{1,0},{2,3},{3,2},{4,5},{5,4},{6,7},{7,6},{8,9},{9,8},{10,11... | collective-permute-start | bytes 589832 | tf_op jit(solution)/shard_map/ppermute | solution.py:474
  293.5 21.8 %collective-permute-start.39 = (bf16[4,48,1920]{2,1,0:T(8,128)(2,1)}, bf16[4,48,1920]{2,1,0:T(8,128)(2,1)}, u32[]{:S(2)}, u32[]{:S(2)}) collective-permute-start(bf16[4,48,1920]{2,1,0:T(8,128)(2,1)} %fusion.25), channel_id=1, source_target_pairs={{0,16},{16,0},{1,17},{17,1},{2,18},{18,2},{3,19},{19,3},{4,20},{20... | collective-permute-start | bytes 2211848 | tf_op jit(solution)/shard_map/ppermute | solution.py:474
  297.1 18.2 %collective-permute-start.38 = (bf16[4,192,384]{2,1,0:T(8,128)(2,1)}, bf16[4,192,384]{2,1,0:T(8,128)(2,1)}, u32[]{:S(2)}, u32[]{:S(2)}) collective-permute-start(bf16[4,192,384]{2,1,0:T(8,128)(2,1)} %fusion.28), channel_id=1, source_target_pairs={{0,2},{2,0},{1,3},{3,1},{4,6},{6,4},{5,7},{7,5},{8,10},{10,8},{9,1... | collective-permute-start | bytes 1769480 | tf_op jit(solution)/shard_map/ppermute | solution.py:474
  317.7 25.4 %all-to-all-start = ((bf16[4,192,384]{2,1,0:T(8,128)(2,1)}), bf16[4,192,384]{2,1,0:T(8,128)(2,1)}, u32[]{:S(2)}, u32[]{:S(2)}) async-start(bf16[4,192,384]{2,1,0:T(8,128)(2,1)} %add_convert_fusion.3), calls=%async_computation | async-start | bytes 1179648 | tf_op jit(solution)/shard_map/all_to_all | solution.py:535
  343.1 46.8 %all-to-all-start.1 = ((bf16[4,48,1920]{2,1,0:T(8,128)(2,1)}), bf16[4,48,1920]{2,1,0:T(8,128)(2,1)}, u32[]{:S(2)}, u32[]{:S(2)}) async-start(bf16[4,48,1920]{2,1,0:T(8,128)(2,1)} %add_convert_fusion.2), calls=%async_computation.1 | async-start | bytes 1474560 | tf_op jit(solution)/shard_map/all_to_all | solution.py:535
  367.2 22.7 %collective-permute-start.40 = (bf16[768,1152]{1,0:T(8,128)(2,1)}, bf16[768,1152]{1,0:T(8,128)(2,1)}, u32[]{:S(2)}, u32[]{:S(2)}) collective-permute-start(bf16[768,1152]{1,0:T(8,128)(2,1)} %get-tuple-element.447), channel_id=1, source_target_pairs={{0,1},{1,0},{2,3},{3,2},{4,5},{5,4},{6,7},{7,6},{8,9},{9,8},{10,11... | collective-permute-start | bytes 5308424 | tf_op jit(solution)/shard_map/ppermute | solution.py:474
  377.1 25.8 %collective-permute-start.41 = (bf16[4,256,384]{2,1,0:T(8,128)(2,1)}, bf16[4,256,384]{2,1,0:T(8,128)(2,1)}, u32[]{:S(2)}, u32[]{:S(2)}) collective-permute-start(bf16[4,256,384]{2,1,0:T(8,128)(2,1)} %get-tuple-element.449), channel_id=1, source_target_pairs={{0,2},{2,0},{1,3},{3,1},{4,6},{6,4},{5,7},{7,5},{8,10},{10,8},{9,1... | collective-permute-start | bytes 2359304 | tf_op jit(solution)/shard_map/ppermute | solution.py:474
  382.9 20.0 %collective-permute-start.44 = (bf16[192,384]{1,0:T(8,128)(2,1)}, bf16[192,384]{1,0:T(8,128)(2,1)}, u32[]{:S(2)}, u32[]{:S(2)}) collective-permute-start(bf16[192,384]{1,0:T(8,128)(2,1)} %reduce_sum.193), channel_id=1, source_target_pairs={{0,12},{4,0},{8,4},{12,8},{1,13},{5,1},{9,5},{13,9},{2,14},{6,2},{... | collective-permute-start | bytes 442376 | tf_op jit(solution)/shard_map/ppermute | solution.py:474
  386.4 16.5 %collective-permute-start.43 = (bf16[192,384]{1,0:T(8,128)(2,1)}, bf16[192,384]{1,0:T(8,128)(2,1)}, u32[]{:S(2)}, u32[]{:S(2)}) collective-permute-start(bf16[192,384]{1,0:T(8,128)(2,1)} %reduce_sum.193), channel_id=1, source_target_pairs={{0,8},{4,12},{8,0},{12,4},{1,9},{5,13},{9,1},{13,5},{2,10},{6,14},... | collective-permute-start | bytes 442376 | tf_op jit(solution)/shard_map/ppermute | solution.py:474
  386.4 16.5 %collective-permute-start.42 = (bf16[192,384]{1,0:T(8,128)(2,1)}, bf16[192,384]{1,0:T(8,128)(2,1)}, u32[]{:S(2)}, u32[]{:S(2)}) collective-permute-start(bf16[192,384]{1,0:T(8,128)(2,1)} %reduce_sum.193), channel_id=1, source_target_pairs={{0,4},{4,8},{8,12},{12,0},{1,5},{5,9},{9,13},{13,1},{2,6},{6,10},{... | collective-permute-start | bytes 442376 | tf_op jit(solution)/shard_map/ppermute | solution.py:474
  405.7 31.4 %collective-permute-start.48 = (bf16[4,256,384]{2,1,0:T(8,128)(2,1)}, bf16[4,256,384]{2,1,0:T(8,128)(2,1)}, u32[]{:S(2)}, u32[]{:S(2)}) collective-permute-start(bf16[4,256,384]{2,1,0:T(8,128)(2,1)} %get-tuple-element.459), channel_id=1, source_target_pairs={{0,2},{2,0},{1,3},{3,1},{4,6},{6,4},{5,7},{7,5},{8,10},{10,8},{9,1... | collective-permute-start | bytes 2359304 | tf_op jit(solution)/shard_map/ppermute | solution.py:474
  409.1 27.9 %collective-permute-start.49 = (bf16[2,4,48,1152]{3,2,1,0:T(8,128)(2,1)}, bf16[2,4,48,1152]{3,2,1,0:T(8,128)(2,1)}, u32[]{:S(2)}, u32[]{:S(2)}) collective-permute-start(bf16[2,4,48,1152]{3,2,1,0:T(8,128)(2,1)} %get-tuple-element.455), channel_id=1, source_target_pairs={{0,16},{16,0},{1,17},{17,1},{2,18},{18,2},{3,19},{19,3},{4,20},{20... | collective-permute-start | bytes 2654216 | tf_op jit(solution)/shard_map/ppermute | solution.py:474
  414.7 20.2 %collective-permute-start.47 = (bf16[256,384]{1,0:T(8,128)(2,1)}, bf16[256,384]{1,0:T(8,128)(2,1)S(1)}, u32[]{:S(2)}, u32[]{:S(2)}) collective-permute-start(bf16[256,384]{1,0:T(8,128)(2,1)} %get-tuple-element.470), channel_id=1, source_target_pairs={{0,4},{4,8},{8,12},{12,0},{1,5},{5,9},{9,13},{13,1},{2,6},{6,10},{... | collective-permute-start | bytes 589832 | tf_op jit(solution)/shard_map/ppermute | solution.py:474
  416.8 19.7 %collective-permute-start.46 = (bf16[256,384]{1,0:T(8,128)(2,1)}, bf16[256,384]{1,0:T(8,128)(2,1)S(1)}, u32[]{:S(2)}, u32[]{:S(2)}) collective-permute-start(bf16[256,384]{1,0:T(8,128)(2,1)} %get-tuple-element.471), channel_id=1, source_target_pairs={{0,8},{4,12},{8,0},{12,4},{1,9},{5,13},{9,1},{13,5},{2,10},{6,14},... | collective-permute-start | bytes 589832 | tf_op jit(solution)/shard_map/ppermute | solution.py:474
  417.7 18.8 %collective-permute-start.45 = (bf16[256,384]{1,0:T(8,128)(2,1)}, bf16[256,384]{1,0:T(8,128)(2,1)S(1)}, u32[]{:S(2)}, u32[]{:S(2)}) collective-permute-start(bf16[256,384]{1,0:T(8,128)(2,1)} %get-tuple-element.472), channel_id=1, source_target_pairs={{0,12},{4,0},{8,4},{12,8},{1,13},{5,1},{9,5},{13,9},{2,14},{6,2},{... | collective-permute-start | bytes 589832 | tf_op jit(solution)/shard_map/ppermute | solution.py:474
  435.0 22.9 %collective-permute-start.56 = (bf16[48,1920]{1,0:T(8,128)(2,1)}, bf16[48,1920]{1,0:T(8,128)(2,1)}, u32[]{:S(2)}, u32[]{:S(2)}) collective-permute-start(bf16[48,1920]{1,0:T(8,128)(2,1)} %reduce_sum.194), channel_id=1, source_target_pairs={{0,12},{4,0},{8,4},{12,8},{1,13},{5,1},{9,5},{13,9},{2,14},{6,2},{... | collective-permute-start | bytes 552968 | tf_op jit(solution)/shard_map/ppermute | solution.py:474
  436.5 22.5 %collective-permute-start.55 = (bf16[48,1920]{1,0:T(8,128)(2,1)}, bf16[48,1920]{1,0:T(8,128)(2,1)}, u32[]{:S(2)}, u32[]{:S(2)}) collective-permute-start(bf16[48,1920]{1,0:T(8,128)(2,1)} %reduce_sum.194), channel_id=1, source_target_pairs={{0,8},{4,12},{8,0},{12,4},{1,9},{5,13},{9,1},{13,5},{2,10},{6,14},... | collective-permute-start | bytes 552968 | tf_op jit(solution)/shard_map/ppermute | solution.py:474
  436.5 23.7 %collective-permute-start.54 = (bf16[48,1920]{1,0:T(8,128)(2,1)}, bf16[48,1920]{1,0:T(8,128)(2,1)}, u32[]{:S(2)}, u32[]{:S(2)}) collective-permute-start(bf16[48,1920]{1,0:T(8,128)(2,1)} %reduce_sum.194), channel_id=1, source_target_pairs={{0,4},{4,8},{8,12},{12,0},{1,5},{5,9},{9,13},{13,1},{2,6},{6,10},{... | collective-permute-start | bytes 552968 | tf_op jit(solution)/shard_map/ppermute | solution.py:474
  452.4 18.6 %collective-permute-start.53 = (bf16[4,48,1152]{2,1,0:T(8,128)(2,1)}, bf16[4,48,1152]{2,1,0:T(8,128)(2,1)S(1)}, u32[]{:S(2)}, u32[]{:S(2)}) collective-permute-start(bf16[4,48,1152]{2,1,0:T(8,128)(2,1)} %fusion.32), channel_id=1, source_target_pairs={{0,2},{2,0},{1,3},{3,1},{4,6},{6,4},{5,7},{7,5},{8,10},{10,8},{9,1... | collective-permute-start | bytes 1327112 | tf_op jit(solution)/shard_map/ppermute | solution.py:474
  457.9 13.1 %collective-permute-start.51 = (bf16[256,384]{1,0:T(8,128)(2,1)S(1)}, bf16[256,384]{1,0:T(8,128)(2,1)S(1)}, u32[]{:S(2)}, u32[]{:S(2)}) collective-permute-start(bf16[256,384]{1,0:T(8,128)(2,1)S(1)} %get-tuple-element.468), channel_id=1, source_target_pairs={{0,8},{4,12},{8,0},{12,4},{1,9},{5,13},{9,1},{13,5},{2,10},{6,14},... | collective-permute-start | bytes 589832 | tf_op jit(solution)/shard_map/ppermute | solution.py:474
  458.9 12.1 %collective-permute-start.50 = (bf16[256,384]{1,0:T(8,128)(2,1)S(1)}, bf16[256,384]{1,0:T(8,128)(2,1)S(1)}, u32[]{:S(2)}, u32[]{:S(2)}) collective-permute-start(bf16[256,384]{1,0:T(8,128)(2,1)S(1)} %get-tuple-element.469), channel_id=1, source_target_pairs={{0,12},{4,0},{8,4},{12,8},{1,13},{5,1},{9,5},{13,9},{2,14},{6,2},{... | collective-permute-start | bytes 589832 | tf_op jit(solution)/shard_map/ppermute | solution.py:474
  460.2 38.8 %collective-permute-start.58 = (bf16[4,192,384]{2,1,0:T(8,128)(2,1)}, bf16[4,192,384]{2,1,0:T(8,128)(2,1)}, u32[]{:S(2)}, u32[]{:S(2)}) collective-permute-start(bf16[4,192,384]{2,1,0:T(8,128)(2,1)} %pad_maximum_fusion.3.refs_0_), channel_id=1, source_target_pairs={{0,2},{2,0},{1,3},{3,1},{4,6},{6,4},{5,7},{7,5},{8,10},{10,8},{9,1... | collective-permute-start | bytes 1769480 | tf_op jit(solution)/shard_map/ppermute | solution.py:474
  473.6 30.7 %collective-permute-start.57 = (f32[128,768]{1,0:T(8,128)S(1)}, f32[128,768]{1,0:T(8,128)}, u32[]{:S(2)}, u32[]{:S(2)}) collective-permute-start(f32[128,768]{1,0:T(8,128)S(1)} %slice.225), channel_id=1, source_target_pairs={{0,1},{1,0},{2,3},{3,2},{4,5},{5,4},{6,7},{7,6},{8,9},{9,8},{10,11... | collective-permute-start | bytes 1179656 | tf_op jit(solution)/shard_map/ppermute | solution.py:474
  478.2 20.8 %all-to-all-start.2 = ((bf16[4,48,1152]{2,1,0:T(8,128)(2,1)}), bf16[4,48,1152]{2,1,0:T(8,128)(2,1)S(1)}, u32[]{:S(2)}, u32[]{:S(2)}) async-start(bf16[4,48,1152]{2,1,0:T(8,128)(2,1)} %add_convert_fusion.4), calls=%async_computation.2 | async-start | bytes 884736 | tf_op jit(solution)/shard_map/all_to_all | solution.py:535
  485.2 34.2 %collective-permute-start.67 = (bf16[4,48,1920]{2,1,0:T(8,128)(2,1)S(1)}, bf16[4,48,1920]{2,1,0:T(8,128)(2,1)}, u32[]{:S(2)}, u32[]{:S(2)}) collective-permute-start(bf16[4,48,1920]{2,1,0:T(8,128)(2,1)S(1)} %pad_maximum_fusion.2.refs_0_), channel_id=1, source_target_pairs={{0,2},{2,0},{1,3},{3,1},{4,6},{6,4},{5,7},{7,5},{8,10},{10,8},{9,1... | collective-permute-start | bytes 2211848 | tf_op jit(solution)/shard_map/ppermute | solution.py:474
  505.4 10.4 %collective-permute-start.72 = (bf16[48,1152]{1,0:T(8,128)(2,1)S(1)}, bf16[48,1152]{1,0:T(8,128)(2,1)S(1)}, u32[]{:S(2)}, u32[]{:S(2)}) collective-permute-start(bf16[48,1152]{1,0:T(8,128)(2,1)S(1)} %reduce_sum.204), channel_id=1, source_target_pairs={{0,12},{4,0},{8,4},{12,8},{1,13},{5,1},{9,5},{13,9},{2,14},{6,2},{... | collective-permute-start | bytes 331784 | tf_op jit(solution)/shard_map/ppermute | solution.py:474
  509.0 9.6 %collective-permute-start.71 = (bf16[48,1152]{1,0:T(8,128)(2,1)S(1)}, bf16[48,1152]{1,0:T(8,128)(2,1)S(1)}, u32[]{:S(2)}, u32[]{:S(2)}) collective-permute-start(bf16[48,1152]{1,0:T(8,128)(2,1)S(1)} %reduce_sum.204), channel_id=1, source_target_pairs={{0,8},{4,12},{8,0},{12,4},{1,9},{5,13},{9,1},{13,5},{2,10},{6,14},... | collective-permute-start | bytes 331784 | tf_op jit(solution)/shard_map/ppermute | solution.py:474
  509.0 10.1 %collective-permute-start.70 = (bf16[48,1152]{1,0:T(8,128)(2,1)S(1)}, bf16[48,1152]{1,0:T(8,128)(2,1)S(1)}, u32[]{:S(2)}, u32[]{:S(2)}) collective-permute-start(bf16[48,1152]{1,0:T(8,128)(2,1)S(1)} %reduce_sum.204), channel_id=1, source_target_pairs={{0,4},{4,8},{8,12},{12,0},{1,5},{5,9},{9,13},{13,1},{2,6},{6,10},{... | collective-permute-start | bytes 331784 | tf_op jit(solution)/shard_map/ppermute | solution.py:474
  513.1 28.6 %collective-permute-start.65 = (bf16[4,192,384]{2,1,0:T(8,128)(2,1)}, bf16[4,192,384]{2,1,0:T(8,128)(2,1)S(1)}, u32[]{:S(2)}, u32[]{:S(2)}) collective-permute-start(bf16[4,192,384]{2,1,0:T(8,128)(2,1)} %pad_maximum_fusion.3.refs_0_), channel_id=1, source_target_pairs={{0,1},{1,0},{2,3},{3,2},{4,5},{5,4},{6,7},{7,6},{8,9},{9,8},{10,11... | collective-permute-start | bytes 1769480 | tf_op jit(solution)/shard_map/ppermute | solution.py:474
  518.6 9.8 %collective-permute-start.63 = (f32[25,768]{1,0:T(8,128)S(1)}, f32[25,768]{1,0:T(8,128)S(1)}, u32[]{:S(2)}, u32[]{:S(2)}) collective-permute-start(f32[25,768]{1,0:T(8,128)S(1)} %add.327), channel_id=1, source_target_pairs={{0,8},{4,12},{8,0},{12,4},{1,9},{5,13},{9,1},{13,5},{2,10},{6,14},... | collective-permute-start | bytes 230408 | tf_op jit(solution)/shard_map/ppermute | solution.py:474
  519.1 10.1 %collective-permute-start.62 = (f32[25,768]{1,0:T(8,128)S(1)}, f32[25,768]{1,0:T(8,128)S(1)}, u32[]{:S(2)}, u32[]{:S(2)}) collective-permute-start(f32[25,768]{1,0:T(8,128)S(1)} %add.327), channel_id=1, source_target_pairs={{0,4},{4,8},{8,12},{12,0},{1,5},{5,9},{9,13},{13,1},{2,6},{6,10},{... | collective-permute-start | bytes 230408 | tf_op jit(solution)/shard_map/ppermute | solution.py:474
  519.5 29.6 %collective-permute-start.68 = (bf16[4,48,1920]{2,1,0:T(8,128)(2,1)S(1)}, bf16[4,48,1920]{2,1,0:T(8,128)(2,1)}, u32[]{:S(2)}, u32[]{:S(2)}) collective-permute-start(bf16[4,48,1920]{2,1,0:T(8,128)(2,1)S(1)} %pad_maximum_fusion.2.refs_0_), channel_id=1, source_target_pairs={{0,1},{1,0},{2,3},{3,2},{4,5},{5,4},{6,7},{7,6},{8,9},{9,8},{10,11... | collective-permute-start | bytes 2211848 | tf_op jit(solution)/shard_map/ppermute | solution.py:474
  522.2 21.4 %collective-permute-start.66 = (bf16[4,192,384]{2,1,0:T(8,128)(2,1)}, bf16[4,192,384]{2,1,0:T(8,128)(2,1)S(1)}, u32[]{:S(2)}, u32[]{:S(2)}) collective-permute-start(bf16[4,192,384]{2,1,0:T(8,128)(2,1)} %collective-permute-done.58.refs_1_), channel_id=1, source_target_pairs={{0,1},{1,0},{2,3},{3,2},{4,5},{5,4},{6,7},{7,6},{8,9},{9,8},{10,11... | collective-permute-start | bytes 1769480 | tf_op jit(solution)/shard_map/ppermute | solution.py:474
  528.4 20.7 %collective-permute-start.69 = (bf16[4,48,1920]{2,1,0:T(8,128)(2,1)}, bf16[4,48,1920]{2,1,0:T(8,128)(2,1)}, u32[]{:S(2)}, u32[]{:S(2)}) collective-permute-start(bf16[4,48,1920]{2,1,0:T(8,128)(2,1)} %collective-permute-done.67.refs_1_), channel_id=1, source_target_pairs={{0,1},{1,0},{2,3},{3,2},{4,5},{5,4},{6,7},{7,6},{8,9},{9,8},{10,11... | collective-permute-start | bytes 2211848 | tf_op jit(solution)/shard_map/ppermute | solution.py:474
  529.1 11.8 %collective-permute-start.73 = (bf16[4,48,1152]{2,1,0:T(8,128)(2,1)S(1)}, bf16[4,48,1152]{2,1,0:T(8,128)(2,1)S(1)}, u32[]{:S(2)}, u32[]{:S(2)}) collective-permute-start(bf16[4,48,1152]{2,1,0:T(8,128)(2,1)S(1)} %pad_maximum_fusion.7.refs_0_), channel_id=1, source_target_pairs={{0,2},{2,0},{1,3},{3,1},{4,6},{6,4},{5,7},{7,5},{8,10},{10,8},{9,1... | collective-permute-start | bytes 1327112 | tf_op jit(solution)/shard_map/ppermute | solution.py:474
  540.9 13.7 %collective-permute-start.74 = (bf16[4,48,1152]{2,1,0:T(8,128)(2,1)S(1)}, bf16[4,48,1152]{2,1,0:T(8,128)(2,1)S(1)}, u32[]{:S(2)}, u32[]{:S(2)}) collective-permute-start(bf16[4,48,1152]{2,1,0:T(8,128)(2,1)S(1)} %pad_maximum_fusion.7.refs_0_), channel_id=1, source_target_pairs={{0,1},{1,0},{2,3},{3,2},{4,5},{5,4},{6,7},{7,6},{8,9},{9,8},{10,11... | collective-permute-start | bytes 1327112 | tf_op jit(solution)/shard_map/ppermute | solution.py:474
  541.7 12.9 %collective-permute-start.75 = (bf16[4,48,1152]{2,1,0:T(8,128)(2,1)S(1)}, bf16[4,48,1152]{2,1,0:T(8,128)(2,1)}, u32[]{:S(2)}, u32[]{:S(2)}) collective-permute-start(bf16[4,48,1152]{2,1,0:T(8,128)(2,1)S(1)} %collective-permute-done.73.refs_1_), channel_id=1, source_target_pairs={{0,1},{1,0},{2,3},{3,2},{4,5},{5,4},{6,7},{7,6},{8,9},{9,8},{10,11... | collective-permute-start | bytes 1327112 | tf_op jit(solution)/shard_map/ppermute | solution.py:474
  (115 other events, 1502.4 us)
